TPU v7x, 256 devices: a whole 4x4x8 slice. The times are simulated.
256 devices in a mesh: seq: 32 (over x, z_hi, y), uly: 8 (over z_lo, core).
Axes of the slice: x: 4, y: 4, z: 8 (z_hi: 2, z_lo: 4; z = z_hi * 4 + z_lo), core: 2. Of those that a mesh axis runs over, the one named last changes fastest.
Arguments:
- queries: bfloat16 [32768, 3072], P(('seq', 'uly')), may hold values from -6 to 6
- keys: bfloat16 [32768, 3072], P(('seq', 'uly')), may hold values from -6 to 6
- values: bfloat16 [32768, 3072], P(('seq', 'uly')), may hold values from -6 to 6
- cotangent: bfloat16 [32768, 3072], P(('seq', 'uly')), may hold values from -6 to 6
- doc_ids: int32 [32768], replicated, may hold values from 0 to 63, never falling along the last dimension, each value on 1 to 1024 neighbouring positions
Outputs:
- attended: bfloat16 [32768, 3072], P(('seq', 'uly'))
- grad_queries: bfloat16 [32768, 3072], P(('seq', 'uly'))
- grad_keys: bfloat16 [32768, 3072], P(('seq', 'uly'))
- grad_values: bfloat16 [32768, 3072], P(('seq', 'uly'))
Inputs may be any that keep to these rules, and one draw needn't show every extreme that they name: `doc_ids`: no document has more than 1024 tokens; some document has exactly 1024.
All inputs are finite; a program needn't handle non-finite values.
Results may differ from a plain program's by a relative error of at most 0.034.
Values may be sent and summed in bfloat16 or wider, within the bound.
No kernel may reach another device: no remote copies, remote signals or barrier semaphores. Data moves between devices by JAX's collectives and lax.ppermute only.
A program may use at most 128 MiB of HBM per device.

v0:
```python
import math

import jax
import jax.numpy as jnp
from jax import lax
from jax.sharding import PartitionSpec as P

HEAD_DIM = 96


NEG = -1e30


def passed_along(value, axis, by):
    devices = lax.axis_size(axis)
    pairs = [(i, i + by) for i in range(devices) if 0 <= i + by < devices]
    return lax.ppermute(value, axis, pairs)


def tile_forward(query_tile, key_w, value_w, allowed, scaling):
    scores = (
        jnp.einsum("qhd,khd->hqk", query_tile, key_w, preferred_element_type=jnp.float32) * scaling
    )
    scores = jnp.where(allowed[None], scores, NEG)
    row_max = jnp.max(scores, axis=2)
    log_total = row_max + jnp.log(jnp.sum(jnp.exp(scores - row_max[:, :, None]), axis=2))
    weights_b = jnp.where(allowed[None], jnp.exp(scores - log_total[:, :, None]), 0.0).astype(
        jnp.bfloat16
    )
    out_tile = jnp.einsum("hqk,khd->qhd", weights_b, value_w, preferred_element_type=jnp.float32)
    return (out_tile.astype(jnp.bfloat16), log_total, weights_b)


def tile_backward(query_tile, grad_tile, weights_b, row_delta, key_w, value_w):
    grad_prob = jnp.einsum("qhd,khd->hqk", grad_tile, value_w, preferred_element_type=jnp.float32)
    dscore = (weights_b * (grad_prob - row_delta[:, :, None])).astype(jnp.bfloat16)
    grad_q = jnp.einsum("hqk,khd->qhd", dscore, key_w, preferred_element_type=jnp.float32)
    grad_k = jnp.einsum("hqk,qhd->khd", dscore, query_tile, preferred_element_type=jnp.float32)
    grad_v = jnp.einsum("hqk,qhd->khd", weights_b, grad_tile, preferred_element_type=jnp.float32)
    return (grad_q, grad_k, grad_v)


def shards(queries, keys, values, cotangent, doc_ids):
    scaling = 1.0 / math.sqrt(HEAD_DIM)
    q_heads, k_heads, v_heads, g_heads = (
        lax.all_to_all(queries, "uly", split_axis=1, concat_axis=0, tiled=True),
        lax.all_to_all(keys, "uly", split_axis=1, concat_axis=0, tiled=True),
        lax.all_to_all(values, "uly", split_axis=1, concat_axis=0, tiled=True),
        lax.all_to_all(cotangent, "uly", split_axis=1, concat_axis=0, tiled=True),
    )
    prev_k, prev_v = passed_along((k_heads, v_heads), "seq", 1)
    block_len = q_heads.shape[0]
    half_len = block_len // 2

    def shaped(array):
        return array.reshape(block_len, -1, HEAD_DIM)

    own_q, own_k, own_v, own_g = (
        shaped(q_heads),
        shaped(k_heads),
        shaped(v_heads),
        shaped(g_heads),
    )
    local_heads = own_q.shape[1]
    key_cat = jnp.concatenate([shaped(prev_k), own_k], 0)
    value_cat = jnp.concatenate([shaped(prev_v), own_v], 0)
    seq_index = lax.axis_index("seq")
    own_docs = lax.dynamic_slice_in_dim(doc_ids, seq_index * block_len, block_len)
    prev_docs = jnp.where(
        seq_index > 0,
        lax.dynamic_slice_in_dim(doc_ids, jnp.maximum(seq_index - 1, 0) * block_len, block_len),
        -1,
    )
    cat_docs = jnp.concatenate([prev_docs, own_docs])
    positions = jnp.arange(2 * block_len)

    def tile_rows(array, tile):
        return array[tile * half_len : (tile + 1) * half_len]

    key_from = 0
    key_parts = jnp.zeros((2 * block_len, local_heads, HEAD_DIM), jnp.float32)
    value_parts = jnp.zeros((2 * block_len, local_heads, HEAD_DIM), jnp.float32)
    out_tiles = []
    stat_tiles = []
    delta_tiles = []
    query_tiles = []
    for tile in range(2):
        tile_first_row = tile * half_len
        tile_finish = (tile + 3) * half_len
        query_tile = tile_rows(own_q, tile)
        grad_tile = tile_rows(own_g, tile)
        low = block_len + tile * half_len
        row_pos = positions[low : low + half_len]
        col_pos = positions[tile_first_row:tile_finish]
        same_doc = (
            cat_docs[low : low + half_len][:, None] == cat_docs[tile_first_row:tile_finish][None, :]
        )
        out_tile, log_tile, weights_b = tile_forward(
            query_tile,
            key_cat[tile_first_row:tile_finish],
            value_cat[tile_first_row:tile_finish],
            same_doc & (col_pos[None, :] <= row_pos[:, None]),
            scaling,
        )
        delta_tile = jnp.sum(out_tile.astype(jnp.float32) * grad_tile.astype(jnp.float32), axis=2).T
        start = max(key_from, tile_first_row)
        grad_q, grad_k, grad_v = tile_backward(
            query_tile,
            grad_tile,
            weights_b,
            delta_tile,
            key_cat[start:tile_finish],
            value_cat[start:tile_finish],
        )
        result = (out_tile, log_tile, delta_tile, grad_q, grad_k, grad_v)
        out_tiles.append(result[0])
        stat_tiles.append(result[1])
        delta_tiles.append(result[2])
        query_tiles.append(result[3])
        key_parts = key_parts.at[tile * half_len : (tile + 3) * half_len].add(result[4])
        value_parts = value_parts.at[tile * half_len : (tile + 3) * half_len].add(result[5])
    out_heads = jnp.concatenate(out_tiles, 0)
    query_sum = jnp.concatenate(query_tiles, 0)
    attended = lax.all_to_all(
        out_heads.reshape(block_len, -1), "uly", split_axis=0, concat_axis=1, tiled=True
    )
    back_k, back_v = (
        passed_along(
            key_parts[:block_len].reshape(block_len, -1).astype(jnp.bfloat16), "seq", -1
        ).astype(jnp.float32),
        passed_along(
            value_parts[:block_len].reshape(block_len, -1).astype(jnp.bfloat16), "seq", -1
        ).astype(jnp.float32),
    )
    key_sum = key_parts[block_len:] + shaped(back_k)
    value_sum = value_parts[block_len:] + shaped(back_v)
    grad_q_b = (query_sum * scaling).astype(jnp.bfloat16).reshape(block_len, -1)
    grad_k_b = (key_sum * scaling).astype(jnp.bfloat16).reshape(block_len, -1)
    grad_v_b = value_sum.astype(jnp.bfloat16).reshape(block_len, -1)
    grad_queries, grad_keys, grad_values = (
        lax.all_to_all(grad_q_b, "uly", split_axis=0, concat_axis=1, tiled=True),
        lax.all_to_all(grad_k_b, "uly", split_axis=0, concat_axis=1, tiled=True),
        lax.all_to_all(grad_v_b, "uly", split_axis=0, concat_axis=1, tiled=True),
    )
    return (attended, grad_queries, grad_keys, grad_values)


def solution(mesh):
    return jax.shard_map(
        shards,
        mesh=mesh,
        in_specs=(
            P(("seq", "uly"), None),
            P(("seq", "uly"), None),
            P(("seq", "uly"), None),
            P(("seq", "uly"), None),
            P(),
        ),
        out_specs=(
            P(("seq", "uly"), None),
            P(("seq", "uly"), None),
            P(("seq", "uly"), None),
            P(("seq", "uly"), None),
        ),
        check_vma=False,
    )
```

profile of v0, /device:TPU:4, one launch (start us, length us, event | category | flops | bytes accessed | tf_op | source)
XLA Modules:
  0.0 361.9 jit_solution(852389021848919783)
XLA Ops:
  0.7 2.4 copy.64
  3.1 5.9 %all-to-all-start.4 = ((bf16[128,8,384]{0,2,1:T(8,128)(2,1)}), bf16[128,8,384]{0,2,1:T(8,128)(2,1)S(1)}, u32[]{:S(2)}, u32[]{:S(2)}) async-start(bf16[128,8,384]{0,2,1:T(8,128)(2,1)} %bitcast.18), calls=%async_computation.4 | async-start | bytes 1572864 | tf_op jit(solution)/shard_map/all_to_all | solution.py:49
  10.1 19.8 %all-to-all-done.4 = bf16[128,8,384]{0,2,1:T(8,128)(2,1)S(1)} async-done(((bf16[128,8,384]{0,2,1:T(8,128)(2,1)}), bf16[128,8,384]{0,2,1:T(8,128)(2,1)S(1)}, u32[]{:S(2)}, u32[]{:S(2)}) %all-to-all-start.4) | async-done | bytes 786464 | tf_op jit(solution)/shard_map/all_to_all | solution.py:49
  29.9 3.5 all-to-all-start.2
  34.7 19.7 %all-to-all-done.2 = bf16[128,8,384]{0,2,1:T(8,128)(2,1)S(1)} async-done(((bf16[128,8,384]{0,2,1:T(8,128)(2,1)}), bf16[128,8,384]{0,2,1:T(8,128)(2,1)S(1)}, u32[]{:S(2)}, u32[]{:S(2)}) %all-to-all-start.2) | async-done | bytes 786464 | tf_op jit(solution)/shard_map/all_to_all | solution.py:46
  54.4 3.5 all-to-all-start.1
  59.9 19.0 %all-to-all-done.1 = bf16[128,8,384]{0,2,1:T(8,128)(2,1)S(1)} async-done(((bf16[128,8,384]{0,2,1:T(8,128)(2,1)}), bf16[128,8,384]{0,2,1:T(8,128)(2,1)S(1)}, u32[]{:S(2)}, u32[]{:S(2)}) %all-to-all-start.1) | async-done | bytes 786464 | tf_op jit(solution)/shard_map/all_to_all | solution.py:47
  78.8 3.5 all-to-all-start
  83.6 3.5 collective-permute-start.1
  87.1 1.6 compare_and_fusion
  88.7 1.9 fusion.26
  92.9 1.9 fusion.27
  95.8 1.9 slice.185
  99.2 2.2 reshape.328
  101.3 1.9 all-to-all-done
  107.0 2.3 copy.51
  109.3 3.7 %collective-permute-start = (bf16[1024,384]{1,0:T(8,128)(2,1)}, bf16[1024,384]{1,0:T(8,128)(2,1)}, u32[]{:S(2)}, u32[]{:S(2)}) collective-permute-start(bf16[1024,384]{1,0:T(8,128)(2,1)} %bitcast.154), channel_id=1, source_target_pairs={{0,8},{8,16},{16,24},{24,32},{32,40},{40,48},{48,56},{56,64},{64,7... | collective-permute-start | bytes 2359304 | tf_op jit(solution)/shard_map/ppermute | solution.py:17
  115.2 2.2 copy.59
  117.4 1.9 slice.177
  119.3 18.3 %collective-permute-done.1 = bf16[1024,384]{1,0:T(8,128)(2,1)} collective-permute-done((bf16[1024,384]{1,0:T(8,128)(2,1)}, bf16[1024,384]{1,0:T(8,128)(2,1)}, u32[]{:S(2)}, u32[]{:S(2)}) %collective-permute-start.1) | collective-permute-done | bytes 786464 | tf_op jit(solution)/shard_map/ppermute | solution.py:17
  137.5 2.3 copy.56
  139.8 4.1 %fusion.3 = (f32[4,512]{1,0:T(4,128)S(1)}, f32[4,1536,512]{2,1,0:T(8,128)S(1)}) fusion(pred[512,1536]{0,1:T(8,128)(4,1)S(1)} %get-tuple-element.82, bf16[512,4,96]{0,2,1:T(8,128)(2,1)} %slice.185, bf16[1024,4,96]{0,2,1:T(8,128)(2,1)} %reshape.328, bf16[1024,4,96]{0,2,1:T(8,128)(2,1)} %bitcast.134), kind=kOutput, calls=%fused_computation.11 | convolution fusion | flops 615774208 | bytes 15343616 | tf_op jit(solution)/shard_map/qhd,khd->hqk/dot_general | solution.py:22
  143.9 2.8 exponential_reduce_fusion
  146.8 4.9 %select_convert_fusion = bf16[4,512,1536]{1,2,0:T(8,128)(2,1)} fusion(f32[4,1536,512]{2,1,0:T(8,128)S(1)} %get-tuple-element.71, f32[4,512]{1,0:T(4,128)S(1)} %log_add_fusion, pred[512,1536]{0,1:T(8,128)(4,1)S(1)} %get-tuple-element.82), kind=kLoop, calls=%fused_computation.6 | loop fusion | flops 15728640 | bytes 19668992 | tf_op jit(solution)/shard_map/convert_element_type | solution.py:27
  151.7 2.6 fusion.2
  154.3 2.8 exponential_reduce_fusion.1
  157.2 4.8 %select_convert_fusion.1 = bf16[4,512,1536]{1,2,0:T(8,128)(2,1)} fusion(f32[4,1536,512]{2,1,0:T(8,128)S(1)} %get-tuple-element.73, f32[4,512]{1,0:T(4,128)S(1)} %log_add_fusion.1, pred[512,1536]{0,1:T(8,128)(4,1)S(1)} %get-tuple-element.83), kind=kLoop, calls=%fused_computation.8 | loop fusion | flops 15728640 | bytes 19668992 | tf_op jit(solution)/shard_map/convert_element_type | solution.py:27
  162.0 22.7 %collective-permute-done = bf16[1024,384]{1,0:T(8,128)(2,1)} collective-permute-done((bf16[1024,384]{1,0:T(8,128)(2,1)}, bf16[1024,384]{1,0:T(8,128)(2,1)}, u32[]{:S(2)}, u32[]{:S(2)}) %collective-permute-start) | collective-permute-done | bytes 786464 | tf_op jit(solution)/shard_map/ppermute | solution.py:17
  186.1 4.3 %multiply_reduce_fusion = (f32[512,4]{0,1:T(4,128)S(1)}, bf16[512,4,96]{0,2,1:T(8,128)(2,1)S(1)}) fusion(bf16[512,4,96]{0,2,1:T(8,128)(2,1)S(1)} %slice.189, bf16[4,512,1536]{1,2,0:T(8,128)(2,1)} %select_convert_fusion, bf16[1024,4,96]{0,2,1:T(8,128)(2,1)S(1)} %reshape.326, bf16[1024,4,96]{0,2,1:T(8,128)(2,1)S(1)} %bitcast.130), kind=kOutput, calls=%fused_computation.42 | convolution fusion | flops 607320064 | bytes 8658944 | tf_op jit(solution)/shard_map/hqk,khd->qhd/dot_general | solution.py:30
  193.5 4.6 %all-to-all-start.3 = ((bf16[8,128,384]{1,2,0:T(8,128)(2,1)}), bf16[8,128,384]{1,2,0:T(8,128)(2,1)}, u32[]{:S(2)}, u32[]{:S(2)}) async-start(bf16[8,128,384]{1,2,0:T(8,128)(2,1)} %copy.63), calls=%async_computation.3 | async-start | bytes 1572864 | tf_op jit(solution)/shard_map/all_to_all | solution.py:124
  198.1 4.9 %fusion = bf16[4,512,1536]{1,2,0:T(8,128)(2,1)S(1)} fusion(bf16[4,512,1536]{1,2,0:T(8,128)(2,1)} %select_convert_fusion, bf16[512,4,96]{0,2,1:T(8,128)(2,1)S(1)} %slice.189, f32[4,512]{1,0:T(4,128)S(1)} %bitcast.159, bf16[1024,4,96]{0,2,1:T(8,128)(2,1)S(1)} %reshape.326, bf16[1024,4,96]{0,2,1:T(8,128)(2,1)} %bitcast.132), kind=kOutput, calls=%fused_computation.1 | convolution fusion | flops 618921984 | bytes 14557184 | tf_op jit(solution)/shard_map/qhd,khd->hqk/dot_general | solution.py:35
  203.1 2.1 fusion.1
  206.8 1.5 copy-done.2
  210.8 4.8 %convolution_bitcast_fusion.3 = f32[1536,4,96]{0,2,1:T(8,128)S(1)} fusion(bf16[4,512,1536]{1,2,0:T(8,128)(2,1)} %copy-done.2, bf16[512,4,96]{0,2,1:T(8,128)(2,1)S(1)} %copy-done.19), kind=kOutput, calls=%fused_computation.19 | convolution fusion | flops 603979776 | bytes 9043968 | tf_op jit(solution)/shard_map/hqk,qhd->khd/dot_general | solution.py:38
  218.8 4.5 %all-to-all-start.5 = ((bf16[8,128,384]{2,1,0:T(8,128)(2,1)}), bf16[8,128,384]{2,1,0:T(8,128)(2,1)}, u32[]{:S(2)}, u32[]{:S(2)}) async-start(bf16[8,128,384]{2,1,0:T(8,128)(2,1)} %bitcast.28), calls=%async_computation.5 | async-start | bytes 1572864 | tf_op jit(solution)/shard_map/all_to_all | solution.py:141
  223.3 6.5 %constant_dynamic-update-slice_fusion.1 = (bf16[2048,4,96]{0,2,1:T(8,128)(2,1)}, f32[1536,4,96]{0,2,1:T(8,128)S(1)}) fusion(bf16[2048,4,96]{0,2,1:T(8,128)(2,1)} %scatter-add.14, bf16[4,512,1536]{1,2,0:T(8,128)(2,1)} %copy-done.1, bf16[512,4,96]{0,2,1:T(8,128)(2,1)S(1)} %copy-done.21, f32[1536,4,96]{0,2,1:T(8,128)} %copy-done.5), kind=kOutput, calls=%fused_computation.56 | convolution fusion | flops 604569600 | bytes 13762560 | tf_op jit(solution)/shard_map/hqk,qhd->khd/dot_general | solution.py:38
  231.0 1.9 collective-permute-start.2
  233.0 2.0 convolution_bitcast_fusion.1
  236.5 34.3 %collective-permute-done.2 = bf16[1024,384]{0,1:T(8,128)(2,1)S(1)} collective-permute-done((bf16[1024,384]{0,1:T(8,128)(2,1)S(1)}, bf16[1024,384]{0,1:T(8,128)(2,1)S(1)}, u32[]{:S(2)}, u32[]{:S(2)}) %collective-permute-start.2) | collective-permute-done | bytes 786464 | tf_op jit(solution)/shard_map/ppermute | solution.py:17
  272.3 5.8 %all-to-all-done.5 = bf16[8,128,384]{2,1,0:T(8,128)(2,1)} async-done(((bf16[8,128,384]{2,1,0:T(8,128)(2,1)}), bf16[8,128,384]{2,1,0:T(8,128)(2,1)}, u32[]{:S(2)}, u32[]{:S(2)}) %all-to-all-start.5) | async-done | bytes 786464 | tf_op jit(solution)/shard_map/all_to_all | solution.py:141
  278.1 3.5 all-to-all-start.6
  281.7 5.9 %constant_dynamic-update-slice_fusion = (bf16[2048,4,96]{0,2,1:T(8,128)(2,1)}, f32[1536,4,96]{0,2,1:T(8,128)S(1)}) fusion(bf16[2048,4,96]{0,2,1:T(8,128)(2,1)} %scatter-add.16, bf16[4,512,1536]{1,2,0:T(8,128)(2,1)} %select_convert_fusion, bf16[512,4,96]{0,2,1:T(8,128)(2,1)S(1)} %slice.189, f32[1536,4,96]{0,2,1:T(8,128)S(1)} %copy-done.4), kind=kOutput, calls=%fused_computation.55 | convolution fusion | flops 604569600 | bytes 13762560 | tf_op jit(solution)/shard_map/hqk,qhd->khd/dot_general | solution.py:39
  288.7 6.8 %collective-permute-start.3 = (bf16[1024,384]{0,1:T(8,128)(2,1)S(1)}, bf16[1024,384]{0,1:T(8,128)(2,1)S(1)}, u32[]{:S(2)}, u32[]{:S(2)}) collective-permute-start(bf16[1024,384]{0,1:T(8,128)(2,1)S(1)} %bitcast.156), channel_id=1, source_target_pairs={{8,0},{16,8},{24,16},{32,24},{40,32},{48,40},{56,48},{64,56},{72,6... | collective-permute-start | bytes 2359304 | tf_op jit(solution)/shard_map/ppermute | solution.py:17
  295.5 18.3 %collective-permute-done.3 = bf16[1024,384]{0,1:T(8,128)(2,1)S(1)} collective-permute-done((bf16[1024,384]{0,1:T(8,128)(2,1)S(1)}, bf16[1024,384]{0,1:T(8,128)(2,1)S(1)}, u32[]{:S(2)}, u32[]{:S(2)}) %collective-permute-start.3) | collective-permute-done | bytes 786464 | tf_op jit(solution)/shard_map/ppermute | solution.py:17
  315.3 21.0 %all-to-all-done.6 = bf16[8,128,384]{1,2,0:T(8,128)(2,1)S(1)} async-done(((bf16[8,128,384]{1,2,0:T(8,128)(2,1)}), bf16[8,128,384]{1,2,0:T(8,128)(2,1)S(1)}, u32[]{:S(2)}, u32[]{:S(2)}) %all-to-all-start.6) | async-done | bytes 786464 | tf_op jit(solution)/shard_map/all_to_all | solution.py:142
  336.3 3.5 all-to-all-start.7
  339.8 2.3 copy.77
  345.9 14.8 %all-to-all-done.7 = bf16[8,128,384]{1,2,0:T(8,128)(2,1)S(1)} async-done(((bf16[8,128,384]{1,2,0:T(8,128)(2,1)}), bf16[8,128,384]{1,2,0:T(8,128)(2,1)S(1)}, u32[]{:S(2)}, u32[]{:S(2)}) %all-to-all-start.7) | async-done | bytes 786464 | tf_op jit(solution)/shard_map/all_to_all | solution.py:143
  (104 shorter events, 39.4 us)
Async XLA Ops:
  0.6 8.3 %copy-start.22 = (bf16[128,3072]{1,0:T(8,128)(2,1)S(1)}, bf16[128,3072]{1,0:T(8,128)(2,1)}, u32[]{:S(2)}) copy-start(bf16[128,3072]{1,0:T(8,128)(2,1)} %param.13) | copy-start | bytes 2359300
  0.6 32.9 %copy-start.23 = (bf16[128,3072]{1,0:T(8,128)(2,1)S(1)}, bf16[128,3072]{1,0:T(8,128)(2,1)}, u32[]{:S(2)}) copy-start(bf16[128,3072]{1,0:T(8,128)(2,1)} %param.14) | copy-start | bytes 2359300
  3.1 26.9 %all-to-all-start.4 = ((bf16[128,8,384]{0,2,1:T(8,128)(2,1)}), bf16[128,8,384]{0,2,1:T(8,128)(2,1)S(1)}, u32[]{:S(2)}, u32[]{:S(2)}) async-start(bf16[128,8,384]{0,2,1:T(8,128)(2,1)} %bitcast.18), calls=%async_computation.4 | async-start | bytes 1572864 | tf_op jit(solution)/shard_map/all_to_all | solution.py:49
  9.0 49.0 %copy-start.24 = (bf16[128,3072]{1,0:T(8,128)(2,1)S(1)}, bf16[128,3072]{1,0:T(8,128)(2,1)}, u32[]{:S(2)}) copy-start(bf16[128,3072]{1,0:T(8,128)(2,1)} %param.15) | copy-start | bytes 2359300
  29.9 29.2 %copy-start.16 = (bf16[128,8,384]{0,2,1:T(8,128)(2,1)}, bf16[128,8,384]{0,2,1:T(8,128)(2,1)S(1)}, u32[]{:S(2)}) copy-start(bf16[128,8,384]{0,2,1:T(8,128)(2,1)S(1)} %all-to-all-done.4) | copy-start | bytes 2359300
  29.9 24.5 %all-to-all-start.2 = ((bf16[128,8,384]{0,2,1:T(8,128)(2,1)}), bf16[128,8,384]{0,2,1:T(8,128)(2,1)S(1)}, u32[]{:S(2)}, u32[]{:S(2)}) async-start(bf16[128,8,384]{0,2,1:T(8,128)(2,1)} %bitcast.10), calls=%async_computation.2 | async-start | bytes 1572864 | tf_op jit(solution)/shard_map/all_to_all | solution.py:46
  54.4 29.2 %copy-start.17 = (bf16[128,8,384]{0,2,1:T(8,128)(2,1)}, bf16[128,8,384]{0,2,1:T(8,128)(2,1)S(1)}, u32[]{:S(2)}) copy-start(bf16[128,8,384]{0,2,1:T(8,128)(2,1)S(1)} %all-to-all-done.2) | copy-start | bytes 2359300
  54.4 24.5 %all-to-all-start.1 = ((bf16[128,8,384]{0,2,1:T(8,128)(2,1)}), bf16[128,8,384]{0,2,1:T(8,128)(2,1)S(1)}, u32[]{:S(2)}, u32[]{:S(2)}) async-start(bf16[128,8,384]{0,2,1:T(8,128)(2,1)} %bitcast.5), calls=%async_computation.1 | async-start | bytes 1572864 | tf_op jit(solution)/shard_map/all_to_all | solution.py:47
  78.8 24.5 %all-to-all-start = ((bf16[128,8,384]{0,2,1:T(8,128)(2,1)}), bf16[128,8,384]{0,2,1:T(8,128)(2,1)S(1)}, u32[]{:S(2)}, u32[]{:S(2)}) async-start(bf16[128,8,384]{0,2,1:T(8,128)(2,1)} %bitcast.142), calls=%async_computation | async-start | bytes 1572864 | tf_op jit(solution)/shard_map/all_to_all | solution.py:48
  83.6 53.9 %collective-permute-start.1 = (bf16[1024,384]{1,0:T(8,128)(2,1)}, bf16[1024,384]{1,0:T(8,128)(2,1)}, u32[]{:S(2)}, u32[]{:S(2)}) collective-permute-start(bf16[1024,384]{1,0:T(8,128)(2,1)} %bitcast.7), channel_id=1, source_target_pairs={{0,8},{8,16},{16,24},{24,32},{32,40},{40,48},{48,56},{56,64},{64,7... | collective-permute-start | bytes 2359304 | tf_op jit(solution)/shard_map/ppermute | solution.py:17
  99.2 13.8 %copy-start.20 = (bf16[4,128,384]{1,2,0:T(8,128)(2,1)S(1)}, bf16[4,128,384]{1,2,0:T(8,128)(2,1)}, u32[]{:S(2)}) copy-start(bf16[4,128,384]{1,2,0:T(8,128)(2,1)} %get-tuple-element.60) | copy-start | bytes 1179652
  103.3 0.9 copy-start.12
  109.3 75.4 %collective-permute-start = (bf16[1024,384]{1,0:T(8,128)(2,1)}, bf16[1024,384]{1,0:T(8,128)(2,1)}, u32[]{:S(2)}, u32[]{:S(2)}) collective-permute-start(bf16[1024,384]{1,0:T(8,128)(2,1)} %bitcast.154), channel_id=1, source_target_pairs={{0,8},{8,16},{16,24},{24,32},{32,40},{40,48},{48,56},{56,64},{64,7... | collective-permute-start | bytes 2359304 | tf_op jit(solution)/shard_map/ppermute | solution.py:17
  115.2 75.2 %copy-start.13 = (bf16[512,4,96]{0,2,1:T(8,128)(2,1)}, bf16[512,4,96]{0,2,1:T(8,128)(2,1)S(1)}, u32[]{:S(2)}) copy-start(bf16[512,4,96]{0,2,1:T(8,128)(2,1)S(1)} %slice.187) | copy-start | bytes 1179652
  146.7 5.0 %copy-start.8 = (bf16[1024,4,96]{0,2,1:T(8,128)(2,1)S(1)}, bf16[1024,4,96]{0,2,1:T(8,128)(2,1)}, u32[]{:S(2)}) copy-start(bf16[1024,4,96]{0,2,1:T(8,128)(2,1)} %reshape.328) | copy-start | bytes 2359300
  146.7 5.0 %copy-start.10 = (bf16[1024,384]{0,1:T(8,128)(2,1)S(1)}, bf16[1024,384]{0,1:T(8,128)(2,1)}, u32[]{:S(2)}) copy-start(bf16[1024,384]{0,1:T(8,128)(2,1)} %copy.56) | copy-start | bytes 2359300
  146.7 4.9 %copy-start.18 = (bf16[512,4,96]{0,2,1:T(8,128)(2,1)S(1)}, bf16[512,4,96]{0,2,1:T(8,128)(2,1)}, u32[]{:S(2)}) copy-start(bf16[512,4,96]{0,2,1:T(8,128)(2,1)} %slice.177) | copy-start | bytes 1179652
  186.1 4.3 %copy-start.6 = (bf16[1024,384]{0,1:T(8,128)(2,1)}, bf16[1024,384]{0,1:T(8,128)(2,1)S(1)}, u32[]{:S(2)}) copy-start(bf16[1024,384]{0,1:T(8,128)(2,1)S(1)} %copy.52) | copy-start | bytes 2359300
  186.1 4.9 %copy-start = (bf16[4,512,1536]{1,2,0:T(8,128)(2,1)S(1)}, bf16[4,512,1536]{1,2,0:T(8,128)(2,1)}, u32[]{:S(2)}) copy-start(bf16[4,512,1536]{1,2,0:T(8,128)(2,1)} %select_convert_fusion.1) | copy-start | bytes 18874372
  193.5 9.5 %slice-start = ((s8[6291456]{0:T(1024)(128)(4,1)}), s8[2097152]{0:T(1024)(128)(4,1)S(1)}, s32[]{:S(2)}) async-start(s8[6291456]{0:T(1024)(128)(4,1)} %bitcast.126), calls=%async_computation.8 | async-start | bytes 4194304
  193.5 25.3 %all-to-all-start.3 = ((bf16[8,128,384]{1,2,0:T(8,128)(2,1)}), bf16[8,128,384]{1,2,0:T(8,128)(2,1)}, u32[]{:S(2)}, u32[]{:S(2)}) async-start(bf16[8,128,384]{1,2,0:T(8,128)(2,1)} %copy.63), calls=%async_computation.3 | async-start | bytes 1572864 | tf_op jit(solution)/shard_map/all_to_all | solution.py:124
  198.1 5.0 %slice-start.1 = ((s8[6291456]{0:T(1024)(128)(4,1)}), s8[4194304]{0:T(1024)(128)(4,1)S(1)}, s32[]{:S(2)}) async-start(s8[6291456]{0:T(1024)(128)(4,1)} %bitcast.126), calls=%async_computation.9 | async-start | bytes 8388608
  198.1 5.0 %copy-start.7 = (bf16[1024,384]{0,1:T(8,128)(2,1)S(1)}, bf16[1024,384]{0,1:T(8,128)(2,1)}, u32[]{:S(2)}) copy-start(bf16[1024,384]{0,1:T(8,128)(2,1)} %copy-done.6) | copy-start | bytes 2359300
  198.1 5.0 %copy-start.14 = (bf16[512,4,96]{0,2,1:T(8,128)(2,1)S(1)}, bf16[512,4,96]{0,2,1:T(8,128)(2,1)}, u32[]{:S(2)}) copy-start(bf16[512,4,96]{0,2,1:T(8,128)(2,1)} %copy-done.13) | copy-start | bytes 1179652
  203.0 2.7 copy-start.1
  203.1 2.6 copy-start.9
  203.1 2.6 copy-start.11
  205.7 2.7 copy-start.2
  209.5 1.3 copy-start.19
  215.6 1.5 copy-start.5
  217.0 6.3 %copy-start.21 = (bf16[512,4,96]{0,2,1:T(8,128)(2,1)S(1)}, bf16[512,4,96]{0,2,1:T(8,128)(2,1)}, u32[]{:S(2)}) copy-start(bf16[512,4,96]{0,2,1:T(8,128)(2,1)} %slice.185) | copy-start | bytes 1179652
  218.8 14.1 %slice-start.2 = ((s8[6291456]{0:T(1024)(128)(4,1)}), s8[2097152]{0:T(1024)(128)(4,1)S(1)}, s32[]{:S(2)}) async-start(s8[6291456]{0:T(1024)(128)(4,1)} %bitcast.128), calls=%async_computation.10 | async-start | bytes 4194304
  218.8 59.3 %all-to-all-start.5 = ((bf16[8,128,384]{2,1,0:T(8,128)(2,1)}), bf16[8,128,384]{2,1,0:T(8,128)(2,1)}, u32[]{:S(2)}, u32[]{:S(2)}) async-start(bf16[8,128,384]{2,1,0:T(8,128)(2,1)} %bitcast.28), calls=%async_computation.5 | async-start | bytes 1572864 | tf_op jit(solution)/shard_map/all_to_all | solution.py:141
  223.3 9.7 %slice-start.3 = ((s8[6291456]{0:T(1024)(128)(4,1)}), s8[4194304]{0:T(1024)(128)(4,1)S(1)}, s32[]{:S(2)}) async-start(s8[6291456]{0:T(1024)(128)(4,1)} %bitcast.128), calls=%async_computation.11 | async-start | bytes 8388608
  223.3 9.7 %copy-start.15 = (bf16[512,4,96]{0,2,1:T(8,128)(2,1)S(1)}, bf16[512,4,96]{0,2,1:T(8,128)(2,1)}, u32[]{:S(2)}) copy-start(bf16[512,4,96]{0,2,1:T(8,128)(2,1)} %copy-done.13) | copy-start | bytes 1179652
  231.0 39.8 %collective-permute-start.2 = (bf16[1024,384]{0,1:T(8,128)(2,1)S(1)}, bf16[1024,384]{0,1:T(8,128)(2,1)S(1)}, u32[]{:S(2)}, u32[]{:S(2)}) collective-permute-start(bf16[1024,384]{0,1:T(8,128)(2,1)S(1)} %bitcast.155), channel_id=1, source_target_pairs={{8,0},{16,8},{24,16},{32,24},{40,32},{48,40},{56,48},{64,56},{72,6... | collective-permute-start | bytes 2359304 | tf_op jit(solution)/shard_map/ppermute | solution.py:17
  235.0 36.0 %copy-start.3 = (f32[1536,4,96]{0,2,1:T(8,128)}, f32[1536,4,96]{0,2,1:T(8,128)S(1)}, u32[]{:S(2)}) copy-start(f32[1536,4,96]{0,2,1:T(8,128)S(1)} %convolution_bitcast_fusion.1) | copy-start | bytes 7077892
  271.1 10.6 %copy-start.4 = (f32[1536,4,96]{0,2,1:T(8,128)S(1)}, f32[1536,4,96]{0,2,1:T(8,128)}, u32[]{:S(2)}) copy-start(f32[1536,4,96]{0,2,1:T(8,128)} %copy-done.3) | copy-start | bytes 7077892
  278.1 58.2 %all-to-all-start.6 = ((bf16[8,128,384]{1,2,0:T(8,128)(2,1)}), bf16[8,128,384]{1,2,0:T(8,128)(2,1)S(1)}, u32[]{:S(2)}, u32[]{:S(2)}) async-start(bf16[8,128,384]{1,2,0:T(8,128)(2,1)} %copy.73), calls=%async_computation.6 | async-start | bytes 1572864 | tf_op jit(solution)/shard_map/all_to_all | solution.py:142
  288.7 25.1 %collective-permute-start.3 = (bf16[1024,384]{0,1:T(8,128)(2,1)S(1)}, bf16[1024,384]{0,1:T(8,128)(2,1)S(1)}, u32[]{:S(2)}, u32[]{:S(2)}) collective-permute-start(bf16[1024,384]{0,1:T(8,128)(2,1)S(1)} %bitcast.156), channel_id=1, source_target_pairs={{8,0},{16,8},{24,16},{32,24},{40,32},{48,40},{56,48},{64,56},{72,6... | collective-permute-start | bytes 2359304 | tf_op jit(solution)/shard_map/ppermute | solution.py:17
  336.3 24.5 %all-to-all-start.7 = ((bf16[8,128,384]{1,2,0:T(8,128)(2,1)}), bf16[8,128,384]{1,2,0:T(8,128)(2,1)S(1)}, u32[]{:S(2)}, u32[]{:S(2)}) async-start(bf16[8,128,384]{1,2,0:T(8,128)(2,1)} %copy.76), calls=%async_computation.7 | async-start | bytes 1572864 | tf_op jit(solution)/shard_map/all_to_all | solution.py:143
where the time goes:
time: 364 us; the launch traced here: 362 us
  waiting for transfers between devices  196 us (54%)
  local copies, waits for them, and re-layouts  57 us (16%)
  starting transfers between devices  48.5 us (13%)
  matrix products  40.6 us (11%)
  other arithmetic  18.5 us (5%)
    ppermute x4, waiting for transfers between devices, passed_along(): return lax.ppermute(value, axis, pairs)  93.6 us
    all_to_all x1, waiting for transfers between devices, shards(): lax.all_to_all(grad_k_b, 'uly', split_axis=0, concat_axis=1, tiled=True)  21 us
    all_to_all x1, waiting for transfers between devices, shards(): lax.all_to_all(cotangent, 'uly', split_axis=1, concat_axis=0, tiled=True)  19.8 us
    all_to_all x1, waiting for transfers between devices, shards(): lax.all_to_all(queries, 'uly', split_axis=1, concat_axis=0, tiled=True)  19.7 us
    all_to_all x1, waiting for transfers between devices, shards(): lax.all_to_all(keys, 'uly', split_axis=1, concat_axis=0, tiled=True)  19 us
    unnamed x69, local copies, waits for them, and re-layouts  17.2 us
    ppermute x4, starting transfers between devices, passed_along(): return lax.ppermute(value, axis, pairs)  15.8 us
    slice x10, local copies, waits for them, and re-layouts, tile_rows(): return array[tile * half_len:(tile + 1) * half_len]  15.3 us
  transfers between devices with their start and end apart: 12, of which 12 were waited for; matrix products, arithmetic and copies ran while one was open for 27% of the time, Pallas kernels for 0%

commit v1 on v0

v1 whole, which is shorter than its diff:
```python
import functools
import math

import jax
import jax.numpy as jnp
from jax import lax
from jax.experimental import pallas as pl
from jax.experimental.pallas import tpu as pltpu
from jax.sharding import Mesh
from jax.sharding import PartitionSpec as P

HEAD_DIM = 96
HEADS = 32
CHUNK = 128
CHUNKS = 32
HALO = 8
DOCS = 64
GROUP = CHUNK * CHUNKS
AHEAD = CHUNK * HALO
WINDOW = GROUP + AHEAD
TILE = 256
TILES = GROUP // TILE
AHEAD_TILES = AHEAD // TILE
REACH = AHEAD_TILES + 1
NEG = -1e30
SCALE = 1.0 / math.sqrt(HEAD_DIM)
LOG2E = 1.4426950408889634
VMEM_LIMIT = 56 * 1024 * 1024

AXES = ("x", "zh", "y", "zl", "c")
GROUP_AXES = ("y", "zl", "c")
F32 = jnp.float32
BF16 = jnp.bfloat16


def vmem():
    return pl.BlockSpec(memory_space=pltpu.VMEM)


def smem():
    return pl.BlockSpec(memory_space=pltpu.SMEM)


def pack_kernel(mirror_ref, *refs):
    sources, out_ref = refs[:-1], refs[-1]
    mirrored = mirror_ref[0]
    for n, ref in enumerate(sources):
        turned = ref[...].T
        for zl in range(4):
            slot = 2 * jnp.where(mirrored == 1, 3 - zl, zl)
            piece = turned[zl * 192 : (zl + 1) * 192]
            out_ref[pl.ds(slot, 2), n] = piece.reshape(2, HEAD_DIM, CHUNK)


def pack(mirror, *arrays):
    count = len(arrays)
    return pl.pallas_call(
        pack_kernel,
        grid=(4,),
        in_specs=[smem()] + [pl.BlockSpec((CHUNK, 768), lambda y: (0, y))] * count,
        out_specs=pl.BlockSpec((8, count, HEAD_DIM, CHUNK), lambda y: (y, 0, 0, 0)),
        out_shape=jax.ShapeDtypeStruct((HEADS, count, HEAD_DIM, CHUNK), BF16),
        compiler_params=pltpu.CompilerParams(vmem_limit_bytes=VMEM_LIMIT),
        name="pack",
    )(mirror, *arrays)


def unpack_kernel(mirror_ref, in_ref, *out_refs):
    mirrored = mirror_ref[0]
    for n, out_ref in enumerate(out_refs):
        pieces = []
        for zl in range(4):
            slot = 2 * jnp.where(mirrored == 1, 3 - zl, zl)
            pieces.append(in_ref[pl.ds(slot, 2), n].reshape(192, CHUNK))
        out_ref[...] = jnp.concatenate(pieces, 0).T


def unpack(mirror, array):
    count = array.shape[1]
    return pl.pallas_call(
        unpack_kernel,
        grid=(4,),
        in_specs=[
            smem(),
            pl.BlockSpec((8, count, HEAD_DIM, CHUNK), lambda y: (y, 0, 0, 0)),
        ],
        out_specs=[pl.BlockSpec((CHUNK, 768), lambda y: (0, y))] * count,
        out_shape=[jax.ShapeDtypeStruct((CHUNK, HEADS * HEAD_DIM), BF16)] * count,
        compiler_params=pltpu.CompilerParams(vmem_limit_bytes=VMEM_LIMIT),
        name="unpack",
    )(mirror, array)


def tile_of(ref, n, i):
    return jnp.concatenate([ref[2 * i, n], ref[2 * i + 1, n]], 1)


def nn(a, b):
    return lax.dot_general(a, b, (((1,), (0,)), ((), ())), preferred_element_type=F32)


def nt(a, b):
    return lax.dot_general(a, b, (((1,), (1,)), ((), ())), preferred_element_type=F32)


def fill(halo_ref, own_ref, n, flat, turned):
    for chunk in range(HALO + CHUNKS):
        piece = halo_ref[chunk, n] if chunk < HALO else own_ref[chunk - HALO, n]
        if turned is not None:
            turned[:, chunk * CHUNK : (chunk + 1) * CHUNK] = piece
        if flat is not None:
            flat[chunk * CHUNK : (chunk + 1) * CHUNK, :] = piece.T


def allowed_in(start, first, diagonal):
    row = lax.broadcasted_iota(jnp.int32, (TILE, TILE), 0)
    ok = row >= start - first
    if diagonal:
        ok = ok & (row <= lax.broadcasted_iota(jnp.int32, (TILE, TILE), 1))
    return ok


def per_tile(tile_start_ref, i, body):
    reach = jnp.clip(i + REACH - tile_start_ref[i], 1, REACH)
    for count in range(1, REACH + 1):
        pl.when(reach == count)(functools.partial(body, count))


def forward_kernel(
    tile_start_ref, start_ref, kvq_ref, halo_ref, out_ref, stat_ref, key_flat, value_turned
):
    fill(halo_ref, kvq_ref, 0, key_flat, None)
    fill(halo_ref, kvq_ref, 1, None, value_turned)

    def tile(i, _):
        def body(count):
            q = tile_of(kvq_ref, 2, i)
            start = start_ref[pl.ds(i, 1), :]
            scores = []
            top = None
            for j in range(count):
                first = pl.multiple_of((i + REACH - count + j) * TILE, TILE)
                s = nn(key_flat[pl.ds(first, TILE), :], q)
                s = jnp.where(allowed_in(start, first, j == count - 1), s, NEG)
                scores.append(s)
                t = jnp.max(s, axis=0, keepdims=True)
                top = t if top is None else jnp.maximum(top, t)
            shift = top * (SCALE * LOG2E)
            total = None
            out = None
            for j in range(count):
                first = pl.multiple_of((i + REACH - count + j) * TILE, TILE)
                e = jnp.exp2(scores[j] * (SCALE * LOG2E) - shift)
                t = jnp.sum(e, axis=0, keepdims=True)
                total = t if total is None else total + t
                o = nn(value_turned[:, pl.ds(first, TILE)], e.astype(BF16))
                out = o if out is None else out + o
            out = (out / total).astype(BF16)
            out_ref[2 * i, 0] = out[:, :CHUNK]
            out_ref[2 * i + 1, 0] = out[:, CHUNK:]
            stat_ref[pl.ds(i, 1), :] = shift + jnp.log2(total)

        per_tile(tile_start_ref, i, body)
        return 0

    lax.fori_loop(0, TILES, tile, 0)


def forward(tile_start, start, kvq, halo):
    return pl.pallas_call(
        forward_kernel,
        in_specs=[smem(), vmem(), vmem(), vmem()],
        out_specs=[vmem(), vmem()],
        out_shape=[
            jax.ShapeDtypeStruct((CHUNKS, 1, HEAD_DIM, CHUNK), BF16),
            jax.ShapeDtypeStruct((TILES, TILE), F32),
        ],
        scratch_shapes=[
            pltpu.VMEM((WINDOW, HEAD_DIM), BF16),
            pltpu.VMEM((HEAD_DIM, WINDOW), BF16),
        ],
        compiler_params=pltpu.CompilerParams(vmem_limit_bytes=VMEM_LIMIT),
        cost_estimate=pl.CostEstimate(
            flops=2 * 2 * 2560 * GROUP * 256, bytes_accessed=8 << 20, transcendentals=GROUP * 1280
        ),
        name="forward",
    )(tile_start, start, kvq, halo)


def backward_tiles(
    tile_start_ref, start_ref, kvq_ref, g_ref, out_ref, stat_ref, grads_ref,
    key_flat, key_turned, value_flat, key_sum, value_sum, low, high
):
    def tile(i, _):
        def body(count):
            q = tile_of(kvq_ref, 2, i)
            g = tile_of(g_ref, 0, i)
            o = tile_of(out_ref, 0, i)
            delta = jnp.sum(o.astype(F32) * g.astype(F32), axis=0, keepdims=True)
            start = start_ref[pl.ds(i, 1), :]
            stat = stat_ref[pl.ds(i, 1), :]
            grad_q = None
            for j in range(count):
                first = pl.multiple_of((i + REACH - count + j) * TILE, TILE)
                span = pl.ds(first, TILE)
                s = nn(key_flat[span, :], q)
                p = jnp.exp2(s * (SCALE * LOG2E) - stat)
                p = jnp.where(allowed_in(start, first, j == count - 1), p, 0.0)
                p_b = p.astype(BF16)
                grad_p = nn(value_flat[span, :], g)
                d = (p * (grad_p - delta)).astype(BF16)
                t = nn(key_turned[:, span], d)
                grad_q = t if grad_q is None else grad_q + t
                key_sum[:, span] += nt(q, d)
                value_sum[:, span] += nt(g, p_b)
            grad_q = (grad_q * SCALE).astype(BF16)
            grads_ref[2 * i, 2] = grad_q[:, :CHUNK]
            grads_ref[2 * i + 1, 2] = grad_q[:, CHUNK:]

        per_tile(tile_start_ref, i, body)
        return 0

    lax.fori_loop(low, high, tile, 0)


def backward_kernel(
    tile_start_ref, start_ref, kvq_ref, halo_ref, g_ref, out_ref, stat_ref,
    grads_ref, back_ref, rest_ref, key_flat, key_turned, value_flat, key_sum, value_sum
):
    fill(halo_ref, kvq_ref, 0, key_flat, key_turned)
    fill(halo_ref, kvq_ref, 1, value_flat, None)
    key_sum[...] = jnp.zeros_like(key_sum)
    value_sum[...] = jnp.zeros_like(value_sum)
    backward_tiles(
        tile_start_ref, start_ref, kvq_ref, g_ref, out_ref, stat_ref, grads_ref,
        key_flat, key_turned, value_flat, key_sum, value_sum, 0, TILES
    )
    for n, (sums, factor) in enumerate(((key_sum, SCALE), (value_sum, 1.0))):
        for chunk in range(HALO + CHUNKS):
            piece = sums[:, chunk * CHUNK : (chunk + 1) * CHUNK] * factor
            if chunk < HALO:
                back_ref[chunk, n] = piece.astype(BF16)
            else:
                grads_ref[chunk - HALO, n] = piece.astype(BF16)
            if chunk >= CHUNKS:
                rest_ref[chunk - CHUNKS, n] = piece


def backward(tile_start, start, kvq, halo, g, out, stat):
    return pl.pallas_call(
        backward_kernel,
        in_specs=[smem()] + [vmem()] * 6,
        out_specs=[vmem()] * 3,
        out_shape=[
            jax.ShapeDtypeStruct((CHUNKS, 3, HEAD_DIM, CHUNK), BF16),
            jax.ShapeDtypeStruct((HALO, 2, HEAD_DIM, CHUNK), BF16),
            jax.ShapeDtypeStruct((HALO, 2, HEAD_DIM, CHUNK), F32),
        ],
        scratch_shapes=[
            pltpu.VMEM((WINDOW, HEAD_DIM), BF16),
            pltpu.VMEM((HEAD_DIM, WINDOW), BF16),
            pltpu.VMEM((WINDOW, HEAD_DIM), BF16),
            pltpu.VMEM((HEAD_DIM, WINDOW), F32),
            pltpu.VMEM((HEAD_DIM, WINDOW), F32),
        ],
        compiler_params=pltpu.CompilerParams(vmem_limit_bytes=VMEM_LIMIT),
        cost_estimate=pl.CostEstimate(
            flops=2 * 5 * 2560 * GROUP * 256, bytes_accessed=12 << 20, transcendentals=GROUP * 1280
        ),
        name="backward",
    )(tile_start, start, kvq, halo, g, out, stat)


def join_kernel(back_ref, rest_ref, _, out_ref):
    out_ref[...] = (rest_ref[...] + back_ref[...].astype(F32)).astype(BF16)


def join(back, rest, grads):
    whole = (HALO, 2, HEAD_DIM, CHUNK)
    return pl.pallas_call(
        join_kernel,
        grid=(1,),
        in_specs=[
            pl.BlockSpec(whole, lambda i: (0, 0, 0, 0)),
            pl.BlockSpec(whole, lambda i: (0, 0, 0, 0)),
            pl.BlockSpec(memory_space=pl.ANY),
        ],
        out_specs=pl.BlockSpec(whole, lambda i: (CHUNKS // HALO - 1, 0, 0, 0)),
        out_shape=jax.ShapeDtypeStruct(grads.shape, BF16),
        input_output_aliases={2: 0},
        name="join",
    )(back, rest, grads)


def group_pairs():
    def index(x, zh, y, zl, c):
        return (((x * 2 + zh) * 4 + y) * 4 + zl) * 2 + c

    pairs = []
    for group in range(7):
        for y in range(4):
            for zl in range(4):
                for c in range(2):
                    pairs.append(
                        (
                            index(group // 2, group % 2, y, zl, c),
                            index((group + 1) // 2, (group + 1) % 2, y, 3 - zl, c),
                        )
                    )
    return pairs


def to_heads(array):
    return lax.all_to_all(array, GROUP_AXES, split_axis=0, concat_axis=0, tiled=True)


def places(doc_ids):
    group = lax.axis_index("x") * 2 + lax.axis_index("zh")
    own = lax.dynamic_slice_in_dim(doc_ids, group * GROUP, GROUP)
    ahead = lax.dynamic_slice_in_dim(doc_ids, jnp.maximum(group * GROUP - AHEAD, 0), AHEAD)
    ahead = jnp.where(group > 0, ahead, -1)
    docs = jnp.arange(DOCS, dtype=jnp.int32)[:, None]
    first = jnp.sum((own[None] < docs).astype(jnp.int32), 1) + jnp.sum(
        (ahead[None] < docs).astype(jnp.int32), 1
    )
    start = jnp.sum(jnp.where(own[None] == docs, first[:, None], 0), 0)
    start = start.reshape(TILES, TILE)
    return start[:, 0] // TILE, start


def shards(queries, keys, values, cotangent, doc_ids):
    mirror = lax.axis_index("zh").astype(jnp.int32).reshape(1)
    kvq = to_heads(pack(mirror, keys, values, queries))
    g = to_heads(pack(mirror, cotangent))
    tile_start, start = places(doc_ids)
    pairs = group_pairs()
    halo = lax.ppermute(kvq[CHUNKS - HALO :, :2], AXES, pairs)
    out, stat = forward(tile_start, start, kvq, halo)
    grads, back, rest = backward(tile_start, start, kvq, halo, g, out, stat)
    back = lax.ppermute(back, AXES, [(b, a) for a, b in pairs])
    grads = join(back, rest, grads)
    (attended,) = unpack(mirror, to_heads(out))
    grad_k, grad_v, grad_q = unpack(mirror, to_heads(grads))
    return attended, grad_q, grad_k, grad_v


def solution(mesh):
    wide = Mesh(mesh.devices.reshape(4, 2, 4, 4, 2), AXES)
    rows = P(AXES, None)
    return jax.shard_map(
        shards,
        mesh=wide,
        in_specs=(rows, rows, rows, rows, P()),
        out_specs=(rows, rows, rows, rows),
        check_vma=False,
    )
```

time: 364 us -> 241 us (0.66)
  waiting for transfers between devices: 196 us -> 137 us
  local copies, waits for them, and re-layouts: 57 us -> 5.49 us
  Pallas kernels: 0 us -> 51 us
  matrix products: 40.6 us -> 0 us
  other arithmetic: 18.5 us -> 2.47 us
  starting transfers between devices: 48.5 us -> 40.7 us
    ppermute x4 -> x2, waiting for transfers between devices: 93.6 us -> 33 us  [the longest x1 18 us: shards(): back = lax.ppermute(back, AXES, [(b, a) for a, b in pairs])]
    pallas_call x0 -> x7, Pallas kernels: none -> 51 us  [the longest x1 20.7 us: backward(): pl.pallas_call(backward_kernel, in_specs=[smem()] + [vmem()] * 6, out_spe...]
    dot_general x12 -> x0, matrix products: 40.6 us -> none  [the longest x2 11.3 us: tile_backward(): jnp.einsum('hqk,qhd->khd', dscore, query_tile, preferred_element_type=jnp...]
    slice x13 -> x2, local copies, waits for them, and re-layouts: 17.7 us -> 0.14 us  [the longest x1 0.11 us: places(): return (start[:, 0] // TILE, start)]
    unnamed x69 -> x12, local copies, waits for them, and re-layouts: 17.2 us -> 3.91 us
    all_to_all x8 -> x0, local copies, waits for them, and re-layouts: 10.8 us -> none  [the longest x2 3.68 us: shards(): lax.all_to_all(values, 'uly', split_axis=1, concat_axis=0, tiled=True)]
    convert_element_type x5 -> x0, other arithmetic: 10.4 us -> none  [the longest x2 9.77 us: tile_forward(): jnp.where(allowed[None], jnp.exp(scores - log_total[:, :, None]), 0.0)]
    reduce_sum x2 -> x3, other arithmetic: 5.61 us -> 1.18 us  [the longest x1 0.84 us: places(): start = jnp.sum(jnp.where(own[None] == docs, first[:, None], 0), 0)]
  transfers between devices with their start and end apart: 12 -> 6, of which waited for: 12 -> 4; matrix products, arithmetic and copies ran while one was open for 27% -> 2% of each run, Pallas kernels for 0% -> 18%
where the time goes in v1:
time: 241 us; the launch traced here: 237 us
  waiting for transfers between devices  137 us (57%)
  Pallas kernels  51 us (21%)
  starting transfers between devices  40.7 us (17%)
  local copies, waits for them, and re-layouts  5.49 us (2%)
  other arithmetic  2.47 us (1%)
    all_to_all x4, waiting for transfers between devices, to_heads(): lax.all_to_all(array, GROUP_AXES, split_axis=0, concat_axis=0, tiled=True)  104 us
    all_to_all x4, starting transfers between devices, to_heads(): lax.all_to_all(array, GROUP_AXES, split_axis=0, concat_axis=0, tiled=True)  28.5 us
    pallas_call x1, Pallas kernels, backward(): pl.pallas_call(backward_kernel, in_specs=[smem()] + [vmem()] * 6, out_spe...  20.7 us
    ppermute x1, waiting for transfers between devices, shards(): back = lax.ppermute(back, AXES, [(b, a) for a, b in pairs])  18 us
    ppermute x1, waiting for transfers between devices, shards(): halo = lax.ppermute(kvq[CHUNKS - HALO:, :2], AXES, pairs)  14.9 us
    pallas_call x1, Pallas kernels, forward(): pl.pallas_call(forward_kernel, in_specs=[smem(), vmem(), vmem(), vmem()],...  13 us
    pallas_call x2, Pallas kernels, pack(): pl.pallas_call(pack_kernel, grid=(4,), in_specs=[smem()] + [pl.BlockSpec(...  7.73 us
    pallas_call x2, Pallas kernels, unpack(): pl.pallas_call(unpack_kernel, grid=(4,), in_specs=[smem(), pl.BlockSpec((...  7.46 us
  transfers between devices with their start and end apart: 6, of which 4 were waited for; matrix products, arithmetic and copies ran while one was open for 2% of the time, Pallas kernels for 18%

profile of v1, /device:TPU:4, one launch (start us, length us, event | category | flops | bytes accessed | tf_op | source)
XLA Modules:
  0.0 236.8 jit_solution(11353889016850794291)
XLA Ops:
  0.6 4.3 %pack.2 = bf16[32,3,96,128]{3,2,1,0:T(8,128)(2,1)} custom-call(s32[1]{0:T(128)} %bitcast.mirror_ref, bf16[128,3072]{1,0:T(8,128)(2,1)} %refs_0_.2, bf16[128,3072]{1,0:T(8,128)(2,1)} %refs_1_.1, bf16[128,3072]{1,0:T(8,128)(2,1)} %refs_2_.1), custom_call_target="tpu_custom_call" | custom-call | tf_op jit(solution)/shard_map/pack/pallas_call | solution.py:57
  4.9 8.9 %all-to-all-start = ((bf16[32,3,96,128]{3,2,1,0:T(8,128)(2,1)}), bf16[32,3,96,128]{3,2,1,0:T(8,128)(2,1)S(1)}, u32[]{:S(2)}, u32[]{:S(2)}) async-start(bf16[32,3,96,128]{3,2,1,0:T(8,128)(2,1)} %pack.2), calls=%async_computation | async-start | bytes 4718592 | tf_op jit(solution)/shard_map/all_to_all | solution.py:314
  13.9 3.4 %pack.3 = bf16[32,1,96,128]{3,2,1,0:T(8,128)(2,1)} custom-call(s32[1]{0:T(128)} %bitcast.mirror_ref, bf16[128,3072]{1,0:T(8,128)(2,1)} %refs_0_.3), custom_call_target="tpu_custom_call" | custom-call | tf_op jit(solution)/shard_map/pack/pallas_call | solution.py:57
  17.3 0.7 dynamic_slice.6
  18.0 0.8 dynamic-slice_select_fusion
  18.8 0.2 convert_reduce_fusion
  19.0 50.9 %all-to-all-done.kvq_ref = bf16[32,3,96,128]{3,2,1,0:T(8,128)(2,1)S(1)} async-done(((bf16[32,3,96,128]{3,2,1,0:T(8,128)(2,1)}), bf16[32,3,96,128]{3,2,1,0:T(8,128)(2,1)S(1)}, u32[]{:S(2)}, u32[]{:S(2)}) %all-to-all-start) | async-done | bytes 2359328 | tf_op jit(solution)/shard_map/all_to_all | solution.py:314
  69.9 0.0 copy-start.1
  69.9 3.9 %all-to-all-start.2 = ((bf16[32,1,96,128]{3,2,1,0:T(8,128)(2,1)}), bf16[32,1,96,128]{3,2,1,0:T(8,128)(2,1)S(1)}, u32[]{:S(2)}, u32[]{:S(2)}) async-start(bf16[32,1,96,128]{3,2,1,0:T(8,128)(2,1)} %pack.3), calls=%async_computation.2 | async-start | bytes 1572864 | tf_op jit(solution)/shard_map/all_to_all | solution.py:314
  73.9 0.1 convert_reduce_fusion.1
  74.0 6.7 %collective-permute-start = (bf16[8,2,96,128]{3,2,1,0:T(8,128)(2,1)S(1)}, bf16[8,2,96,128]{3,2,1,0:T(8,128)(2,1)}, u32[]{:S(2)}, u32[]{:S(2)}) collective-permute-start(bf16[8,2,96,128]{3,2,1,0:T(8,128)(2,1)S(1)} %slice.9), channel_id=1, source_target_pairs={{0,38},{1,39},{2,36},{3,37},{4,34},{5,35},{6,32},{7,33},{8,46},{9,... | collective-permute-start | bytes 1179656 | tf_op jit(solution)/shard_map/ppermute | solution.py:337
  80.7 0.8 select_reduce_fusion
  81.5 0.7 reshape.22.start_ref
  82.2 0.0 copy-start.5
  82.3 0.1 slice_reduce_fusion
  82.4 0.5 and_select_fusion.tile_start_ref
  82.9 14.9 %collective-permute-done.halo_ref = bf16[8,2,96,128]{3,2,1,0:T(8,128)(2,1)} collective-permute-done((bf16[8,2,96,128]{3,2,1,0:T(8,128)(2,1)S(1)}, bf16[8,2,96,128]{3,2,1,0:T(8,128)(2,1)}, u32[]{:S(2)}, u32[]{:S(2)}) %collective-permute-start) | collective-permute-done | bytes 393248 | tf_op jit(solution)/shard_map/ppermute | solution.py:337
  97.8 0.0 copy-done.1
  97.8 0.0 copy-done.5
  97.8 13.0 %forward.1 = (bf16[32,1,96,128]{3,2,1,0:T(8,128)(2,1)}, f32[16,256]{1,0:T(8,128)}) custom-call(s32[16]{0:T(128)} %and_select_fusion.tile_start_ref, s32[16,256]{1,0:T(8,128)} %copy-done.5, bf16[32,3,96,128]{3,2,1,0:T(8,128)(2,1)} %copy-done.1, bf16[8,2,96,128]{3,2,1,0:T(8,128)(2,1)} %collective-permute-done.halo_ref), custom_call_target="tpu_custom_call" | custom-call | flops 10737418240 | bytes 8388608 | tf_op jit(solution)/shard_map/forward/pallas_call | solution.py:170
  110.8 0.0 all-to-all-done.2.g_ref
  110.8 0.0 copy-start.3
  110.8 0.9 copy-done.3
  111.7 8.6 %all-to-all-start.1 = ((bf16[32,1,96,128]{3,2,1,0:T(8,128)(2,1)}), bf16[32,1,96,128]{3,2,1,0:T(8,128)(2,1)S(1)}, u32[]{:S(2)}, u32[]{:S(2)}) async-start(bf16[32,1,96,128]{3,2,1,0:T(8,128)(2,1)} %get-tuple-element.12.out_ref), calls=%async_computation.1 | async-start | bytes 1572864 | tf_op jit(solution)/shard_map/all_to_all | solution.py:314
  120.3 20.7 %backward.1 = (bf16[32,3,96,128]{3,2,1,0:T(8,128)(2,1)}, bf16[8,2,96,128]{3,2,1,0:T(8,128)(2,1)}, f32[8,2,96,128]{3,2,1,0:T(8,128)}) custom-call(s32[16]{0:T(128)} %and_select_fusion.tile_start_ref, s32[16,256]{1,0:T(8,128)} %copy-done.5, bf16[32,3,96,128]{3,2,1,0:T(8,128)(2,1)} %copy-done.1, bf16[8,2,96,128]{3,2,1,0:T(8,128)(2,1)} %collective-permute-done.halo_ref, ...), custom_call_target="tpu_custom_call" | custom-call | flops 26843545600 | bytes 12582912 | tf_op jit(solution)/shard_map/backward/pallas_call | solution.py:250
  141.0 5.5 %collective-permute-start.1 = (bf16[8,2,96,128]{3,2,1,0:T(8,128)(2,1)}, bf16[8,2,96,128]{3,2,1,0:T(8,128)(2,1)S(1)}, u32[]{:S(2)}, u32[]{:S(2)}) collective-permute-start(bf16[8,2,96,128]{3,2,1,0:T(8,128)(2,1)} %get-tuple-element.14), channel_id=1, source_target_pairs={{38,0},{39,1},{36,2},{37,3},{34,4},{35,5},{32,6},{33,7},{46,8},{47... | collective-permute-start | bytes 1179656 | tf_op jit(solution)/shard_map/ppermute | solution.py:340
  146.5 18.0 %collective-permute-done.1.back_ref = bf16[8,2,96,128]{3,2,1,0:T(8,128)(2,1)S(1)} collective-permute-done((bf16[8,2,96,128]{3,2,1,0:T(8,128)(2,1)}, bf16[8,2,96,128]{3,2,1,0:T(8,128)(2,1)S(1)}, u32[]{:S(2)}, u32[]{:S(2)}) %collective-permute-start.1) | collective-permute-done | bytes 393248 | tf_op jit(solution)/shard_map/ppermute | solution.py:340
  164.5 0.0 copy-start.4
  164.5 0.7 copy-done.4
  165.3 2.1 join.1
  167.4 0.0 all-to-all-done.1.in_ref
  167.4 0.0 copy-start.2
  167.4 0.9 copy-done.2
  168.3 7.0 %all-to-all-start.3 = ((bf16[32,3,96,128]{3,2,1,0:T(8,128)(2,1)}), bf16[32,3,96,128]{3,2,1,0:T(8,128)(2,1)S(1)}, u32[]{:S(2)}, u32[]{:S(2)}) async-start(bf16[32,3,96,128]{3,2,1,0:T(8,128)(2,1)} %join.1), calls=%async_computation.3 | async-start | bytes 4718592 | tf_op jit(solution)/shard_map/all_to_all | solution.py:314
  175.3 3.5 %unpack.2 = bf16[128,3072]{1,0:T(8,128)(2,1)} custom-call(s32[1]{0:T(128)} %bitcast.mirror_ref, bf16[32,1,96,128]{3,2,1,0:T(8,128)(2,1)} %copy-done.2), custom_call_target="tpu_custom_call" | custom-call | tf_op jit(solution)/shard_map/unpack/pallas_call | solution.py:80
  178.8 52.6 %all-to-all-done.3.in_ref = bf16[32,3,96,128]{3,2,1,0:T(8,128)(2,1)S(1)} async-done(((bf16[32,3,96,128]{3,2,1,0:T(8,128)(2,1)}), bf16[32,3,96,128]{3,2,1,0:T(8,128)(2,1)S(1)}, u32[]{:S(2)}, u32[]{:S(2)}) %all-to-all-start.3) | async-done | bytes 2359328 | tf_op jit(solution)/shard_map/all_to_all | solution.py:314
  231.4 0.0 copy-start
  231.4 1.4 copy-done
  232.8 4.0 %unpack.3 = (bf16[128,3072]{1,0:T(8,128)(2,1)}, bf16[128,3072]{1,0:T(8,128)(2,1)}, bf16[128,3072]{1,0:T(8,128)(2,1)}) custom-call(s32[1]{0:T(128)} %bitcast.mirror_ref, bf16[32,3,96,128]{3,2,1,0:T(8,128)(2,1)} %copy-done), custom_call_target="tpu_custom_call" | custom-call | tf_op jit(solution)/shard_map/unpack/pallas_call | solution.py:80
  (2 shorter events, 0.0 us)
Async XLA Ops:
  4.9 65.0 %all-to-all-start = ((bf16[32,3,96,128]{3,2,1,0:T(8,128)(2,1)}), bf16[32,3,96,128]{3,2,1,0:T(8,128)(2,1)S(1)}, u32[]{:S(2)}, u32[]{:S(2)}) async-start(bf16[32,3,96,128]{3,2,1,0:T(8,128)(2,1)} %pack.2), calls=%async_computation | async-start | bytes 4718592 | tf_op jit(solution)/shard_map/all_to_all | solution.py:314
  69.9 27.9 %copy-start.1 = (bf16[32,3,96,128]{3,2,1,0:T(8,128)(2,1)}, bf16[32,3,96,128]{3,2,1,0:T(8,128)(2,1)S(1)}, u32[]{:S(2)}) copy-start(bf16[32,3,96,128]{3,2,1,0:T(8,128)(2,1)S(1)} %all-to-all-done.kvq_ref) | copy-start | bytes 7077892
  69.9 40.8 %all-to-all-start.2 = ((bf16[32,1,96,128]{3,2,1,0:T(8,128)(2,1)}), bf16[32,1,96,128]{3,2,1,0:T(8,128)(2,1)S(1)}, u32[]{:S(2)}, u32[]{:S(2)}) async-start(bf16[32,1,96,128]{3,2,1,0:T(8,128)(2,1)} %pack.3), calls=%async_computation.2 | async-start | bytes 1572864 | tf_op jit(solution)/shard_map/all_to_all | solution.py:314
  74.0 23.8 %collective-permute-start = (bf16[8,2,96,128]{3,2,1,0:T(8,128)(2,1)S(1)}, bf16[8,2,96,128]{3,2,1,0:T(8,128)(2,1)}, u32[]{:S(2)}, u32[]{:S(2)}) collective-permute-start(bf16[8,2,96,128]{3,2,1,0:T(8,128)(2,1)S(1)} %slice.9), channel_id=1, source_target_pairs={{0,38},{1,39},{2,36},{3,37},{4,34},{5,35},{6,32},{7,33},{8,46},{9,... | collective-permute-start | bytes 1179656 | tf_op jit(solution)/shard_map/ppermute | solution.py:337
  82.2 15.6 %copy-start.5 = (s32[16,256]{1,0:T(8,128)}, s32[16,256]{1,0:T(8,128)S(1)}, u32[]{:S(2)}) copy-start(s32[16,256]{1,0:T(8,128)S(1)} %reshape.22.start_ref) | copy-start | bytes 49156
  110.8 0.9 copy-start.3
  111.7 55.8 %all-to-all-start.1 = ((bf16[32,1,96,128]{3,2,1,0:T(8,128)(2,1)}), bf16[32,1,96,128]{3,2,1,0:T(8,128)(2,1)S(1)}, u32[]{:S(2)}, u32[]{:S(2)}) async-start(bf16[32,1,96,128]{3,2,1,0:T(8,128)(2,1)} %get-tuple-element.12.out_ref), calls=%async_computation.1 | async-start | bytes 1572864 | tf_op jit(solution)/shard_map/all_to_all | solution.py:314
  141.0 23.6 %collective-permute-start.1 = (bf16[8,2,96,128]{3,2,1,0:T(8,128)(2,1)}, bf16[8,2,96,128]{3,2,1,0:T(8,128)(2,1)S(1)}, u32[]{:S(2)}, u32[]{:S(2)}) collective-permute-start(bf16[8,2,96,128]{3,2,1,0:T(8,128)(2,1)} %get-tuple-element.14), channel_id=1, source_target_pairs={{38,0},{39,1},{36,2},{37,3},{34,4},{35,5},{32,6},{33,7},{46,8},{47... | collective-permute-start | bytes 1179656 | tf_op jit(solution)/shard_map/ppermute | solution.py:340
  164.5 0.7 copy-start.4
  167.4 0.9 copy-start.2
  168.3 63.1 %all-to-all-start.3 = ((bf16[32,3,96,128]{3,2,1,0:T(8,128)(2,1)}), bf16[32,3,96,128]{3,2,1,0:T(8,128)(2,1)S(1)}, u32[]{:S(2)}, u32[]{:S(2)}) async-start(bf16[32,3,96,128]{3,2,1,0:T(8,128)(2,1)} %join.1), calls=%async_computation.3 | async-start | bytes 4718592 | tf_op jit(solution)/shard_map/all_to_all | solution.py:314
  231.4 1.4 copy-start

commit v2 on v1

--- a/solution.py
+++ b/solution.py
@@ -103,8 +103,8 @@
     return lax.dot_general(a, b, (((1,), (1,)), ((), ())), preferred_element_type=F32)
 
 
-def fill(halo_ref, own_ref, n, flat, turned):
-    for chunk in range(HALO + CHUNKS):
+def fill(halo_ref, own_ref, n, chunks, flat, turned):
+    for chunk in chunks:
         piece = halo_ref[chunk, n] if chunk < HALO else own_ref[chunk - HALO, n]
         if turned is not None:
             turned[:, chunk * CHUNK : (chunk + 1) * CHUNK] = piece
@@ -126,13 +126,12 @@
         pl.when(reach == count)(functools.partial(body, count))
 
 
-def forward_kernel(
-    tile_start_ref, start_ref, kvq_ref, halo_ref, out_ref, stat_ref, key_flat, value_turned
-):
-    fill(halo_ref, kvq_ref, 0, key_flat, None)
-    fill(halo_ref, kvq_ref, 1, None, value_turned)
-
-    def tile(i, _):
+def forward_tiles(
+    low, tile_start_ref, start_ref, kvq_ref, out_ref, stat_ref, key_flat, value_turned
+):
+    def tile(step, _):
+        i = low + step
+
         def body(count):
             q = tile_of(kvq_ref, 2, i)
             start = start_ref[pl.ds(i, 1), :]
@@ -156,40 +155,100 @@
                 o = nn(value_turned[:, pl.ds(first, TILE)], e.astype(BF16))
                 out = o if out is None else out + o
             out = (out / total).astype(BF16)
-            out_ref[2 * i, 0] = out[:, :CHUNK]
-            out_ref[2 * i + 1, 0] = out[:, CHUNK:]
-            stat_ref[pl.ds(i, 1), :] = shift + jnp.log2(total)
+            out_ref[2 * step, 0] = out[:, :CHUNK]
+            out_ref[2 * step + 1, 0] = out[:, CHUNK:]
+            stat_ref[0, pl.ds(step, 1), :] = shift + jnp.log2(total)
 
         per_tile(tile_start_ref, i, body)
         return 0
 
-    lax.fori_loop(0, TILES, tile, 0)
-
-
-def forward(tile_start, start, kvq, halo):
-    return pl.pallas_call(
-        forward_kernel,
-        in_specs=[smem(), vmem(), vmem(), vmem()],
-        out_specs=[vmem(), vmem()],
-        out_shape=[
-            jax.ShapeDtypeStruct((CHUNKS, 1, HEAD_DIM, CHUNK), BF16),
-            jax.ShapeDtypeStruct((TILES, TILE), F32),
-        ],
+    lax.fori_loop(0, AHEAD_TILES, tile, 0)
+
+
+def late_forward_kernel(
+    tile_start_ref, start_ref, kvq_ref, out_ref, stat_ref, key_flat, value_turned
+):
+    @pl.when(pl.program_id(0) == 0)
+    def _():
+        fill(None, kvq_ref, 0, range(HALO, HALO + CHUNKS), key_flat, None)
+        fill(None, kvq_ref, 1, range(HALO, HALO + CHUNKS), None, value_turned)
+
+    forward_tiles(
+        (pl.program_id(0) + 1) * AHEAD_TILES,
+        tile_start_ref, start_ref, kvq_ref, out_ref, stat_ref, key_flat, value_turned
+    )
+
+
+def early_forward_kernel(
+    tile_start_ref, start_ref, kvq_ref, halo_ref, _, __, out_ref, stat_ref, key_flat, value_turned
+):
+    fill(halo_ref, kvq_ref, 0, range(2 * HALO), key_flat, None)
+    fill(halo_ref, kvq_ref, 1, range(2 * HALO), None, value_turned)
+    forward_tiles(
+        0, tile_start_ref, start_ref, kvq_ref, out_ref, stat_ref, key_flat, value_turned
+    )
+
+
+def cost(products, tiles):
+    return pl.CostEstimate(
+        flops=2 * products * tiles * REACH * TILE * TILE * 256,
+        bytes_accessed=8 << 20,
+        transcendentals=tiles * REACH * TILE * TILE,
+    )
+
+
+OUT_SHAPES = [
+    jax.ShapeDtypeStruct((CHUNKS, 1, HEAD_DIM, CHUNK), BF16),
+    jax.ShapeDtypeStruct((TILES // AHEAD_TILES, AHEAD_TILES, TILE), F32),
+]
+
+
+def out_specs(first):
+    return [
+        pl.BlockSpec((HALO, 1, HEAD_DIM, CHUNK), lambda b: (b + first, 0, 0, 0)),
+        pl.BlockSpec((1, AHEAD_TILES, TILE), lambda b: (b + first, 0, 0)),
+    ]
+
+
+def late_forward(tile_start, start, kvq):
+    return pl.pallas_call(
+        late_forward_kernel,
+        grid=(TILES // AHEAD_TILES - 1,),
+        in_specs=[smem(), vmem(), vmem()],
+        out_specs=out_specs(1),
+        out_shape=OUT_SHAPES,
         scratch_shapes=[
             pltpu.VMEM((WINDOW, HEAD_DIM), BF16),
             pltpu.VMEM((HEAD_DIM, WINDOW), BF16),
         ],
         compiler_params=pltpu.CompilerParams(vmem_limit_bytes=VMEM_LIMIT),
-        cost_estimate=pl.CostEstimate(
-            flops=2 * 2 * 2560 * GROUP * 256, bytes_accessed=8 << 20, transcendentals=GROUP * 1280
-        ),
-        name="forward",
-    )(tile_start, start, kvq, halo)
+        cost_estimate=cost(2, TILES - AHEAD_TILES),
+        name="late_forward",
+    )(tile_start, start, kvq)
+
+
+def early_forward(tile_start, start, kvq, halo, out, stat):
+    whole = pl.BlockSpec((2 * HALO, 3, HEAD_DIM, CHUNK), lambda b: (0, 0, 0, 0))
+    return pl.pallas_call(
+        early_forward_kernel,
+        grid=(1,),
+        in_specs=[smem(), vmem(), whole, vmem()] + [pl.BlockSpec(memory_space=pl.ANY)] * 2,
+        out_specs=out_specs(0),
+        out_shape=OUT_SHAPES,
+        input_output_aliases={4: 0, 5: 1},
+        scratch_shapes=[
+            pltpu.VMEM((2 * AHEAD, HEAD_DIM), BF16),
+            pltpu.VMEM((HEAD_DIM, 2 * AHEAD), BF16),
+        ],
+        compiler_params=pltpu.CompilerParams(vmem_limit_bytes=VMEM_LIMIT),
+        cost_estimate=cost(2, AHEAD_TILES),
+        name="early_forward",
+    )(tile_start, start, kvq, halo, out, stat)
 
 
 def backward_tiles(
-    tile_start_ref, start_ref, kvq_ref, g_ref, out_ref, stat_ref, grads_ref,
-    key_flat, key_turned, value_flat, key_sum, value_sum, low, high
+    low, high, tile_start_ref, start_ref, kvq_ref, g_ref, out_ref, stat_ref, store,
+    key_flat, key_turned, value_flat, key_sum, value_sum
 ):
     def tile(i, _):
         def body(count):
@@ -198,7 +257,7 @@
             o = tile_of(out_ref, 0, i)
             delta = jnp.sum(o.astype(F32) * g.astype(F32), axis=0, keepdims=True)
             start = start_ref[pl.ds(i, 1), :]
-            stat = stat_ref[pl.ds(i, 1), :]
+            stat = stat_ref[i // AHEAD_TILES, pl.ds(i % AHEAD_TILES, 1), :]
             grad_q = None
             for j in range(count):
                 first = pl.multiple_of((i + REACH - count + j) * TILE, TILE)
@@ -206,16 +265,15 @@
                 s = nn(key_flat[span, :], q)
                 p = jnp.exp2(s * (SCALE * LOG2E) - stat)
                 p = jnp.where(allowed_in(start, first, j == count - 1), p, 0.0)
-                p_b = p.astype(BF16)
                 grad_p = nn(value_flat[span, :], g)
                 d = (p * (grad_p - delta)).astype(BF16)
                 t = nn(key_turned[:, span], d)
                 grad_q = t if grad_q is None else grad_q + t
                 key_sum[:, span] += nt(q, d)
-                value_sum[:, span] += nt(g, p_b)
+                value_sum[:, span] += nt(g, p.astype(BF16))
             grad_q = (grad_q * SCALE).astype(BF16)
-            grads_ref[2 * i, 2] = grad_q[:, :CHUNK]
-            grads_ref[2 * i + 1, 2] = grad_q[:, CHUNK:]
+            store(2 * i, grad_q[:, :CHUNK])
+            store(2 * i + 1, grad_q[:, CHUNK:])
 
         per_tile(tile_start_ref, i, body)
         return 0
@@ -223,52 +281,102 @@
     lax.fori_loop(low, high, tile, 0)
 
 
-def backward_kernel(
+def early_backward_kernel(
     tile_start_ref, start_ref, kvq_ref, halo_ref, g_ref, out_ref, stat_ref,
-    grads_ref, back_ref, rest_ref, key_flat, key_turned, value_flat, key_sum, value_sum
-):
-    fill(halo_ref, kvq_ref, 0, key_flat, key_turned)
-    fill(halo_ref, kvq_ref, 1, value_flat, None)
+    back_ref, carry_ref, grad_q_ref, key_flat, key_turned, value_flat, key_sum, value_sum
+):
+    fill(halo_ref, kvq_ref, 0, range(2 * HALO), key_flat, key_turned)
+    fill(halo_ref, kvq_ref, 1, range(2 * HALO), value_flat, None)
     key_sum[...] = jnp.zeros_like(key_sum)
     value_sum[...] = jnp.zeros_like(value_sum)
+
+    def store(chunk, value):
+        grad_q_ref[chunk] = value
+
     backward_tiles(
-        tile_start_ref, start_ref, kvq_ref, g_ref, out_ref, stat_ref, grads_ref,
-        key_flat, key_turned, value_flat, key_sum, value_sum, 0, TILES
+        0, AHEAD_TILES, tile_start_ref, start_ref, kvq_ref, g_ref, out_ref, stat_ref, store,
+        key_flat, key_turned, value_flat, key_sum, value_sum
     )
     for n, (sums, factor) in enumerate(((key_sum, SCALE), (value_sum, 1.0))):
-        for chunk in range(HALO + CHUNKS):
+        for chunk in range(HALO):
             piece = sums[:, chunk * CHUNK : (chunk + 1) * CHUNK] * factor
-            if chunk < HALO:
-                back_ref[chunk, n] = piece.astype(BF16)
-            else:
-                grads_ref[chunk - HALO, n] = piece.astype(BF16)
+            back_ref[chunk, n] = piece.astype(BF16)
+        carry_ref[n] = sums[:, AHEAD:]
+
+
+def late_backward_kernel(
+    tile_start_ref, start_ref, kvq_ref, g_ref, out_ref, stat_ref, carry_ref, grad_q_ref,
+    grads_ref, rest_ref, key_flat, key_turned, value_flat, key_sum, value_sum
+):
+    chunks = range(HALO, HALO + CHUNKS)
+    fill(None, kvq_ref, 0, chunks, key_flat, key_turned)
+    fill(None, kvq_ref, 1, chunks, value_flat, None)
+    for n, sums in enumerate((key_sum, value_sum)):
+        sums[:, AHEAD : 2 * AHEAD] = carry_ref[n]
+        sums[:, 2 * AHEAD :] = jnp.zeros((HEAD_DIM, WINDOW - 2 * AHEAD), F32)
+    for chunk in range(HALO):
+        grads_ref[chunk, 2] = grad_q_ref[chunk]
+
+    def store(chunk, value):
+        grads_ref[chunk, 2] = value
+
+    backward_tiles(
+        AHEAD_TILES, TILES, tile_start_ref, start_ref, kvq_ref, g_ref, out_ref, stat_ref, store,
+        key_flat, key_turned, value_flat, key_sum, value_sum
+    )
+    for n, (sums, factor) in enumerate(((key_sum, SCALE), (value_sum, 1.0))):
+        for chunk in chunks:
+            piece = sums[:, chunk * CHUNK : (chunk + 1) * CHUNK] * factor
+            grads_ref[chunk - HALO, n] = piece.astype(BF16)
             if chunk >= CHUNKS:
                 rest_ref[chunk - CHUNKS, n] = piece
 
 
-def backward(tile_start, start, kvq, halo, g, out, stat):
-    return pl.pallas_call(
-        backward_kernel,
-        in_specs=[smem()] + [vmem()] * 6,
+def sums_scratch(window):
+    return [
+        pltpu.VMEM((window, HEAD_DIM), BF16),
+        pltpu.VMEM((HEAD_DIM, window), BF16),
+        pltpu.VMEM((window, HEAD_DIM), BF16),
+        pltpu.VMEM((HEAD_DIM, window), F32),
+        pltpu.VMEM((HEAD_DIM, window), F32),
+    ]
+
+
+def early_backward(tile_start, start, kvq, halo, g, out, stat):
+    def part(count, width):
+        return pl.BlockSpec((count, width, HEAD_DIM, CHUNK), lambda b: (0, 0, 0, 0))
+
+    return pl.pallas_call(
+        early_backward_kernel,
+        grid=(1,),
+        in_specs=[smem(), vmem(), part(HALO, 3), vmem(), part(HALO, 1), part(HALO, 1), vmem()],
         out_specs=[vmem()] * 3,
         out_shape=[
+            jax.ShapeDtypeStruct((HALO, 2, HEAD_DIM, CHUNK), BF16),
+            jax.ShapeDtypeStruct((2, HEAD_DIM, AHEAD), F32),
+            jax.ShapeDtypeStruct((HALO, HEAD_DIM, CHUNK), BF16),
+        ],
+        scratch_shapes=sums_scratch(2 * AHEAD),
+        compiler_params=pltpu.CompilerParams(vmem_limit_bytes=VMEM_LIMIT),
+        cost_estimate=cost(5, AHEAD_TILES),
+        name="early_backward",
+    )(tile_start, start, kvq, halo, g, out, stat)
+
+
+def late_backward(tile_start, start, kvq, g, out, stat, carry, grad_q):
+    return pl.pallas_call(
+        late_backward_kernel,
+        in_specs=[smem()] + [vmem()] * 7,
+        out_specs=[vmem()] * 2,
+        out_shape=[
             jax.ShapeDtypeStruct((CHUNKS, 3, HEAD_DIM, CHUNK), BF16),
-            jax.ShapeDtypeStruct((HALO, 2, HEAD_DIM, CHUNK), BF16),
             jax.ShapeDtypeStruct((HALO, 2, HEAD_DIM, CHUNK), F32),
         ],
-        scratch_shapes=[
-            pltpu.VMEM((WINDOW, HEAD_DIM), BF16),
-            pltpu.VMEM((HEAD_DIM, WINDOW), BF16),
-            pltpu.VMEM((WINDOW, HEAD_DIM), BF16),
-            pltpu.VMEM((HEAD_DIM, WINDOW), F32),
-            pltpu.VMEM((HEAD_DIM, WINDOW), F32),
-        ],
-        compiler_params=pltpu.CompilerParams(vmem_limit_bytes=VMEM_LIMIT),
-        cost_estimate=pl.CostEstimate(
-            flops=2 * 5 * 2560 * GROUP * 256, bytes_accessed=12 << 20, transcendentals=GROUP * 1280
-        ),
-        name="backward",
-    )(tile_start, start, kvq, halo, g, out, stat)
+        scratch_shapes=sums_scratch(WINDOW),
+        compiler_params=pltpu.CompilerParams(vmem_limit_bytes=VMEM_LIMIT),
+        cost_estimate=cost(5, TILES - AHEAD_TILES),
+        name="late_backward",
+    )(tile_start, start, kvq, g, out, stat, carry, grad_q)
 
 
 def join_kernel(back_ref, rest_ref, _, out_ref):
@@ -335,8 +443,10 @@
     tile_start, start = places(doc_ids)
     pairs = group_pairs()
     halo = lax.ppermute(kvq[CHUNKS - HALO :, :2], AXES, pairs)
-    out, stat = forward(tile_start, start, kvq, halo)
-    grads, back, rest = backward(tile_start, start, kvq, halo, g, out, stat)
+    out, stat = late_forward(tile_start, start, kvq)
+    out, stat = early_forward(tile_start, start, kvq, halo, out, stat)
+    back, carry, early_q = early_backward(tile_start, start, kvq, halo, g, out, stat)
+    grads, rest = late_backward(tile_start, start, kvq, g, out, stat, carry, early_q)
     back = lax.ppermute(back, AXES, [(b, a) for a, b in pairs])
     grads = join(back, rest, grads)
     (attended,) = unpack(mirror, to_heads(out))

time: 241 us -> 218 us (0.905); the launches traced: 237 us -> 217 us
  waiting for transfers between devices: 137 us -> 114 us
  Pallas kernels: 51 us -> 56.5 us
  starting transfers between devices: 40.7 us -> 38.1 us
    ppermute x1, waiting for transfers between devices: 18 us -> 1.74 us  [shards(): back = lax.ppermute(back, AXES, [(b, a) for a, b in pairs])]
    ppermute x1, waiting for transfers between devices: 14.9 us -> 6.89 us  [shards(): halo = lax.ppermute(kvq[CHUNKS - HALO:, :2], AXES, pairs)]
    pallas_call x2 -> x4, Pallas kernels: 33.6 us -> 39.3 us  [the longest x1 17 us: late_backward(): pl.pallas_call(late_backward_kernel, in_specs=[smem()] + [vmem()] * 7, ou...]
    all_to_all x4, starting transfers between devices: 28.5 us -> 25.5 us  [to_heads(): lax.all_to_all(array, GROUP_AXES, split_axis=0, concat_axis=0, tiled=True)]
  transfers between devices with their start and end apart: 6 -> 6, of which waited for: 4 -> 4; matrix products, arithmetic and copies ran while one was open for 2% -> 1% of each run, Pallas kernels for 18% -> 22%
where the time goes in v2:
time: 218 us; the launch traced here: 217 us
  waiting for transfers between devices  114 us (52%)
  Pallas kernels  56.5 us (26%)
  starting transfers between devices  38.1 us (17%)
  local copies, waits for them, and re-layouts  5.53 us (3%)
    all_to_all x4, waiting for transfers between devices, to_heads(): lax.all_to_all(array, GROUP_AXES, split_axis=0, concat_axis=0, tiled=True)  105 us
    all_to_all x4, starting transfers between devices, to_heads(): lax.all_to_all(array, GROUP_AXES, split_axis=0, concat_axis=0, tiled=True)  25.5 us
    pallas_call x1, Pallas kernels, late_backward(): pl.pallas_call(late_backward_kernel, in_specs=[smem()] + [vmem()] * 7, ou...  17 us
    pallas_call x1, Pallas kernels, late_forward(): pl.pallas_call(late_forward_kernel, grid=(TILES // AHEAD_TILES - 1,), in_...  10.4 us
    pallas_call x2, Pallas kernels, pack(): pl.pallas_call(pack_kernel, grid=(4,), in_specs=[smem()] + [pl.BlockSpec(...  7.72 us
    pallas_call x2, Pallas kernels, unpack(): pl.pallas_call(unpack_kernel, grid=(4,), in_specs=[smem(), pl.BlockSpec((...  7.46 us
    pallas_call x1, Pallas kernels, early_backward(): pl.pallas_call(early_backward_kernel, grid=(1,), in_specs=[smem(), vmem()...  7 us
    ppermute x1, waiting for transfers between devices, shards(): halo = lax.ppermute(kvq[CHUNKS - HALO:, :2], AXES, pairs)  6.89 us
  transfers between devices with their start and end apart: 6, of which 4 were waited for; matrix products, arithmetic and copies ran while one was open for 1% of the time, Pallas kernels for 22%

profile of v2, /device:TPU:4, one launch (start us, length us, event | category | flops | bytes accessed | tf_op | source)
XLA Modules:
  0.0 216.7 jit_solution(16506646439987129292)
XLA Ops:
  0.6 4.3 %pack.2 = bf16[32,3,96,128]{3,2,1,0:T(8,128)(2,1)} custom-call(s32[1]{0:T(128)} %bitcast.mirror_ref, bf16[128,3072]{1,0:T(8,128)(2,1)} %refs_0_.2, bf16[128,3072]{1,0:T(8,128)(2,1)} %refs_1_.1, bf16[128,3072]{1,0:T(8,128)(2,1)} %refs_2_.1), custom_call_target="tpu_custom_call" | custom-call | tf_op jit(solution)/shard_map/pack/pallas_call | solution.py:57
  4.9 8.9 %all-to-all-start = ((bf16[32,3,96,128]{3,2,1,0:T(8,128)(2,1)}), bf16[32,3,96,128]{3,2,1,0:T(8,128)(2,1)S(1)}, u32[]{:S(2)}, u32[]{:S(2)}) async-start(bf16[32,3,96,128]{3,2,1,0:T(8,128)(2,1)} %pack.2), calls=%async_computation | async-start | bytes 4718592 | tf_op jit(solution)/shard_map/all_to_all | solution.py:422
  13.8 3.4 %pack.3 = bf16[32,1,96,128]{3,2,1,0:T(8,128)(2,1)} custom-call(s32[1]{0:T(128)} %bitcast.mirror_ref, bf16[128,3072]{1,0:T(8,128)(2,1)} %refs_0_.3), custom_call_target="tpu_custom_call" | custom-call | tf_op jit(solution)/shard_map/pack/pallas_call | solution.py:57
  17.3 52.6 %all-to-all-done.kvq_ref = bf16[32,3,96,128]{3,2,1,0:T(8,128)(2,1)S(1)} async-done(((bf16[32,3,96,128]{3,2,1,0:T(8,128)(2,1)}), bf16[32,3,96,128]{3,2,1,0:T(8,128)(2,1)S(1)}, u32[]{:S(2)}, u32[]{:S(2)}) %all-to-all-start) | async-done | bytes 2359328 | tf_op jit(solution)/shard_map/all_to_all | solution.py:422
  69.9 0.0 copy-start.1
  69.9 3.9 %all-to-all-start.2 = ((bf16[32,1,96,128]{3,2,1,0:T(8,128)(2,1)}), bf16[32,1,96,128]{3,2,1,0:T(8,128)(2,1)S(1)}, u32[]{:S(2)}, u32[]{:S(2)}) async-start(bf16[32,1,96,128]{3,2,1,0:T(8,128)(2,1)} %pack.3), calls=%async_computation.2 | async-start | bytes 1572864 | tf_op jit(solution)/shard_map/all_to_all | solution.py:422
  73.9 0.7 dynamic_slice.6
  74.6 0.8 dynamic-slice_select_fusion
  75.4 0.1 convert_reduce_fusion.1
  75.5 0.2 convert_reduce_fusion
  75.7 0.2 select_reduce_fusion
  76.0 0.0 copy-start.5
  76.0 0.1 slice_reduce_fusion
  76.1 6.7 %collective-permute-start = (bf16[8,2,96,128]{3,2,1,0:T(8,128)(2,1)S(1)}, bf16[8,2,96,128]{3,2,1,0:T(8,128)(2,1)S(1)}, u32[]{:S(2)}, u32[]{:S(2)}) collective-permute-start(bf16[8,2,96,128]{3,2,1,0:T(8,128)(2,1)S(1)} %slice.9), channel_id=1, source_target_pairs={{0,38},{1,39},{2,36},{3,37},{4,34},{5,35},{6,32},{7,33},{8,46},{9,... | collective-permute-start | bytes 1179656 | tf_op jit(solution)/shard_map/ppermute | solution.py:445
  82.8 0.5 and_select_fusion.tile_start_ref
  83.3 0.0 copy-done.1
  83.3 0.0 copy-done.5
  83.3 10.4 %late_forward.1 = (bf16[32,1,96,128]{3,2,1,0:T(8,128)(2,1)}, f32[4,4,256]{2,1,0:T(4,128)}) custom-call(s32[16]{0:T(128)} %and_select_fusion.tile_start_ref, s32[16,256]{1,0:T(8,128)} %copy-done.5, bf16[32,3,96,128]{3,2,1,0:T(8,128)(2,1)} %copy-done.1), custom_call_target="tpu_custom_call" | custom-call | flops 4026531840 | bytes 8388608 | tf_op jit(solution)/shard_map/late_forward/pallas_call | solution.py:214
  93.7 6.9 %collective-permute-done.halo_ref = bf16[8,2,96,128]{3,2,1,0:T(8,128)(2,1)S(1)} collective-permute-done((bf16[8,2,96,128]{3,2,1,0:T(8,128)(2,1)S(1)}, bf16[8,2,96,128]{3,2,1,0:T(8,128)(2,1)S(1)}, u32[]{:S(2)}, u32[]{:S(2)}) %collective-permute-start) | collective-permute-done | bytes 393248 | tf_op jit(solution)/shard_map/ppermute | solution.py:445
  100.6 0.0 copy-start.6
  100.6 0.7 copy-done.6
  101.3 4.8 %early_forward.1 = (bf16[32,1,96,128]{3,2,1,0:T(8,128)(2,1)}, f32[4,4,256]{2,1,0:T(4,128)}) custom-call(s32[16]{0:T(128)} %and_select_fusion.tile_start_ref, s32[16,256]{1,0:T(8,128)} %copy-done.5, bf16[32,3,96,128]{3,2,1,0:T(8,128)(2,1)} %copy-done.1, bf16[8,2,96,128]{3,2,1,0:T(8,128)(2,1)} %copy-done.6, ...), custom_call_target="tpu_custom_call", output_to_operand_aliasing={{0}: (4, {}), {1}: (5, {})} | custom-call | flops 1342177280 | bytes 8388608 | tf_op jit(solution)/shard_map/early_forward/pallas_call | solution.py:232
  106.2 0.0 all-to-all-done.2.g_ref
  106.2 0.0 copy-start.3
  106.2 0.9 copy-done.3
  107.1 6.8 %all-to-all-start.1 = ((bf16[32,1,96,128]{3,2,1,0:T(8,128)(2,1)}), bf16[32,1,96,128]{3,2,1,0:T(8,128)(2,1)S(1)}, u32[]{:S(2)}, u32[]{:S(2)}) async-start(bf16[32,1,96,128]{3,2,1,0:T(8,128)(2,1)} %get-tuple-element.18.out_ref), calls=%async_computation.1 | async-start | bytes 1572864 | tf_op jit(solution)/shard_map/all_to_all | solution.py:422
  113.9 7.0 %early_backward.1 = (bf16[8,2,96,128]{3,2,1,0:T(8,128)(2,1)}, f32[2,96,1024]{2,1,0:T(8,128)}, bf16[8,96,128]{2,1,0:T(8,128)(2,1)}) custom-call(s32[16]{0:T(128)} %and_select_fusion.tile_start_ref, s32[16,256]{1,0:T(8,128)} %copy-done.5, bf16[32,3,96,128]{3,2,1,0:T(8,128)(2,1)} %copy-done.1, bf16[8,2,96,128]{3,2,1,0:T(8,128)(2,1)} %copy-done.6, ...), custom_call_target="tpu_custom_call" | custom-call | flops 3355443200 | bytes 8388608 | tf_op jit(solution)/shard_map/early_backward/pallas_call | solution.py:349
  120.9 5.9 %collective-permute-start.1 = (bf16[8,2,96,128]{3,2,1,0:T(8,128)(2,1)}, bf16[8,2,96,128]{3,2,1,0:T(8,128)(2,1)S(1)}, u32[]{:S(2)}, u32[]{:S(2)}) collective-permute-start(bf16[8,2,96,128]{3,2,1,0:T(8,128)(2,1)} %get-tuple-element.20), channel_id=1, source_target_pairs={{38,0},{39,1},{36,2},{37,3},{34,4},{35,5},{32,6},{33,7},{46,8},{47... | collective-permute-start | bytes 1179656 | tf_op jit(solution)/shard_map/ppermute | solution.py:450
  126.8 17.0 %late_backward.1 = (bf16[32,3,96,128]{3,2,1,0:T(8,128)(2,1)}, f32[8,2,96,128]{3,2,1,0:T(8,128)}) custom-call(s32[16]{0:T(128)} %and_select_fusion.tile_start_ref, s32[16,256]{1,0:T(8,128)} %copy-done.5, bf16[32,3,96,128]{3,2,1,0:T(8,128)(2,1)} %copy-done.1, bf16[32,1,96,128]{3,2,1,0:T(8,128)(2,1)} %copy-done.3, ...), custom_call_target="tpu_custom_call" | custom-call | flops 10066329600 | bytes 8388608 | tf_op jit(solution)/shard_map/late_backward/pallas_call | solution.py:367
  143.9 1.7 collective-permute-done.1.back_ref
  145.6 0.0 copy-start.4
  145.6 0.7 copy-done.4
  146.4 2.1 join.1
  148.4 0.0 all-to-all-done.1.in_ref
  148.5 0.0 copy-start.2
  148.5 0.9 copy-done.2
  149.3 5.9 %all-to-all-start.3 = ((bf16[32,3,96,128]{3,2,1,0:T(8,128)(2,1)}), bf16[32,3,96,128]{3,2,1,0:T(8,128)(2,1)S(1)}, u32[]{:S(2)}, u32[]{:S(2)}) async-start(bf16[32,3,96,128]{3,2,1,0:T(8,128)(2,1)} %join.1), calls=%async_computation.3 | async-start | bytes 4718592 | tf_op jit(solution)/shard_map/all_to_all | solution.py:422
  155.2 3.5 %unpack.2 = bf16[128,3072]{1,0:T(8,128)(2,1)} custom-call(s32[1]{0:T(128)} %bitcast.mirror_ref, bf16[32,1,96,128]{3,2,1,0:T(8,128)(2,1)} %copy-done.2), custom_call_target="tpu_custom_call" | custom-call | tf_op jit(solution)/shard_map/unpack/pallas_call | solution.py:80
  158.6 52.6 %all-to-all-done.3.in_ref = bf16[32,3,96,128]{3,2,1,0:T(8,128)(2,1)S(1)} async-done(((bf16[32,3,96,128]{3,2,1,0:T(8,128)(2,1)}), bf16[32,3,96,128]{3,2,1,0:T(8,128)(2,1)S(1)}, u32[]{:S(2)}, u32[]{:S(2)}) %all-to-all-start.3) | async-done | bytes 2359328 | tf_op jit(solution)/shard_map/all_to_all | solution.py:422
  211.3 0.0 copy-start
  211.3 1.4 copy-done
  212.7 4.0 %unpack.3 = (bf16[128,3072]{1,0:T(8,128)(2,1)}, bf16[128,3072]{1,0:T(8,128)(2,1)}, bf16[128,3072]{1,0:T(8,128)(2,1)}) custom-call(s32[1]{0:T(128)} %bitcast.mirror_ref, bf16[32,3,96,128]{3,2,1,0:T(8,128)(2,1)} %copy-done), custom_call_target="tpu_custom_call" | custom-call | tf_op jit(solution)/shard_map/unpack/pallas_call | solution.py:80
  (3 shorter events, 0.0 us)
Async XLA Ops:
  4.9 65.0 %all-to-all-start = ((bf16[32,3,96,128]{3,2,1,0:T(8,128)(2,1)}), bf16[32,3,96,128]{3,2,1,0:T(8,128)(2,1)S(1)}, u32[]{:S(2)}, u32[]{:S(2)}) async-start(bf16[32,3,96,128]{3,2,1,0:T(8,128)(2,1)} %pack.2), calls=%async_computation | async-start | bytes 4718592 | tf_op jit(solution)/shard_map/all_to_all | solution.py:422
  69.9 13.4 %copy-start.1 = (bf16[32,3,96,128]{3,2,1,0:T(8,128)(2,1)}, bf16[32,3,96,128]{3,2,1,0:T(8,128)(2,1)S(1)}, u32[]{:S(2)}) copy-start(bf16[32,3,96,128]{3,2,1,0:T(8,128)(2,1)S(1)} %all-to-all-done.kvq_ref) | copy-start | bytes 7077892
  69.9 36.3 %all-to-all-start.2 = ((bf16[32,1,96,128]{3,2,1,0:T(8,128)(2,1)}), bf16[32,1,96,128]{3,2,1,0:T(8,128)(2,1)S(1)}, u32[]{:S(2)}, u32[]{:S(2)}) async-start(bf16[32,1,96,128]{3,2,1,0:T(8,128)(2,1)} %pack.3), calls=%async_computation.2 | async-start | bytes 1572864 | tf_op jit(solution)/shard_map/all_to_all | solution.py:422
  76.0 7.4 %copy-start.5 = (s32[16,256]{1,0:T(8,128)}, s32[16,256]{1,0:T(8,128)S(1)}, u32[]{:S(2)}) copy-start(s32[16,256]{1,0:T(8,128)S(1)} %reshape.22.start_ref) | copy-start | bytes 49156
  76.1 24.5 %collective-permute-start = (bf16[8,2,96,128]{3,2,1,0:T(8,128)(2,1)S(1)}, bf16[8,2,96,128]{3,2,1,0:T(8,128)(2,1)S(1)}, u32[]{:S(2)}, u32[]{:S(2)}) collective-permute-start(bf16[8,2,96,128]{3,2,1,0:T(8,128)(2,1)S(1)} %slice.9), channel_id=1, source_target_pairs={{0,38},{1,39},{2,36},{3,37},{4,34},{5,35},{6,32},{7,33},{8,46},{9,... | collective-permute-start | bytes 1179656 | tf_op jit(solution)/shard_map/ppermute | solution.py:445
  100.6 0.7 copy-start.6
  106.2 0.9 copy-start.3
  107.1 41.4 %all-to-all-start.1 = ((bf16[32,1,96,128]{3,2,1,0:T(8,128)(2,1)}), bf16[32,1,96,128]{3,2,1,0:T(8,128)(2,1)S(1)}, u32[]{:S(2)}, u32[]{:S(2)}) async-start(bf16[32,1,96,128]{3,2,1,0:T(8,128)(2,1)} %get-tuple-element.18.out_ref), calls=%async_computation.1 | async-start | bytes 1572864 | tf_op jit(solution)/shard_map/all_to_all | solution.py:422
  120.9 24.7 %collective-permute-start.1 = (bf16[8,2,96,128]{3,2,1,0:T(8,128)(2,1)}, bf16[8,2,96,128]{3,2,1,0:T(8,128)(2,1)S(1)}, u32[]{:S(2)}, u32[]{:S(2)}) collective-permute-start(bf16[8,2,96,128]{3,2,1,0:T(8,128)(2,1)} %get-tuple-element.20), channel_id=1, source_target_pairs={{38,0},{39,1},{36,2},{37,3},{34,4},{35,5},{32,6},{33,7},{46,8},{47... | collective-permute-start | bytes 1179656 | tf_op jit(solution)/shard_map/ppermute | solution.py:450
  145.6 0.7 copy-start.4
  148.5 0.9 copy-start.2
  149.3 61.9 %all-to-all-start.3 = ((bf16[32,3,96,128]{3,2,1,0:T(8,128)(2,1)}), bf16[32,3,96,128]{3,2,1,0:T(8,128)(2,1)S(1)}, u32[]{:S(2)}, u32[]{:S(2)}) async-start(bf16[32,3,96,128]{3,2,1,0:T(8,128)(2,1)} %join.1), calls=%async_computation.3 | async-start | bytes 4718592 | tf_op jit(solution)/shard_map/all_to_all | solution.py:422
  211.3 1.4 copy-start

commit v3 on v2

v3 whole, which is shorter than its diff:
```python
import functools
import math

import jax
import jax.numpy as jnp
from jax import lax
from jax.experimental import pallas as pl
from jax.experimental.pallas import tpu as pltpu
from jax.sharding import Mesh
from jax.sharding import PartitionSpec as P

HEAD_DIM = 96
HEADS = 32
CHUNK = 128
CHUNKS = 32
HALO = 8
DOC_BITS = 6
EXTRA = 16
WIDE = HEAD_DIM + EXTRA
FAR = 2.0**20
GROUP = CHUNK * CHUNKS
AHEAD = CHUNK * HALO
WINDOW = GROUP + AHEAD
TILE = 256
TILES = GROUP // TILE
AHEAD_TILES = AHEAD // TILE
REACH = AHEAD_TILES + 1
NEG = -1e30
SCALE = 1.0 / math.sqrt(HEAD_DIM)
LOG2E = 1.4426950408889634
MIB = 1024 * 1024

AXES = ("x", "zh", "y", "zl", "c")
GROUP_AXES = ("y", "zl", "c")
F32 = jnp.float32
BF16 = jnp.bfloat16


def vmem():
    return pl.BlockSpec(memory_space=pltpu.VMEM)


def smem():
    return pl.BlockSpec(memory_space=pltpu.SMEM)


def pack_kernel(mirror_ref, *refs):
    sources, out_ref = refs[:-1], refs[-1]
    mirrored = mirror_ref[0]
    for n, ref in enumerate(sources):
        turned = ref[...].T
        for zl in range(4):
            slot = 2 * jnp.where(mirrored == 1, 3 - zl, zl)
            piece = turned[zl * 192 : (zl + 1) * 192]
            out_ref[pl.ds(slot, 2), n] = piece.reshape(2, HEAD_DIM, CHUNK)


def pack(mirror, *arrays):
    count = len(arrays)
    return pl.pallas_call(
        pack_kernel,
        grid=(4,),
        in_specs=[smem()] + [pl.BlockSpec((CHUNK, 768), lambda y: (0, y))] * count,
        out_specs=pl.BlockSpec((8, count, HEAD_DIM, CHUNK), lambda y: (y, 0, 0, 0)),
        out_shape=jax.ShapeDtypeStruct((HEADS, count, HEAD_DIM, CHUNK), BF16),
        compiler_params=pltpu.CompilerParams(vmem_limit_bytes=8 * MIB),
        name="pack",
    )(mirror, *arrays)


def unpack_kernel(mirror_ref, in_ref, *out_refs):
    mirrored = mirror_ref[0]
    for n, out_ref in enumerate(out_refs):
        pieces = []
        for zl in range(4):
            slot = 2 * jnp.where(mirrored == 1, 3 - zl, zl)
            pieces.append(in_ref[pl.ds(slot, 2), n].reshape(192, CHUNK))
        out_ref[...] = jnp.concatenate(pieces, 0).T


def unpack(mirror, array):
    count = array.shape[1]
    return pl.pallas_call(
        unpack_kernel,
        grid=(4,),
        in_specs=[
            smem(),
            pl.BlockSpec((8, count, HEAD_DIM, CHUNK), lambda y: (y, 0, 0, 0)),
        ],
        out_specs=[pl.BlockSpec((CHUNK, 768), lambda y: (0, y))] * count,
        out_shape=[jax.ShapeDtypeStruct((CHUNK, HEADS * HEAD_DIM), BF16)] * count,
        compiler_params=pltpu.CompilerParams(vmem_limit_bytes=8 * MIB),
        name="unpack",
    )(mirror, array)


def tile_of(ref, n, i):
    return jnp.concatenate([ref[2 * i, n], ref[2 * i + 1, n]], 1)


def nn(a, b):
    return lax.dot_general(a, b, (((1,), (0,)), ((), ())), preferred_element_type=F32)


def nt(a, b):
    return lax.dot_general(a, b, (((1,), (1,)), ((), ())), preferred_element_type=F32)


def each_chunk(halo_ref, own_ref, n, chunks):
    for chunk in chunks:
        piece = halo_ref[chunk, n] if chunk < HALO else own_ref[chunk - HALO, n]
        yield slice(chunk * CHUNK, (chunk + 1) * CHUNK), piece


def fill_keys(halo_ref, own_ref, code_ref, chunks, flat, turned):
    for span, piece in each_chunk(halo_ref, own_ref, 0, chunks):
        flat[span, :] = jnp.concatenate([piece, code_ref[:, span]], 0).T
        if turned is not None:
            turned[:, span] = piece


def fill_value_rows(halo_ref, own_ref, chunks, flat):
    row = lax.broadcasted_iota(jnp.int32, (EXTRA, CHUNK), 0)
    minus = jnp.where(row < 3, -1.0, 0.0).astype(BF16)
    for span, piece in each_chunk(halo_ref, own_ref, 1, chunks):
        flat[span, :] = jnp.concatenate([piece, minus], 0).T


def fill_value_columns(halo_ref, own_ref, chunks, turned):
    for span, piece in each_chunk(halo_ref, own_ref, 1, chunks):
        turned[:HEAD_DIM, span] = piece
        turned[HEAD_DIM:, span] = jnp.ones((EXTRA, CHUNK), BF16)


def with_row(extra, first, value):
    high = value.astype(BF16).astype(F32)
    middle = (value - high).astype(BF16).astype(F32)
    low = value - high - middle
    row = lax.broadcasted_iota(jnp.int32, (EXTRA, TILE), 0)
    for n, part in enumerate((high, middle, low)):
        extra = jnp.where(row == first + n, part, extra)
    return extra.astype(BF16)


def causal():
    row = lax.broadcasted_iota(jnp.int32, (TILE, TILE), 0)
    return row <= lax.broadcasted_iota(jnp.int32, (TILE, TILE), 1)


def per_tile(tile_start_ref, i, body):
    reach = jnp.clip(i + REACH - tile_start_ref[i], 1, REACH)
    for count in range(1, REACH + 1):
        pl.when(reach == count)(functools.partial(body, count))


def forward_tiles(
    low, tile_start_ref, query_code_ref, kvq_ref, out_ref, stat_ref, key_flat, value_turned
):
    def tile(step, _):
        i = low + step

        def body(count):
            q = jnp.concatenate([tile_of(kvq_ref, 2, i), query_code_ref[i]], 0)
            scores = []
            top = None
            for j in range(count):
                first = pl.multiple_of((i + REACH - count + j) * TILE, TILE)
                s = nn(key_flat[pl.ds(first, TILE), :], q)
                if j == count - 1:
                    s = jnp.where(causal(), s, NEG)
                scores.append(s)
                t = jnp.max(s, axis=0, keepdims=True)
                top = t if top is None else jnp.maximum(top, t)
            shift = top * (SCALE * LOG2E)
            out = None
            for j in range(count):
                first = pl.multiple_of((i + REACH - count + j) * TILE, TILE)
                e = jnp.exp2(scores[j] * (SCALE * LOG2E) - shift)
                o = nn(value_turned[:, pl.ds(first, TILE)], e.astype(BF16))
                out = o if out is None else out + o
            total = out[HEAD_DIM : HEAD_DIM + 1]
            out = (out[:HEAD_DIM] / total).astype(BF16)
            out_ref[2 * step, 0] = out[:, :CHUNK]
            out_ref[2 * step + 1, 0] = out[:, CHUNK:]
            stat_ref[0, pl.ds(step, 1), :] = top + jnp.log(total) * (1.0 / SCALE)

        per_tile(tile_start_ref, i, body)
        return 0

    lax.fori_loop(0, AHEAD_TILES, tile, 0)


def late_forward_kernel(
    tile_start_ref, key_code_ref, query_code_ref, kvq_ref, out_ref, stat_ref, key_flat, value_turned
):
    @pl.when(pl.program_id(0) == 0)
    def _():
        chunks = range(HALO, HALO + CHUNKS)
        fill_keys(None, kvq_ref, key_code_ref, chunks, key_flat, None)
        fill_value_columns(None, kvq_ref, chunks, value_turned)

    forward_tiles(
        (pl.program_id(0) + 1) * AHEAD_TILES,
        tile_start_ref, query_code_ref, kvq_ref, out_ref, stat_ref, key_flat, value_turned
    )


def early_forward_kernel(
    tile_start_ref, key_code_ref, query_code_ref, kvq_ref, halo_ref, _, __, out_ref, stat_ref,
    key_flat, value_turned
):
    fill_keys(halo_ref, kvq_ref, key_code_ref, range(2 * HALO), key_flat, None)
    fill_value_columns(halo_ref, kvq_ref, range(2 * HALO), value_turned)
    forward_tiles(
        0, tile_start_ref, query_code_ref, kvq_ref, out_ref, stat_ref, key_flat, value_turned
    )


def cost(products, tiles):
    return pl.CostEstimate(
        flops=2 * products * tiles * REACH * TILE * TILE * 256,
        bytes_accessed=8 << 20,
        transcendentals=tiles * REACH * TILE * TILE,
    )


OUT_SHAPES = [
    jax.ShapeDtypeStruct((CHUNKS, 1, HEAD_DIM, CHUNK), BF16),
    jax.ShapeDtypeStruct((TILES // AHEAD_TILES, AHEAD_TILES, TILE), F32),
]


def out_specs(first):
    return [
        pl.BlockSpec((HALO, 1, HEAD_DIM, CHUNK), lambda b: (b + first, 0, 0, 0)),
        pl.BlockSpec((1, AHEAD_TILES, TILE), lambda b: (b + first, 0, 0)),
    ]


def late_forward(tile_start, codes, kvq):
    return pl.pallas_call(
        late_forward_kernel,
        grid=(TILES // AHEAD_TILES - 1,),
        in_specs=[smem(), vmem(), vmem(), vmem()],
        out_specs=out_specs(1),
        out_shape=OUT_SHAPES,
        scratch_shapes=[
            pltpu.VMEM((WINDOW, WIDE), BF16),
            pltpu.VMEM((WIDE, WINDOW), BF16),
        ],
        compiler_params=pltpu.CompilerParams(vmem_limit_bytes=18 * MIB),
        cost_estimate=cost(2, TILES - AHEAD_TILES),
        name="late_forward",
    )(tile_start, *codes, kvq)


def early_forward(tile_start, codes, kvq, halo, out, stat):
    whole = pl.BlockSpec((2 * HALO, 3, HEAD_DIM, CHUNK), lambda b: (0, 0, 0, 0))
    return pl.pallas_call(
        early_forward_kernel,
        grid=(1,),
        in_specs=[smem(), vmem(), vmem(), whole, vmem()] + [pl.BlockSpec(memory_space=pl.ANY)] * 2,
        out_specs=out_specs(0),
        out_shape=OUT_SHAPES,
        input_output_aliases={5: 0, 6: 1},
        scratch_shapes=[
            pltpu.VMEM((2 * AHEAD, WIDE), BF16),
            pltpu.VMEM((WIDE, 2 * AHEAD), BF16),
        ],
        compiler_params=pltpu.CompilerParams(vmem_limit_bytes=14 * MIB),
        cost_estimate=cost(2, AHEAD_TILES),
        name="early_forward",
    )(tile_start, *codes, kvq, halo, out, stat)


def backward_tiles(
    low, high, tile_start_ref, query_code_ref, kvq_ref, g_ref, out_ref, stat_ref, store,
    key_flat, key_turned, value_flat, key_sum, value_sum
):
    def tile(i, _):
        def body(count):
            q = tile_of(kvq_ref, 2, i)
            g = tile_of(g_ref, 0, i)
            o = tile_of(out_ref, 0, i)
            delta = jnp.sum(o.astype(F32) * g.astype(F32), axis=0, keepdims=True)
            stat = stat_ref[i // AHEAD_TILES, pl.ds(i % AHEAD_TILES, 1), :]
            code = query_code_ref[i].astype(F32)
            q_wide = jnp.concatenate([q, with_row(code, 2 * DOC_BITS, stat)], 0)
            g_wide = jnp.concatenate([g, with_row(jnp.zeros_like(code), 0, delta)], 0)
            grad_q = None
            for j in range(count):
                first = pl.multiple_of((i + REACH - count + j) * TILE, TILE)
                span = pl.ds(first, TILE)
                p = jnp.exp2(nn(key_flat[span, :], q_wide) * (SCALE * LOG2E))
                if j == count - 1:
                    p = jnp.where(causal(), p, 0.0)
                d = (p * nn(value_flat[span, :], g_wide)).astype(BF16)
                t = nn(key_turned[:, span], d)
                grad_q = t if grad_q is None else grad_q + t
                key_sum[:, span] += nt(q, d)
                value_sum[:, span] += nt(g, p.astype(BF16))
            grad_q = (grad_q * SCALE).astype(BF16)
            store(2 * i, grad_q[:, :CHUNK])
            store(2 * i + 1, grad_q[:, CHUNK:])

        per_tile(tile_start_ref, i, body)
        return 0

    lax.fori_loop(low, high, tile, 0)


def early_backward_kernel(
    tile_start_ref, key_code_ref, query_code_ref, kvq_ref, halo_ref, g_ref, out_ref, stat_ref,
    back_ref, carry_ref, grad_q_ref, key_flat, key_turned, value_flat, key_sum, value_sum
):
    fill_keys(halo_ref, kvq_ref, key_code_ref, range(2 * HALO), key_flat, key_turned)
    fill_value_rows(halo_ref, kvq_ref, range(2 * HALO), value_flat)
    key_sum[...] = jnp.zeros_like(key_sum)
    value_sum[...] = jnp.zeros_like(value_sum)

    def store(chunk, value):
        grad_q_ref[chunk] = value

    backward_tiles(
        0, AHEAD_TILES, tile_start_ref, query_code_ref, kvq_ref, g_ref, out_ref, stat_ref, store,
        key_flat, key_turned, value_flat, key_sum, value_sum
    )
    for n, (sums, factor) in enumerate(((key_sum, SCALE), (value_sum, 1.0))):
        for chunk in range(HALO):
            piece = sums[:, chunk * CHUNK : (chunk + 1) * CHUNK] * factor
            back_ref[chunk, n] = piece.astype(BF16)
        carry_ref[n] = sums[:, AHEAD:]


def late_backward_kernel(
    tile_start_ref, key_code_ref, query_code_ref, kvq_ref, g_ref, out_ref, stat_ref, carry_ref,
    grad_q_ref,
    grads_ref, rest_ref, key_flat, key_turned, value_flat, key_sum, value_sum
):
    chunks = range(HALO, HALO + CHUNKS)
    fill_keys(None, kvq_ref, key_code_ref, chunks, key_flat, key_turned)
    fill_value_rows(None, kvq_ref, chunks, value_flat)
    for n, sums in enumerate((key_sum, value_sum)):
        sums[:, AHEAD : 2 * AHEAD] = carry_ref[n]
        sums[:, 2 * AHEAD :] = jnp.zeros((HEAD_DIM, WINDOW - 2 * AHEAD), F32)
    for chunk in range(HALO):
        grads_ref[chunk, 2] = grad_q_ref[chunk]

    def store(chunk, value):
        grads_ref[chunk, 2] = value

    backward_tiles(
        AHEAD_TILES, TILES, tile_start_ref, query_code_ref, kvq_ref, g_ref, out_ref, stat_ref, store,
        key_flat, key_turned, value_flat, key_sum, value_sum
    )
    for n, (sums, factor) in enumerate(((key_sum, SCALE), (value_sum, 1.0))):
        for chunk in chunks:
            piece = sums[:, chunk * CHUNK : (chunk + 1) * CHUNK] * factor
            grads_ref[chunk - HALO, n] = piece.astype(BF16)
            if chunk >= CHUNKS:
                rest_ref[chunk - CHUNKS, n] = piece


def sums_scratch(window):
    return [
        pltpu.VMEM((window, WIDE), BF16),
        pltpu.VMEM((HEAD_DIM, window), BF16),
        pltpu.VMEM((window, WIDE), BF16),
        pltpu.VMEM((HEAD_DIM, window), F32),
        pltpu.VMEM((HEAD_DIM, window), F32),
    ]


def early_backward(tile_start, codes, kvq, halo, g, out, stat):
    def part(count, width):
        return pl.BlockSpec((count, width, HEAD_DIM, CHUNK), lambda b: (0, 0, 0, 0))

    return pl.pallas_call(
        early_backward_kernel,
        grid=(1,),
        in_specs=[smem(), vmem(), vmem(), part(HALO, 3), vmem(), part(HALO, 1), part(HALO, 1), vmem()],
        out_specs=[vmem()] * 3,
        out_shape=[
            jax.ShapeDtypeStruct((HALO, 2, HEAD_DIM, CHUNK), BF16),
            jax.ShapeDtypeStruct((2, HEAD_DIM, AHEAD), F32),
            jax.ShapeDtypeStruct((HALO, HEAD_DIM, CHUNK), BF16),
        ],
        scratch_shapes=sums_scratch(2 * AHEAD),
        compiler_params=pltpu.CompilerParams(vmem_limit_bytes=16 * MIB),
        cost_estimate=cost(5, AHEAD_TILES),
        name="early_backward",
    )(tile_start, *codes, kvq, halo, g, out, stat)


def late_backward(tile_start, codes, kvq, g, out, stat, carry, grad_q):
    return pl.pallas_call(
        late_backward_kernel,
        in_specs=[smem()] + [vmem()] * 8,
        out_specs=[vmem()] * 2,
        out_shape=[
            jax.ShapeDtypeStruct((CHUNKS, 3, HEAD_DIM, CHUNK), BF16),
            jax.ShapeDtypeStruct((HALO, 2, HEAD_DIM, CHUNK), F32),
        ],
        scratch_shapes=sums_scratch(WINDOW),
        compiler_params=pltpu.CompilerParams(vmem_limit_bytes=28 * MIB),
        cost_estimate=cost(5, TILES - AHEAD_TILES),
        name="late_backward",
    )(tile_start, *codes, kvq, g, out, stat, carry, grad_q)


def join_kernel(back_ref, rest_ref, _, out_ref):
    out_ref[...] = (rest_ref[...] + back_ref[...].astype(F32)).astype(BF16)


def join(back, rest, grads):
    whole = (HALO, 2, HEAD_DIM, CHUNK)
    return pl.pallas_call(
        join_kernel,
        grid=(1,),
        in_specs=[
            pl.BlockSpec(whole, lambda i: (0, 0, 0, 0)),
            pl.BlockSpec(whole, lambda i: (0, 0, 0, 0)),
            pl.BlockSpec(memory_space=pl.ANY),
        ],
        out_specs=pl.BlockSpec(whole, lambda i: (CHUNKS // HALO - 1, 0, 0, 0)),
        out_shape=jax.ShapeDtypeStruct(grads.shape, BF16),
        input_output_aliases={2: 0},
        compiler_params=pltpu.CompilerParams(vmem_limit_bytes=6 * MIB),
        name="join",
    )(back, rest, grads)


def gate_kernel(_, __, ___):
    pass


def after(array, other):
    return pl.pallas_call(
        gate_kernel,
        in_specs=[pl.BlockSpec(memory_space=pl.ANY)] * 2,
        out_specs=pl.BlockSpec(memory_space=pl.ANY),
        out_shape=jax.ShapeDtypeStruct(array.shape, array.dtype),
        input_output_aliases={0: 0},
        name="after",
    )(array, other)


def group_pairs():
    def index(x, zh, y, zl, c):
        return (((x * 2 + zh) * 4 + y) * 4 + zl) * 2 + c

    pairs = []
    for group in range(7):
        for y in range(4):
            for zl in range(4):
                for c in range(2):
                    pairs.append(
                        (
                            index(group // 2, group % 2, y, zl, c),
                            index((group + 1) // 2, (group + 1) % 2, y, 3 - zl, c),
                        )
                    )
    return pairs


def to_heads(array):
    return lax.all_to_all(array, GROUP_AXES, split_axis=0, concat_axis=0, tiled=True)


def places(doc_ids):
    group = lax.axis_index("x") * 2 + lax.axis_index("zh")
    own = lax.dynamic_slice_in_dim(doc_ids, group * GROUP, GROUP)
    ahead = lax.dynamic_slice_in_dim(doc_ids, jnp.maximum(group * GROUP - AHEAD, 0), AHEAD)
    ahead = jnp.where(group > 0, ahead, -1)
    docs = jnp.concatenate([ahead, own])
    leads = own.reshape(TILES, TILE)[:, :1]
    tile_start = jnp.sum((docs[None] < leads).astype(jnp.int32), 1) // TILE
    row = jnp.arange(EXTRA, dtype=jnp.int32)[:, None]
    bits = (docs[None] >> (row // 2)) & 1
    coded = row < 2 * DOC_BITS
    differs = (bits != row % 2) | (docs[None] < 0)
    key_code = jnp.where(coded, jnp.where(differs, -FAR, 0.0), jnp.where(row < 15, -1.0, 0.0))
    query_code = jnp.where(coded & (bits[:, AHEAD:] == row % 2), 1.0, 0.0)
    query_code = query_code.reshape(EXTRA, TILES, TILE).transpose(1, 0, 2)
    return tile_start, (key_code.astype(BF16), query_code.astype(BF16))


def shards(queries, keys, values, cotangent, doc_ids):
    mirror = lax.axis_index("zh").astype(jnp.int32).reshape(1)
    kvq = to_heads(pack(mirror, keys, values, queries))
    tile_start, codes = places(doc_ids)
    cotangent, tile_start, codes = lax.optimization_barrier((cotangent, tile_start, codes))
    pairs = group_pairs()
    last = kvq[CHUNKS - HALO :, :2]
    halo = lax.ppermute(last, AXES, pairs)
    g = to_heads(after(pack(mirror, cotangent), last))
    out, stat = late_forward(tile_start, codes, kvq)
    out, stat = early_forward(tile_start, codes, kvq, halo, out, stat)
    back, carry, early_q = early_backward(tile_start, codes, kvq, halo, g, out, stat)
    grads, rest = late_backward(tile_start, codes, kvq, g, out, stat, carry, early_q)
    back = lax.ppermute(back, AXES, [(b, a) for a, b in pairs])
    grads = join(back, rest, grads)
    (attended,) = unpack(mirror, to_heads(out))
    grad_k, grad_v, grad_q = unpack(mirror, to_heads(grads))
    return attended, grad_q, grad_k, grad_v


def solution(mesh):
    wide = Mesh(mesh.devices.reshape(4, 2, 4, 4, 2), AXES)
    rows = P(AXES, None)
    return jax.shard_map(
        shards,
        mesh=wide,
        in_specs=(rows, rows, rows, rows, P()),
        out_specs=(rows, rows, rows, rows),
        check_vma=False,
    )
```

time: 218 us -> 215 us (0.986)
  Pallas kernels: 56.5 us -> 38 us
  local copies, waits for them, and re-layouts: 5.53 us -> 13.1 us
  waiting for transfers between devices: 114 us -> 119 us
  starting transfers between devices: 38.1 us -> 40.7 us
    unnamed x14 -> x28, local copies, waits for them, and re-layouts: 4.66 us -> 11.5 us
    pallas_call x2, Pallas kernels: 7.72 us -> 3 us  [pack(): pl.pallas_call(pack_kernel, grid=(4,), in_specs=[smem()] + [pl.BlockSpec(...]
    pallas_call x2, Pallas kernels: 7.46 us -> 3.77 us  [unpack(): pl.pallas_call(unpack_kernel, grid=(4,), in_specs=[smem(), pl.BlockSpec((...]
    pallas_call x1 -> x2, Pallas kernels: 17 us -> 13.7 us  [the longest x1 13.7 us: late_backward(): pl.pallas_call(late_backward_kernel, in_specs=[smem()] + [vmem()] * 8, ou...]
    all_to_all x4, starting transfers between devices: 25.5 us -> 28.2 us  [to_heads(): lax.all_to_all(array, GROUP_AXES, split_axis=0, concat_axis=0, tiled=True)]
    ppermute x1, waiting for transfers between devices: 1.74 us -> 3.97 us  [shards(): back = lax.ppermute(back, AXES, [(b, a) for a, b in pairs])]
  transfers between devices with their start and end apart: 6 -> 6, of which waited for: 4 -> 4; matrix products, arithmetic and copies ran while one was open for 1% -> 1% of each run, Pallas kernels for 22% -> 16%
where the time goes in v3:
time: 215 us; the launch traced here: 213 us
  waiting for transfers between devices  119 us (55%)
  starting transfers between devices  40.7 us (19%)
  Pallas kernels  38 us (18%)
  local copies, waits for them, and re-layouts  13.1 us (6%)
    all_to_all x4, waiting for transfers between devices, to_heads(): lax.all_to_all(array, GROUP_AXES, split_axis=0, concat_axis=0, tiled=True)  107 us
    all_to_all x4, starting transfers between devices, to_heads(): lax.all_to_all(array, GROUP_AXES, split_axis=0, concat_axis=0, tiled=True)  28.2 us
    pallas_call x1, Pallas kernels, late_backward(): pl.pallas_call(late_backward_kernel, in_specs=[smem()] + [vmem()] * 8, ou...  13.7 us
    unnamed x28, local copies, waits for them, and re-layouts  11.5 us
    pallas_call x1, Pallas kernels, late_forward(): pl.pallas_call(late_forward_kernel, grid=(TILES // AHEAD_TILES - 1,), in_...  8.89 us
    ppermute x1, waiting for transfers between devices, shards(): halo = lax.ppermute(last, AXES, pairs)  8.54 us
    ppermute x1, starting transfers between devices, shards(): halo = lax.ppermute(last, AXES, pairs)  6.65 us
    ppermute x1, starting transfers between devices, shards(): back = lax.ppermute(back, AXES, [(b, a) for a, b in pairs])  5.86 us
  transfers between devices with their start and end apart: 6, of which 4 were waited for; matrix products, arithmetic and copies ran while one was open for 1% of the time, Pallas kernels for 16%

profile of v3, /device:TPU:4, one launch (start us, length us, event | category | flops | bytes accessed | tf_op | source)
XLA Modules:
  0.0 213.3 jit_solution(839788452305984125)
XLA Ops:
  0.6 0.0 copy-start.2
  0.6 1.1 copy-done.2
  1.8 0.0 copy-start.3
  1.8 1.1 copy-done.3
  2.9 1.1 copy-done.4
  4.0 2.4 %pack.2 = bf16[32,3,96,128]{3,2,1,0:T(8,128)(2,1)} custom-call(s32[1]{0:T(128)} %bitcast.mirror_ref, bf16[128,3072]{1,0:T(8,128)(2,1)S(1)} %copy-done.2, bf16[128,3072]{1,0:T(8,128)(2,1)S(1)} %copy-done.3, bf16[128,3072]{1,0:T(8,128)(2,1)S(1)} %copy-done.4), custom_call_target="tpu_custom_call" | custom-call | tf_op jit(solution)/shard_map/pack/pallas_call | solution.py:60
  6.5 9.1 %all-to-all-start = ((bf16[32,3,96,128]{3,2,1,0:T(8,128)(2,1)}), bf16[32,3,96,128]{3,2,1,0:T(8,128)(2,1)S(1)}, u32[]{:S(2)}, u32[]{:S(2)}) async-start(bf16[32,3,96,128]{3,2,1,0:T(8,128)(2,1)} %pack.2), calls=%async_computation | async-start | bytes 4718592 | tf_op jit(solution)/shard_map/all_to_all | solution.py:467
  15.6 0.7 dynamic_slice.7
  16.3 0.8 dynamic-slice_select_fusion
  17.1 0.1 slice_reduce_fusion
  17.2 0.2 shift-right-arithmetic_and_fusion
  17.5 0.1 select_convert_fusion.1
  17.6 0.2 select_convert_fusion.key_code_ref
  17.8 0.0 copy-done.5
  17.8 0.5 pack.3._
  18.4 0.0 copy-start.1
  18.4 0.9 copy-done.1
  19.3 52.4 %all-to-all-done.kvq_ref = bf16[32,3,96,128]{3,2,1,0:T(8,128)(2,1)S(1)} async-done(((bf16[32,3,96,128]{3,2,1,0:T(8,128)(2,1)}), bf16[32,3,96,128]{3,2,1,0:T(8,128)(2,1)S(1)}, u32[]{:S(2)}, u32[]{:S(2)}) %all-to-all-start) | async-done | bytes 2359328 | tf_op jit(solution)/shard_map/all_to_all | solution.py:467
  71.6 0.8 slice.14.__
  72.4 3.9 %all-to-all-start.2 = ((bf16[32,1,96,128]{3,2,1,0:T(8,128)(2,1)}), bf16[32,1,96,128]{3,2,1,0:T(8,128)(2,1)S(1)}, u32[]{:S(2)}, u32[]{:S(2)}) async-start(bf16[32,1,96,128]{3,2,1,0:T(8,128)(2,1)} %after.1), calls=%async_computation.2 | async-start | bytes 1572864 | tf_op jit(solution)/shard_map/all_to_all | solution.py:467
  76.3 6.7 %collective-permute-start = (bf16[8,2,96,128]{3,2,1,0:T(8,128)(2,1)}, bf16[8,2,96,128]{3,2,1,0:T(8,128)(2,1)S(1)}, u32[]{:S(2)}, u32[]{:S(2)}) collective-permute-start(bf16[8,2,96,128]{3,2,1,0:T(8,128)(2,1)} %slice.14.__), channel_id=1, source_target_pairs={{0,38},{1,39},{2,36},{3,37},{4,34},{5,35},{6,32},{7,33},{8,46},{9,... | collective-permute-start | bytes 1179656 | tf_op jit(solution)/shard_map/ppermute | solution.py:495
  83.0 8.9 %late_forward.1 = (bf16[32,1,96,128]{3,2,1,0:T(8,128)(2,1)S(1)}, f32[4,4,256]{2,1,0:T(4,128)S(1)}) custom-call(s32[16]{0:T(128)S(1)} %and_select_fusion.2.tile_start_ref, bf16[16,5120]{1,0:T(8,128)(2,1)S(1)} %select_convert_fusion.key_code_ref, bf16[16,16,256]{2,1,0:T(8,128)(2,1)S(1)} %bitcast.8, bf16[32,3,96,128]{3,2,1,0:T(8,128)(2,1)S(1)} %all-to-all-done.kvq_ref), custom_call_target="tpu_custom_call" | custom-call | flops 4026531840 | bytes 8388608 | tf_op jit(solution)/shard_map/late_forward/pallas_call | solution.py:241
  91.9 8.5 %collective-permute-done.halo_ref = bf16[8,2,96,128]{3,2,1,0:T(8,128)(2,1)S(1)} collective-permute-done((bf16[8,2,96,128]{3,2,1,0:T(8,128)(2,1)}, bf16[8,2,96,128]{3,2,1,0:T(8,128)(2,1)S(1)}, u32[]{:S(2)}, u32[]{:S(2)}) %collective-permute-start) | collective-permute-done | bytes 393248 | tf_op jit(solution)/shard_map/ppermute | solution.py:495
  100.4 3.4 %early_forward.1 = (bf16[32,1,96,128]{3,2,1,0:T(8,128)(2,1)S(1)}, f32[4,4,256]{2,1,0:T(4,128)S(1)}) custom-call(s32[16]{0:T(128)S(1)} %and_select_fusion.2.tile_start_ref, bf16[16,5120]{1,0:T(8,128)(2,1)S(1)} %select_convert_fusion.key_code_ref, bf16[16,16,256]{2,1,0:T(8,128)(2,1)S(1)} %bitcast.9, ...), custom_call_target="tpu_custom_call", output_to_operand_aliasing={{0}: (5, {}), {1}: (6, {})} | custom-call | flops 1342177280 | bytes 8388608 | tf_op jit(solution)/shard_map/early_forward/pallas_call | solution.py:259
  103.8 0.0 copy-start.9
  103.9 0.9 copy-done.9
  104.7 0.7 copy-done.12
  105.5 0.0 all-to-all-done.2.g_ref
  105.5 0.9 copy-done.6
  106.4 8.4 %all-to-all-start.1 = ((bf16[32,1,96,128]{3,2,1,0:T(8,128)(2,1)}), bf16[32,1,96,128]{3,2,1,0:T(8,128)(2,1)S(1)}, u32[]{:S(2)}, u32[]{:S(2)}) async-start(bf16[32,1,96,128]{3,2,1,0:T(8,128)(2,1)} %copy-done.9), calls=%async_computation.1 | async-start | bytes 1572864 | tf_op jit(solution)/shard_map/all_to_all | solution.py:467
  114.7 0.0 copy-start.7
  114.7 1.1 copy-done.7
  115.9 1.1 copy-done.10
  117.0 1.0 copy-done.13
  118.0 5.1 %early_backward.1 = (bf16[8,2,96,128]{3,2,1,0:T(8,128)(2,1)S(1)}, f32[2,96,1024]{2,1,0:T(8,128)S(1)}, bf16[8,96,128]{2,1,0:T(8,128)(2,1)S(1)}) custom-call(s32[16]{0:T(128)S(1)} %and_select_fusion.2.tile_start_ref, bf16[16,5120]{1,0:T(8,128)(2,1)S(1)} %select_convert_fusion.key_code_ref, bf16[16,16,256]{2,1,0:T(8,128)(2,1)S(1)} %bitcast.10, ...), custom_call_target="tpu_custom_call" | custom-call | flops 3355443200 | bytes 8388608 | tf_op jit(solution)/shard_map/early_backward/pallas_call | solution.py:378
  123.1 5.9 %collective-permute-start.1 = (bf16[8,2,96,128]{3,2,1,0:T(8,128)(2,1)S(1)}, bf16[8,2,96,128]{3,2,1,0:T(8,128)(2,1)S(1)}, u32[]{:S(2)}, u32[]{:S(2)}) collective-permute-start(bf16[8,2,96,128]{3,2,1,0:T(8,128)(2,1)S(1)} %get-tuple-element.28), channel_id=1, source_target_pairs={{38,0},{39,1},{36,2},{37,3},{34,4},{35,5},{32,6},{33,7},{46,8},{47... | collective-permute-start | bytes 1179656 | tf_op jit(solution)/shard_map/ppermute | solution.py:501
  129.0 0.0 copy-done.8
  129.0 0.0 copy-done.11
  129.0 13.7 %late_backward.1 = (bf16[32,3,96,128]{3,2,1,0:T(8,128)(2,1)S(1)}, f32[8,2,96,128]{3,2,1,0:T(8,128)S(1)}) custom-call(s32[16]{0:T(128)S(1)} %and_select_fusion.2.tile_start_ref, bf16[16,5120]{1,0:T(8,128)(2,1)S(1)} %select_convert_fusion.key_code_ref, bf16[16,16,256]{2,1,0:T(8,128)(2,1)S(1)} %bitcast.11, bf16[32,3,96,128]{3,2,1,0:T(8,128)(2,1)S(1)} %all-to-all-done.kvq_ref, ...), custom_call_target="tpu_custom_call" | custom-call | flops 10066329600 | bytes 8388608 | tf_op jit(solution)/shard_map/late_backward/pallas_call | solution.py:396
  142.7 4.0 %collective-permute-done.1.back_ref = bf16[8,2,96,128]{3,2,1,0:T(8,128)(2,1)S(1)} collective-permute-done((bf16[8,2,96,128]{3,2,1,0:T(8,128)(2,1)S(1)}, bf16[8,2,96,128]{3,2,1,0:T(8,128)(2,1)S(1)}, u32[]{:S(2)}, u32[]{:S(2)}) %collective-permute-start.1) | collective-permute-done | bytes 393248 | tf_op jit(solution)/shard_map/ppermute | solution.py:501
  146.7 0.2 join.1
  146.9 0.0 copy-start
  146.9 1.4 copy-done
  148.3 0.0 all-to-all-done.1.in_ref
  148.3 6.8 %all-to-all-start.3 = ((bf16[32,3,96,128]{3,2,1,0:T(8,128)(2,1)}), bf16[32,3,96,128]{3,2,1,0:T(8,128)(2,1)S(1)}, u32[]{:S(2)}, u32[]{:S(2)}) async-start(bf16[32,3,96,128]{3,2,1,0:T(8,128)(2,1)} %copy-done), calls=%async_computation.3 | async-start | bytes 4718592 | tf_op jit(solution)/shard_map/all_to_all | solution.py:467
  155.1 1.7 unpack.2
  156.9 54.4 %all-to-all-done.3.in_ref = bf16[32,3,96,128]{3,2,1,0:T(8,128)(2,1)S(1)} async-done(((bf16[32,3,96,128]{3,2,1,0:T(8,128)(2,1)}), bf16[32,3,96,128]{3,2,1,0:T(8,128)(2,1)S(1)}, u32[]{:S(2)}, u32[]{:S(2)}) %all-to-all-start.3) | async-done | bytes 2359328 | tf_op jit(solution)/shard_map/all_to_all | solution.py:467
  211.2 2.1 unpack.3
  (17 shorter events, 0.1 us)
Async XLA Ops:
  0.6 1.1 copy-start.2
  1.8 1.1 copy-start.3
  2.9 1.1 copy-start.4
  6.5 11.3 %copy-start.5 = (bf16[128,3072]{1,0:T(8,128)(2,1)S(1)}, bf16[128,3072]{1,0:T(8,128)(2,1)}, u32[]{:S(2)}) copy-start(bf16[128,3072]{1,0:T(8,128)(2,1)} %refs_0_.2) | copy-start | bytes 2359300
  6.5 65.1 %all-to-all-start = ((bf16[32,3,96,128]{3,2,1,0:T(8,128)(2,1)}), bf16[32,3,96,128]{3,2,1,0:T(8,128)(2,1)S(1)}, u32[]{:S(2)}, u32[]{:S(2)}) async-start(bf16[32,3,96,128]{3,2,1,0:T(8,128)(2,1)} %pack.2), calls=%async_computation | async-start | bytes 4718592 | tf_op jit(solution)/shard_map/all_to_all | solution.py:467
  18.4 0.9 copy-start.1
  72.4 33.1 %all-to-all-start.2 = ((bf16[32,1,96,128]{3,2,1,0:T(8,128)(2,1)}), bf16[32,1,96,128]{3,2,1,0:T(8,128)(2,1)S(1)}, u32[]{:S(2)}, u32[]{:S(2)}) async-start(bf16[32,1,96,128]{3,2,1,0:T(8,128)(2,1)} %after.1), calls=%async_computation.2 | async-start | bytes 1572864 | tf_op jit(solution)/shard_map/all_to_all | solution.py:467
  76.3 24.1 %collective-permute-start = (bf16[8,2,96,128]{3,2,1,0:T(8,128)(2,1)}, bf16[8,2,96,128]{3,2,1,0:T(8,128)(2,1)S(1)}, u32[]{:S(2)}, u32[]{:S(2)}) collective-permute-start(bf16[8,2,96,128]{3,2,1,0:T(8,128)(2,1)} %slice.14.__), channel_id=1, source_target_pairs={{0,38},{1,39},{2,36},{3,37},{4,34},{5,35},{6,32},{7,33},{8,46},{9,... | collective-permute-start | bytes 1179656 | tf_op jit(solution)/shard_map/ppermute | solution.py:495
  103.8 0.9 copy-start.9
  104.7 0.7 copy-start.12
  105.5 0.9 copy-start.6
  106.4 41.9 %all-to-all-start.1 = ((bf16[32,1,96,128]{3,2,1,0:T(8,128)(2,1)}), bf16[32,1,96,128]{3,2,1,0:T(8,128)(2,1)S(1)}, u32[]{:S(2)}, u32[]{:S(2)}) async-start(bf16[32,1,96,128]{3,2,1,0:T(8,128)(2,1)} %copy-done.9), calls=%async_computation.1 | async-start | bytes 1572864 | tf_op jit(solution)/shard_map/all_to_all | solution.py:467
  114.7 1.1 copy-start.7
  115.9 1.1 copy-start.10
  117.0 1.0 copy-start.13
  118.0 11.0 %copy-start.8 = (bf16[32,1,96,128]{3,2,1,0:T(8,128)(2,1)S(1)}, bf16[32,1,96,128]{3,2,1,0:T(8,128)(2,1)}, u32[]{:S(2)}) copy-start(bf16[32,1,96,128]{3,2,1,0:T(8,128)(2,1)} %copy-done.6) | copy-start | bytes 2359300
  118.0 11.0 %copy-start.11 = (bf16[32,1,96,128]{3,2,1,0:T(8,128)(2,1)S(1)}, bf16[32,1,96,128]{3,2,1,0:T(8,128)(2,1)}, u32[]{:S(2)}) copy-start(bf16[32,1,96,128]{3,2,1,0:T(8,128)(2,1)} %copy-done.9) | copy-start | bytes 2359300
  123.1 23.6 %collective-permute-start.1 = (bf16[8,2,96,128]{3,2,1,0:T(8,128)(2,1)S(1)}, bf16[8,2,96,128]{3,2,1,0:T(8,128)(2,1)S(1)}, u32[]{:S(2)}, u32[]{:S(2)}) collective-permute-start(bf16[8,2,96,128]{3,2,1,0:T(8,128)(2,1)S(1)} %get-tuple-element.28), channel_id=1, source_target_pairs={{38,0},{39,1},{36,2},{37,3},{34,4},{35,5},{32,6},{33,7},{46,8},{47... | collective-permute-start | bytes 1179656 | tf_op jit(solution)/shard_map/ppermute | solution.py:501
  146.9 1.4 copy-start
  148.3 62.9 %all-to-all-start.3 = ((bf16[32,3,96,128]{3,2,1,0:T(8,128)(2,1)}), bf16[32,3,96,128]{3,2,1,0:T(8,128)(2,1)S(1)}, u32[]{:S(2)}, u32[]{:S(2)}) async-start(bf16[32,3,96,128]{3,2,1,0:T(8,128)(2,1)} %copy-done), calls=%async_computation.3 | async-start | bytes 4718592 | tf_op jit(solution)/shard_map/all_to_all | solution.py:467

commit v4 on v3

v4 whole, which is shorter than its diff:
```python
import functools
import math

import jax
import jax.numpy as jnp
from jax import lax
from jax.experimental import pallas as pl
from jax.experimental.pallas import tpu as pltpu
from jax.sharding import Mesh
from jax.sharding import PartitionSpec as P

HEAD_DIM = 96
HEADS = 32
CHUNK = 128
CHUNKS = 32
HALO = 8
DOC_BITS = 6
EXTRA = 16
WIDE = HEAD_DIM + EXTRA
FAR = 2.0**20
GROUP = CHUNK * CHUNKS
AHEAD = CHUNK * HALO
WINDOW = GROUP + AHEAD
TILE = 256
TILES = GROUP // TILE
BLOCKS = CHUNKS // HALO
AHEAD_TILES = AHEAD // TILE
REACH = AHEAD_TILES + 1
NEG = -1e30
SCALE = 1.0 / math.sqrt(HEAD_DIM)
LOG2E = 1.4426950408889634
MIB = 1024 * 1024

AXES = ("x", "zh", "y", "zl", "c")
GROUP_AXES = ("y", "zl", "c")
F32 = jnp.float32
BF16 = jnp.bfloat16


def vmem():
    return pl.BlockSpec(memory_space=pltpu.VMEM)


def smem():
    return pl.BlockSpec(memory_space=pltpu.SMEM)


def hbm():
    return pl.BlockSpec(memory_space=pltpu.HBM)


def in_hbm(*arrays):
    return [pltpu.with_memory_space_constraint(array, pltpu.HBM) for array in arrays]


def pack_kernel(mirror_ref, *refs):
    count = len(refs) - 5
    sources, (out_ref, rows, blocks, arrived, sent) = refs[:count], refs[count:]
    mirrored = mirror_ref[0]

    def fetch(y, n):
        return pltpu.make_async_copy(
            sources[n].at[:, pl.ds(y * 768, 768)], rows.at[n, y], arrived.at[n, y]
        )

    def send(y):
        part = pl.ds(y * 8, 8)
        return pltpu.make_async_copy(blocks.at[part], out_ref.at[part], sent.at[y])

    for y in range(4):
        for n in range(count):
            fetch(y, n).start()
    for y in range(4):
        for n in range(count):
            fetch(y, n).wait()
            turned = rows[n, y].T
            for zl in range(4):
                slot = 8 * y + 2 * jnp.where(mirrored == 1, 3 - zl, zl)
                piece = turned[zl * 192 : (zl + 1) * 192]
                blocks[pl.ds(slot, 2), n] = piece.reshape(2, HEAD_DIM, CHUNK)
        send(y).start()
    for y in range(4):
        send(y).wait()


def pack(mirror, *arrays):
    count = len(arrays)
    shape = (HEADS, count, HEAD_DIM, CHUNK)
    return pl.pallas_call(
        pack_kernel,
        in_specs=[smem()] + [hbm()] * count,
        out_specs=hbm(),
        out_shape=pltpu.HBM(shape, BF16),
        scratch_shapes=[
            pltpu.VMEM((count, 4, CHUNK, 768), BF16),
            pltpu.VMEM(shape, BF16),
            pltpu.SemaphoreType.DMA((count, 4)),
            pltpu.SemaphoreType.DMA((4,)),
        ],
        compiler_params=pltpu.CompilerParams(vmem_limit_bytes=40 * MIB),
        name="pack",
    )(mirror, *in_hbm(*arrays))


def unpack_kernel(mirror_ref, in_ref, *out_refs):
    mirrored = mirror_ref[0]
    for n, out_ref in enumerate(out_refs):
        pieces = []
        for zl in range(4):
            slot = 2 * jnp.where(mirrored == 1, 3 - zl, zl)
            pieces.append(in_ref[pl.ds(slot, 2), n].reshape(192, CHUNK))
        out_ref[...] = jnp.concatenate(pieces, 0).T


def unpack(mirror, array):
    count = array.shape[1]
    return pl.pallas_call(
        unpack_kernel,
        grid=(4,),
        in_specs=[
            smem(),
            pl.BlockSpec((8, count, HEAD_DIM, CHUNK), lambda y: (y, 0, 0, 0)),
        ],
        out_specs=[pl.BlockSpec((CHUNK, 768), lambda y: (0, y))] * count,
        out_shape=[jax.ShapeDtypeStruct((CHUNK, HEADS * HEAD_DIM), BF16)] * count,
        compiler_params=pltpu.CompilerParams(vmem_limit_bytes=28 * MIB),
        name="unpack",
    )(mirror, array)


def tile_of(ref, n, i):
    return jnp.concatenate([ref[2 * i, n], ref[2 * i + 1, n]], 1)


def nn(a, b):
    return lax.dot_general(a, b, (((1,), (0,)), ((), ())), preferred_element_type=F32)


def nt(a, b):
    return lax.dot_general(a, b, (((1,), (1,)), ((), ())), preferred_element_type=F32)


def each_chunk(halo_ref, own_ref, n, chunks):
    for chunk in chunks:
        if isinstance(chunk, int) and chunk < HALO:
            piece = halo_ref[chunk, n]
        else:
            piece = own_ref[chunk - HALO, n]
        if isinstance(chunk, int):
            first = chunk * CHUNK
        else:
            first = pl.multiple_of(chunk * CHUNK, CHUNK)
        yield pl.ds(first, CHUNK), piece


def fill_keys(halo_ref, own_ref, code_ref, chunks, flat, turned):
    for span, piece in each_chunk(halo_ref, own_ref, 0, chunks):
        flat[span, :] = jnp.concatenate([piece, code_ref[:, span]], 0).T
        if turned is not None:
            turned[:, span] = piece


def fill_value_rows(halo_ref, own_ref, chunks, flat):
    row = lax.broadcasted_iota(jnp.int32, (EXTRA, CHUNK), 0)
    minus = jnp.where(row < 3, -1.0, 0.0).astype(BF16)
    for span, piece in each_chunk(halo_ref, own_ref, 1, chunks):
        flat[span, :] = jnp.concatenate([piece, minus], 0).T


def fill_value_columns(halo_ref, own_ref, chunks, turned):
    for span, piece in each_chunk(halo_ref, own_ref, 1, chunks):
        turned[:HEAD_DIM, span] = piece
        turned[HEAD_DIM:, span] = jnp.ones((EXTRA, CHUNK), BF16)


def with_row(extra, first, value):
    high = value.astype(BF16).astype(F32)
    middle = (value - high).astype(BF16).astype(F32)
    low = value - high - middle
    row = lax.broadcasted_iota(jnp.int32, (EXTRA, TILE), 0)
    for n, part in enumerate((high, middle, low)):
        extra = jnp.where(row == first + n, part, extra)
    return extra.astype(BF16)


def causal():
    row = lax.broadcasted_iota(jnp.int32, (TILE, TILE), 0)
    return row <= lax.broadcasted_iota(jnp.int32, (TILE, TILE), 1)


def per_tile(tile_start_ref, i, body):
    reach = jnp.clip(i + REACH - tile_start_ref[i], 1, REACH)
    for count in range(1, REACH + 1):
        pl.when(reach == count)(functools.partial(body, count))


def send_block(buffer, out_ref, sent, block):
    part = pl.ds(block * HALO, HALO)
    return pltpu.make_async_copy(buffer.at[part], out_ref.at[part], sent.at[block])


def forward_tiles(
    block, tile_start_ref, query_code_ref, kvq_ref, store, stat_ref, key_flat, value_turned
):
    def tile(step, _):
        i = block * AHEAD_TILES + step

        def body(count):
            q = jnp.concatenate([tile_of(kvq_ref, 2, i), query_code_ref[i]], 0)
            scores = []
            top = None
            for j in range(count):
                first = pl.multiple_of((i + REACH - count + j) * TILE, TILE)
                s = nn(key_flat[pl.ds(first, TILE), :], q)
                if j == count - 1:
                    s = jnp.where(causal(), s, NEG)
                scores.append(s)
                t = jnp.max(s, axis=0, keepdims=True)
                top = t if top is None else jnp.maximum(top, t)
            shift = top * (SCALE * LOG2E)
            out = None
            for j in range(count):
                first = pl.multiple_of((i + REACH - count + j) * TILE, TILE)
                e = jnp.exp2(scores[j] * (SCALE * LOG2E) - shift)
                o = nn(value_turned[:, pl.ds(first, TILE)], e.astype(BF16))
                out = o if out is None else out + o
            total = out[HEAD_DIM : HEAD_DIM + 1]
            out = (out[:HEAD_DIM] / total).astype(BF16)
            store(2 * i, out[:, :CHUNK])
            store(2 * i + 1, out[:, CHUNK:])
            stat_ref[i] = top + jnp.log(total) * (1.0 / SCALE)

        per_tile(tile_start_ref, i, body)
        return 0

    lax.fori_loop(0, AHEAD_TILES, tile, 0)


def late_forward_kernel(
    tile_start_ref, key_code_ref, query_code_ref, kvq_ref, out_ref, stat_ref,
    key_flat, value_turned, buffer, sent
):
    chunks = range(HALO, HALO + CHUNKS)
    fill_keys(None, kvq_ref, key_code_ref, chunks, key_flat, None)
    fill_value_columns(None, kvq_ref, chunks, value_turned)

    def store(chunk, value):
        buffer[chunk, 0] = value

    def block(b, _):
        forward_tiles(
            b, tile_start_ref, query_code_ref, kvq_ref, store, stat_ref, key_flat, value_turned
        )
        send_block(buffer, out_ref, sent, b).start()
        return 0

    lax.fori_loop(1, BLOCKS, block, 0)
    for b in range(1, BLOCKS):
        send_block(buffer, out_ref, sent, b).wait()


def cost(time):
    return pl.CostEstimate(flops=int(time * 1.1e9), bytes_accessed=0, transcendentals=0)


OUT_SHAPE = pltpu.HBM((CHUNKS, 1, HEAD_DIM, CHUNK), BF16)


def part(count, width):
    return pl.BlockSpec((count, width, HEAD_DIM, CHUNK), lambda b: (0, 0, 0, 0))


def forward_scratch(window, chunks):
    return [
        pltpu.VMEM((window, WIDE), BF16),
        pltpu.VMEM((WIDE, window), BF16),
        pltpu.VMEM((chunks, 1, HEAD_DIM, CHUNK), BF16),
        pltpu.SemaphoreType.DMA((BLOCKS,)),
    ]


def late_forward(tile_start, codes, kvq):
    return pl.pallas_call(
        late_forward_kernel,
        in_specs=[smem(), vmem(), vmem(), vmem()],
        out_specs=[hbm(), vmem()],
        out_shape=[OUT_SHAPE, jax.ShapeDtypeStruct((TILES, 1, TILE), F32)],
        scratch_shapes=forward_scratch(WINDOW, CHUNKS),
        compiler_params=pltpu.CompilerParams(vmem_limit_bytes=40 * MIB),
        cost_estimate=cost(30),
        name="late_forward",
    )(tile_start, *codes, kvq)


def backward_tiles(
    low, high, tile_start_ref, query_code_ref, kvq_ref, g_ref, out_ref, stat_ref, store,
    key_flat, key_turned, value_flat, key_sum, value_sum
):
    def tile(i, _):
        def body(count):
            q = tile_of(kvq_ref, 2, i)
            g = tile_of(g_ref, 0, i)
            o = tile_of(out_ref, 0, i)
            delta = jnp.sum(o.astype(F32) * g.astype(F32), axis=0, keepdims=True)
            stat = stat_ref[i]
            code = query_code_ref[i].astype(F32)
            q_wide = jnp.concatenate([q, with_row(code, 2 * DOC_BITS, stat)], 0)
            g_wide = jnp.concatenate([g, with_row(jnp.zeros_like(code), 0, delta)], 0)
            grad_q = None
            for j in range(count):
                first = pl.multiple_of((i + REACH - count + j) * TILE, TILE)
                span = pl.ds(first, TILE)
                p = jnp.exp2(nn(key_flat[span, :], q_wide) * (SCALE * LOG2E))
                if j == count - 1:
                    p = jnp.where(causal(), p, 0.0)
                d = (p * nn(value_flat[span, :], g_wide)).astype(BF16)
                t = nn(key_turned[:, span], d)
                grad_q = t if grad_q is None else grad_q + t
                key_sum[:, span] += nt(q, d)
                value_sum[:, span] += nt(g, p.astype(BF16))
            grad_q = (grad_q * SCALE).astype(BF16)
            store(2 * i, grad_q[:, :CHUNK])
            store(2 * i + 1, grad_q[:, CHUNK:])

        per_tile(tile_start_ref, i, body)
        return 0

    lax.fori_loop(low, high, tile, 0)


def early_forward_kernel(
    tile_start_ref, key_code_ref, query_code_ref, kvq_ref, halo_ref, _, out_ref, stat_ref,
    key_flat, value_turned, buffer, sent
):
    fill_keys(halo_ref, kvq_ref, key_code_ref, range(2 * HALO), key_flat, None)
    fill_value_columns(halo_ref, kvq_ref, range(2 * HALO), value_turned)

    def store(chunk, value):
        buffer[chunk, 0] = value

    forward_tiles(
        0, tile_start_ref, query_code_ref, kvq_ref, store, stat_ref, key_flat, value_turned
    )
    copy = send_block(buffer, out_ref, sent, 0)
    copy.start()
    copy.wait()


def early_backward_kernel(
    tile_start_ref, key_code_ref, query_code_ref, kvq_ref, halo_ref, g_ref, out_ref, stat_ref,
    back_ref, carry_ref, grad_q_ref,
    key_flat, key_turned, value_flat, key_sum, value_sum, g_part, out_part, back_part, grad_q_part,
    sent
):
    fetches = [
        pltpu.make_async_copy(source.at[pl.ds(0, HALO)], target, sent.at[n])
        for n, (source, target) in enumerate(((g_ref, g_part), (out_ref, out_part)))
    ]
    for copy in fetches:
        copy.start()
    fill_keys(halo_ref, kvq_ref, key_code_ref, range(2 * HALO), key_flat, key_turned)
    fill_value_rows(halo_ref, kvq_ref, range(2 * HALO), value_flat)
    key_sum[...] = jnp.zeros_like(key_sum)
    value_sum[...] = jnp.zeros_like(value_sum)
    for copy in fetches:
        copy.wait()

    def store(chunk, value):
        grad_q_part[chunk] = value

    backward_tiles(
        0, AHEAD_TILES, tile_start_ref, query_code_ref, kvq_ref, g_part, out_part, stat_ref, store,
        key_flat, key_turned, value_flat, key_sum, value_sum
    )
    copies = [pltpu.make_async_copy(grad_q_part, grad_q_ref, sent.at[2])]
    for n, sums in enumerate((key_sum, value_sum)):
        copies.append(
            pltpu.make_async_copy(
                sums.at[:, pl.ds(AHEAD, AHEAD)], carry_ref.at[n], sent.at[3 + n]
            )
        )
    for copy in copies:
        copy.start()
    for n, (sums, factor) in enumerate(((key_sum, SCALE), (value_sum, 1.0))):
        for chunk in range(HALO):
            piece = sums[:, chunk * CHUNK : (chunk + 1) * CHUNK] * factor
            back_part[chunk, n] = piece.astype(BF16)
    back_copy = pltpu.make_async_copy(back_part, back_ref, sent.at[5])
    back_copy.start()
    for copy in (*copies, back_copy):
        copy.wait()


def late_backward_kernel(
    tile_start_ref, key_code_ref, query_code_ref, kvq_ref, g_ref, out_ref, stat_ref, carry_ref,
    grad_q_ref, grads_ref, rest_ref,
    key_flat, key_turned, value_flat, key_sum, value_sum, buffer, g_all, out_all,
    sent, fetched
):
    later = pl.ds(HALO, CHUNKS - HALO)
    early = pl.ds(AHEAD, AHEAD)
    fetches = [
        pltpu.make_async_copy(source, target, fetched.at[n])
        for n, (source, target) in enumerate(
            (
                (g_ref.at[later], g_all.at[later]),
                (out_ref.at[later], out_all.at[later]),
                (carry_ref.at[0], key_sum.at[:, early]),
                (carry_ref.at[1], value_sum.at[:, early]),
                (grad_q_ref, buffer.at[pl.ds(0, HALO), 2]),
            )
        )
    ]
    for copy in fetches:
        copy.start()

    def fill(b):
        chunks = [(b + 1) * HALO + n for n in range(HALO)]
        fill_keys(None, kvq_ref, key_code_ref, chunks, key_flat, key_turned)
        fill_value_rows(None, kvq_ref, chunks, value_flat)

    fill(0)
    for sums in (key_sum, value_sum):
        sums[:, 2 * AHEAD :] = jnp.zeros((HEAD_DIM, WINDOW - 2 * AHEAD), F32)
    for copy in fetches:
        copy.wait()

    def store(chunk, value):
        buffer[chunk, 2] = value

    def block(b, _):
        fill(b)
        backward_tiles(
            b * AHEAD_TILES, (b + 1) * AHEAD_TILES,
            tile_start_ref, query_code_ref, kvq_ref, g_all, out_all, stat_ref, store,
            key_flat, key_turned, value_flat, key_sum, value_sum
        )
        for n, (sums, factor) in enumerate(((key_sum, SCALE), (value_sum, 1.0))):
            for chunk in range(HALO):
                first = pl.multiple_of(b * AHEAD + chunk * CHUNK, CHUNK)
                piece = sums[:, pl.ds(first, CHUNK)] * factor
                buffer[(b - 1) * HALO + chunk, n] = piece.astype(BF16)
        send_block(buffer, grads_ref, sent, b - 1).start()
        return 0

    lax.fori_loop(1, BLOCKS, block, 0)
    part = (pl.ds(CHUNKS - HALO, HALO), pl.ds(2, 1))
    last = pltpu.make_async_copy(buffer.at[part], grads_ref.at[part], sent.at[BLOCKS - 1])
    last.start()
    for n, sums in enumerate((key_sum, value_sum)):
        rest_ref[n] = sums[:, GROUP:]
    for b in range(BLOCKS - 1):
        send_block(buffer, grads_ref, sent, b).wait()
    last.wait()


def sums_scratch(window):
    return [
        pltpu.VMEM((window, WIDE), BF16),
        pltpu.VMEM((HEAD_DIM, window), BF16),
        pltpu.VMEM((window, WIDE), BF16),
        pltpu.VMEM((HEAD_DIM, window), F32),
        pltpu.VMEM((HEAD_DIM, window), F32),
    ]


def early_forward(tile_start, codes, kvq, halo, out):
    return pl.pallas_call(
        early_forward_kernel,
        grid=(1,),
        in_specs=[smem(), vmem(), vmem(), part(HALO, 3), vmem(), hbm()],
        out_specs=[hbm(), vmem()],
        out_shape=[OUT_SHAPE, jax.ShapeDtypeStruct((AHEAD_TILES, 1, TILE), F32)],
        input_output_aliases={5: 0},
        scratch_shapes=forward_scratch(2 * AHEAD, HALO),
        compiler_params=pltpu.CompilerParams(vmem_limit_bytes=40 * MIB),
        cost_estimate=cost(1),
        name="early_forward",
    )(tile_start, *codes, kvq, halo, *in_hbm(out))


def early_backward(tile_start, codes, kvq, halo, g, out, stat):
    return pl.pallas_call(
        early_backward_kernel,
        grid=(1,),
        in_specs=[smem(), vmem(), vmem(), part(HALO, 3), vmem(), hbm(), hbm(), vmem()],
        out_specs=[hbm()] * 3,
        out_shape=[
            pltpu.HBM((HALO, 2, HEAD_DIM, CHUNK), BF16),
            pltpu.HBM((2, HEAD_DIM, AHEAD), F32),
            pltpu.HBM((HALO, HEAD_DIM, CHUNK), BF16),
        ],
        scratch_shapes=sums_scratch(2 * AHEAD)
        + [
            pltpu.VMEM((HALO, 1, HEAD_DIM, CHUNK), BF16),
            pltpu.VMEM((HALO, 1, HEAD_DIM, CHUNK), BF16),
            pltpu.VMEM((HALO, 2, HEAD_DIM, CHUNK), BF16),
            pltpu.VMEM((HALO, HEAD_DIM, CHUNK), BF16),
            pltpu.SemaphoreType.DMA((6,)),
        ],
        compiler_params=pltpu.CompilerParams(vmem_limit_bytes=40 * MIB),
        cost_estimate=cost(1),
        name="early_backward",
    )(tile_start, *codes, kvq, halo, *in_hbm(g, out), stat)


def late_backward(tile_start, codes, kvq, g, out, stat, carry, grad_q):
    return pl.pallas_call(
        late_backward_kernel,
        in_specs=[smem(), vmem(), vmem(), vmem(), hbm(), hbm(), vmem(), hbm(), hbm()],
        out_specs=[hbm(), vmem()],
        out_shape=[
            pltpu.HBM((CHUNKS, 3, HEAD_DIM, CHUNK), BF16),
            jax.ShapeDtypeStruct((2, HEAD_DIM, AHEAD), F32),
        ],
        scratch_shapes=sums_scratch(WINDOW)
        + [
            pltpu.VMEM((CHUNKS, 3, HEAD_DIM, CHUNK), BF16),
            pltpu.VMEM((CHUNKS, 1, HEAD_DIM, CHUNK), BF16),
            pltpu.VMEM((CHUNKS, 1, HEAD_DIM, CHUNK), BF16),
            pltpu.SemaphoreType.DMA((BLOCKS,)),
            pltpu.SemaphoreType.DMA((5,)),
        ],
        compiler_params=pltpu.CompilerParams(vmem_limit_bytes=40 * MIB),
        cost_estimate=cost(10),
        name="late_backward",
    )(tile_start, *codes, kvq, *in_hbm(g, out), stat, *in_hbm(carry, grad_q))


def join_kernel(back_ref, rest_ref, _, out_ref, buffer, moved):
    sends = []
    for n, factor in enumerate((SCALE, 1.0)):
        for chunk in range(HALO):
            own = rest_ref[n, :, chunk * CHUNK : (chunk + 1) * CHUNK] * factor
            buffer[chunk, n] = (own + back_ref[chunk, n].astype(F32)).astype(BF16)
        target = out_ref.at[pl.ds(CHUNKS - HALO, HALO), n]
        sends.append(pltpu.make_async_copy(buffer.at[:, n], target, moved.at[n]))
        sends[n].start()
    for copy in sends:
        copy.wait()


def join(back, rest, grads):
    return pl.pallas_call(
        join_kernel,
        in_specs=[vmem(), vmem(), hbm()],
        out_specs=hbm(),
        out_shape=pltpu.HBM(grads.shape, BF16),
        input_output_aliases={2: 0},
        scratch_shapes=[
            pltpu.VMEM((HALO, 2, HEAD_DIM, CHUNK), BF16),
            pltpu.SemaphoreType.DMA((2,)),
        ],
        compiler_params=pltpu.CompilerParams(vmem_limit_bytes=40 * MIB),
        name="join",
    )(back, rest, *in_hbm(grads))


def gate_kernel(_, __, ___):
    pass


def after(array, other):
    return pl.pallas_call(
        gate_kernel,
        in_specs=[hbm(), pl.BlockSpec(memory_space=pl.ANY)],
        out_specs=hbm(),
        out_shape=pltpu.HBM(array.shape, array.dtype),
        input_output_aliases={0: 0},
        name="after",
    )(array, other)


def group_pairs():
    def index(x, zh, y, zl, c):
        return (((x * 2 + zh) * 4 + y) * 4 + zl) * 2 + c

    pairs = []
    for group in range(7):
        for y in range(4):
            for zl in range(4):
                for c in range(2):
                    pairs.append(
                        (
                            index(group // 2, group % 2, y, zl, c),
                            index((group + 1) // 2, (group + 1) % 2, y, 3 - zl, c),
                        )
                    )
    return pairs


def to_heads(array):
    return lax.all_to_all(array, GROUP_AXES, split_axis=0, concat_axis=0, tiled=True)


def places(doc_ids):
    group = lax.axis_index("x") * 2 + lax.axis_index("zh")
    own = lax.dynamic_slice_in_dim(doc_ids, group * GROUP, GROUP)
    ahead = lax.dynamic_slice_in_dim(doc_ids, jnp.maximum(group * GROUP - AHEAD, 0), AHEAD)
    ahead = jnp.where(group > 0, ahead, -1)
    docs = jnp.concatenate([ahead, own])
    leads = own.reshape(TILES, TILE)[:, :1]
    tile_start = jnp.sum((docs[None] < leads).astype(jnp.int32), 1) // TILE
    row = jnp.arange(EXTRA, dtype=jnp.int32)[:, None]
    bits = (docs[None] >> (row // 2)) & 1
    coded = row < 2 * DOC_BITS
    differs = (bits != row % 2) | (docs[None] < 0)
    key_code = jnp.where(coded, jnp.where(differs, -FAR, 0.0), jnp.where(row < 15, -1.0, 0.0))
    query_code = jnp.where(coded & (bits[:, AHEAD:] == row % 2), 1.0, 0.0)
    query_code = query_code.reshape(EXTRA, TILES, TILE).transpose(1, 0, 2)
    return tile_start, (key_code.astype(BF16), query_code.astype(BF16))


def shards(queries, keys, values, cotangent, doc_ids):
    mirror = lax.axis_index("zh").astype(jnp.int32).reshape(1)
    kvq = to_heads(pack(mirror, keys, values, queries))
    tile_start, codes = places(doc_ids)
    cotangent, tile_start, codes = lax.optimization_barrier((cotangent, tile_start, codes))
    pairs = group_pairs()
    last = kvq[CHUNKS - HALO :, :2]
    halo = lax.ppermute(last, AXES, pairs)
    g = to_heads(after(pack(mirror, cotangent), last))
    out, stat = late_forward(tile_start, codes, kvq)
    out, early_stat = early_forward(tile_start, codes, kvq, halo, out)
    back, carry, early_q = early_backward(tile_start, codes, kvq, halo, g, out, early_stat)
    grads, rest = late_backward(tile_start, codes, kvq, g, out, stat, carry, early_q)
    back = lax.ppermute(back, AXES, [(b, a) for a, b in pairs])
    grads = join(back, rest, grads)
    (attended,) = unpack(mirror, to_heads(out))
    grad_k, grad_v, grad_q = unpack(mirror, to_heads(grads))
    return attended, grad_q, grad_k, grad_v


def solution(mesh):
    wide = Mesh(mesh.devices.reshape(4, 2, 4, 4, 2), AXES)
    rows = P(AXES, None)
    return jax.shard_map(
        shards,
        mesh=wide,
        in_specs=(rows, rows, rows, rows, P()),
        out_specs=(rows, rows, rows, rows),
        check_vma=False,
    )
```

time: 215 us -> 203 us (0.944)
  local copies, waits for them, and re-layouts: 13.1 us -> 1.88 us
  Pallas kernels: 38 us -> 46.7 us
  starting transfers between devices: 40.7 us -> 33.3 us
    unnamed x28 -> x6, local copies, waits for them, and re-layouts: 11.5 us -> 1 us
    ppermute x1, waiting for transfers between devices: 8.54 us -> 1.95 us  [shards(): halo = lax.ppermute(last, AXES, pairs)]
    all_to_all x4, waiting for transfers between devices: 107 us -> 113 us  [to_heads(): lax.all_to_all(array, GROUP_AXES, split_axis=0, concat_axis=0, tiled=True)]
    pallas_call x6, Pallas kernels: 25.7 us -> 31.2 us  [the longest x1 15.7 us: late_backward(): pl.pallas_call(late_backward_kernel, in_specs=[smem(), vmem(), vmem(), vm...]
    ppermute x1, starting transfers between devices: 6.65 us -> 2.65 us  [shards(): halo = lax.ppermute(last, AXES, pairs)]
    ppermute x1, starting transfers between devices: 5.86 us -> 3.49 us  [shards(): back = lax.ppermute(back, AXES, [(b, a) for a, b in pairs])]
    pallas_call x1, Pallas kernels: 5.13 us -> 7.33 us  [early_backward(): pl.pallas_call(early_backward_kernel, grid=(1,), in_specs=[smem(), vmem()...]
  transfers between devices with their start and end apart: 6 -> 6, of which waited for: 4 -> 5; matrix products, arithmetic and copies ran while one was open for 1% -> 1% of each run, Pallas kernels for 16% -> 21%
where the time goes in v4:
time: 203 us; the launch traced here: 202 us
  waiting for transfers between devices  118 us (58%)
  Pallas kernels  46.7 us (23%)
  starting transfers between devices  33.3 us (16%)
    all_to_all x4, waiting for transfers between devices, to_heads(): lax.all_to_all(array, GROUP_AXES, split_axis=0, concat_axis=0, tiled=True)  113 us
    all_to_all x4, starting transfers between devices, to_heads(): lax.all_to_all(array, GROUP_AXES, split_axis=0, concat_axis=0, tiled=True)  27.2 us
    pallas_call x1, Pallas kernels, late_backward(): pl.pallas_call(late_backward_kernel, in_specs=[smem(), vmem(), vmem(), vm...  15.7 us
    pallas_call x1, Pallas kernels, late_forward(): pl.pallas_call(late_forward_kernel, in_specs=[smem(), vmem(), vmem(), vme...  9.43 us
    pallas_call x1, Pallas kernels, early_backward(): pl.pallas_call(early_backward_kernel, grid=(1,), in_specs=[smem(), vmem()...  7.33 us
    pallas_call x2, Pallas kernels, pack(): pl.pallas_call(pack_kernel, in_specs=[smem()] + [hbm()] * count, out_spec...  5.25 us
    pallas_call x1, Pallas kernels, early_forward(): pl.pallas_call(early_forward_kernel, grid=(1,), in_specs=[smem(), vmem(),...  4.39 us
  transfers between devices with their start and end apart: 6, of which 5 were waited for; matrix products, arithmetic and copies ran while one was open for 1% of the time, Pallas kernels for 21%

profile of v4, /device:TPU:4, one launch (start us, length us, event | category | flops | bytes accessed | tf_op | source)
XLA Modules:
  0.0 202.4 jit_solution(12819950421786361113)
XLA Ops:
  0.6 3.2 %pack.2 = bf16[32,3,96,128]{3,2,1,0:T(8,128)(2,1)} custom-call(s32[1]{0:T(128)} %bitcast.mirror_ref, bf16[128,3072]{1,0:T(8,128)(2,1)} %refs_0_.1, bf16[128,3072]{1,0:T(8,128)(2,1)} %refs_1_.1, bf16[128,3072]{1,0:T(8,128)(2,1)} %refs_2_.1), custom_call_target="tpu_custom_call" | custom-call | tf_op jit(solution)/shard_map/pack/pallas_call | solution.py:89
  3.8 8.9 %all-to-all-start = ((bf16[32,3,96,128]{3,2,1,0:T(8,128)(2,1)}), bf16[32,3,96,128]{3,2,1,0:T(8,128)(2,1)S(1)}, u32[]{:S(2)}, u32[]{:S(2)}) async-start(bf16[32,3,96,128]{3,2,1,0:T(8,128)(2,1)} %pack.2), calls=%async_computation | async-start | bytes 4718592 | tf_op jit(solution)/shard_map/all_to_all | solution.py:593
  12.8 0.7 dynamic_slice.7
  13.5 0.8 dynamic-slice_select_fusion
  14.3 0.1 slice_reduce_fusion
  14.4 0.2 shift-right-arithmetic_and_fusion
  14.7 0.1 select_convert_fusion.1
  14.8 0.2 select_convert_fusion.key_code_ref
  15.0 2.1 %pack.3._ = bf16[32,1,96,128]{3,2,1,0:T(8,128)(2,1)} custom-call(s32[1]{0:T(128)} %bitcast.mirror_ref, bf16[128,3072]{1,0:T(8,128)(2,1)} %refs_0_.2), custom_call_target="tpu_custom_call" | custom-call | tf_op jit(solution)/shard_map/pack/pallas_call | solution.py:89
  17.1 51.7 %all-to-all-done.kvq_ref = bf16[32,3,96,128]{3,2,1,0:T(8,128)(2,1)S(1)} async-done(((bf16[32,3,96,128]{3,2,1,0:T(8,128)(2,1)}), bf16[32,3,96,128]{3,2,1,0:T(8,128)(2,1)S(1)}, u32[]{:S(2)}, u32[]{:S(2)}) %all-to-all-start) | async-done | bytes 2359328 | tf_op jit(solution)/shard_map/all_to_all | solution.py:593
  68.8 0.0 copy-start.2
  68.9 2.7 %collective-permute-start = (bf16[8,2,96,128]{3,2,1,0:T(8,128)(2,1)S(1)}, bf16[8,2,96,128]{3,2,1,0:T(8,128)(2,1)S(1)}, u32[]{:S(2)}, u32[]{:S(2)}) collective-permute-start(bf16[8,2,96,128]{3,2,1,0:T(8,128)(2,1)S(1)} %slice.14.__), channel_id=1, source_target_pairs={{0,38},{1,39},{2,36},{3,37},{4,34},{5,35},{6,32},{7,33},{8,46},{9,... | collective-permute-start | bytes 1179656 | tf_op jit(solution)/shard_map/ppermute | solution.py:621
  71.5 0.0 copy-done.2
  71.5 6.6 %all-to-all-start.2 = ((bf16[32,1,96,128]{3,2,1,0:T(8,128)(2,1)}), bf16[32,1,96,128]{3,2,1,0:T(8,128)(2,1)}, u32[]{:S(2)}, u32[]{:S(2)}) async-start(bf16[32,1,96,128]{3,2,1,0:T(8,128)(2,1)} %after.1), calls=%async_computation.2 | async-start | bytes 1572864 | tf_op jit(solution)/shard_map/all_to_all | solution.py:593
  78.2 9.4 %late_forward.1 = (bf16[32,1,96,128]{3,2,1,0:T(8,128)(2,1)}, f32[16,1,256]{2,1,0:T(1,128)S(1)}) custom-call(s32[16]{0:T(128)S(1)} %and_select_fusion.2.tile_start_ref, bf16[16,5120]{1,0:T(8,128)(2,1)S(1)} %select_convert_fusion.key_code_ref, bf16[16,16,256]{2,1,0:T(8,128)(2,1)S(1)} %bitcast.8, bf16[32,3,96,128]{3,2,1,0:T(8,128)(2,1)S(1)} %all-to-all-done.kvq_ref), custom_call_target="tpu_custom_call" | custom-call | flops 32999999488 | tf_op jit(solution)/shard_map/late_forward/pallas_call | solution.py:283
  87.6 2.0 collective-permute-done.halo_ref
  89.6 0.0 copy-start
  89.6 4.4 %early_forward.1 = (bf16[32,1,96,128]{3,2,1,0:T(8,128)(2,1)}, f32[4,1,256]{2,1,0:T(1,128)S(1)}) custom-call(s32[16]{0:T(128)S(1)} %and_select_fusion.2.tile_start_ref, bf16[16,5120]{1,0:T(8,128)(2,1)S(1)} %select_convert_fusion.key_code_ref, bf16[16,16,256]{2,1,0:T(8,128)(2,1)S(1)} %bitcast.9, ...), custom_call_target="tpu_custom_call", output_to_operand_aliasing={{0}: (5, {})} | custom-call | flops 1100000000 | tf_op jit(solution)/shard_map/early_forward/pallas_call | solution.py:468
  94.0 6.5 %all-to-all-done.2.g_ref = bf16[32,1,96,128]{3,2,1,0:T(8,128)(2,1)} async-done(((bf16[32,1,96,128]{3,2,1,0:T(8,128)(2,1)}), bf16[32,1,96,128]{3,2,1,0:T(8,128)(2,1)}, u32[]{:S(2)}, u32[]{:S(2)}) %all-to-all-start.2) | async-done | bytes 786464 | tf_op jit(solution)/shard_map/all_to_all | solution.py:593
  100.5 0.0 copy-done
  100.5 3.9 %all-to-all-start.1 = ((bf16[32,1,96,128]{3,2,1,0:T(8,128)(2,1)}), bf16[32,1,96,128]{3,2,1,0:T(8,128)(2,1)S(1)}, u32[]{:S(2)}, u32[]{:S(2)}) async-start(bf16[32,1,96,128]{3,2,1,0:T(8,128)(2,1)} %get-tuple-element.24.out_ref), calls=%async_computation.1 | async-start | bytes 1572864 | tf_op jit(solution)/shard_map/all_to_all | solution.py:593
  104.4 0.0 copy-start.1
  104.4 1.0 copy-done.1
  105.4 7.3 %early_backward.1 = (bf16[8,2,96,128]{3,2,1,0:T(8,128)(2,1)}, f32[2,96,1024]{2,1,0:T(8,128)}, bf16[8,96,128]{2,1,0:T(8,128)(2,1)}) custom-call(s32[16]{0:T(128)S(1)} %and_select_fusion.2.tile_start_ref, bf16[16,5120]{1,0:T(8,128)(2,1)S(1)} %select_convert_fusion.key_code_ref, bf16[16,16,256]{2,1,0:T(8,128)(2,1)S(1)} %bitcast.10, ...), custom_call_target="tpu_custom_call" | custom-call | flops 1100000000 | tf_op jit(solution)/shard_map/early_backward/pallas_call | solution.py:483
  112.8 3.5 %collective-permute-start.1 = (bf16[8,2,96,128]{3,2,1,0:T(8,128)(2,1)}, bf16[8,2,96,128]{3,2,1,0:T(8,128)(2,1)S(1)}, u32[]{:S(2)}, u32[]{:S(2)}) collective-permute-start(bf16[8,2,96,128]{3,2,1,0:T(8,128)(2,1)} %get-tuple-element.27), channel_id=1, source_target_pairs={{38,0},{39,1},{36,2},{37,3},{34,4},{35,5},{32,6},{33,7},{46,8},{47... | collective-permute-start | bytes 1179656 | tf_op jit(solution)/shard_map/ppermute | solution.py:627
  116.3 15.7 %late_backward.1 = (bf16[32,3,96,128]{3,2,1,0:T(8,128)(2,1)}, f32[2,96,1024]{2,1,0:T(8,128)S(1)}) custom-call(s32[16]{0:T(128)S(1)} %and_select_fusion.2.tile_start_ref, bf16[16,5120]{1,0:T(8,128)(2,1)S(1)} %select_convert_fusion.key_code_ref, bf16[16,16,256]{2,1,0:T(8,128)(2,1)S(1)} %bitcast.11, bf16[32,3,96,128]{3,2,1,0:T(8,128)(2,1)S(1)} %all-to-all-done.kvq_ref, ...), custom_call_target="tpu_custom_call" | custom-call | flops 11000000512 | tf_op jit(solution)/shard_map/late_backward/pallas_call | solution.py:508
  132.0 3.7 %collective-permute-done.1.back_ref = bf16[8,2,96,128]{3,2,1,0:T(8,128)(2,1)S(1)} collective-permute-done((bf16[8,2,96,128]{3,2,1,0:T(8,128)(2,1)}, bf16[8,2,96,128]{3,2,1,0:T(8,128)(2,1)S(1)}, u32[]{:S(2)}, u32[]{:S(2)}) %collective-permute-start.1) | collective-permute-done | bytes 393248 | tf_op jit(solution)/shard_map/ppermute | solution.py:627
  135.7 0.8 join.1
  136.5 0.0 all-to-all-done.1.in_ref
  136.5 7.7 %all-to-all-start.3 = ((bf16[32,3,96,128]{3,2,1,0:T(8,128)(2,1)}), bf16[32,3,96,128]{3,2,1,0:T(8,128)(2,1)S(1)}, u32[]{:S(2)}, u32[]{:S(2)}) async-start(bf16[32,3,96,128]{3,2,1,0:T(8,128)(2,1)} %join.1), calls=%async_computation.3 | async-start | bytes 4718592 | tf_op jit(solution)/shard_map/all_to_all | solution.py:593
  144.2 1.7 unpack.2
  146.0 54.4 %all-to-all-done.3.in_ref = bf16[32,3,96,128]{3,2,1,0:T(8,128)(2,1)S(1)} async-done(((bf16[32,3,96,128]{3,2,1,0:T(8,128)(2,1)}), bf16[32,3,96,128]{3,2,1,0:T(8,128)(2,1)S(1)}, u32[]{:S(2)}, u32[]{:S(2)}) %all-to-all-start.3) | async-done | bytes 2359328 | tf_op jit(solution)/shard_map/all_to_all | solution.py:593
  200.3 2.1 %unpack.3 = (bf16[128,3072]{1,0:T(8,128)(2,1)}, bf16[128,3072]{1,0:T(8,128)(2,1)}, bf16[128,3072]{1,0:T(8,128)(2,1)}) custom-call(s32[1]{0:T(128)} %bitcast.mirror_ref, bf16[32,3,96,128]{3,2,1,0:T(8,128)(2,1)S(1)} %all-to-all-done.3.in_ref), custom_call_target="tpu_custom_call" | custom-call | tf_op jit(solution)/shard_map/unpack/pallas_call | solution.py:117
  (10 shorter events, 0.1 us)
Async XLA Ops:
  3.8 65.0 %all-to-all-start = ((bf16[32,3,96,128]{3,2,1,0:T(8,128)(2,1)}), bf16[32,3,96,128]{3,2,1,0:T(8,128)(2,1)S(1)}, u32[]{:S(2)}, u32[]{:S(2)}) async-start(bf16[32,3,96,128]{3,2,1,0:T(8,128)(2,1)} %pack.2), calls=%async_computation | async-start | bytes 4718592 | tf_op jit(solution)/shard_map/all_to_all | solution.py:593
  68.8 2.7 %copy-start.2 = (bf16[8,2,96,128]{3,2,1,0:T(8,128)(2,1)}, bf16[8,2,96,128]{3,2,1,0:T(8,128)(2,1)S(1)}, u32[]{:S(2)}) copy-start(bf16[8,2,96,128]{3,2,1,0:T(8,128)(2,1)S(1)} %slice.14.__) | copy-start | bytes 1179652
  68.9 20.7 %collective-permute-start = (bf16[8,2,96,128]{3,2,1,0:T(8,128)(2,1)S(1)}, bf16[8,2,96,128]{3,2,1,0:T(8,128)(2,1)S(1)}, u32[]{:S(2)}, u32[]{:S(2)}) collective-permute-start(bf16[8,2,96,128]{3,2,1,0:T(8,128)(2,1)S(1)} %slice.14.__), channel_id=1, source_target_pairs={{0,38},{1,39},{2,36},{3,37},{4,34},{5,35},{6,32},{7,33},{8,46},{9,... | collective-permute-start | bytes 1179656 | tf_op jit(solution)/shard_map/ppermute | solution.py:621
  71.5 29.0 %all-to-all-start.2 = ((bf16[32,1,96,128]{3,2,1,0:T(8,128)(2,1)}), bf16[32,1,96,128]{3,2,1,0:T(8,128)(2,1)}, u32[]{:S(2)}, u32[]{:S(2)}) async-start(bf16[32,1,96,128]{3,2,1,0:T(8,128)(2,1)} %after.1), calls=%async_computation.2 | async-start | bytes 1572864 | tf_op jit(solution)/shard_map/all_to_all | solution.py:593
  89.6 10.9 %copy-start = (bf16[8,2,96,128]{3,2,1,0:T(8,128)(2,1)}, bf16[8,2,96,128]{3,2,1,0:T(8,128)(2,1)S(1)}, u32[]{:S(2)}) copy-start(bf16[8,2,96,128]{3,2,1,0:T(8,128)(2,1)S(1)} %collective-permute-done.halo_ref) | copy-start | bytes 1179652
  100.5 36.0 %all-to-all-start.1 = ((bf16[32,1,96,128]{3,2,1,0:T(8,128)(2,1)}), bf16[32,1,96,128]{3,2,1,0:T(8,128)(2,1)S(1)}, u32[]{:S(2)}, u32[]{:S(2)}) async-start(bf16[32,1,96,128]{3,2,1,0:T(8,128)(2,1)} %get-tuple-element.24.out_ref), calls=%async_computation.1 | async-start | bytes 1572864 | tf_op jit(solution)/shard_map/all_to_all | solution.py:593
  104.4 1.0 copy-start.1
  112.8 22.9 %collective-permute-start.1 = (bf16[8,2,96,128]{3,2,1,0:T(8,128)(2,1)}, bf16[8,2,96,128]{3,2,1,0:T(8,128)(2,1)S(1)}, u32[]{:S(2)}, u32[]{:S(2)}) collective-permute-start(bf16[8,2,96,128]{3,2,1,0:T(8,128)(2,1)} %get-tuple-element.27), channel_id=1, source_target_pairs={{38,0},{39,1},{36,2},{37,3},{34,4},{35,5},{32,6},{33,7},{46,8},{47... | collective-permute-start | bytes 1179656 | tf_op jit(solution)/shard_map/ppermute | solution.py:627
  136.5 63.8 %all-to-all-start.3 = ((bf16[32,3,96,128]{3,2,1,0:T(8,128)(2,1)}), bf16[32,3,96,128]{3,2,1,0:T(8,128)(2,1)S(1)}, u32[]{:S(2)}, u32[]{:S(2)}) async-start(bf16[32,3,96,128]{3,2,1,0:T(8,128)(2,1)} %join.1), calls=%async_computation.3 | async-start | bytes 4718592 | tf_op jit(solution)/shard_map/all_to_all | solution.py:593

commit v5 on v4

--- a/solution.py
+++ b/solution.py
@@ -142,15 +142,8 @@
 
 def each_chunk(halo_ref, own_ref, n, chunks):
     for chunk in chunks:
-        if isinstance(chunk, int) and chunk < HALO:
-            piece = halo_ref[chunk, n]
-        else:
-            piece = own_ref[chunk - HALO, n]
-        if isinstance(chunk, int):
-            first = chunk * CHUNK
-        else:
-            first = pl.multiple_of(chunk * CHUNK, CHUNK)
-        yield pl.ds(first, CHUNK), piece
+        piece = halo_ref[chunk, n] if chunk < HALO else own_ref[chunk - HALO, n]
+        yield slice(chunk * CHUNK, (chunk + 1) * CHUNK), piece
 
 
 def fill_keys(halo_ref, own_ref, code_ref, chunks, flat, turned):
@@ -306,18 +299,16 @@
             code = query_code_ref[i].astype(F32)
             q_wide = jnp.concatenate([q, with_row(code, 2 * DOC_BITS, stat)], 0)
             g_wide = jnp.concatenate([g, with_row(jnp.zeros_like(code), 0, delta)], 0)
-            grad_q = None
-            for j in range(count):
-                first = pl.multiple_of((i + REACH - count + j) * TILE, TILE)
-                span = pl.ds(first, TILE)
-                p = jnp.exp2(nn(key_flat[span, :], q_wide) * (SCALE * LOG2E))
-                if j == count - 1:
-                    p = jnp.where(causal(), p, 0.0)
-                d = (p * nn(value_flat[span, :], g_wide)).astype(BF16)
-                t = nn(key_turned[:, span], d)
-                grad_q = t if grad_q is None else grad_q + t
-                key_sum[:, span] += nt(q, d)
-                value_sum[:, span] += nt(g, p.astype(BF16))
+            first = pl.multiple_of((i + REACH - count) * TILE, TILE)
+            span = pl.ds(first, count * TILE)
+            p = jnp.exp2(nn(key_flat[span, :], q_wide) * (SCALE * LOG2E))
+            last = (count - 1) * TILE
+            tail = jnp.where(causal(), p[last:], 0.0)
+            p = jnp.concatenate([p[:last], tail], 0) if last else tail
+            d = (p * nn(value_flat[span, :], g_wide)).astype(BF16)
+            grad_q = nn(key_turned[:, span], d)
+            key_sum[:, span] += nt(q, d)
+            value_sum[:, span] += nt(g, p.astype(BF16))
             grad_q = (grad_q * SCALE).astype(BF16)
             store(2 * i, grad_q[:, :CHUNK])
             store(2 * i + 1, grad_q[:, CHUNK:])
@@ -392,66 +383,78 @@
 
 
 def late_backward_kernel(
-    tile_start_ref, key_code_ref, query_code_ref, kvq_ref, g_ref, out_ref, stat_ref, carry_ref,
-    grad_q_ref, grads_ref, rest_ref,
-    key_flat, key_turned, value_flat, key_sum, value_sum, buffer, g_all, out_all,
-    sent, fetched
+    place_ref, tile_start_ref, key_code_ref, query_code_ref, kvq_ref, g_ref, out_ref, stat_ref,
+    carry_ref, grad_q_ref, grads_ref, rest_ref, part_0, part_1, part_2, part_3,
+    key_flat, key_turned, value_flat, key_sum, value_sum, buffer, queries, g_all,
+    out_all, carry, sent, fetched, parted
 ):
-    later = pl.ds(HALO, CHUNKS - HALO)
-    early = pl.ds(AHEAD, AHEAD)
-    fetches = [
-        pltpu.make_async_copy(source, target, fetched.at[n])
-        for n, (source, target) in enumerate(
-            (
-                (g_ref.at[later], g_all.at[later]),
-                (out_ref.at[later], out_all.at[later]),
-                (carry_ref.at[0], key_sum.at[:, early]),
-                (carry_ref.at[1], value_sum.at[:, early]),
-                (grad_q_ref, buffer.at[pl.ds(0, HALO), 2]),
+    def fetch(b):
+        part = pl.ds(b * HALO, HALO)
+        return (
+            pltpu.make_async_copy(g_ref.at[part], g_all.at[part], fetched.at[0, b]),
+            pltpu.make_async_copy(out_ref.at[part], out_all.at[part], fetched.at[1, b]),
+        )
+
+    first = (
+        pltpu.make_async_copy(carry_ref, carry, fetched.at[0, 0]),
+        pltpu.make_async_copy(grad_q_ref, queries.at[pl.ds(0, HALO)], fetched.at[1, 0]),
+    )
+    for copy in (*fetch(1), *first, *fetch(2), *fetch(3)):
+        copy.start()
+    chunks = range(HALO, HALO + CHUNKS)
+    fill_keys(None, kvq_ref, key_code_ref, chunks, key_flat, key_turned)
+    fill_value_rows(None, kvq_ref, chunks, value_flat)
+    for sums in (key_sum, value_sum):
+        sums[:, AHEAD:] = jnp.zeros((HEAD_DIM, GROUP), F32)
+
+    def store(chunk, value):
+        queries[chunk] = value
+
+    def send_queries(b):
+        copies = []
+        for d, ref in enumerate((part_0, part_1, part_2, part_3)):
+            chunk = b * HALO + 2 * (place_ref[2] ^ d)
+            copies.append(
+                pltpu.make_async_copy(queries.at[pl.ds(chunk, 2)], ref.at[b], parted.at[b, d])
             )
-        )
-    ]
-    for copy in fetches:
-        copy.start()
-
-    def fill(b):
-        chunks = [(b + 1) * HALO + n for n in range(HALO)]
-        fill_keys(None, kvq_ref, key_code_ref, chunks, key_flat, key_turned)
-        fill_value_rows(None, kvq_ref, chunks, value_flat)
-
-    fill(0)
-    for sums in (key_sum, value_sum):
-        sums[:, 2 * AHEAD :] = jnp.zeros((HEAD_DIM, WINDOW - 2 * AHEAD), F32)
-    for copy in fetches:
-        copy.wait()
-
-    def store(chunk, value):
-        buffer[chunk, 2] = value
+        return copies
 
     def block(b, _):
-        fill(b)
+        for copy in fetch(b):
+            copy.wait()
         backward_tiles(
             b * AHEAD_TILES, (b + 1) * AHEAD_TILES,
             tile_start_ref, query_code_ref, kvq_ref, g_all, out_all, stat_ref, store,
             key_flat, key_turned, value_flat, key_sum, value_sum
         )
+
+        @pl.when(b == 1)
+        def _():
+            for copy in first:
+                copy.wait()
+            for copy in send_queries(0):
+                copy.start()
+            key_sum[:, AHEAD : 2 * AHEAD] += carry[0]
+            value_sum[:, AHEAD : 2 * AHEAD] += carry[1]
+
         for n, (sums, factor) in enumerate(((key_sum, SCALE), (value_sum, 1.0))):
             for chunk in range(HALO):
-                first = pl.multiple_of(b * AHEAD + chunk * CHUNK, CHUNK)
-                piece = sums[:, pl.ds(first, CHUNK)] * factor
+                place = pl.multiple_of(b * AHEAD + chunk * CHUNK, CHUNK)
+                piece = sums[:, pl.ds(place, CHUNK)] * factor
                 buffer[(b - 1) * HALO + chunk, n] = piece.astype(BF16)
         send_block(buffer, grads_ref, sent, b - 1).start()
+        for copy in send_queries(b):
+            copy.start()
         return 0
 
     lax.fori_loop(1, BLOCKS, block, 0)
-    part = (pl.ds(CHUNKS - HALO, HALO), pl.ds(2, 1))
-    last = pltpu.make_async_copy(buffer.at[part], grads_ref.at[part], sent.at[BLOCKS - 1])
-    last.start()
     for n, sums in enumerate((key_sum, value_sum)):
         rest_ref[n] = sums[:, GROUP:]
     for b in range(BLOCKS - 1):
         send_block(buffer, grads_ref, sent, b).wait()
-    last.wait()
+    for b in range(BLOCKS):
+        for copy in send_queries(b):
+            copy.wait()
 
 
 def sums_scratch(window):
@@ -504,27 +507,31 @@
     )(tile_start, *codes, kvq, halo, *in_hbm(g, out), stat)
 
 
-def late_backward(tile_start, codes, kvq, g, out, stat, carry, grad_q):
+def late_backward(place, tile_start, codes, kvq, g, out, stat, carry, grad_q):
     return pl.pallas_call(
         late_backward_kernel,
-        in_specs=[smem(), vmem(), vmem(), vmem(), hbm(), hbm(), vmem(), hbm(), hbm()],
-        out_specs=[hbm(), vmem()],
+        in_specs=[smem(), smem(), vmem(), vmem(), vmem(), hbm(), hbm(), vmem(), hbm(), hbm()],
+        out_specs=[hbm(), vmem()] + [hbm()] * 4,
         out_shape=[
-            pltpu.HBM((CHUNKS, 3, HEAD_DIM, CHUNK), BF16),
+            pltpu.HBM((CHUNKS, 2, HEAD_DIM, CHUNK), BF16),
             jax.ShapeDtypeStruct((2, HEAD_DIM, AHEAD), F32),
-        ],
+        ]
+        + [pltpu.HBM((4, 2, HEAD_DIM, CHUNK), BF16)] * 4,
         scratch_shapes=sums_scratch(WINDOW)
         + [
-            pltpu.VMEM((CHUNKS, 3, HEAD_DIM, CHUNK), BF16),
+            pltpu.VMEM((CHUNKS, 2, HEAD_DIM, CHUNK), BF16),
+            pltpu.VMEM((CHUNKS, HEAD_DIM, CHUNK), BF16),
             pltpu.VMEM((CHUNKS, 1, HEAD_DIM, CHUNK), BF16),
             pltpu.VMEM((CHUNKS, 1, HEAD_DIM, CHUNK), BF16),
+            pltpu.VMEM((2, HEAD_DIM, AHEAD), F32),
             pltpu.SemaphoreType.DMA((BLOCKS,)),
-            pltpu.SemaphoreType.DMA((5,)),
+            pltpu.SemaphoreType.DMA((2, BLOCKS)),
+            pltpu.SemaphoreType.DMA((BLOCKS, 4)),
         ],
         compiler_params=pltpu.CompilerParams(vmem_limit_bytes=40 * MIB),
         cost_estimate=cost(10),
         name="late_backward",
-    )(tile_start, *codes, kvq, *in_hbm(g, out), stat, *in_hbm(carry, grad_q))
+    )(place, tile_start, *codes, kvq, *in_hbm(g, out), stat, *in_hbm(carry, grad_q))
 
 
 def join_kernel(back_ref, rest_ref, _, out_ref, buffer, moved):
@@ -556,19 +563,120 @@
     )(back, rest, *in_hbm(grads))
 
 
-def gate_kernel(_, __, ___):
+def turn_kernel(axis, place_ref, *refs):
+    sources, targets, sent = refs[:4], refs[4:8], refs[8]
+    here = place_ref[axis]
+    copies = []
+    for d in range(4):
+        for e in range(4):
+            copies.append(
+                pltpu.make_async_copy(sources[d].at[here ^ e], targets[e].at[d], sent.at[d, e])
+            )
+    for copy in copies:
+        copy.start()
+    for copy in copies:
+        copy.wait()
+
+
+def turn(place, axis, parts):
+    return pl.pallas_call(
+        functools.partial(turn_kernel, axis),
+        in_specs=[smem()] + [pl.BlockSpec(memory_space=pl.ANY)] * 4,
+        out_specs=[hbm()] * 4,
+        out_shape=[pltpu.HBM((4, 2, HEAD_DIM, CHUNK), BF16)] * 4,
+        scratch_shapes=[pltpu.SemaphoreType.DMA((4, 4))],
+        compiler_params=pltpu.CompilerParams(vmem_limit_bytes=40 * MIB),
+        cost_estimate=cost(1),
+        name="turn",
+    )(place, *parts)
+
+
+def other_core_kernel(place_ref, *refs):
+    sources, target, sent = refs[:4], refs[4], refs[5]
+    copies = [
+        pltpu.make_async_copy(sources[e].at[:, 1 - place_ref[3]], target.at[e], sent.at[e])
+        for e in range(4)
+    ]
+    for copy in copies:
+        copy.start()
+    for copy in copies:
+        copy.wait()
+
+
+def other_core(place, parts):
+    return pl.pallas_call(
+        other_core_kernel,
+        in_specs=[smem()] + [pl.BlockSpec(memory_space=pl.ANY)] * 4,
+        out_specs=hbm(),
+        out_shape=pltpu.HBM((4, 4, HEAD_DIM, CHUNK), BF16),
+        scratch_shapes=[pltpu.SemaphoreType.DMA((4,))],
+        compiler_params=pltpu.CompilerParams(vmem_limit_bytes=40 * MIB),
+        cost_estimate=cost(1),
+        name="other_core",
+    )(place, *parts)
+
+
+def by_distance(parts, axis):
+    return [parts[0]] + [
+        lax.ppermute(parts[d], axis, [(i, i ^ d) for i in range(4)]) for d in range(1, 4)
+    ]
+
+
+def rows_kernel(place_ref, part_0, part_1, part_2, part_3, other_ref, out_ref, rows, sent):
+    mirrored, y, zl, core = place_ref[0], place_ref[1], place_ref[2], place_ref[3]
+    copies = []
+    for e, ref in enumerate((part_0, part_1, part_2, part_3)):
+        pieces = []
+        for head_zl in range(4):
+            d = zl ^ jnp.where(mirrored == 1, 3 - head_zl, head_zl)
+            own, other = ref[d, core], other_ref[e, d]
+            pieces.append(jnp.where(core == 0, own, other))
+            pieces.append(jnp.where(core == 0, other, own))
+        rows[e] = jnp.concatenate(pieces, 0).T
+        first = pl.multiple_of((y ^ e) * 768, 768)
+        copies.append(
+            pltpu.make_async_copy(rows.at[e], out_ref.at[:, pl.ds(first, 768)], sent.at[e])
+        )
+        copies[e].start()
+    for copy in copies:
+        copy.wait()
+
+
+def rows_of(place, parts, other):
+    return pl.pallas_call(
+        rows_kernel,
+        in_specs=[smem()] + [vmem()] * 5,
+        out_specs=hbm(),
+        out_shape=pltpu.HBM((CHUNK, HEADS * HEAD_DIM), BF16),
+        scratch_shapes=[
+            pltpu.VMEM((4, CHUNK, 768), BF16),
+            pltpu.SemaphoreType.DMA((4,)),
+        ],
+        compiler_params=pltpu.CompilerParams(vmem_limit_bytes=28 * MIB),
+        cost_estimate=cost(1),
+        name="rows_of",
+    )(place, *parts, other)
+
+
+def to_rows(place, parts):
+    parts = by_distance(turn(place, 1, parts), "y")
+    other = lax.ppermute(other_core(place, parts), "c", [(0, 1), (1, 0)])
+    return rows_of(place, parts, other)
+
+
+def gate_kernel(*_):
     pass
 
 
-def after(array, other):
+def after(array, *others):
     return pl.pallas_call(
         gate_kernel,
-        in_specs=[hbm(), pl.BlockSpec(memory_space=pl.ANY)],
+        in_specs=[hbm()] + [pl.BlockSpec(memory_space=pl.ANY)] * len(others),
         out_specs=hbm(),
         out_shape=pltpu.HBM(array.shape, array.dtype),
         input_output_aliases={0: 0},
         name="after",
-    )(array, other)
+    )(array, *others)
 
 
 def group_pairs():
@@ -612,7 +720,8 @@
 
 
 def shards(queries, keys, values, cotangent, doc_ids):
-    mirror = lax.axis_index("zh").astype(jnp.int32).reshape(1)
+    place = jnp.stack([lax.axis_index(axis) for axis in ("zh", "y", "zl", "c")]).astype(jnp.int32)
+    mirror = place[:1]
     kvq = to_heads(pack(mirror, keys, values, queries))
     tile_start, codes = places(doc_ids)
     cotangent, tile_start, codes = lax.optimization_barrier((cotangent, tile_start, codes))
@@ -623,11 +732,15 @@
     out, stat = late_forward(tile_start, codes, kvq)
     out, early_stat = early_forward(tile_start, codes, kvq, halo, out)
     back, carry, early_q = early_backward(tile_start, codes, kvq, halo, g, out, early_stat)
-    grads, rest = late_backward(tile_start, codes, kvq, g, out, stat, carry, early_q)
+    grads, rest, *grad_q_parts = late_backward(
+        place, tile_start, codes, kvq, g, out, stat, carry, early_q
+    )
+    grad_q_parts = by_distance(grad_q_parts, "zl")
+    grad_q = to_rows(place, grad_q_parts)
     back = lax.ppermute(back, AXES, [(b, a) for a, b in pairs])
-    grads = join(back, rest, grads)
+    grads = after(join(back, rest, grads), *grad_q_parts[1:])
     (attended,) = unpack(mirror, to_heads(out))
-    grad_k, grad_v, grad_q = unpack(mirror, to_heads(grads))
+    grad_k, grad_v = unpack(mirror, to_heads(grads))
     return attended, grad_q, grad_k, grad_v
 
 

time: 203 us -> 197 us (0.970)
  waiting for transfers between devices: 118 us -> 101 us
  starting transfers between devices: 33.3 us -> 43.9 us
  local copies, waits for them, and re-layouts: 1.88 us -> 4.18 us
  Pallas kernels: 46.7 us -> 44.5 us
    all_to_all x4, waiting for transfers between devices: 113 us -> 65.4 us  [to_heads(): lax.all_to_all(array, GROUP_AXES, split_axis=0, concat_axis=0, tiled=True)]
    ppermute x0 -> x7, waiting for transfers between devices: none -> 33.2 us  [the longest x6 33 us: by_distance(): lax.ppermute(parts[d], axis, [(i, i ^ d) for i in range(4)])]
    ppermute x0 -> x7, starting transfers between devices: none -> 9.35 us  [the longest x6 9.26 us: by_distance(): lax.ppermute(parts[d], axis, [(i, i ^ d) for i in range(4)])]
    ppermute x1, waiting for transfers between devices: 3.69 us -> 1.26 us  [shards(): back = lax.ppermute(back, AXES, [(b, a) for a, b in pairs])]
    unnamed x6 -> x22, local copies, waits for them, and re-layouts: 1 us -> 3.3 us
    pallas_call x1, Pallas kernels: 7.33 us -> 5.11 us  [early_backward(): pl.pallas_call(early_backward_kernel, grid=(1,), in_specs=[smem(), vmem()...]
    pallas_call x2 -> x6, Pallas kernels: 15.7 us -> 16.2 us  [the longest x1 11.8 us: late_backward(): pl.pallas_call(late_backward_kernel, in_specs=[smem(), smem(), vmem(), vm...]
  transfers between devices with their start and end apart: 6 -> 13, of which waited for: 5 -> 10; matrix products, arithmetic and copies ran while one was open for 1% -> 1% of each run, Pallas kernels for 21% -> 20%
where the time goes in v5:
time: 197 us; the launch traced here: 196 us
  waiting for transfers between devices  101 us (51%)
  Pallas kernels  44.5 us (23%)
  starting transfers between devices  43.9 us (22%)
  local copies, waits for them, and re-layouts  4.18 us (2%)
    all_to_all x4, waiting for transfers between devices, to_heads(): lax.all_to_all(array, GROUP_AXES, split_axis=0, concat_axis=0, tiled=True)  65.4 us
    ppermute x6, waiting for transfers between devices, by_distance(): lax.ppermute(parts[d], axis, [(i, i ^ d) for i in range(4)])  33 us
    all_to_all x4, starting transfers between devices, to_heads(): lax.all_to_all(array, GROUP_AXES, split_axis=0, concat_axis=0, tiled=True)  26.5 us
    pallas_call x1, Pallas kernels, late_backward(): pl.pallas_call(late_backward_kernel, in_specs=[smem(), smem(), vmem(), vm...  11.8 us
    pallas_call x1, Pallas kernels, late_forward(): pl.pallas_call(late_forward_kernel, in_specs=[smem(), vmem(), vmem(), vme...  9.88 us
    ppermute x6, starting transfers between devices, by_distance(): lax.ppermute(parts[d], axis, [(i, i ^ d) for i in range(4)])  9.26 us
    ppermute x1, starting transfers between devices, shards(): back = lax.ppermute(back, AXES, [(b, a) for a, b in pairs])  5.4 us
    pallas_call x2, Pallas kernels, pack(): pl.pallas_call(pack_kernel, in_specs=[smem()] + [hbm()] * count, out_spec...  5.26 us
  transfers between devices with their start and end apart: 13, of which 10 were waited for; matrix products, arithmetic and copies ran while one was open for 1% of the time, Pallas kernels for 20%

profile of v5, /device:TPU:4, one launch (start us, length us, event | category | flops | bytes accessed | tf_op | source)
XLA Modules:
  0.0 196.3 jit_solution(11200877982260716884)
XLA Ops:
  0.6 3.2 %pack.2 = bf16[32,3,96,128]{3,2,1,0:T(8,128)(2,1)} custom-call(s32[1]{0:T(128)} %bitcast.mirror_ref, bf16[128,3072]{1,0:T(8,128)(2,1)} %refs_0_.1, bf16[128,3072]{1,0:T(8,128)(2,1)} %refs_1_.1, bf16[128,3072]{1,0:T(8,128)(2,1)} %refs_2_.1), custom_call_target="tpu_custom_call" | custom-call | tf_op jit(solution)/shard_map/pack/pallas_call | solution.py:89
  3.8 8.9 %all-to-all-start = ((bf16[32,3,96,128]{3,2,1,0:T(8,128)(2,1)}), bf16[32,3,96,128]{3,2,1,0:T(8,128)(2,1)S(1)}, u32[]{:S(2)}, u32[]{:S(2)}) async-start(bf16[32,3,96,128]{3,2,1,0:T(8,128)(2,1)} %pack.2), calls=%async_computation | async-start | bytes 4718592 | tf_op jit(solution)/shard_map/all_to_all | solution.py:701
  12.8 0.7 dynamic_slice.7
  13.5 0.8 dynamic-slice_select_fusion
  14.3 0.1 slice_reduce_fusion
  14.4 0.2 shift-right-arithmetic_and_fusion
  14.7 0.1 select_convert_fusion.1
  14.8 0.2 select_convert_fusion.key_code_ref
  15.0 2.1 %pack.3.__0_ = bf16[32,1,96,128]{3,2,1,0:T(8,128)(2,1)} custom-call(s32[1]{0:T(128)} %bitcast.mirror_ref, bf16[128,3072]{1,0:T(8,128)(2,1)} %refs_0_.2), custom_call_target="tpu_custom_call" | custom-call | tf_op jit(solution)/shard_map/pack/pallas_call | solution.py:89
  17.1 51.7 %all-to-all-done.kvq_ref = bf16[32,3,96,128]{3,2,1,0:T(8,128)(2,1)S(1)} async-done(((bf16[32,3,96,128]{3,2,1,0:T(8,128)(2,1)}), bf16[32,3,96,128]{3,2,1,0:T(8,128)(2,1)S(1)}, u32[]{:S(2)}, u32[]{:S(2)}) %all-to-all-start) | async-done | bytes 2359328 | tf_op jit(solution)/shard_map/all_to_all | solution.py:701
  68.9 0.0 copy-start.10
  68.9 2.7 %collective-permute-start = (bf16[8,2,96,128]{3,2,1,0:T(8,128)(2,1)S(1)}, bf16[8,2,96,128]{3,2,1,0:T(8,128)(2,1)S(1)}, u32[]{:S(2)}, u32[]{:S(2)}) collective-permute-start(bf16[8,2,96,128]{3,2,1,0:T(8,128)(2,1)S(1)} %slice.14.__1_), channel_id=1, source_target_pairs={{0,38},{1,39},{2,36},{3,37},{4,34},{5,35},{6,32},{7,33},{8,46},{9,... | collective-permute-start | bytes 1179656 | tf_op jit(solution)/shard_map/ppermute | solution.py:730
  71.6 6.6 %all-to-all-start.2 = ((bf16[32,1,96,128]{3,2,1,0:T(8,128)(2,1)}), bf16[32,1,96,128]{3,2,1,0:T(8,128)(2,1)}, u32[]{:S(2)}, u32[]{:S(2)}) async-start(bf16[32,1,96,128]{3,2,1,0:T(8,128)(2,1)} %after.2), calls=%async_computation.2 | async-start | bytes 1572864 | tf_op jit(solution)/shard_map/all_to_all | solution.py:701
  78.2 9.9 %late_forward.1 = (bf16[32,1,96,128]{3,2,1,0:T(8,128)(2,1)}, f32[16,1,256]{2,1,0:T(1,128)S(1)}) custom-call(s32[16]{0:T(128)S(1)} %and_select_fusion.2.tile_start_ref, bf16[16,5120]{1,0:T(8,128)(2,1)S(1)} %select_convert_fusion.key_code_ref, bf16[16,16,256]{2,1,0:T(8,128)(2,1)S(1)} %bitcast.11, bf16[32,3,96,128]{3,2,1,0:T(8,128)(2,1)S(1)} %all-to-all-done.kvq_ref), custom_call_target="tpu_custom_call" | custom-call | flops 32999999488 | tf_op jit(solution)/shard_map/late_forward/pallas_call | solution.py:276
  88.1 1.5 collective-permute-done.halo_ref
  89.6 3.7 %early_forward.1 = (bf16[32,1,96,128]{3,2,1,0:T(8,128)(2,1)}, f32[4,1,256]{2,1,0:T(1,128)S(1)}) custom-call(s32[16]{0:T(128)S(1)} %and_select_fusion.2.tile_start_ref, bf16[16,5120]{1,0:T(8,128)(2,1)S(1)} %select_convert_fusion.key_code_ref, bf16[16,16,256]{2,1,0:T(8,128)(2,1)S(1)} %bitcast.12, ...), custom_call_target="tpu_custom_call", output_to_operand_aliasing={{0}: (5, {})} | custom-call | flops 1100000000 | tf_op jit(solution)/shard_map/early_forward/pallas_call | solution.py:471
  93.2 7.3 %all-to-all-done.2.g_ref = bf16[32,1,96,128]{3,2,1,0:T(8,128)(2,1)} async-done(((bf16[32,1,96,128]{3,2,1,0:T(8,128)(2,1)}), bf16[32,1,96,128]{3,2,1,0:T(8,128)(2,1)}, u32[]{:S(2)}, u32[]{:S(2)}) %all-to-all-start.2) | async-done | bytes 786464 | tf_op jit(solution)/shard_map/all_to_all | solution.py:701
  100.5 3.9 %all-to-all-start.1 = ((bf16[32,1,96,128]{3,2,1,0:T(8,128)(2,1)}), bf16[32,1,96,128]{3,2,1,0:T(8,128)(2,1)S(1)}, u32[]{:S(2)}, u32[]{:S(2)}) async-start(bf16[32,1,96,128]{3,2,1,0:T(8,128)(2,1)} %get-tuple-element.31.out_ref), calls=%async_computation.1 | async-start | bytes 1572864 | tf_op jit(solution)/shard_map/all_to_all | solution.py:701
  104.4 0.1 pad_add_fusion.1.place_ref
  104.5 1.0 copy-done.1
  105.5 5.1 %early_backward.1 = (bf16[8,2,96,128]{3,2,1,0:T(8,128)(2,1)}, f32[2,96,1024]{2,1,0:T(8,128)}, bf16[8,96,128]{2,1,0:T(8,128)(2,1)}) custom-call(s32[16]{0:T(128)S(1)} %and_select_fusion.2.tile_start_ref, bf16[16,5120]{1,0:T(8,128)(2,1)S(1)} %select_convert_fusion.key_code_ref, bf16[16,16,256]{2,1,0:T(8,128)(2,1)S(1)} %bitcast.13, ...), custom_call_target="tpu_custom_call" | custom-call | flops 1100000000 | tf_op jit(solution)/shard_map/early_backward/pallas_call | solution.py:486
  110.6 5.4 %collective-permute-start.8 = (bf16[8,2,96,128]{3,2,1,0:T(8,128)(2,1)}, bf16[8,2,96,128]{3,2,1,0:T(8,128)(2,1)S(1)}, u32[]{:S(2)}, u32[]{:S(2)}) collective-permute-start(bf16[8,2,96,128]{3,2,1,0:T(8,128)(2,1)} %get-tuple-element.45), channel_id=1, source_target_pairs={{38,0},{39,1},{36,2},{37,3},{34,4},{35,5},{32,6},{33,7},{46,8},{47... | collective-permute-start | bytes 1179656 | tf_op jit(solution)/shard_map/ppermute | solution.py:740
  116.0 11.8 %late_backward.1 = (bf16[32,2,96,128]{3,2,1,0:T(8,128)(2,1)}, f32[2,96,1024]{2,1,0:T(8,128)S(1)}, bf16[4,2,96,128]{3,2,1,0:T(8,128)(2,1)}, bf16[4,2,96,128]{3,2,...) custom-call(s32[4]{0:T(128)S(1)} %pad_add_fusion.1.place_ref, ...), custom_call_target="tpu_custom_call" | custom-call | flops 11000000512 | tf_op jit(solution)/shard_map/late_backward/pallas_call | solution.py:511
  127.8 1.5 collective-permute-start.1
  129.4 0.1 collective-permute-start.2
  129.4 2.9 %collective-permute-start.3 = (bf16[4,2,96,128]{3,2,1,0:T(8,128)(2,1)}, bf16[4,2,96,128]{3,2,1,0:T(8,128)(2,1)S(1)}, u32[]{:S(2)}, u32[]{:S(2)}) collective-permute-start(bf16[4,2,96,128]{3,2,1,0:T(8,128)(2,1)} %get-tuple-element.40), channel_id=1, source_target_pairs={{0,6},{2,4},{4,2},{6,0},{1,7},{3,5},{5,3},{7,1},{8,14},{10,12},{12... | collective-permute-start | bytes 589832 | tf_op jit(solution)/shard_map/ppermute | solution.py:621
  132.3 1.3 collective-permute-done.8.back_ref
  133.6 0.8 join.1.__0_
  134.4 3.8 %collective-permute-done.1.refs_1_.__1_ = bf16[4,2,96,128]{3,2,1,0:T(8,128)(2,1)S(1)} collective-permute-done((bf16[4,2,96,128]{3,2,1,0:T(8,128)(2,1)}, bf16[4,2,96,128]{3,2,1,0:T(8,128)(2,1)S(1)}, u32[]{:S(2)}, u32[]{:S(2)}) %collective-permute-start.1) | collective-permute-done | bytes 196640 | tf_op jit(solution)/shard_map/ppermute | solution.py:621
  138.2 8.5 %collective-permute-done.2.refs_2_.__2_ = bf16[4,2,96,128]{3,2,1,0:T(8,128)(2,1)S(1)} collective-permute-done((bf16[4,2,96,128]{3,2,1,0:T(8,128)(2,1)}, bf16[4,2,96,128]{3,2,1,0:T(8,128)(2,1)S(1)}, u32[]{:S(2)}, u32[]{:S(2)}) %collective-permute-start.2) | collective-permute-done | bytes 196640 | tf_op jit(solution)/shard_map/ppermute | solution.py:621
  146.7 0.7 copy-done.4
  147.4 0.7 copy-done.6
  148.1 7.0 %all-to-all-start.3 = ((bf16[32,2,96,128]{3,2,1,0:T(8,128)(2,1)}), bf16[32,2,96,128]{3,2,1,0:T(8,128)(2,1)S(1)}, u32[]{:S(2)}, u32[]{:S(2)}) async-start(bf16[32,2,96,128]{3,2,1,0:T(8,128)(2,1)} %after.3), calls=%async_computation.3 | async-start | bytes 3145728 | tf_op jit(solution)/shard_map/all_to_all | solution.py:701
  155.2 1.5 turn.1
  156.7 1.9 collective-permute-start.4
  158.6 2.7 %collective-permute-start.5 = (bf16[4,2,96,128]{3,2,1,0:T(8,128)(2,1)}, bf16[4,2,96,128]{3,2,1,0:T(8,128)(2,1)S(1)}, u32[]{:S(2)}, u32[]{:S(2)}) collective-permute-start(bf16[4,2,96,128]{3,2,1,0:T(8,128)(2,1)} %get-tuple-element.43), channel_id=1, source_target_pairs={{0,16},{8,24},{16,0},{24,8},{1,17},{9,25},{17,1},{25,9},{2,18},{10... | collective-permute-start | bytes 589832 | tf_op jit(solution)/shard_map/ppermute | solution.py:621
  161.3 0.2 collective-permute-start.6
  161.5 12.8 %collective-permute-done.4.refs_1_.part_1 = bf16[4,2,96,128]{3,2,1,0:T(8,128)(2,1)S(1)} collective-permute-done((bf16[4,2,96,128]{3,2,1,0:T(8,128)(2,1)}, bf16[4,2,96,128]{3,2,1,0:T(8,128)(2,1)S(1)}, u32[]{:S(2)}, u32[]{:S(2)}) %collective-permute-start.4) | collective-permute-done | bytes 196640 | tf_op jit(solution)/shard_map/ppermute | solution.py:621
  174.3 7.9 %collective-permute-done.5.refs_2_.part_2 = bf16[4,2,96,128]{3,2,1,0:T(8,128)(2,1)S(1)} collective-permute-done((bf16[4,2,96,128]{3,2,1,0:T(8,128)(2,1)}, bf16[4,2,96,128]{3,2,1,0:T(8,128)(2,1)S(1)}, u32[]{:S(2)}, u32[]{:S(2)}) %collective-permute-start.5) | collective-permute-done | bytes 196640 | tf_op jit(solution)/shard_map/ppermute | solution.py:621
  182.2 0.0 collective-permute-done.6.refs_3_.part_3
  182.2 0.9 copy-done.8
  183.1 1.3 other_core.1
  184.4 0.1 collective-permute-start.7
  184.5 1.7 unpack.2
  186.2 0.2 collective-permute-done.7.other_ref
  186.4 1.6 rows_of.1
  188.0 6.4 %all-to-all-done.3.in_ref = bf16[32,2,96,128]{3,2,1,0:T(8,128)(2,1)S(1)} async-done(((bf16[32,2,96,128]{3,2,1,0:T(8,128)(2,1)}), bf16[32,2,96,128]{3,2,1,0:T(8,128)(2,1)S(1)}, u32[]{:S(2)}, u32[]{:S(2)}) %all-to-all-start.3) | async-done | bytes 1572896 | tf_op jit(solution)/shard_map/all_to_all | solution.py:701
  194.4 1.9 unpack.3
  (30 shorter events, 0.1 us)
Async XLA Ops:
  3.8 65.0 %all-to-all-start = ((bf16[32,3,96,128]{3,2,1,0:T(8,128)(2,1)}), bf16[32,3,96,128]{3,2,1,0:T(8,128)(2,1)S(1)}, u32[]{:S(2)}, u32[]{:S(2)}) async-start(bf16[32,3,96,128]{3,2,1,0:T(8,128)(2,1)} %pack.2), calls=%async_computation | async-start | bytes 4718592 | tf_op jit(solution)/shard_map/all_to_all | solution.py:701
  68.9 2.7 %copy-start.10 = (bf16[8,2,96,128]{3,2,1,0:T(8,128)(2,1)}, bf16[8,2,96,128]{3,2,1,0:T(8,128)(2,1)S(1)}, u32[]{:S(2)}) copy-start(bf16[8,2,96,128]{3,2,1,0:T(8,128)(2,1)S(1)} %slice.14.__1_) | copy-start | bytes 1179652
  68.9 20.7 %collective-permute-start = (bf16[8,2,96,128]{3,2,1,0:T(8,128)(2,1)S(1)}, bf16[8,2,96,128]{3,2,1,0:T(8,128)(2,1)S(1)}, u32[]{:S(2)}, u32[]{:S(2)}) collective-permute-start(bf16[8,2,96,128]{3,2,1,0:T(8,128)(2,1)S(1)} %slice.14.__1_), channel_id=1, source_target_pairs={{0,38},{1,39},{2,36},{3,37},{4,34},{5,35},{6,32},{7,33},{8,46},{9,... | collective-permute-start | bytes 1179656 | tf_op jit(solution)/shard_map/ppermute | solution.py:730
  71.6 29.0 %all-to-all-start.2 = ((bf16[32,1,96,128]{3,2,1,0:T(8,128)(2,1)}), bf16[32,1,96,128]{3,2,1,0:T(8,128)(2,1)}, u32[]{:S(2)}, u32[]{:S(2)}) async-start(bf16[32,1,96,128]{3,2,1,0:T(8,128)(2,1)} %after.2), calls=%async_computation.2 | async-start | bytes 1572864 | tf_op jit(solution)/shard_map/all_to_all | solution.py:701
  89.6 3.7 %copy-start = (bf16[8,2,96,128]{3,2,1,0:T(8,128)(2,1)}, bf16[8,2,96,128]{3,2,1,0:T(8,128)(2,1)S(1)}, u32[]{:S(2)}) copy-start(bf16[8,2,96,128]{3,2,1,0:T(8,128)(2,1)S(1)} %collective-permute-done.halo_ref) | copy-start | bytes 1179652
  100.5 47.6 %all-to-all-start.1 = ((bf16[32,1,96,128]{3,2,1,0:T(8,128)(2,1)}), bf16[32,1,96,128]{3,2,1,0:T(8,128)(2,1)S(1)}, u32[]{:S(2)}, u32[]{:S(2)}) async-start(bf16[32,1,96,128]{3,2,1,0:T(8,128)(2,1)} %get-tuple-element.31.out_ref), calls=%async_computation.1 | async-start | bytes 1572864 | tf_op jit(solution)/shard_map/all_to_all | solution.py:701
  104.5 1.0 copy-start.1
  110.6 22.9 %collective-permute-start.8 = (bf16[8,2,96,128]{3,2,1,0:T(8,128)(2,1)}, bf16[8,2,96,128]{3,2,1,0:T(8,128)(2,1)S(1)}, u32[]{:S(2)}, u32[]{:S(2)}) collective-permute-start(bf16[8,2,96,128]{3,2,1,0:T(8,128)(2,1)} %get-tuple-element.45), channel_id=1, source_target_pairs={{38,0},{39,1},{36,2},{37,3},{34,4},{35,5},{32,6},{33,7},{46,8},{47... | collective-permute-start | bytes 1179656 | tf_op jit(solution)/shard_map/ppermute | solution.py:740
  127.8 10.4 %collective-permute-start.1 = (bf16[4,2,96,128]{3,2,1,0:T(8,128)(2,1)}, bf16[4,2,96,128]{3,2,1,0:T(8,128)(2,1)S(1)}, u32[]{:S(2)}, u32[]{:S(2)}) collective-permute-start(bf16[4,2,96,128]{3,2,1,0:T(8,128)(2,1)} %get-tuple-element.38), channel_id=1, source_target_pairs={{0,2},{2,0},{4,6},{6,4},{1,3},{3,1},{5,7},{7,5},{8,10},{10,8},{12,... | collective-permute-start | bytes 589832 | tf_op jit(solution)/shard_map/ppermute | solution.py:621
  129.4 17.4 %collective-permute-start.2 = (bf16[4,2,96,128]{3,2,1,0:T(8,128)(2,1)}, bf16[4,2,96,128]{3,2,1,0:T(8,128)(2,1)S(1)}, u32[]{:S(2)}, u32[]{:S(2)}) collective-permute-start(bf16[4,2,96,128]{3,2,1,0:T(8,128)(2,1)} %get-tuple-element.39), channel_id=1, source_target_pairs={{0,4},{2,6},{4,0},{6,2},{1,5},{3,7},{5,1},{7,3},{8,12},{10,14},{12... | collective-permute-start | bytes 589832 | tf_op jit(solution)/shard_map/ppermute | solution.py:621
  129.4 17.3 %collective-permute-start.3 = (bf16[4,2,96,128]{3,2,1,0:T(8,128)(2,1)}, bf16[4,2,96,128]{3,2,1,0:T(8,128)(2,1)S(1)}, u32[]{:S(2)}, u32[]{:S(2)}) collective-permute-start(bf16[4,2,96,128]{3,2,1,0:T(8,128)(2,1)} %get-tuple-element.40), channel_id=1, source_target_pairs={{0,6},{2,4},{4,2},{6,0},{1,7},{3,5},{5,3},{7,1},{8,14},{10,12},{12... | collective-permute-start | bytes 589832 | tf_op jit(solution)/shard_map/ppermute | solution.py:621
  138.2 8.5 %copy-start.2 = (bf16[4,2,96,128]{3,2,1,0:T(8,128)(2,1)}, bf16[4,2,96,128]{3,2,1,0:T(8,128)(2,1)S(1)}, u32[]{:S(2)}) copy-start(bf16[4,2,96,128]{3,2,1,0:T(8,128)(2,1)S(1)} %collective-permute-done.1.refs_1_.__1_) | copy-start | bytes 589828
  146.7 0.7 copy-start.4
  147.4 0.7 copy-start.6
  148.1 7.1 %copy-start.3 = (bf16[4,2,96,128]{3,2,1,0:T(8,128)(2,1)S(1)}, bf16[4,2,96,128]{3,2,1,0:T(8,128)(2,1)}, u32[]{:S(2)}) copy-start(bf16[4,2,96,128]{3,2,1,0:T(8,128)(2,1)} %copy-done.2) | copy-start | bytes 589828
  148.1 7.1 %copy-start.5 = (bf16[4,2,96,128]{3,2,1,0:T(8,128)(2,1)S(1)}, bf16[4,2,96,128]{3,2,1,0:T(8,128)(2,1)}, u32[]{:S(2)}) copy-start(bf16[4,2,96,128]{3,2,1,0:T(8,128)(2,1)} %copy-done.4) | copy-start | bytes 589828
  148.1 7.1 %copy-start.7 = (bf16[4,2,96,128]{3,2,1,0:T(8,128)(2,1)S(1)}, bf16[4,2,96,128]{3,2,1,0:T(8,128)(2,1)}, u32[]{:S(2)}) copy-start(bf16[4,2,96,128]{3,2,1,0:T(8,128)(2,1)} %copy-done.6) | copy-start | bytes 589828
  148.1 7.1 %copy-start.9 = (bf16[4,2,96,128]{3,2,1,0:T(8,128)(2,1)S(1)}, bf16[4,2,96,128]{3,2,1,0:T(8,128)(2,1)}, u32[]{:S(2)}) copy-start(bf16[4,2,96,128]{3,2,1,0:T(8,128)(2,1)} %get-tuple-element.37.refs_0_) | copy-start | bytes 589828
  148.1 46.3 %all-to-all-start.3 = ((bf16[32,2,96,128]{3,2,1,0:T(8,128)(2,1)}), bf16[32,2,96,128]{3,2,1,0:T(8,128)(2,1)S(1)}, u32[]{:S(2)}, u32[]{:S(2)}) async-start(bf16[32,2,96,128]{3,2,1,0:T(8,128)(2,1)} %after.3), calls=%async_computation.3 | async-start | bytes 3145728 | tf_op jit(solution)/shard_map/all_to_all | solution.py:701
  156.7 17.6 %collective-permute-start.4 = (bf16[4,2,96,128]{3,2,1,0:T(8,128)(2,1)}, bf16[4,2,96,128]{3,2,1,0:T(8,128)(2,1)S(1)}, u32[]{:S(2)}, u32[]{:S(2)}) collective-permute-start(bf16[4,2,96,128]{3,2,1,0:T(8,128)(2,1)} %get-tuple-element.42), channel_id=1, source_target_pairs={{0,8},{8,0},{16,24},{24,16},{1,9},{9,1},{17,25},{25,17},{2,10},{10... | collective-permute-start | bytes 589832 | tf_op jit(solution)/shard_map/ppermute | solution.py:621
  158.6 23.6 %collective-permute-start.5 = (bf16[4,2,96,128]{3,2,1,0:T(8,128)(2,1)}, bf16[4,2,96,128]{3,2,1,0:T(8,128)(2,1)S(1)}, u32[]{:S(2)}, u32[]{:S(2)}) collective-permute-start(bf16[4,2,96,128]{3,2,1,0:T(8,128)(2,1)} %get-tuple-element.43), channel_id=1, source_target_pairs={{0,16},{8,24},{16,0},{24,8},{1,17},{9,25},{17,1},{25,9},{2,18},{10... | collective-permute-start | bytes 589832 | tf_op jit(solution)/shard_map/ppermute | solution.py:621
  161.3 20.8 %collective-permute-start.6 = (bf16[4,2,96,128]{3,2,1,0:T(8,128)(2,1)}, bf16[4,2,96,128]{3,2,1,0:T(8,128)(2,1)S(1)}, u32[]{:S(2)}, u32[]{:S(2)}) collective-permute-start(bf16[4,2,96,128]{3,2,1,0:T(8,128)(2,1)} %get-tuple-element.44), channel_id=1, source_target_pairs={{0,24},{8,16},{16,8},{24,0},{1,25},{9,17},{17,9},{25,1},{2,26},{10... | collective-permute-start | bytes 589832 | tf_op jit(solution)/shard_map/ppermute | solution.py:621
  182.2 0.9 copy-start.8
  184.4 2.0 %collective-permute-start.7 = (bf16[4,4,96,128]{3,2,1,0:T(8,128)(2,1)}, bf16[4,4,96,128]{3,2,1,0:T(8,128)(2,1)S(1)}, u32[]{:S(2)}, u32[]{:S(2)}) collective-permute-start(bf16[4,4,96,128]{3,2,1,0:T(8,128)(2,1)} %other_core.1), channel_id=1, source_target_pairs={{0,1},{1,0},{2,3},{3,2},{4,5},{5,4},{6,7},{7,6},{8,9},{9,8},{10,11... | collective-permute-start | bytes 1179656 | tf_op jit(solution)/shard_map/ppermute | solution.py:663

commit v6 on v5

--- a/solution.py
+++ b/solution.py
@@ -229,34 +229,47 @@
     lax.fori_loop(0, AHEAD_TILES, tile, 0)
 
 
+def part_copies(place_ref, buffer, parts, b, sems, fetch=False):
+    copies = []
+    for d, ref in enumerate(parts):
+        here = buffer.at[pl.ds(b * HALO + 2 * (place_ref[2] ^ d), 2)]
+        there = ref.at[b]
+        ends = (there, here) if fetch else (here, there)
+        copies.append(pltpu.make_async_copy(*ends, sems.at[b, d]))
+    return copies
+
+
 def late_forward_kernel(
-    tile_start_ref, key_code_ref, query_code_ref, kvq_ref, out_ref, stat_ref,
-    key_flat, value_turned, buffer, sent
+    place_ref, tile_start_ref, key_code_ref, query_code_ref, kvq_ref,
+    part_0, part_1, part_2, part_3, stat_ref, key_flat, value_turned, buffer, sent
 ):
+    parts = (part_0, part_1, part_2, part_3)
     chunks = range(HALO, HALO + CHUNKS)
     fill_keys(None, kvq_ref, key_code_ref, chunks, key_flat, None)
     fill_value_columns(None, kvq_ref, chunks, value_turned)
 
     def store(chunk, value):
-        buffer[chunk, 0] = value
+        buffer[chunk] = value
 
     def block(b, _):
         forward_tiles(
             b, tile_start_ref, query_code_ref, kvq_ref, store, stat_ref, key_flat, value_turned
         )
-        send_block(buffer, out_ref, sent, b).start()
+        for copy in part_copies(place_ref, buffer, parts, b, sent):
+            copy.start()
         return 0
 
     lax.fori_loop(1, BLOCKS, block, 0)
     for b in range(1, BLOCKS):
-        send_block(buffer, out_ref, sent, b).wait()
+        for copy in part_copies(place_ref, buffer, parts, b, sent):
+            copy.wait()
 
 
 def cost(time):
     return pl.CostEstimate(flops=int(time * 1.1e9), bytes_accessed=0, transcendentals=0)
 
 
-OUT_SHAPE = pltpu.HBM((CHUNKS, 1, HEAD_DIM, CHUNK), BF16)
+PARTS = [pltpu.HBM((4, 2, HEAD_DIM, CHUNK), BF16)] * 4
 
 
 def part(count, width):
@@ -267,22 +280,22 @@
     return [
         pltpu.VMEM((window, WIDE), BF16),
         pltpu.VMEM((WIDE, window), BF16),
-        pltpu.VMEM((chunks, 1, HEAD_DIM, CHUNK), BF16),
-        pltpu.SemaphoreType.DMA((BLOCKS,)),
+        pltpu.VMEM((chunks, HEAD_DIM, CHUNK), BF16),
+        pltpu.SemaphoreType.DMA((BLOCKS, 4)),
     ]
 
 
-def late_forward(tile_start, codes, kvq):
+def late_forward(place, tile_start, codes, kvq):
     return pl.pallas_call(
         late_forward_kernel,
-        in_specs=[smem(), vmem(), vmem(), vmem()],
-        out_specs=[hbm(), vmem()],
-        out_shape=[OUT_SHAPE, jax.ShapeDtypeStruct((TILES, 1, TILE), F32)],
+        in_specs=[smem(), smem(), vmem(), vmem(), vmem()],
+        out_specs=[hbm()] * 4 + [vmem()],
+        out_shape=PARTS + [jax.ShapeDtypeStruct((TILES, 1, TILE), F32)],
         scratch_shapes=forward_scratch(WINDOW, CHUNKS),
         compiler_params=pltpu.CompilerParams(vmem_limit_bytes=40 * MIB),
         cost_estimate=cost(30),
         name="late_forward",
-    )(tile_start, *codes, kvq)
+    )(place, tile_start, *codes, kvq)
 
 
 def backward_tiles(
@@ -292,8 +305,8 @@
     def tile(i, _):
         def body(count):
             q = tile_of(kvq_ref, 2, i)
-            g = tile_of(g_ref, 0, i)
-            o = tile_of(out_ref, 0, i)
+            g = jnp.concatenate([g_ref[2 * i], g_ref[2 * i + 1]], 1)
+            o = jnp.concatenate([out_ref[2 * i], out_ref[2 * i + 1]], 1)
             delta = jnp.sum(o.astype(F32) * g.astype(F32), axis=0, keepdims=True)
             stat = stat_ref[i]
             code = query_code_ref[i].astype(F32)
@@ -320,33 +333,34 @@
 
 
 def early_forward_kernel(
-    tile_start_ref, key_code_ref, query_code_ref, kvq_ref, halo_ref, _, out_ref, stat_ref,
-    key_flat, value_turned, buffer, sent
+    place_ref, tile_start_ref, key_code_ref, query_code_ref, kvq_ref, halo_ref, _, __, ___, ____,
+    part_0, part_1, part_2, part_3, stat_ref, key_flat, value_turned, buffer, sent
 ):
     fill_keys(halo_ref, kvq_ref, key_code_ref, range(2 * HALO), key_flat, None)
     fill_value_columns(halo_ref, kvq_ref, range(2 * HALO), value_turned)
 
     def store(chunk, value):
-        buffer[chunk, 0] = value
+        buffer[chunk] = value
 
     forward_tiles(
         0, tile_start_ref, query_code_ref, kvq_ref, store, stat_ref, key_flat, value_turned
     )
-    copy = send_block(buffer, out_ref, sent, 0)
-    copy.start()
-    copy.wait()
+    copies = part_copies(place_ref, buffer, (part_0, part_1, part_2, part_3), 0, sent)
+    for copy in copies:
+        copy.start()
+    for copy in copies:
+        copy.wait()
 
 
 def early_backward_kernel(
-    tile_start_ref, key_code_ref, query_code_ref, kvq_ref, halo_ref, g_ref, out_ref, stat_ref,
+    place_ref, tile_start_ref, key_code_ref, query_code_ref, kvq_ref, halo_ref, stat_ref,
+    g_0, g_1, g_2, g_3, out_0, out_1, out_2, out_3,
     back_ref, carry_ref, grad_q_ref,
     key_flat, key_turned, value_flat, key_sum, value_sum, g_part, out_part, back_part, grad_q_part,
-    sent
+    sent, fetched_g, fetched_out
 ):
-    fetches = [
-        pltpu.make_async_copy(source.at[pl.ds(0, HALO)], target, sent.at[n])
-        for n, (source, target) in enumerate(((g_ref, g_part), (out_ref, out_part)))
-    ]
+    fetches = part_copies(place_ref, g_part, (g_0, g_1, g_2, g_3), 0, fetched_g, True)
+    fetches += part_copies(place_ref, out_part, (out_0, out_1, out_2, out_3), 0, fetched_out, True)
     for copy in fetches:
         copy.start()
     fill_keys(halo_ref, kvq_ref, key_code_ref, range(2 * HALO), key_flat, key_turned)
@@ -383,21 +397,19 @@
 
 
 def late_backward_kernel(
-    place_ref, tile_start_ref, key_code_ref, query_code_ref, kvq_ref, g_ref, out_ref, stat_ref,
-    carry_ref, grad_q_ref, grads_ref, rest_ref, part_0, part_1, part_2, part_3,
+    place_ref, tile_start_ref, key_code_ref, query_code_ref, kvq_ref, stat_ref,
+    g_0, g_1, g_2, g_3, out_0, out_1, out_2, out_3, carry_ref, grad_q_ref, grads_ref, rest_ref, part_0, part_1, part_2, part_3,
     key_flat, key_turned, value_flat, key_sum, value_sum, buffer, queries, g_all,
-    out_all, carry, sent, fetched, parted
+    out_all, carry, sent, fetched, parted, fetched_g, fetched_out
 ):
     def fetch(b):
-        part = pl.ds(b * HALO, HALO)
-        return (
-            pltpu.make_async_copy(g_ref.at[part], g_all.at[part], fetched.at[0, b]),
-            pltpu.make_async_copy(out_ref.at[part], out_all.at[part], fetched.at[1, b]),
-        )
+        return part_copies(
+            place_ref, g_all, (g_0, g_1, g_2, g_3), b, fetched_g, True
+        ) + part_copies(place_ref, out_all, (out_0, out_1, out_2, out_3), b, fetched_out, True)
 
     first = (
-        pltpu.make_async_copy(carry_ref, carry, fetched.at[0, 0]),
-        pltpu.make_async_copy(grad_q_ref, queries.at[pl.ds(0, HALO)], fetched.at[1, 0]),
+        pltpu.make_async_copy(carry_ref, carry, fetched.at[0]),
+        pltpu.make_async_copy(grad_q_ref, queries.at[pl.ds(0, HALO)], fetched.at[1]),
     )
     for copy in (*fetch(1), *first, *fetch(2), *fetch(3)):
         copy.start()
@@ -411,13 +423,7 @@
         queries[chunk] = value
 
     def send_queries(b):
-        copies = []
-        for d, ref in enumerate((part_0, part_1, part_2, part_3)):
-            chunk = b * HALO + 2 * (place_ref[2] ^ d)
-            copies.append(
-                pltpu.make_async_copy(queries.at[pl.ds(chunk, 2)], ref.at[b], parted.at[b, d])
-            )
-        return copies
+        return part_copies(place_ref, queries, (part_0, part_1, part_2, part_3), b, parted)
 
     def block(b, _):
         for copy in fetch(b):
@@ -467,26 +473,26 @@
     ]
 
 
-def early_forward(tile_start, codes, kvq, halo, out):
+def early_forward(place, tile_start, codes, kvq, halo, parts):
     return pl.pallas_call(
         early_forward_kernel,
         grid=(1,),
-        in_specs=[smem(), vmem(), vmem(), part(HALO, 3), vmem(), hbm()],
-        out_specs=[hbm(), vmem()],
-        out_shape=[OUT_SHAPE, jax.ShapeDtypeStruct((AHEAD_TILES, 1, TILE), F32)],
-        input_output_aliases={5: 0},
+        in_specs=[smem(), smem(), vmem(), vmem(), part(HALO, 3), vmem()] + [hbm()] * 4,
+        out_specs=[hbm()] * 4 + [vmem()],
+        out_shape=PARTS + [jax.ShapeDtypeStruct((AHEAD_TILES, 1, TILE), F32)],
+        input_output_aliases={6 + d: d for d in range(4)},
         scratch_shapes=forward_scratch(2 * AHEAD, HALO),
         compiler_params=pltpu.CompilerParams(vmem_limit_bytes=40 * MIB),
         cost_estimate=cost(1),
         name="early_forward",
-    )(tile_start, *codes, kvq, halo, *in_hbm(out))
-
-
-def early_backward(tile_start, codes, kvq, halo, g, out, stat):
+    )(place, tile_start, *codes, kvq, halo, *in_hbm(*parts))
+
+
+def early_backward(place, tile_start, codes, kvq, halo, stat, g, out):
     return pl.pallas_call(
         early_backward_kernel,
         grid=(1,),
-        in_specs=[smem(), vmem(), vmem(), part(HALO, 3), vmem(), hbm(), hbm(), vmem()],
+        in_specs=[smem(), smem(), vmem(), vmem(), part(HALO, 3), vmem(), vmem()] + [hbm()] * 8,
         out_specs=[hbm()] * 3,
         out_shape=[
             pltpu.HBM((HALO, 2, HEAD_DIM, CHUNK), BF16),
@@ -495,22 +501,24 @@
         ],
         scratch_shapes=sums_scratch(2 * AHEAD)
         + [
-            pltpu.VMEM((HALO, 1, HEAD_DIM, CHUNK), BF16),
-            pltpu.VMEM((HALO, 1, HEAD_DIM, CHUNK), BF16),
+            pltpu.VMEM((HALO, HEAD_DIM, CHUNK), BF16),
+            pltpu.VMEM((HALO, HEAD_DIM, CHUNK), BF16),
             pltpu.VMEM((HALO, 2, HEAD_DIM, CHUNK), BF16),
             pltpu.VMEM((HALO, HEAD_DIM, CHUNK), BF16),
             pltpu.SemaphoreType.DMA((6,)),
+            pltpu.SemaphoreType.DMA((1, 4)),
+            pltpu.SemaphoreType.DMA((1, 4)),
         ],
         compiler_params=pltpu.CompilerParams(vmem_limit_bytes=40 * MIB),
         cost_estimate=cost(1),
         name="early_backward",
-    )(tile_start, *codes, kvq, halo, *in_hbm(g, out), stat)
-
-
-def late_backward(place, tile_start, codes, kvq, g, out, stat, carry, grad_q):
+    )(place, tile_start, *codes, kvq, halo, stat, *in_hbm(*g, *out))
+
+
+def late_backward(place, tile_start, codes, kvq, stat, g, out, carry, grad_q):
     return pl.pallas_call(
         late_backward_kernel,
-        in_specs=[smem(), smem(), vmem(), vmem(), vmem(), hbm(), hbm(), vmem(), hbm(), hbm()],
+        in_specs=[smem(), smem(), vmem(), vmem(), vmem(), vmem()] + [hbm()] * 10,
         out_specs=[hbm(), vmem()] + [hbm()] * 4,
         out_shape=[
             pltpu.HBM((CHUNKS, 2, HEAD_DIM, CHUNK), BF16),
@@ -521,17 +529,19 @@
         + [
             pltpu.VMEM((CHUNKS, 2, HEAD_DIM, CHUNK), BF16),
             pltpu.VMEM((CHUNKS, HEAD_DIM, CHUNK), BF16),
-            pltpu.VMEM((CHUNKS, 1, HEAD_DIM, CHUNK), BF16),
-            pltpu.VMEM((CHUNKS, 1, HEAD_DIM, CHUNK), BF16),
+            pltpu.VMEM((CHUNKS, HEAD_DIM, CHUNK), BF16),
+            pltpu.VMEM((CHUNKS, HEAD_DIM, CHUNK), BF16),
             pltpu.VMEM((2, HEAD_DIM, AHEAD), F32),
             pltpu.SemaphoreType.DMA((BLOCKS,)),
-            pltpu.SemaphoreType.DMA((2, BLOCKS)),
+            pltpu.SemaphoreType.DMA((2,)),
+            pltpu.SemaphoreType.DMA((BLOCKS, 4)),
+            pltpu.SemaphoreType.DMA((BLOCKS, 4)),
             pltpu.SemaphoreType.DMA((BLOCKS, 4)),
         ],
         compiler_params=pltpu.CompilerParams(vmem_limit_bytes=40 * MIB),
         cost_estimate=cost(10),
         name="late_backward",
-    )(place, tile_start, *codes, kvq, *in_hbm(g, out), stat, *in_hbm(carry, grad_q))
+    )(place, tile_start, *codes, kvq, stat, *in_hbm(*g, *out, carry, grad_q))
 
 
 def join_kernel(back_ref, rest_ref, _, out_ref, buffer, moved):
@@ -563,39 +573,64 @@
     )(back, rest, *in_hbm(grads))
 
 
-def turn_kernel(axis, place_ref, *refs):
-    sources, targets, sent = refs[:4], refs[4:8], refs[8]
-    here = place_ref[axis]
-    copies = []
-    for d in range(4):
-        for e in range(4):
-            copies.append(
-                pltpu.make_async_copy(sources[d].at[here ^ e], targets[e].at[d], sent.at[d, e])
-            )
+def move(copies):
     for copy in copies:
         copy.start()
     for copy in copies:
         copy.wait()
 
 
-def turn(place, axis, parts):
-    return pl.pallas_call(
-        functools.partial(turn_kernel, axis),
+def turn_kernel(back, place_ref, *refs):
+    sources, targets, (buffer, fetched, sent) = refs[:4], refs[4:8], refs[8:]
+    y = place_ref[1]
+    fetches = []
+    for d in range(4):
+        for e in range(4):
+            if back:
+                ends = (sources[e].at[d], buffer.at[d, y ^ e])
+            else:
+                ends = (sources[d].at[y ^ e], buffer.at[e, d])
+            fetches.append(pltpu.make_async_copy(*ends, fetched.at[d, e]))
+    move(fetches)
+    move([pltpu.make_async_copy(buffer.at[e], targets[e], sent.at[e]) for e in range(4)])
+
+
+def turn(place, parts, back=False):
+    return pl.pallas_call(
+        functools.partial(turn_kernel, back),
         in_specs=[smem()] + [pl.BlockSpec(memory_space=pl.ANY)] * 4,
         out_specs=[hbm()] * 4,
-        out_shape=[pltpu.HBM((4, 2, HEAD_DIM, CHUNK), BF16)] * 4,
-        scratch_shapes=[pltpu.SemaphoreType.DMA((4, 4))],
+        out_shape=PARTS,
+        scratch_shapes=[
+            pltpu.VMEM((4, 4, 2, HEAD_DIM, CHUNK), BF16),
+            pltpu.SemaphoreType.DMA((4, 4)),
+            pltpu.SemaphoreType.DMA((4,)),
+        ],
         compiler_params=pltpu.CompilerParams(vmem_limit_bytes=40 * MIB),
         cost_estimate=cost(1),
         name="turn",
     )(place, *parts)
 
 
-def other_core_kernel(place_ref, *refs):
-    sources, target, sent = refs[:4], refs[4], refs[5]
+def pack_cores_kernel(place_ref, source, own_ref, other_ref, rows, blocks, arrived, sent):
+    mirrored, y, zl, core = place_ref[0], place_ref[1], place_ref[2], place_ref[3]
+    fetches = [
+        pltpu.make_async_copy(source.at[:, pl.ds(n * 768, 768)], rows.at[n], arrived.at[n])
+        for n in range(4)
+    ]
+    for copy in fetches:
+        copy.start()
+    for n in range(4):
+        fetches[n].wait()
+        turned = rows[n].T
+        for head_zl in range(4):
+            d = zl ^ jnp.where(mirrored == 1, 3 - head_zl, head_zl)
+            for head_core in range(2):
+                first = (2 * head_zl + head_core) * HEAD_DIM
+                blocks[core ^ head_core, y ^ n, d] = turned[first : first + HEAD_DIM]
     copies = [
-        pltpu.make_async_copy(sources[e].at[:, 1 - place_ref[3]], target.at[e], sent.at[e])
-        for e in range(4)
+        pltpu.make_async_copy(blocks.at[n], ref, sent.at[n])
+        for n, ref in enumerate((own_ref, other_ref))
     ]
     for copy in copies:
         copy.start()
@@ -603,13 +638,85 @@
         copy.wait()
 
 
+CORE_SHAPE = (4, 4, HEAD_DIM, CHUNK)
+
+
+def pack_cores(place, array):
+    return pl.pallas_call(
+        pack_cores_kernel,
+        in_specs=[smem(), hbm()],
+        out_specs=[hbm()] * 2,
+        out_shape=[pltpu.HBM(CORE_SHAPE, BF16)] * 2,
+        scratch_shapes=[
+            pltpu.VMEM((4, CHUNK, 768), BF16),
+            pltpu.VMEM((2, *CORE_SHAPE), BF16),
+            pltpu.SemaphoreType.DMA((4,)),
+            pltpu.SemaphoreType.DMA((2,)),
+        ],
+        compiler_params=pltpu.CompilerParams(vmem_limit_bytes=40 * MIB),
+        cost_estimate=cost(1),
+        name="pack_cores",
+    )(place, *in_hbm(array))
+
+
+def both_cores_kernel(place_ref, own_ref, other_ref, *refs):
+    targets, (buffer, fetched, sent) = refs[:4], refs[4:]
+    core = place_ref[3]
+    fetches = []
+    for e in range(4):
+        for n, (ref, side) in enumerate(((own_ref, core), (other_ref, 1 - core))):
+            fetches.append(
+                pltpu.make_async_copy(ref.at[e], buffer.at[e, :, side], fetched.at[n, e])
+            )
+    move(fetches)
+    move([pltpu.make_async_copy(buffer.at[e], targets[e], sent.at[e]) for e in range(4)])
+
+
+def both_cores(place, own, other):
+    return pl.pallas_call(
+        both_cores_kernel,
+        in_specs=[smem()] + [pl.BlockSpec(memory_space=pl.ANY)] * 2,
+        out_specs=[hbm()] * 4,
+        out_shape=PARTS,
+        scratch_shapes=[
+            pltpu.VMEM((4, 4, 2, HEAD_DIM, CHUNK), BF16),
+            pltpu.SemaphoreType.DMA((2, 4)),
+            pltpu.SemaphoreType.DMA((4,)),
+        ],
+        compiler_params=pltpu.CompilerParams(vmem_limit_bytes=40 * MIB),
+        cost_estimate=cost(1),
+        name="both_cores",
+    )(place, own, other)
+
+
+def to_parts(place, array):
+    own, other = pack_cores(place, array)
+    other = lax.ppermute(other, "c", [(0, 1), (1, 0)])
+    return turn(place, by_distance(both_cores(place, own, other), "y"), back=True)
+
+
+def other_core_kernel(place_ref, *refs):
+    sources, (target, buffer, fetched, sent) = refs[:4], refs[4:]
+    move(
+        [
+            pltpu.make_async_copy(sources[e].at[:, 1 - place_ref[3]], buffer.at[e], fetched.at[e])
+            for e in range(4)
+        ]
+    )
+    move([pltpu.make_async_copy(buffer, target, sent)])
+
+
 def other_core(place, parts):
     return pl.pallas_call(
         other_core_kernel,
         in_specs=[smem()] + [pl.BlockSpec(memory_space=pl.ANY)] * 4,
         out_specs=hbm(),
         out_shape=pltpu.HBM((4, 4, HEAD_DIM, CHUNK), BF16),
-        scratch_shapes=[pltpu.SemaphoreType.DMA((4,))],
+        scratch_shapes=[
+            pltpu.VMEM((4, 4, HEAD_DIM, CHUNK), BF16),
+            pltpu.SemaphoreType.DMA((4,)),
+            pltpu.SemaphoreType.DMA(()),
+        ],
         compiler_params=pltpu.CompilerParams(vmem_limit_bytes=40 * MIB),
         cost_estimate=cost(1),
         name="other_core",
@@ -659,7 +766,6 @@
 
 
 def to_rows(place, parts):
-    parts = by_distance(turn(place, 1, parts), "y")
     other = lax.ppermute(other_core(place, parts), "c", [(0, 1), (1, 0)])
     return rows_of(place, parts, other)
 
@@ -668,15 +774,16 @@
     pass
 
 
-def after(array, *others):
+def after(arrays, others):
+    count = len(arrays)
     return pl.pallas_call(
         gate_kernel,
-        in_specs=[hbm()] + [pl.BlockSpec(memory_space=pl.ANY)] * len(others),
-        out_specs=hbm(),
-        out_shape=pltpu.HBM(array.shape, array.dtype),
-        input_output_aliases={0: 0},
+        in_specs=[hbm()] * count + [pl.BlockSpec(memory_space=pl.ANY)] * len(others),
+        out_specs=[hbm()] * count,
+        out_shape=[pltpu.HBM(array.shape, array.dtype) for array in arrays],
+        input_output_aliases={n: n for n in range(count)},
         name="after",
-    )(array, *others)
+    )(*arrays, *others)
 
 
 def group_pairs():
@@ -728,18 +835,22 @@
     pairs = group_pairs()
     last = kvq[CHUNKS - HALO :, :2]
     halo = lax.ppermute(last, AXES, pairs)
-    g = to_heads(after(pack(mirror, cotangent), last))
-    out, stat = late_forward(tile_start, codes, kvq)
-    out, early_stat = early_forward(tile_start, codes, kvq, halo, out)
-    back, carry, early_q = early_backward(tile_start, codes, kvq, halo, g, out, early_stat)
-    grads, rest, *grad_q_parts = late_backward(
-        place, tile_start, codes, kvq, g, out, stat, carry, early_q
+    g = by_distance(after(to_parts(place, cotangent), [last]), "zl")
+    *out, stat = late_forward(place, tile_start, codes, kvq)
+    *out, early_stat = early_forward(place, tile_start, codes, kvq, halo, out)
+    back, carry, early_q = early_backward(
+        place, tile_start, codes, kvq, halo, early_stat, g, out
     )
-    grad_q_parts = by_distance(grad_q_parts, "zl")
-    grad_q = to_rows(place, grad_q_parts)
+    grads, rest, *grad_q = late_backward(
+        place, tile_start, codes, kvq, stat, g, out, carry, early_q
+    )
+    out = by_distance(out, "zl")
+    grad_q = by_distance(after(grad_q, out[1:]), "zl")
+    out = by_distance(turn(place, out), "y")
     back = lax.ppermute(back, AXES, [(b, a) for a, b in pairs])
-    grads = after(join(back, rest, grads), *grad_q_parts[1:])
-    (attended,) = unpack(mirror, to_heads(out))
+    (grads,) = after([join(back, rest, grads)], grad_q[1:] + out[1:])
+    attended = to_rows(place, out)
+    grad_q = to_rows(place, by_distance(turn(place, grad_q), "y"))
     grad_k, grad_v = unpack(mirror, to_heads(grads))
     return attended, grad_q, grad_k, grad_v
 

time: 197 us -> 191 us (0.970)
  waiting for transfers between devices: 101 us -> 73.9 us
  Pallas kernels: 44.5 us -> 56.9 us
  starting transfers between devices: 43.9 us -> 49.9 us
    all_to_all x4 -> x2, waiting for transfers between devices: 65.4 us -> 29.4 us  [to_heads(): lax.all_to_all(array, GROUP_AXES, split_axis=0, concat_axis=0, tiled=True)]
    ppermute x6 -> x18, starting transfers between devices: 9.26 us -> 28 us  [by_distance(): lax.ppermute(parts[d], axis, [(i, i ^ d) for i in range(4)])]
    all_to_all x4 -> x2, starting transfers between devices: 26.5 us -> 14.2 us  [to_heads(): lax.all_to_all(array, GROUP_AXES, split_axis=0, concat_axis=0, tiled=True)]
    pallas_call x6 -> x11, Pallas kernels: 20.2 us -> 32.3 us  [the longest x1 8.94 us: late_forward(): pl.pallas_call(late_forward_kernel, in_specs=[smem(), smem(), vmem(), vme...]
    ppermute x6 -> x18, waiting for transfers between devices: 33 us -> 38.3 us  [by_distance(): lax.ppermute(parts[d], axis, [(i, i ^ d) for i in range(4)])]
    ppermute x1, waiting for transfers between devices: 1.5 us -> 4.11 us  [shards(): halo = lax.ppermute(last, AXES, pairs)]
    pallas_call x2 -> x1, Pallas kernels: 5.26 us -> 3.16 us  [pack(): pl.pallas_call(pack_kernel, in_specs=[smem()] + [hbm()] * count, out_spec...]
    unnamed x22 -> x44, local copies, waits for them, and re-layouts: 3.3 us -> 4.34 us
  transfers between devices with their start and end apart: 13 -> 25, of which waited for: 10 -> 12; matrix products, arithmetic and copies ran while one was open for 1% -> 1% of each run, Pallas kernels for 20% -> 28%
where the time goes in v6:
time: 191 us; the launch traced here: 188 us
  waiting for transfers between devices  73.9 us (39%)
  Pallas kernels  56.9 us (30%)
  starting transfers between devices  49.9 us (26%)
  local copies, waits for them, and re-layouts  5.22 us (3%)
    ppermute x18, waiting for transfers between devices, by_distance(): lax.ppermute(parts[d], axis, [(i, i ^ d) for i in range(4)])  38.3 us
    all_to_all x2, waiting for transfers between devices, to_heads(): lax.all_to_all(array, GROUP_AXES, split_axis=0, concat_axis=0, tiled=True)  29.4 us
    ppermute x18, starting transfers between devices, by_distance(): lax.ppermute(parts[d], axis, [(i, i ^ d) for i in range(4)])  28 us
    all_to_all x2, starting transfers between devices, to_heads(): lax.all_to_all(array, GROUP_AXES, split_axis=0, concat_axis=0, tiled=True)  14.2 us
    pallas_call x1, Pallas kernels, late_backward(): pl.pallas_call(late_backward_kernel, in_specs=[smem(), smem(), vmem(), vm...  11.7 us
    pallas_call x1, Pallas kernels, late_forward(): pl.pallas_call(late_forward_kernel, in_specs=[smem(), smem(), vmem(), vme...  8.94 us
    pallas_call x3, Pallas kernels, turn(): pl.pallas_call(functools.partial(turn_kernel, back), in_specs=[smem()] +...  8.19 us
    pallas_call x1, Pallas kernels, early_backward(): pl.pallas_call(early_backward_kernel, grid=(1,), in_specs=[smem(), smem()...  6.02 us
  transfers between devices with their start and end apart: 25, of which 12 were waited for; matrix products, arithmetic and copies ran while one was open for 1% of the time, Pallas kernels for 28%

profile of v6, /device:TPU:4, one launch (start us, length us, event | category | flops | bytes accessed | tf_op | source)
XLA Modules:
  0.0 188.4 jit_solution(15018868156862817200)
XLA Ops:
  0.6 3.2 %pack.1 = bf16[32,3,96,128]{3,2,1,0:T(8,128)(2,1)} custom-call(s32[1]{0:T(128)} %bitcast.mirror_ref, bf16[128,3072]{1,0:T(8,128)(2,1)} %refs_0_.1, bf16[128,3072]{1,0:T(8,128)(2,1)} %refs_1_.1, bf16[128,3072]{1,0:T(8,128)(2,1)} %refs_2_.1), custom_call_target="tpu_custom_call" | custom-call | tf_op jit(solution)/shard_map/pack/pallas_call | solution.py:89
  3.8 8.9 %all-to-all-start = ((bf16[32,3,96,128]{3,2,1,0:T(8,128)(2,1)}), bf16[32,3,96,128]{3,2,1,0:T(8,128)(2,1)S(1)}, u32[]{:S(2)}, u32[]{:S(2)}) async-start(bf16[32,3,96,128]{3,2,1,0:T(8,128)(2,1)} %pack.1), calls=%async_computation | async-start | bytes 4718592 | tf_op jit(solution)/shard_map/all_to_all | solution.py:808
  12.8 0.7 dynamic_slice.7
  13.5 0.8 dynamic-slice_select_fusion
  15.1 2.8 %pack_cores.1 = (bf16[4,4,96,128]{3,2,1,0:T(8,128)(2,1)}, bf16[4,4,96,128]{3,2,1,0:T(8,128)(2,1)}) custom-call(s32[4]{0:T(128)S(1)} %pad_add_fusion.1.place_ref, bf16[128,3072]{1,0:T(8,128)(2,1)} %source), custom_call_target="tpu_custom_call" | custom-call | flops 1100000000 | tf_op jit(solution)/shard_map/pack_cores/pallas_call | solution.py:645
  18.3 1.7 collective-permute-done.8.other_ref
  19.9 1.0 copy-done.16
  20.9 1.8 both_cores.1
  22.7 3.4 %collective-permute-start.10 = (bf16[4,2,96,128]{3,2,1,0:T(8,128)(2,1)}, bf16[4,2,96,128]{3,2,1,0:T(8,128)(2,1)S(1)}, u32[]{:S(2)}, u32[]{:S(2)}) collective-permute-start(bf16[4,2,96,128]{3,2,1,0:T(8,128)(2,1)} %get-tuple-element.76), channel_id=1, source_target_pairs={{0,16},{8,24},{16,0},{24,8},{1,17},{9,25},{17,1},{25,9},{2,18},{10... | collective-permute-start | bytes 589832 | tf_op jit(solution)/shard_map/ppermute | solution.py:728
  26.1 1.2 collective-permute-start.11
  27.3 11.1 %collective-permute-done.10.refs_2_ = bf16[4,2,96,128]{3,2,1,0:T(8,128)(2,1)S(1)} collective-permute-done((bf16[4,2,96,128]{3,2,1,0:T(8,128)(2,1)}, bf16[4,2,96,128]{3,2,1,0:T(8,128)(2,1)S(1)}, u32[]{:S(2)}, u32[]{:S(2)}) %collective-permute-start.10) | collective-permute-done | bytes 196640 | tf_op jit(solution)/shard_map/ppermute | solution.py:728
  38.4 4.5 %collective-permute-done.11.refs_3_ = bf16[4,2,96,128]{3,2,1,0:T(8,128)(2,1)S(1)} collective-permute-done((bf16[4,2,96,128]{3,2,1,0:T(8,128)(2,1)}, bf16[4,2,96,128]{3,2,1,0:T(8,128)(2,1)S(1)}, u32[]{:S(2)}, u32[]{:S(2)}) %collective-permute-start.11) | collective-permute-done | bytes 196640 | tf_op jit(solution)/shard_map/ppermute | solution.py:728
  43.0 0.9 copy-done.17
  43.9 2.6 %turn.4 = (bf16[4,2,96,128]{3,2,1,0:T(8,128)(2,1)}, bf16[4,2,96,128]{3,2,1,0:T(8,128)(2,1)}, bf16[4,2,96,128]{3,2,1,0:T(8,128)(2,1)}, bf16[4,2,96,128]{3,2,1,0:T(8,128)(2,1)}) custom-call(s32[4]{0:T(128)S(1)} %pad_add_fusion.1.place_ref, bf16[4,2,96,128]{3,2,1,0:T(8,128)(2,1)S(1)} %copy-done.17, bf16[4,2,96,128]{3,2,1,0:T(8,128)(2,1)S(1)} %collective-permute-done.9.refs_1_, ...), custom_call_target="tpu_custom_call" | custom-call | flops 1100000000 | tf_op jit(solution)/shard_map/turn/pallas_call | solution.py:599
  46.5 22.3 %all-to-all-done.kvq_ref = bf16[32,3,96,128]{3,2,1,0:T(8,128)(2,1)S(1)} async-done(((bf16[32,3,96,128]{3,2,1,0:T(8,128)(2,1)}), bf16[32,3,96,128]{3,2,1,0:T(8,128)(2,1)S(1)}, u32[]{:S(2)}, u32[]{:S(2)}) %all-to-all-start) | async-done | bytes 2359328 | tf_op jit(solution)/shard_map/all_to_all | solution.py:808
  68.9 2.7 %collective-permute-start = (bf16[8,2,96,128]{3,2,1,0:T(8,128)(2,1)S(1)}, bf16[8,2,96,128]{3,2,1,0:T(8,128)(2,1)S(1)}, u32[]{:S(2)}, u32[]{:S(2)}) collective-permute-start(bf16[8,2,96,128]{3,2,1,0:T(8,128)(2,1)S(1)} %slice.14.__4_), channel_id=1, source_target_pairs={{0,38},{1,39},{2,36},{3,37},{4,34},{5,35},{6,32},{7,33},{8,46},{9,... | collective-permute-start | bytes 1179656 | tf_op jit(solution)/shard_map/ppermute | solution.py:837
  71.6 0.9 collective-permute-start.12
  72.4 4.1 %collective-permute-start.13 = (bf16[4,2,96,128]{3,2,1,0:T(8,128)(2,1)}, bf16[4,2,96,128]{3,2,1,0:T(8,128)(2,1)S(1)}, u32[]{:S(2)}, u32[]{:S(2)}) collective-permute-start(bf16[4,2,96,128]{3,2,1,0:T(8,128)(2,1)} %get-tuple-element.84), channel_id=1, source_target_pairs={{0,4},{2,6},{4,0},{6,2},{1,5},{3,7},{5,1},{7,3},{8,12},{10,14},{12... | collective-permute-start | bytes 589832 | tf_op jit(solution)/shard_map/ppermute | solution.py:728
  76.5 8.9 %late_forward.1 = (bf16[4,2,96,128]{3,2,1,0:T(8,128)(2,1)}, bf16[4,2,96,128]{3,2,1,0:T(8,128)(2,1)}, bf16[4,2,96,128]{3,2,1,0:T(8,128)(2,1)}, bf16[4,2,96,128]{3,2,1,0:T(8,128)(2,1)}, f32[16,1,256]{2,1,0:T(1,128)S(1)}) custom-call(s32[4]{0:T(128)S(1)} %pad_add_fusion.1.place_ref, s32[16]{0:T(128)S(1)} %and_select_fusion.2.tile_start_ref, ...), custom_call_target="tpu_custom_call" | custom-call | flops 32999999488 | tf_op jit(solution)/shard_map/late_forward/pallas_call | solution.py:289
  85.5 4.1 %collective-permute-done.halo_ref = bf16[8,2,96,128]{3,2,1,0:T(8,128)(2,1)S(1)} collective-permute-done((bf16[8,2,96,128]{3,2,1,0:T(8,128)(2,1)S(1)}, bf16[8,2,96,128]{3,2,1,0:T(8,128)(2,1)S(1)}, u32[]{:S(2)}, u32[]{:S(2)}) %collective-permute-start) | collective-permute-done | bytes 393248 | tf_op jit(solution)/shard_map/ppermute | solution.py:837
  89.6 4.5 %early_forward.1 = (bf16[4,2,96,128]{3,2,1,0:T(8,128)(2,1)}, bf16[4,2,96,128]{3,2,1,0:T(8,128)(2,1)}, bf16[4,2,96,128]{3,2,1,0:T(8,128)(2,1)}, bf16[4,2,96,128]{3,2,1,0:T(8,128)(2,1)}, f32[4,1,256]{2,1,0:T(1,128)S(1)}) custom-call(s32[4]{0:T(128)S(1)} %pad_add_fusion.1.place_ref, ...), custom_call_target="tpu_custom_call", output_to_operand_aliasing={{0}: (6, {}), {1}: (7, {}), {2}: (8, {}), {3}: (9, {})} | custom-call | flops 1100000000 | tf_op jit(solution)/shard_map/early_forward/pallas_call | solution.py:477
  94.2 3.6 %collective-permute-start.2 = (bf16[4,2,96,128]{3,2,1,0:T(8,128)(2,1)}, bf16[4,2,96,128]{3,2,1,0:T(8,128)(2,1)}, u32[]{:S(2)}, u32[]{:S(2)}) collective-permute-start(bf16[4,2,96,128]{3,2,1,0:T(8,128)(2,1)} %get-tuple-element.64.out_2), channel_id=1, source_target_pairs={{0,4},{2,6},{4,0},{6,2},{1,5},{3,7},{5,1},{7,3},{8,12},{10,14},{12... | collective-permute-start | bytes 589832 | tf_op jit(solution)/shard_map/ppermute | solution.py:728
  97.8 0.8 collective-permute-start.3
  99.3 6.0 %early_backward.1 = (bf16[8,2,96,128]{3,2,1,0:T(8,128)(2,1)}, f32[2,96,1024]{2,1,0:T(8,128)}, bf16[8,96,128]{2,1,0:T(8,128)(2,1)}) custom-call(s32[4]{0:T(128)S(1)} %pad_add_fusion.1.place_ref, s32[16]{0:T(128)S(1)} %and_select_fusion.2.tile_start_ref, bf16[16,5120]{1,0:T(8,128)(2,1)S(1)} %select_convert_fusion.key_code_ref, ...), custom_call_target="tpu_custom_call" | custom-call | flops 1100000000 | tf_op jit(solution)/shard_map/early_backward/pallas_call | solution.py:492
  105.3 4.4 %collective-permute-start.22 = (bf16[8,2,96,128]{3,2,1,0:T(8,128)(2,1)}, bf16[8,2,96,128]{3,2,1,0:T(8,128)(2,1)}, u32[]{:S(2)}, u32[]{:S(2)}) collective-permute-start(bf16[8,2,96,128]{3,2,1,0:T(8,128)(2,1)} %get-tuple-element.101), channel_id=1, source_target_pairs={{38,0},{39,1},{36,2},{37,3},{34,4},{35,5},{32,6},{33,7},{46,8},{47... | collective-permute-start | bytes 1179656 | tf_op jit(solution)/shard_map/ppermute | solution.py:850
  109.8 11.7 %late_backward.1 = (bf16[32,2,96,128]{3,2,1,0:T(8,128)(2,1)}, f32[2,96,1024]{2,1,0:T(8,128)S(1)}, bf16[4,2,96,128]{3,2,1,0:T(8,128)(2,1)}, bf16[4,2,96,128]{3,2,...) custom-call(s32[4]{0:T(128)S(1)} %pad_add_fusion.1.place_ref, ...), custom_call_target="tpu_custom_call" | custom-call | flops 11000000512 | tf_op jit(solution)/shard_map/late_backward/pallas_call | solution.py:519
  121.9 1.1 collective-permute-start.16
  123.0 3.0 %collective-permute-start.17 = (bf16[4,2,96,128]{3,2,1,0:T(8,128)(2,1)}, bf16[4,2,96,128]{3,2,1,0:T(8,128)(2,1)S(1)}, u32[]{:S(2)}, u32[]{:S(2)}) collective-permute-start(bf16[4,2,96,128]{3,2,1,0:T(8,128)(2,1)} %get-tuple-element.96), channel_id=1, source_target_pairs={{0,6},{2,4},{4,2},{6,0},{1,7},{3,5},{5,3},{7,1},{8,14},{10,12},{12... | collective-permute-start | bytes 589832 | tf_op jit(solution)/shard_map/ppermute | solution.py:728
  126.0 0.9 copy-done.12
  126.9 2.9 %turn.3 = (bf16[4,2,96,128]{3,2,1,0:T(8,128)(2,1)}, bf16[4,2,96,128]{3,2,1,0:T(8,128)(2,1)}, bf16[4,2,96,128]{3,2,1,0:T(8,128)(2,1)}, bf16[4,2,96,128]{3,2,1,0:T(8,128)(2,1)}) custom-call(s32[4]{0:T(128)S(1)} %pad_add_fusion.1.place_ref, bf16[4,2,96,128]{3,2,1,0:T(8,128)(2,1)S(1)} %copy-done.12, bf16[4,2,96,128]{3,2,1,0:T(8,128)(2,1)} %collective-permute-done.1.refs_1_.__4_, ...), custom_call_target="tpu_custom_call" | custom-call | flops 1100000000 | tf_op jit(solution)/shard_map/turn/pallas_call | solution.py:599
  129.8 0.9 collective-permute-start.4
  130.7 2.0 %collective-permute-start.5 = (bf16[4,2,96,128]{3,2,1,0:T(8,128)(2,1)}, bf16[4,2,96,128]{3,2,1,0:T(8,128)(2,1)S(1)}, u32[]{:S(2)}, u32[]{:S(2)}) collective-permute-start(bf16[4,2,96,128]{3,2,1,0:T(8,128)(2,1)} %get-tuple-element.68), channel_id=1, source_target_pairs={{0,16},{8,24},{16,0},{24,8},{1,17},{9,25},{17,1},{25,9},{2,18},{10... | collective-permute-start | bytes 589832 | tf_op jit(solution)/shard_map/ppermute | solution.py:728
  132.7 1.9 collective-permute-start.6
  134.6 1.9 join.1.__0_
  136.5 2.3 %collective-permute-done.16.refs_2_.__2_ = bf16[4,2,96,128]{3,2,1,0:T(8,128)(2,1)S(1)} collective-permute-done((bf16[4,2,96,128]{3,2,1,0:T(8,128)(2,1)}, bf16[4,2,96,128]{3,2,1,0:T(8,128)(2,1)S(1)}, u32[]{:S(2)}, u32[]{:S(2)}) %collective-permute-start.16) | collective-permute-done | bytes 196640 | tf_op jit(solution)/shard_map/ppermute | solution.py:728
  139.5 2.0 %collective-permute-done.6.refs_3_.part_3.__6_ = bf16[4,2,96,128]{3,2,1,0:T(8,128)(2,1)S(1)} collective-permute-done((bf16[4,2,96,128]{3,2,1,0:T(8,128)(2,1)}, bf16[4,2,96,128]{3,2,1,0:T(8,128)(2,1)S(1)}, u32[]{:S(2)}, u32[]{:S(2)}) %collective-permute-start.6) | collective-permute-done | bytes 196640 | tf_op jit(solution)/shard_map/ppermute | solution.py:728
  142.2 5.3 %all-to-all-start.1 = ((bf16[32,2,96,128]{3,2,1,0:T(8,128)(2,1)}), bf16[32,2,96,128]{3,2,1,0:T(8,128)(2,1)S(1)}, u32[]{:S(2)}, u32[]{:S(2)}) async-start(bf16[32,2,96,128]{3,2,1,0:T(8,128)(2,1)} %after.5), calls=%async_computation.1 | async-start | bytes 3145728 | tf_op jit(solution)/shard_map/all_to_all | solution.py:808
  147.6 2.6 %turn.5 = (bf16[4,2,96,128]{3,2,1,0:T(8,128)(2,1)}, bf16[4,2,96,128]{3,2,1,0:T(8,128)(2,1)}, bf16[4,2,96,128]{3,2,1,0:T(8,128)(2,1)}, bf16[4,2,96,128]{3,2,1,0:T(8,128)(2,1)}) custom-call(s32[4]{0:T(128)S(1)} %pad_add_fusion.1.place_ref, bf16[4,2,96,128]{3,2,1,0:T(8,128)(2,1)S(1)} %copy-done.13, bf16[4,2,96,128]{3,2,1,0:T(8,128)(2,1)S(1)} %copy-done.7, ...), custom_call_target="tpu_custom_call" | custom-call | flops 1100000000 | tf_op jit(solution)/shard_map/turn/pallas_call | solution.py:599
  150.3 1.7 collective-permute-start.18
  151.9 2.7 %collective-permute-start.19 = (bf16[4,2,96,128]{3,2,1,0:T(8,128)(2,1)}, bf16[4,2,96,128]{3,2,1,0:T(8,128)(2,1)S(1)}, u32[]{:S(2)}, u32[]{:S(2)}) collective-permute-start(bf16[4,2,96,128]{3,2,1,0:T(8,128)(2,1)} %get-tuple-element.99), channel_id=1, source_target_pairs={{0,16},{8,24},{16,0},{24,8},{1,17},{9,25},{17,1},{25,9},{2,18},{10... | collective-permute-start | bytes 589832 | tf_op jit(solution)/shard_map/ppermute | solution.py:728
  155.1 1.5 other_core.2
  156.7 9.8 %collective-permute-done.18.refs_1_.part_1 = bf16[4,2,96,128]{3,2,1,0:T(8,128)(2,1)S(1)} collective-permute-done((bf16[4,2,96,128]{3,2,1,0:T(8,128)(2,1)}, bf16[4,2,96,128]{3,2,1,0:T(8,128)(2,1)S(1)}, u32[]{:S(2)}, u32[]{:S(2)}) %collective-permute-start.18) | collective-permute-done | bytes 196640 | tf_op jit(solution)/shard_map/ppermute | solution.py:728
  166.5 7.9 %collective-permute-done.19.refs_2_.part_2 = bf16[4,2,96,128]{3,2,1,0:T(8,128)(2,1)S(1)} collective-permute-done((bf16[4,2,96,128]{3,2,1,0:T(8,128)(2,1)}, bf16[4,2,96,128]{3,2,1,0:T(8,128)(2,1)S(1)}, u32[]{:S(2)}, u32[]{:S(2)}) %collective-permute-start.19) | collective-permute-done | bytes 196640 | tf_op jit(solution)/shard_map/ppermute | solution.py:728
  174.3 1.5 other_core.3
  175.9 1.6 rows_of.2
  177.8 1.6 rows_of.3
  179.4 7.2 %all-to-all-done.1.in_ref = bf16[32,2,96,128]{3,2,1,0:T(8,128)(2,1)S(1)} async-done(((bf16[32,2,96,128]{3,2,1,0:T(8,128)(2,1)}), bf16[32,2,96,128]{3,2,1,0:T(8,128)(2,1)S(1)}, u32[]{:S(2)}, u32[]{:S(2)}) %all-to-all-start.1) | async-done | bytes 1572896 | tf_op jit(solution)/shard_map/all_to_all | solution.py:808
  186.6 1.9 unpack.1
  (81 shorter events, 4.7 us)
Async XLA Ops:
  3.8 65.0 %all-to-all-start = ((bf16[32,3,96,128]{3,2,1,0:T(8,128)(2,1)}), bf16[32,3,96,128]{3,2,1,0:T(8,128)(2,1)S(1)}, u32[]{:S(2)}, u32[]{:S(2)}) async-start(bf16[32,3,96,128]{3,2,1,0:T(8,128)(2,1)} %pack.1), calls=%async_computation | async-start | bytes 4718592 | tf_op jit(solution)/shard_map/all_to_all | solution.py:808
  17.9 2.0 %collective-permute-start.8 = (bf16[4,4,96,128]{3,2,1,0:T(8,128)(2,1)}, bf16[4,4,96,128]{3,2,1,0:T(8,128)(2,1)S(1)}, u32[]{:S(2)}, u32[]{:S(2)}) collective-permute-start(bf16[4,4,96,128]{3,2,1,0:T(8,128)(2,1)} %get-tuple-element.73), channel_id=1, source_target_pairs={{0,1},{1,0},{2,3},{3,2},{4,5},{5,4},{6,7},{7,6},{8,9},{9,8},{10,11... | collective-permute-start | bytes 1179656 | tf_op jit(solution)/shard_map/ppermute | solution.py:694
  19.9 1.0 copy-start.16
  22.7 15.7 %collective-permute-start.10 = (bf16[4,2,96,128]{3,2,1,0:T(8,128)(2,1)}, bf16[4,2,96,128]{3,2,1,0:T(8,128)(2,1)S(1)}, u32[]{:S(2)}, u32[]{:S(2)}) collective-permute-start(bf16[4,2,96,128]{3,2,1,0:T(8,128)(2,1)} %get-tuple-element.76), channel_id=1, source_target_pairs={{0,16},{8,24},{16,0},{24,8},{1,17},{9,25},{17,1},{25,9},{2,18},{10... | collective-permute-start | bytes 589832 | tf_op jit(solution)/shard_map/ppermute | solution.py:728
  26.1 16.8 %collective-permute-start.11 = (bf16[4,2,96,128]{3,2,1,0:T(8,128)(2,1)}, bf16[4,2,96,128]{3,2,1,0:T(8,128)(2,1)S(1)}, u32[]{:S(2)}, u32[]{:S(2)}) collective-permute-start(bf16[4,2,96,128]{3,2,1,0:T(8,128)(2,1)} %get-tuple-element.77), channel_id=1, source_target_pairs={{0,24},{8,16},{16,8},{24,0},{1,25},{9,17},{17,9},{25,1},{2,26},{10... | collective-permute-start | bytes 589832 | tf_op jit(solution)/shard_map/ppermute | solution.py:728
  27.3 15.7 %collective-permute-start.9 = (bf16[4,2,96,128]{3,2,1,0:T(8,128)(2,1)}, bf16[4,2,96,128]{3,2,1,0:T(8,128)(2,1)S(1)}, u32[]{:S(2)}, u32[]{:S(2)}) collective-permute-start(bf16[4,2,96,128]{3,2,1,0:T(8,128)(2,1)} %get-tuple-element.75), channel_id=1, source_target_pairs={{0,8},{8,0},{16,24},{24,16},{1,9},{9,1},{17,25},{25,17},{2,10},{10... | collective-permute-start | bytes 589832 | tf_op jit(solution)/shard_map/ppermute | solution.py:728
  42.9 0.9 copy-start.17
  68.9 2.7 %copy-start.18 = (bf16[8,2,96,128]{3,2,1,0:T(8,128)(2,1)}, bf16[8,2,96,128]{3,2,1,0:T(8,128)(2,1)S(1)}, u32[]{:S(2)}) copy-start(bf16[8,2,96,128]{3,2,1,0:T(8,128)(2,1)S(1)} %slice.14.__4_) | copy-start | bytes 1179652
  68.9 20.7 %collective-permute-start = (bf16[8,2,96,128]{3,2,1,0:T(8,128)(2,1)S(1)}, bf16[8,2,96,128]{3,2,1,0:T(8,128)(2,1)S(1)}, u32[]{:S(2)}, u32[]{:S(2)}) collective-permute-start(bf16[8,2,96,128]{3,2,1,0:T(8,128)(2,1)S(1)} %slice.14.__4_), channel_id=1, source_target_pairs={{0,38},{1,39},{2,36},{3,37},{4,34},{5,35},{6,32},{7,33},{8,46},{9,... | collective-permute-start | bytes 1179656 | tf_op jit(solution)/shard_map/ppermute | solution.py:837
  71.6 26.2 %collective-permute-start.12 = (bf16[4,2,96,128]{3,2,1,0:T(8,128)(2,1)}, bf16[4,2,96,128]{3,2,1,0:T(8,128)(2,1)S(1)}, u32[]{:S(2)}, u32[]{:S(2)}) collective-permute-start(bf16[4,2,96,128]{3,2,1,0:T(8,128)(2,1)} %get-tuple-element.83), channel_id=1, source_target_pairs={{0,2},{2,0},{4,6},{6,4},{1,3},{3,1},{5,7},{7,5},{8,10},{10,8},{12,... | collective-permute-start | bytes 589832 | tf_op jit(solution)/shard_map/ppermute | solution.py:728
  72.4 26.1 %collective-permute-start.13 = (bf16[4,2,96,128]{3,2,1,0:T(8,128)(2,1)}, bf16[4,2,96,128]{3,2,1,0:T(8,128)(2,1)S(1)}, u32[]{:S(2)}, u32[]{:S(2)}) collective-permute-start(bf16[4,2,96,128]{3,2,1,0:T(8,128)(2,1)} %get-tuple-element.84), channel_id=1, source_target_pairs={{0,4},{2,6},{4,0},{6,2},{1,5},{3,7},{5,1},{7,3},{8,12},{10,14},{12... | collective-permute-start | bytes 589832 | tf_op jit(solution)/shard_map/ppermute | solution.py:728
  76.5 22.0 %collective-permute-start.14 = (bf16[4,2,96,128]{3,2,1,0:T(8,128)(2,1)}, bf16[4,2,96,128]{3,2,1,0:T(8,128)(2,1)S(1)}, u32[]{:S(2)}, u32[]{:S(2)}) collective-permute-start(bf16[4,2,96,128]{3,2,1,0:T(8,128)(2,1)} %get-tuple-element.85), channel_id=1, source_target_pairs={{0,6},{2,4},{4,2},{6,0},{1,7},{3,5},{5,3},{7,1},{8,14},{10,12},{12... | collective-permute-start | bytes 589832 | tf_op jit(solution)/shard_map/ppermute | solution.py:728
  94.1 27.4 %collective-permute-start.1 = (bf16[4,2,96,128]{3,2,1,0:T(8,128)(2,1)}, bf16[4,2,96,128]{3,2,1,0:T(8,128)(2,1)}, u32[]{:S(2)}, u32[]{:S(2)}) collective-permute-start(bf16[4,2,96,128]{3,2,1,0:T(8,128)(2,1)} %get-tuple-element.63.out_1), channel_id=1, source_target_pairs={{0,2},{2,0},{4,6},{6,4},{1,3},{3,1},{5,7},{7,5},{8,10},{10,8},{12,... | collective-permute-start | bytes 589832 | tf_op jit(solution)/shard_map/ppermute | solution.py:728
  94.2 27.3 %collective-permute-start.2 = (bf16[4,2,96,128]{3,2,1,0:T(8,128)(2,1)}, bf16[4,2,96,128]{3,2,1,0:T(8,128)(2,1)}, u32[]{:S(2)}, u32[]{:S(2)}) collective-permute-start(bf16[4,2,96,128]{3,2,1,0:T(8,128)(2,1)} %get-tuple-element.64.out_2), channel_id=1, source_target_pairs={{0,4},{2,6},{4,0},{6,2},{1,5},{3,7},{5,1},{7,3},{8,12},{10,14},{12... | collective-permute-start | bytes 589832 | tf_op jit(solution)/shard_map/ppermute | solution.py:728
  97.7 0.8 copy-start.19
  97.8 23.7 %collective-permute-start.3 = (bf16[4,2,96,128]{3,2,1,0:T(8,128)(2,1)}, bf16[4,2,96,128]{3,2,1,0:T(8,128)(2,1)}, u32[]{:S(2)}, u32[]{:S(2)}) collective-permute-start(bf16[4,2,96,128]{3,2,1,0:T(8,128)(2,1)} %get-tuple-element.65.out_3), channel_id=1, source_target_pairs={{0,6},{2,4},{4,2},{6,0},{1,7},{3,5},{5,3},{7,1},{8,14},{10,12},{12... | collective-permute-start | bytes 589832 | tf_op jit(solution)/shard_map/ppermute | solution.py:728
  98.5 0.7 copy-start.20
  98.6 0.8 copy-start.21
  105.3 25.4 %collective-permute-start.22 = (bf16[8,2,96,128]{3,2,1,0:T(8,128)(2,1)}, bf16[8,2,96,128]{3,2,1,0:T(8,128)(2,1)}, u32[]{:S(2)}, u32[]{:S(2)}) collective-permute-start(bf16[8,2,96,128]{3,2,1,0:T(8,128)(2,1)} %get-tuple-element.101), channel_id=1, source_target_pairs={{38,0},{39,1},{36,2},{37,3},{34,4},{35,5},{32,6},{33,7},{46,8},{47... | collective-permute-start | bytes 1179656 | tf_op jit(solution)/shard_map/ppermute | solution.py:850
  121.5 11.2 %collective-permute-start.15 = (bf16[4,2,96,128]{3,2,1,0:T(8,128)(2,1)}, bf16[4,2,96,128]{3,2,1,0:T(8,128)(2,1)S(1)}, u32[]{:S(2)}, u32[]{:S(2)}) collective-permute-start(bf16[4,2,96,128]{3,2,1,0:T(8,128)(2,1)} %get-tuple-element.94), channel_id=1, source_target_pairs={{0,2},{2,0},{4,6},{6,4},{1,3},{3,1},{5,7},{7,5},{8,10},{10,8},{12,... | collective-permute-start | bytes 589832 | tf_op jit(solution)/shard_map/ppermute | solution.py:728
  121.9 16.9 %collective-permute-start.16 = (bf16[4,2,96,128]{3,2,1,0:T(8,128)(2,1)}, bf16[4,2,96,128]{3,2,1,0:T(8,128)(2,1)S(1)}, u32[]{:S(2)}, u32[]{:S(2)}) collective-permute-start(bf16[4,2,96,128]{3,2,1,0:T(8,128)(2,1)} %get-tuple-element.95), channel_id=1, source_target_pairs={{0,4},{2,6},{4,0},{6,2},{1,5},{3,7},{5,1},{7,3},{8,12},{10,14},{12... | collective-permute-start | bytes 589832 | tf_op jit(solution)/shard_map/ppermute | solution.py:728
  123.0 15.9 %collective-permute-start.17 = (bf16[4,2,96,128]{3,2,1,0:T(8,128)(2,1)}, bf16[4,2,96,128]{3,2,1,0:T(8,128)(2,1)S(1)}, u32[]{:S(2)}, u32[]{:S(2)}) collective-permute-start(bf16[4,2,96,128]{3,2,1,0:T(8,128)(2,1)} %get-tuple-element.96), channel_id=1, source_target_pairs={{0,6},{2,4},{4,2},{6,0},{1,7},{3,5},{5,3},{7,1},{8,14},{10,12},{12... | collective-permute-start | bytes 589832 | tf_op jit(solution)/shard_map/ppermute | solution.py:728
  126.0 0.9 copy-start.12
  129.8 9.0 %collective-permute-start.4 = (bf16[4,2,96,128]{3,2,1,0:T(8,128)(2,1)}, bf16[4,2,96,128]{3,2,1,0:T(8,128)(2,1)S(1)}, u32[]{:S(2)}, u32[]{:S(2)}) collective-permute-start(bf16[4,2,96,128]{3,2,1,0:T(8,128)(2,1)} %get-tuple-element.67), channel_id=1, source_target_pairs={{0,8},{8,0},{16,24},{24,16},{1,9},{9,1},{17,25},{25,17},{2,10},{10... | collective-permute-start | bytes 589832 | tf_op jit(solution)/shard_map/ppermute | solution.py:728
  130.7 8.8 %collective-permute-start.5 = (bf16[4,2,96,128]{3,2,1,0:T(8,128)(2,1)}, bf16[4,2,96,128]{3,2,1,0:T(8,128)(2,1)S(1)}, u32[]{:S(2)}, u32[]{:S(2)}) collective-permute-start(bf16[4,2,96,128]{3,2,1,0:T(8,128)(2,1)} %get-tuple-element.68), channel_id=1, source_target_pairs={{0,16},{8,24},{16,0},{24,8},{1,17},{9,25},{17,1},{25,9},{2,18},{10... | collective-permute-start | bytes 589832 | tf_op jit(solution)/shard_map/ppermute | solution.py:728
  132.7 3.7 %copy-start.6 = (bf16[4,2,96,128]{3,2,1,0:T(8,128)(2,1)}, bf16[4,2,96,128]{3,2,1,0:T(8,128)(2,1)S(1)}, u32[]{:S(2)}) copy-start(bf16[4,2,96,128]{3,2,1,0:T(8,128)(2,1)S(1)} %collective-permute-done.15.refs_1_.__1_) | copy-start | bytes 589828
  132.7 8.7 %collective-permute-start.6 = (bf16[4,2,96,128]{3,2,1,0:T(8,128)(2,1)}, bf16[4,2,96,128]{3,2,1,0:T(8,128)(2,1)S(1)}, u32[]{:S(2)}, u32[]{:S(2)}) collective-permute-start(bf16[4,2,96,128]{3,2,1,0:T(8,128)(2,1)} %get-tuple-element.69), channel_id=1, source_target_pairs={{0,24},{8,16},{16,8},{24,0},{1,25},{9,17},{17,9},{25,1},{2,26},{10... | collective-permute-start | bytes 589832 | tf_op jit(solution)/shard_map/ppermute | solution.py:728
  138.8 2.7 %copy-start.8 = (bf16[4,2,96,128]{3,2,1,0:T(8,128)(2,1)}, bf16[4,2,96,128]{3,2,1,0:T(8,128)(2,1)S(1)}, u32[]{:S(2)}) copy-start(bf16[4,2,96,128]{3,2,1,0:T(8,128)(2,1)S(1)} %collective-permute-done.16.refs_2_.__2_) | copy-start | bytes 589828
  138.8 2.7 %copy-start.10 = (bf16[4,2,96,128]{3,2,1,0:T(8,128)(2,1)}, bf16[4,2,96,128]{3,2,1,0:T(8,128)(2,1)S(1)}, u32[]{:S(2)}) copy-start(bf16[4,2,96,128]{3,2,1,0:T(8,128)(2,1)S(1)} %collective-permute-done.17.refs_3_.__3_) | copy-start | bytes 589828
  138.8 2.7 %copy-start = (bf16[4,2,96,128]{3,2,1,0:T(8,128)(2,1)}, bf16[4,2,96,128]{3,2,1,0:T(8,128)(2,1)S(1)}, u32[]{:S(2)}) copy-start(bf16[4,2,96,128]{3,2,1,0:T(8,128)(2,1)S(1)} %collective-permute-done.4.refs_1_.part_1.__4_) | copy-start | bytes 589828
  139.5 2.0 %copy-start.2 = (bf16[4,2,96,128]{3,2,1,0:T(8,128)(2,1)}, bf16[4,2,96,128]{3,2,1,0:T(8,128)(2,1)S(1)}, u32[]{:S(2)}) copy-start(bf16[4,2,96,128]{3,2,1,0:T(8,128)(2,1)S(1)} %collective-permute-done.5.refs_2_.part_2.__5_) | copy-start | bytes 589828
  141.5 0.7 copy-start.4
  142.2 5.3 %copy-start.7 = (bf16[4,2,96,128]{3,2,1,0:T(8,128)(2,1)S(1)}, bf16[4,2,96,128]{3,2,1,0:T(8,128)(2,1)}, u32[]{:S(2)}) copy-start(bf16[4,2,96,128]{3,2,1,0:T(8,128)(2,1)} %copy-done.6) | copy-start | bytes 589828
  142.2 5.3 %copy-start.9 = (bf16[4,2,96,128]{3,2,1,0:T(8,128)(2,1)S(1)}, bf16[4,2,96,128]{3,2,1,0:T(8,128)(2,1)}, u32[]{:S(2)}) copy-start(bf16[4,2,96,128]{3,2,1,0:T(8,128)(2,1)} %copy-done.8) | copy-start | bytes 589828
  142.2 5.4 %copy-start.11 = (bf16[4,2,96,128]{3,2,1,0:T(8,128)(2,1)S(1)}, bf16[4,2,96,128]{3,2,1,0:T(8,128)(2,1)}, u32[]{:S(2)}) copy-start(bf16[4,2,96,128]{3,2,1,0:T(8,128)(2,1)} %copy-done.10) | copy-start | bytes 589828
  142.2 5.4 %copy-start.13 = (bf16[4,2,96,128]{3,2,1,0:T(8,128)(2,1)S(1)}, bf16[4,2,96,128]{3,2,1,0:T(8,128)(2,1)}, u32[]{:S(2)}) copy-start(bf16[4,2,96,128]{3,2,1,0:T(8,128)(2,1)} %get-tuple-element.93.refs_0_) | copy-start | bytes 589828
  142.2 44.4 %all-to-all-start.1 = ((bf16[32,2,96,128]{3,2,1,0:T(8,128)(2,1)}), bf16[32,2,96,128]{3,2,1,0:T(8,128)(2,1)S(1)}, u32[]{:S(2)}, u32[]{:S(2)}) async-start(bf16[32,2,96,128]{3,2,1,0:T(8,128)(2,1)} %after.5), calls=%async_computation.1 | async-start | bytes 3145728 | tf_op jit(solution)/shard_map/all_to_all | solution.py:808
  147.6 7.5 %copy-start.1 = (bf16[4,2,96,128]{3,2,1,0:T(8,128)(2,1)S(1)}, bf16[4,2,96,128]{3,2,1,0:T(8,128)(2,1)}, u32[]{:S(2)}) copy-start(bf16[4,2,96,128]{3,2,1,0:T(8,128)(2,1)} %copy-done) | copy-start | bytes 589828
  147.6 7.5 %copy-start.3 = (bf16[4,2,96,128]{3,2,1,0:T(8,128)(2,1)S(1)}, bf16[4,2,96,128]{3,2,1,0:T(8,128)(2,1)}, u32[]{:S(2)}) copy-start(bf16[4,2,96,128]{3,2,1,0:T(8,128)(2,1)} %copy-done.2) | copy-start | bytes 589828
  147.6 7.5 %copy-start.5 = (bf16[4,2,96,128]{3,2,1,0:T(8,128)(2,1)S(1)}, bf16[4,2,96,128]{3,2,1,0:T(8,128)(2,1)}, u32[]{:S(2)}) copy-start(bf16[4,2,96,128]{3,2,1,0:T(8,128)(2,1)} %copy-done.4) | copy-start | bytes 589828
  147.6 7.5 %copy-start.14 = (bf16[4,2,96,128]{3,2,1,0:T(8,128)(2,1)S(1)}, bf16[4,2,96,128]{3,2,1,0:T(8,128)(2,1)}, u32[]{:S(2)}) copy-start(bf16[4,2,96,128]{3,2,1,0:T(8,128)(2,1)} %get-tuple-element.66.refs_0_.part_0) | copy-start | bytes 589828
  150.3 16.2 %collective-permute-start.18 = (bf16[4,2,96,128]{3,2,1,0:T(8,128)(2,1)}, bf16[4,2,96,128]{3,2,1,0:T(8,128)(2,1)S(1)}, u32[]{:S(2)}, u32[]{:S(2)}) collective-permute-start(bf16[4,2,96,128]{3,2,1,0:T(8,128)(2,1)} %get-tuple-element.98), channel_id=1, source_target_pairs={{0,8},{8,0},{16,24},{24,16},{1,9},{9,1},{17,25},{25,17},{2,10},{10... | collective-permute-start | bytes 589832 | tf_op jit(solution)/shard_map/ppermute | solution.py:728
  151.9 22.4 %collective-permute-start.19 = (bf16[4,2,96,128]{3,2,1,0:T(8,128)(2,1)}, bf16[4,2,96,128]{3,2,1,0:T(8,128)(2,1)S(1)}, u32[]{:S(2)}, u32[]{:S(2)}) collective-permute-start(bf16[4,2,96,128]{3,2,1,0:T(8,128)(2,1)} %get-tuple-element.99), channel_id=1, source_target_pairs={{0,16},{8,24},{16,0},{24,8},{1,17},{9,25},{17,1},{25,9},{2,18},{10... | collective-permute-start | bytes 589832 | tf_op jit(solution)/shard_map/ppermute | solution.py:728
  154.7 19.7 %collective-permute-start.20 = (bf16[4,2,96,128]{3,2,1,0:T(8,128)(2,1)}, bf16[4,2,96,128]{3,2,1,0:T(8,128)(2,1)S(1)}, u32[]{:S(2)}, u32[]{:S(2)}) collective-permute-start(bf16[4,2,96,128]{3,2,1,0:T(8,128)(2,1)} %get-tuple-element.100), channel_id=1, source_target_pairs={{0,24},{8,16},{16,8},{24,0},{1,25},{9,17},{17,9},{25,1},{2,26},{10... | collective-permute-start | bytes 589832 | tf_op jit(solution)/shard_map/ppermute | solution.py:728
  155.1 19.3 %copy-start.15 = (bf16[4,2,96,128]{3,2,1,0:T(8,128)(2,1)S(1)}, bf16[4,2,96,128]{3,2,1,0:T(8,128)(2,1)}, u32[]{:S(2)}) copy-start(bf16[4,2,96,128]{3,2,1,0:T(8,128)(2,1)} %get-tuple-element.97.refs_0_.part_0) | copy-start | bytes 589828
  156.6 19.4 %collective-permute-start.7 = (bf16[4,4,96,128]{3,2,1,0:T(8,128)(2,1)}, bf16[4,4,96,128]{3,2,1,0:T(8,128)(2,1)S(1)}, u32[]{:S(2)}, u32[]{:S(2)}) collective-permute-start(bf16[4,4,96,128]{3,2,1,0:T(8,128)(2,1)} %other_core.2), channel_id=1, source_target_pairs={{0,1},{1,0},{2,3},{3,2},{4,5},{5,4},{6,7},{7,6},{8,9},{9,8},{10,11... | collective-permute-start | bytes 1179656 | tf_op jit(solution)/shard_map/ppermute | solution.py:769
  175.8 2.0 %collective-permute-start.21 = (bf16[4,4,96,128]{3,2,1,0:T(8,128)(2,1)}, bf16[4,4,96,128]{3,2,1,0:T(8,128)(2,1)S(1)}, u32[]{:S(2)}, u32[]{:S(2)}) collective-permute-start(bf16[4,4,96,128]{3,2,1,0:T(8,128)(2,1)} %other_core.3), channel_id=1, source_target_pairs={{0,1},{1,0},{2,3},{3,2},{4,5},{5,4},{6,7},{7,6},{8,9},{9,8},{10,11... | collective-permute-start | bytes 1179656 | tf_op jit(solution)/shard_map/ppermute | solution.py:769

commit v7 on v6

--- a/solution.py
+++ b/solution.py
@@ -128,8 +128,8 @@
     )(mirror, array)
 
 
-def tile_of(ref, n, i):
-    return jnp.concatenate([ref[2 * i, n], ref[2 * i + 1, n]], 1)
+def tile_of(ref, i):
+    return jnp.concatenate([ref[2 * i], ref[2 * i + 1]], 1)
 
 
 def nn(a, b):
@@ -193,13 +193,13 @@
 
 
 def forward_tiles(
-    block, tile_start_ref, query_code_ref, kvq_ref, store, stat_ref, key_flat, value_turned
+    block, tile_start_ref, query_code_ref, q_ref, store, stat_ref, key_flat, value_turned
 ):
     def tile(step, _):
         i = block * AHEAD_TILES + step
 
         def body(count):
-            q = jnp.concatenate([tile_of(kvq_ref, 2, i), query_code_ref[i]], 0)
+            q = jnp.concatenate([tile_of(q_ref, i), query_code_ref[i]], 0)
             scores = []
             top = None
             for j in range(count):
@@ -240,20 +240,30 @@
 
 
 def late_forward_kernel(
-    place_ref, tile_start_ref, key_code_ref, query_code_ref, kvq_ref,
-    part_0, part_1, part_2, part_3, stat_ref, key_flat, value_turned, buffer, sent
+    place_ref, tile_start_ref, key_code_ref, query_code_ref, kv_ref, q_0, q_1, q_2, q_3,
+    part_0, part_1, part_2, part_3, stat_ref, key_flat, value_turned, buffer, queries,
+    sent, fetched_q
 ):
     parts = (part_0, part_1, part_2, part_3)
+
+    def fetch(b):
+        return part_copies(place_ref, queries, (q_0, q_1, q_2, q_3), b, fetched_q, True)
+
+    for b in range(1, BLOCKS):
+        for copy in fetch(b):
+            copy.start()
     chunks = range(HALO, HALO + CHUNKS)
-    fill_keys(None, kvq_ref, key_code_ref, chunks, key_flat, None)
-    fill_value_columns(None, kvq_ref, chunks, value_turned)
+    fill_keys(None, kv_ref, key_code_ref, chunks, key_flat, None)
+    fill_value_columns(None, kv_ref, chunks, value_turned)
 
     def store(chunk, value):
         buffer[chunk] = value
 
     def block(b, _):
+        for copy in fetch(b):
+            copy.wait()
         forward_tiles(
-            b, tile_start_ref, query_code_ref, kvq_ref, store, stat_ref, key_flat, value_turned
+            b, tile_start_ref, query_code_ref, queries, store, stat_ref, key_flat, value_turned
         )
         for copy in part_copies(place_ref, buffer, parts, b, sent):
             copy.start()
@@ -281,32 +291,34 @@
         pltpu.VMEM((window, WIDE), BF16),
         pltpu.VMEM((WIDE, window), BF16),
         pltpu.VMEM((chunks, HEAD_DIM, CHUNK), BF16),
+        pltpu.VMEM((chunks, HEAD_DIM, CHUNK), BF16),
+        pltpu.SemaphoreType.DMA((BLOCKS, 4)),
         pltpu.SemaphoreType.DMA((BLOCKS, 4)),
     ]
 
 
-def late_forward(place, tile_start, codes, kvq):
+def late_forward(place, tile_start, codes, kv, q):
     return pl.pallas_call(
         late_forward_kernel,
-        in_specs=[smem(), smem(), vmem(), vmem(), vmem()],
+        in_specs=[smem(), smem(), vmem(), vmem(), vmem()] + [hbm()] * 4,
         out_specs=[hbm()] * 4 + [vmem()],
         out_shape=PARTS + [jax.ShapeDtypeStruct((TILES, 1, TILE), F32)],
         scratch_shapes=forward_scratch(WINDOW, CHUNKS),
         compiler_params=pltpu.CompilerParams(vmem_limit_bytes=40 * MIB),
         cost_estimate=cost(30),
         name="late_forward",
-    )(place, tile_start, *codes, kvq)
+    )(place, tile_start, *codes, kv, *in_hbm(*q))
 
 
 def backward_tiles(
-    low, high, tile_start_ref, query_code_ref, kvq_ref, g_ref, out_ref, stat_ref, store,
+    low, high, tile_start_ref, query_code_ref, q_ref, g_ref, out_ref, stat_ref, store,
     key_flat, key_turned, value_flat, key_sum, value_sum
 ):
     def tile(i, _):
         def body(count):
-            q = tile_of(kvq_ref, 2, i)
-            g = jnp.concatenate([g_ref[2 * i], g_ref[2 * i + 1]], 1)
-            o = jnp.concatenate([out_ref[2 * i], out_ref[2 * i + 1]], 1)
+            q = tile_of(q_ref, i)
+            g = tile_of(g_ref, i)
+            o = tile_of(out_ref, i)
             delta = jnp.sum(o.astype(F32) * g.astype(F32), axis=0, keepdims=True)
             stat = stat_ref[i]
             code = query_code_ref[i].astype(F32)
@@ -333,17 +345,24 @@
 
 
 def early_forward_kernel(
-    place_ref, tile_start_ref, key_code_ref, query_code_ref, kvq_ref, halo_ref, _, __, ___, ____,
-    part_0, part_1, part_2, part_3, stat_ref, key_flat, value_turned, buffer, sent
+    place_ref, tile_start_ref, key_code_ref, query_code_ref, kv_ref, halo_ref,
+    q_0, q_1, q_2, q_3, _, __, ___, ____,
+    part_0, part_1, part_2, part_3, stat_ref, key_flat, value_turned, buffer, queries,
+    sent, fetched_q
 ):
-    fill_keys(halo_ref, kvq_ref, key_code_ref, range(2 * HALO), key_flat, None)
-    fill_value_columns(halo_ref, kvq_ref, range(2 * HALO), value_turned)
+    fetches = part_copies(place_ref, queries, (q_0, q_1, q_2, q_3), 0, fetched_q, True)
+    for copy in fetches:
+        copy.start()
+    fill_keys(halo_ref, kv_ref, key_code_ref, range(2 * HALO), key_flat, None)
+    fill_value_columns(halo_ref, kv_ref, range(2 * HALO), value_turned)
+    for copy in fetches:
+        copy.wait()
 
     def store(chunk, value):
         buffer[chunk] = value
 
     forward_tiles(
-        0, tile_start_ref, query_code_ref, kvq_ref, store, stat_ref, key_flat, value_turned
+        0, tile_start_ref, query_code_ref, queries, store, stat_ref, key_flat, value_turned
     )
     copies = part_copies(place_ref, buffer, (part_0, part_1, part_2, part_3), 0, sent)
     for copy in copies:
@@ -353,18 +372,19 @@
 
 
 def early_backward_kernel(
-    place_ref, tile_start_ref, key_code_ref, query_code_ref, kvq_ref, halo_ref, stat_ref,
-    g_0, g_1, g_2, g_3, out_0, out_1, out_2, out_3,
+    place_ref, tile_start_ref, key_code_ref, query_code_ref, kv_ref, halo_ref, stat_ref,
+    q_0, q_1, q_2, q_3, g_0, g_1, g_2, g_3, out_0, out_1, out_2, out_3,
     back_ref, carry_ref, grad_q_ref,
-    key_flat, key_turned, value_flat, key_sum, value_sum, g_part, out_part, back_part, grad_q_part,
-    sent, fetched_g, fetched_out
+    key_flat, key_turned, value_flat, key_sum, value_sum, q_part, g_part, out_part, back_part,
+    grad_q_part, sent, fetched_q, fetched_g, fetched_out
 ):
-    fetches = part_copies(place_ref, g_part, (g_0, g_1, g_2, g_3), 0, fetched_g, True)
+    fetches = part_copies(place_ref, q_part, (q_0, q_1, q_2, q_3), 0, fetched_q, True)
+    fetches += part_copies(place_ref, g_part, (g_0, g_1, g_2, g_3), 0, fetched_g, True)
     fetches += part_copies(place_ref, out_part, (out_0, out_1, out_2, out_3), 0, fetched_out, True)
     for copy in fetches:
         copy.start()
-    fill_keys(halo_ref, kvq_ref, key_code_ref, range(2 * HALO), key_flat, key_turned)
-    fill_value_rows(halo_ref, kvq_ref, range(2 * HALO), value_flat)
+    fill_keys(halo_ref, kv_ref, key_code_ref, range(2 * HALO), key_flat, key_turned)
+    fill_value_rows(halo_ref, kv_ref, range(2 * HALO), value_flat)
     key_sum[...] = jnp.zeros_like(key_sum)
     value_sum[...] = jnp.zeros_like(value_sum)
     for copy in fetches:
@@ -374,7 +394,7 @@
         grad_q_part[chunk] = value
 
     backward_tiles(
-        0, AHEAD_TILES, tile_start_ref, query_code_ref, kvq_ref, g_part, out_part, stat_ref, store,
+        0, AHEAD_TILES, tile_start_ref, query_code_ref, q_part, g_part, out_part, stat_ref, store,
         key_flat, key_turned, value_flat, key_sum, value_sum
     )
     copies = [pltpu.make_async_copy(grad_q_part, grad_q_ref, sent.at[2])]
@@ -397,15 +417,15 @@
 
 
 def late_backward_kernel(
-    place_ref, tile_start_ref, key_code_ref, query_code_ref, kvq_ref, stat_ref,
-    g_0, g_1, g_2, g_3, out_0, out_1, out_2, out_3, carry_ref, grad_q_ref, grads_ref, rest_ref, part_0, part_1, part_2, part_3,
-    key_flat, key_turned, value_flat, key_sum, value_sum, buffer, queries, g_all,
-    out_all, carry, sent, fetched, parted, fetched_g, fetched_out
+    place_ref, tile_start_ref, key_code_ref, query_code_ref, kv_ref, stat_ref,
+    q_0, q_1, q_2, q_3, g_0, g_1, g_2, g_3, out_0, out_1, out_2, out_3, carry_ref, grad_q_ref, grads_ref, rest_ref, part_0, part_1, part_2, part_3,
+    key_flat, key_turned, value_flat, key_sum, value_sum, buffer, queries, q_all, g_all,
+    out_all, carry, sent, fetched, parted, fetched_q, fetched_g, fetched_out
 ):
     def fetch(b):
         return part_copies(
-            place_ref, g_all, (g_0, g_1, g_2, g_3), b, fetched_g, True
-        ) + part_copies(place_ref, out_all, (out_0, out_1, out_2, out_3), b, fetched_out, True)
+            place_ref, q_all, (q_0, q_1, q_2, q_3), b, fetched_q, True
+        ) + part_copies(place_ref, g_all, (g_0, g_1, g_2, g_3), b, fetched_g, True) + part_copies(place_ref, out_all, (out_0, out_1, out_2, out_3), b, fetched_out, True)
 
     first = (
         pltpu.make_async_copy(carry_ref, carry, fetched.at[0]),
@@ -414,8 +434,8 @@
     for copy in (*fetch(1), *first, *fetch(2), *fetch(3)):
         copy.start()
     chunks = range(HALO, HALO + CHUNKS)
-    fill_keys(None, kvq_ref, key_code_ref, chunks, key_flat, key_turned)
-    fill_value_rows(None, kvq_ref, chunks, value_flat)
+    fill_keys(None, kv_ref, key_code_ref, chunks, key_flat, key_turned)
+    fill_value_rows(None, kv_ref, chunks, value_flat)
     for sums in (key_sum, value_sum):
         sums[:, AHEAD:] = jnp.zeros((HEAD_DIM, GROUP), F32)
 
@@ -430,7 +450,7 @@
             copy.wait()
         backward_tiles(
             b * AHEAD_TILES, (b + 1) * AHEAD_TILES,
-            tile_start_ref, query_code_ref, kvq_ref, g_all, out_all, stat_ref, store,
+            tile_start_ref, query_code_ref, q_all, g_all, out_all, stat_ref, store,
             key_flat, key_turned, value_flat, key_sum, value_sum
         )
 
@@ -473,26 +493,26 @@
     ]
 
 
-def early_forward(place, tile_start, codes, kvq, halo, parts):
+def early_forward(place, tile_start, codes, kv, halo, q, parts):
     return pl.pallas_call(
         early_forward_kernel,
         grid=(1,),
-        in_specs=[smem(), smem(), vmem(), vmem(), part(HALO, 3), vmem()] + [hbm()] * 4,
+        in_specs=[smem(), smem(), vmem(), vmem(), part(HALO, 2), vmem()] + [hbm()] * 8,
         out_specs=[hbm()] * 4 + [vmem()],
         out_shape=PARTS + [jax.ShapeDtypeStruct((AHEAD_TILES, 1, TILE), F32)],
-        input_output_aliases={6 + d: d for d in range(4)},
+        input_output_aliases={10 + d: d for d in range(4)},
         scratch_shapes=forward_scratch(2 * AHEAD, HALO),
         compiler_params=pltpu.CompilerParams(vmem_limit_bytes=40 * MIB),
         cost_estimate=cost(1),
         name="early_forward",
-    )(place, tile_start, *codes, kvq, halo, *in_hbm(*parts))
-
-
-def early_backward(place, tile_start, codes, kvq, halo, stat, g, out):
+    )(place, tile_start, *codes, kv, halo, *in_hbm(*q, *parts))
+
+
+def early_backward(place, tile_start, codes, kv, halo, stat, q, g, out):
     return pl.pallas_call(
         early_backward_kernel,
         grid=(1,),
-        in_specs=[smem(), smem(), vmem(), vmem(), part(HALO, 3), vmem(), vmem()] + [hbm()] * 8,
+        in_specs=[smem(), smem(), vmem(), vmem(), part(HALO, 2), vmem(), vmem()] + [hbm()] * 12,
         out_specs=[hbm()] * 3,
         out_shape=[
             pltpu.HBM((HALO, 2, HEAD_DIM, CHUNK), BF16),
@@ -501,6 +521,7 @@
         ],
         scratch_shapes=sums_scratch(2 * AHEAD)
         + [
+            pltpu.VMEM((HALO, HEAD_DIM, CHUNK), BF16),
             pltpu.VMEM((HALO, HEAD_DIM, CHUNK), BF16),
             pltpu.VMEM((HALO, HEAD_DIM, CHUNK), BF16),
             pltpu.VMEM((HALO, 2, HEAD_DIM, CHUNK), BF16),
@@ -508,17 +529,18 @@
             pltpu.SemaphoreType.DMA((6,)),
             pltpu.SemaphoreType.DMA((1, 4)),
             pltpu.SemaphoreType.DMA((1, 4)),
+            pltpu.SemaphoreType.DMA((1, 4)),
         ],
         compiler_params=pltpu.CompilerParams(vmem_limit_bytes=40 * MIB),
         cost_estimate=cost(1),
         name="early_backward",
-    )(place, tile_start, *codes, kvq, halo, stat, *in_hbm(*g, *out))
-
-
-def late_backward(place, tile_start, codes, kvq, stat, g, out, carry, grad_q):
+    )(place, tile_start, *codes, kv, halo, stat, *in_hbm(*q, *g, *out))
+
+
+def late_backward(place, tile_start, codes, kv, stat, q, g, out, carry, grad_q):
     return pl.pallas_call(
         late_backward_kernel,
-        in_specs=[smem(), smem(), vmem(), vmem(), vmem(), vmem()] + [hbm()] * 10,
+        in_specs=[smem(), smem(), vmem(), vmem(), vmem(), vmem()] + [hbm()] * 14,
         out_specs=[hbm(), vmem()] + [hbm()] * 4,
         out_shape=[
             pltpu.HBM((CHUNKS, 2, HEAD_DIM, CHUNK), BF16),
@@ -531,17 +553,19 @@
             pltpu.VMEM((CHUNKS, HEAD_DIM, CHUNK), BF16),
             pltpu.VMEM((CHUNKS, HEAD_DIM, CHUNK), BF16),
             pltpu.VMEM((CHUNKS, HEAD_DIM, CHUNK), BF16),
+            pltpu.VMEM((CHUNKS, HEAD_DIM, CHUNK), BF16),
             pltpu.VMEM((2, HEAD_DIM, AHEAD), F32),
             pltpu.SemaphoreType.DMA((BLOCKS,)),
             pltpu.SemaphoreType.DMA((2,)),
             pltpu.SemaphoreType.DMA((BLOCKS, 4)),
             pltpu.SemaphoreType.DMA((BLOCKS, 4)),
             pltpu.SemaphoreType.DMA((BLOCKS, 4)),
+            pltpu.SemaphoreType.DMA((BLOCKS, 4)),
         ],
         compiler_params=pltpu.CompilerParams(vmem_limit_bytes=40 * MIB),
         cost_estimate=cost(10),
         name="late_backward",
-    )(place, tile_start, *codes, kvq, stat, *in_hbm(*g, *out, carry, grad_q))
+    )(place, tile_start, *codes, kv, stat, *in_hbm(*q, *g, *out, carry, grad_q))
 
 
 def join_kernel(back_ref, rest_ref, _, out_ref, buffer, moved):
@@ -829,20 +853,23 @@
 def shards(queries, keys, values, cotangent, doc_ids):
     place = jnp.stack([lax.axis_index(axis) for axis in ("zh", "y", "zl", "c")]).astype(jnp.int32)
     mirror = place[:1]
-    kvq = to_heads(pack(mirror, keys, values, queries))
+    kv = to_heads(pack(mirror, keys, values))
     tile_start, codes = places(doc_ids)
-    cotangent, tile_start, codes = lax.optimization_barrier((cotangent, tile_start, codes))
+    queries, cotangent, tile_start, codes = lax.optimization_barrier(
+        (queries, cotangent, tile_start, codes)
+    )
     pairs = group_pairs()
-    last = kvq[CHUNKS - HALO :, :2]
+    last = kv[CHUNKS - HALO :]
     halo = lax.ppermute(last, AXES, pairs)
-    g = by_distance(after(to_parts(place, cotangent), [last]), "zl")
-    *out, stat = late_forward(place, tile_start, codes, kvq)
-    *out, early_stat = early_forward(place, tile_start, codes, kvq, halo, out)
+    q = by_distance(after(to_parts(place, queries), [last]), "zl")
+    g = by_distance(after(to_parts(place, cotangent), q[2:3]), "zl")
+    *out, stat = late_forward(place, tile_start, codes, kv, q)
+    *out, early_stat = early_forward(place, tile_start, codes, kv, halo, q, out)
     back, carry, early_q = early_backward(
-        place, tile_start, codes, kvq, halo, early_stat, g, out
+        place, tile_start, codes, kv, halo, early_stat, q, g, out
     )
     grads, rest, *grad_q = late_backward(
-        place, tile_start, codes, kvq, stat, g, out, carry, early_q
+        place, tile_start, codes, kv, stat, q, g, out, carry, early_q
     )
     out = by_distance(out, "zl")
     grad_q = by_distance(after(grad_q, out[1:]), "zl")

time: 191 us -> 186 us (0.974); the launches traced: 188 us -> 186 us
  waiting for transfers between devices: 73.9 us -> 46.9 us
  starting transfers between devices: 49.9 us -> 63.2 us
  Pallas kernels: 56.9 us -> 67.2 us
    all_to_all x2, waiting for transfers between devices: 29.4 us -> 11.4 us  [to_heads(): lax.all_to_all(array, GROUP_AXES, split_axis=0, concat_axis=0, tiled=True)]
    ppermute x18 -> x24, starting transfers between devices: 28 us -> 39.9 us  [by_distance(): lax.ppermute(parts[d], axis, [(i, i ^ d) for i in range(4)])]
    ppermute x1, waiting for transfers between devices: 4.11 us -> 0.01 us  [shards(): halo = lax.ppermute(last, AXES, pairs)]
    ppermute x18 -> x24, waiting for transfers between devices: 38.3 us -> 35.1 us  [by_distance(): lax.ppermute(parts[d], axis, [(i, i ^ d) for i in range(4)])]
    pallas_call x1 -> x2, Pallas kernels: 2.83 us -> 5.65 us  [pack_cores(): pl.pallas_call(pack_cores_kernel, in_specs=[smem(), hbm()], out_specs=[hb...]
    pallas_call x3 -> x4, Pallas kernels: 8.19 us -> 10.8 us  [turn(): pl.pallas_call(functools.partial(turn_kernel, back), in_specs=[smem()] +...]
    pallas_call x1, Pallas kernels: 8.94 us -> 11 us  [late_forward(): pl.pallas_call(late_forward_kernel, in_specs=[smem(), smem(), vmem(), vme...]
    unnamed x44 -> x56, local copies, waits for them, and re-layouts: 4.34 us -> 4.11 us
  transfers between devices with their start and end apart: 25 -> 32, of which waited for: 12 -> 11; matrix products, arithmetic and copies ran while one was open for 1% -> 2% of each run, Pallas kernels for 28% -> 34%
where the time goes in v7:
time: 186 us
  Pallas kernels  67.2 us (36%)
  starting transfers between devices  63.2 us (34%)
  waiting for transfers between devices  46.9 us (25%)
  local copies, waits for them, and re-layouts  5.74 us (3%)
    ppermute x24, starting transfers between devices, by_distance(): lax.ppermute(parts[d], axis, [(i, i ^ d) for i in range(4)])  39.9 us
    ppermute x24, waiting for transfers between devices, by_distance(): lax.ppermute(parts[d], axis, [(i, i ^ d) for i in range(4)])  35.1 us
    all_to_all x2, starting transfers between devices, to_heads(): lax.all_to_all(array, GROUP_AXES, split_axis=0, concat_axis=0, tiled=True)  14 us
    pallas_call x1, Pallas kernels, late_backward(): pl.pallas_call(late_backward_kernel, in_specs=[smem(), smem(), vmem(), vm...  13.1 us
    all_to_all x2, waiting for transfers between devices, to_heads(): lax.all_to_all(array, GROUP_AXES, split_axis=0, concat_axis=0, tiled=True)  11.4 us
    pallas_call x1, Pallas kernels, late_forward(): pl.pallas_call(late_forward_kernel, in_specs=[smem(), smem(), vmem(), vme...  11 us
    pallas_call x4, Pallas kernels, turn(): pl.pallas_call(functools.partial(turn_kernel, back), in_specs=[smem()] +...  10.8 us
    pallas_call x1, Pallas kernels, early_backward(): pl.pallas_call(early_backward_kernel, grid=(1,), in_specs=[smem(), smem()...  6.28 us
  transfers between devices with their start and end apart: 32, of which 11 were waited for; matrix products, arithmetic and copies ran while one was open for 2% of the time, Pallas kernels for 34%

profile of v7, /device:TPU:4, one launch (start us, length us, event | category | flops | bytes accessed | tf_op | source)
XLA Modules:
  0.0 185.6 jit_solution(4827019140015145379)
XLA Ops:
  0.6 2.6 %pack.1 = bf16[32,2,96,128]{3,2,1,0:T(8,128)(2,1)} custom-call(s32[1]{0:T(128)} %bitcast.mirror_ref, bf16[128,3072]{1,0:T(8,128)(2,1)} %refs_0_.1, bf16[128,3072]{1,0:T(8,128)(2,1)} %refs_1_.1), custom_call_target="tpu_custom_call" | custom-call | tf_op jit(solution)/shard_map/pack/pallas_call | solution.py:89
  3.3 8.9 %all-to-all-start = ((bf16[32,2,96,128]{3,2,1,0:T(8,128)(2,1)}), bf16[32,2,96,128]{3,2,1,0:T(8,128)(2,1)S(1)}, u32[]{:S(2)}, u32[]{:S(2)}) async-start(bf16[32,2,96,128]{3,2,1,0:T(8,128)(2,1)} %pack.1), calls=%async_computation | async-start | bytes 3145728 | tf_op jit(solution)/shard_map/all_to_all | solution.py:832
  14.6 2.8 %pack_cores.2 = (bf16[4,4,96,128]{3,2,1,0:T(8,128)(2,1)}, bf16[4,4,96,128]{3,2,1,0:T(8,128)(2,1)}) custom-call(s32[4]{0:T(128)S(1)} %pad_add_fusion.1.place_ref, bf16[128,3072]{1,0:T(8,128)(2,1)} %source), custom_call_target="tpu_custom_call" | custom-call | flops 1100000000 | tf_op jit(solution)/shard_map/pack_cores/pallas_call | solution.py:669
  17.8 2.8 %pack_cores.3 = (bf16[4,4,96,128]{3,2,1,0:T(8,128)(2,1)}, bf16[4,4,96,128]{3,2,1,0:T(8,128)(2,1)}) custom-call(s32[4]{0:T(128)S(1)} %pad_add_fusion.1.place_ref, bf16[128,3072]{1,0:T(8,128)(2,1)} %source.1), custom_call_target="tpu_custom_call" | custom-call | flops 1100000000 | tf_op jit(solution)/shard_map/pack_cores/pallas_call | solution.py:669
  20.9 1.8 both_cores.2
  22.7 1.9 %collective-permute-start.2 = (bf16[4,2,96,128]{3,2,1,0:T(8,128)(2,1)}, bf16[4,2,96,128]{3,2,1,0:T(8,128)(2,1)S(1)}, u32[]{:S(2)}, u32[]{:S(2)}) collective-permute-start(bf16[4,2,96,128]{3,2,1,0:T(8,128)(2,1)} %get-tuple-element.77), channel_id=1, source_target_pairs={{0,8},{8,0},{16,24},{24,16},{1,9},{9,1},{17,25},{25,17},{2,10},{10... | collective-permute-start | bytes 589832 | tf_op jit(solution)/shard_map/ppermute | solution.py:752
  24.6 2.7 %collective-permute-start.3 = (bf16[4,2,96,128]{3,2,1,0:T(8,128)(2,1)}, bf16[4,2,96,128]{3,2,1,0:T(8,128)(2,1)S(1)}, u32[]{:S(2)}, u32[]{:S(2)}) collective-permute-start(bf16[4,2,96,128]{3,2,1,0:T(8,128)(2,1)} %get-tuple-element.78), channel_id=1, source_target_pairs={{0,16},{8,24},{16,0},{24,8},{1,17},{9,25},{17,1},{25,9},{2,18},{10... | collective-permute-start | bytes 589832 | tf_op jit(solution)/shard_map/ppermute | solution.py:752
  27.5 1.8 both_cores.3
  30.0 3.9 %collective-permute-start.17 = (bf16[4,2,96,128]{3,2,1,0:T(8,128)(2,1)}, bf16[4,2,96,128]{3,2,1,0:T(8,128)(2,1)S(1)}, u32[]{:S(2)}, u32[]{:S(2)}) collective-permute-start(bf16[4,2,96,128]{3,2,1,0:T(8,128)(2,1)} %get-tuple-element.106), channel_id=1, source_target_pairs={{0,16},{8,24},{16,0},{24,8},{1,17},{9,25},{17,1},{25,9},{2,18},{10... | collective-permute-start | bytes 589832 | tf_op jit(solution)/shard_map/ppermute | solution.py:752
  34.7 6.3 %collective-permute-done.3.refs_2_ = bf16[4,2,96,128]{3,2,1,0:T(8,128)(2,1)S(1)} collective-permute-done((bf16[4,2,96,128]{3,2,1,0:T(8,128)(2,1)}, bf16[4,2,96,128]{3,2,1,0:T(8,128)(2,1)S(1)}, u32[]{:S(2)}, u32[]{:S(2)}) %collective-permute-start.3) | collective-permute-done | bytes 196640 | tf_op jit(solution)/shard_map/ppermute | solution.py:752
  41.0 3.7 %collective-permute-done.4.refs_3_ = bf16[4,2,96,128]{3,2,1,0:T(8,128)(2,1)S(1)} collective-permute-done((bf16[4,2,96,128]{3,2,1,0:T(8,128)(2,1)}, bf16[4,2,96,128]{3,2,1,0:T(8,128)(2,1)S(1)}, u32[]{:S(2)}, u32[]{:S(2)}) %collective-permute-start.4) | collective-permute-done | bytes 196640 | tf_op jit(solution)/shard_map/ppermute | solution.py:752
  44.7 2.6 %turn.4 = (bf16[4,2,96,128]{3,2,1,0:T(8,128)(2,1)}, bf16[4,2,96,128]{3,2,1,0:T(8,128)(2,1)}, bf16[4,2,96,128]{3,2,1,0:T(8,128)(2,1)}, bf16[4,2,96,128]{3,2,1,0:T(8,128)(2,1)}) custom-call(s32[4]{0:T(128)S(1)} %pad_add_fusion.1.place_ref, bf16[4,2,96,128]{3,2,1,0:T(8,128)(2,1)S(1)} %copy-done.21, bf16[4,2,96,128]{3,2,1,0:T(8,128)(2,1)S(1)} %collective-permute-done.2.refs_1_, ...), custom_call_target="tpu_custom_call" | custom-call | flops 1100000000 | tf_op jit(solution)/shard_map/turn/pallas_call | solution.py:623
  47.4 4.3 %all-to-all-done.kv_ref = bf16[32,2,96,128]{3,2,1,0:T(8,128)(2,1)S(1)} async-done(((bf16[32,2,96,128]{3,2,1,0:T(8,128)(2,1)}), bf16[32,2,96,128]{3,2,1,0:T(8,128)(2,1)S(1)}, u32[]{:S(2)}, u32[]{:S(2)}) %all-to-all-start) | async-done | bytes 1572896 | tf_op jit(solution)/shard_map/all_to_all | solution.py:832
  51.7 0.8 slice.14.__4_
  52.5 4.4 %collective-permute-start.7 = (bf16[4,2,96,128]{3,2,1,0:T(8,128)(2,1)}, bf16[4,2,96,128]{3,2,1,0:T(8,128)(2,1)}, u32[]{:S(2)}, u32[]{:S(2)}) collective-permute-start(bf16[4,2,96,128]{3,2,1,0:T(8,128)(2,1)} %get-tuple-element.87), channel_id=1, source_target_pairs={{0,6},{2,4},{4,2},{6,0},{1,7},{3,5},{5,3},{7,1},{8,14},{10,12},{12... | collective-permute-start | bytes 589832 | tf_op jit(solution)/shard_map/ppermute | solution.py:752
  56.9 2.7 %turn.6 = (bf16[4,2,96,128]{3,2,1,0:T(8,128)(2,1)}, bf16[4,2,96,128]{3,2,1,0:T(8,128)(2,1)}, bf16[4,2,96,128]{3,2,1,0:T(8,128)(2,1)}, bf16[4,2,96,128]{3,2,1,0:T(8,128)(2,1)}) custom-call(s32[4]{0:T(128)S(1)} %pad_add_fusion.1.place_ref, bf16[4,2,96,128]{3,2,1,0:T(8,128)(2,1)S(1)} %copy-done.20, bf16[4,2,96,128]{3,2,1,0:T(8,128)(2,1)S(1)} %collective-permute-done.16.refs_1_, ...), custom_call_target="tpu_custom_call" | custom-call | flops 1100000000 | tf_op jit(solution)/shard_map/turn/pallas_call | solution.py:623
  59.6 3.2 %collective-permute-start = (bf16[8,2,96,128]{3,2,1,0:T(8,128)(2,1)S(1)}, bf16[8,2,96,128]{3,2,1,0:T(8,128)(2,1)S(1)}, u32[]{:S(2)}, u32[]{:S(2)}) collective-permute-start(bf16[8,2,96,128]{3,2,1,0:T(8,128)(2,1)S(1)} %copy-done.22), channel_id=1, source_target_pairs={{0,38},{1,39},{2,36},{3,37},{4,34},{5,35},{6,32},{7,33},{8,46},{9,... | collective-permute-start | bytes 1179656 | tf_op jit(solution)/shard_map/ppermute | solution.py:863
  62.7 0.8 collective-permute-done.6.q_2.__4_
  64.3 1.1 collective-permute-start.19
  65.3 2.5 %collective-permute-start.20 = (bf16[4,2,96,128]{3,2,1,0:T(8,128)(2,1)}, bf16[4,2,96,128]{3,2,1,0:T(8,128)(2,1)S(1)}, u32[]{:S(2)}, u32[]{:S(2)}) collective-permute-start(bf16[4,2,96,128]{3,2,1,0:T(8,128)(2,1)} %get-tuple-element.114), channel_id=1, source_target_pairs={{0,4},{2,6},{4,0},{6,2},{1,5},{3,7},{5,1},{7,3},{8,12},{10,14},{12... | collective-permute-start | bytes 589832 | tf_op jit(solution)/shard_map/ppermute | solution.py:752
  68.9 11.0 %late_forward.1 = (bf16[4,2,96,128]{3,2,1,0:T(8,128)(2,1)}, bf16[4,2,96,128]{3,2,1,0:T(8,128)(2,1)}, bf16[4,2,96,128]{3,2,1,0:T(8,128)(2,1)}, bf16[4,2,96,128]{3,2,1,0:T(8,128)(2,1)}, f32[16,1,256]{2,1,0:T(1,128)S(1)}) custom-call(s32[4]{0:T(128)S(1)} %pad_add_fusion.1.place_ref, s32[16]{0:T(128)S(1)} %and_select_fusion.2.tile_start_ref, ...), custom_call_target="tpu_custom_call" | custom-call | flops 32999999488 | tf_op jit(solution)/shard_map/late_forward/pallas_call | solution.py:301
  79.9 5.4 %early_forward.1 = (bf16[4,2,96,128]{3,2,1,0:T(8,128)(2,1)}, bf16[4,2,96,128]{3,2,1,0:T(8,128)(2,1)}, bf16[4,2,96,128]{3,2,1,0:T(8,128)(2,1)}, bf16[4,2,96,128]{3,2,1,0:T(8,128)(2,1)}, f32[4,1,256]{2,1,0:T(1,128)S(1)}) custom-call(s32[4]{0:T(128)S(1)} %pad_add_fusion.1.place_ref, ...), custom_call_target="tpu_custom_call", output_to_operand_aliasing={{0}: (10, {}), {1}: (11, {}), {2}: (12, {}), {3}: (13, {})} | custom-call | flops 1100000000 | tf_op jit(solution)/shard_map/early_forward/pallas_call | solution.py:497
  85.3 3.2 %collective-permute-start.10 = (bf16[4,2,96,128]{3,2,1,0:T(8,128)(2,1)}, bf16[4,2,96,128]{3,2,1,0:T(8,128)(2,1)S(1)}, u32[]{:S(2)}, u32[]{:S(2)}) collective-permute-start(bf16[4,2,96,128]{3,2,1,0:T(8,128)(2,1)} %get-tuple-element.95.out_3), channel_id=1, source_target_pairs={{0,6},{2,4},{4,2},{6,0},{1,7},{3,5},{5,3},{7,1},{8,14},{10,12},{12... | collective-permute-start | bytes 589832 | tf_op jit(solution)/shard_map/ppermute | solution.py:752
  88.6 3.0 %collective-permute-start.8 = (bf16[4,2,96,128]{3,2,1,0:T(8,128)(2,1)}, bf16[4,2,96,128]{3,2,1,0:T(8,128)(2,1)}, u32[]{:S(2)}, u32[]{:S(2)}) collective-permute-start(bf16[4,2,96,128]{3,2,1,0:T(8,128)(2,1)} %get-tuple-element.93.out_1), channel_id=1, source_target_pairs={{0,2},{2,0},{4,6},{6,4},{1,3},{3,1},{5,7},{7,5},{8,10},{10,8},{12,... | collective-permute-start | bytes 589832 | tf_op jit(solution)/shard_map/ppermute | solution.py:752
  92.4 6.3 %early_backward.1 = (bf16[8,2,96,128]{3,2,1,0:T(8,128)(2,1)}, f32[2,96,1024]{2,1,0:T(8,128)}, bf16[8,96,128]{2,1,0:T(8,128)(2,1)}) custom-call(s32[4]{0:T(128)S(1)} %pad_add_fusion.1.place_ref, s32[16]{0:T(128)S(1)} %and_select_fusion.2.tile_start_ref, bf16[16,5120]{1,0:T(8,128)(2,1)S(1)} %select_convert_fusion.key_code_ref, ...), custom_call_target="tpu_custom_call" | custom-call | flops 1100000000 | tf_op jit(solution)/shard_map/early_backward/pallas_call | solution.py:512
  98.7 5.3 %collective-permute-start.29 = (bf16[8,2,96,128]{3,2,1,0:T(8,128)(2,1)}, bf16[8,2,96,128]{3,2,1,0:T(8,128)(2,1)S(1)}, u32[]{:S(2)}, u32[]{:S(2)}) collective-permute-start(bf16[8,2,96,128]{3,2,1,0:T(8,128)(2,1)} %get-tuple-element.131), channel_id=1, source_target_pairs={{38,0},{39,1},{36,2},{37,3},{34,4},{35,5},{32,6},{33,7},{46,8},{47... | collective-permute-start | bytes 1179656 | tf_op jit(solution)/shard_map/ppermute | solution.py:877
  104.0 13.1 %late_backward.1 = (bf16[32,2,96,128]{3,2,1,0:T(8,128)(2,1)}, f32[2,96,1024]{2,1,0:T(8,128)S(1)}, bf16[4,2,96,128]{3,2,1,0:T(8,128)(2,1)}, bf16[4,2,96,128]{3,2,...) custom-call(s32[4]{0:T(128)S(1)} %pad_add_fusion.1.place_ref, ...), custom_call_target="tpu_custom_call" | custom-call | flops 11000000512 | tf_op jit(solution)/shard_map/late_backward/pallas_call | solution.py:541
  117.8 3.3 %collective-permute-start.22 = (bf16[4,2,96,128]{3,2,1,0:T(8,128)(2,1)}, bf16[4,2,96,128]{3,2,1,0:T(8,128)(2,1)S(1)}, u32[]{:S(2)}, u32[]{:S(2)}) collective-permute-start(bf16[4,2,96,128]{3,2,1,0:T(8,128)(2,1)} %get-tuple-element.124), channel_id=1, source_target_pairs={{0,2},{2,0},{4,6},{6,4},{1,3},{3,1},{5,7},{7,5},{8,10},{10,8},{12,... | collective-permute-start | bytes 589832 | tf_op jit(solution)/shard_map/ppermute | solution.py:752
  121.1 2.4 %collective-permute-start.24 = (bf16[4,2,96,128]{3,2,1,0:T(8,128)(2,1)}, bf16[4,2,96,128]{3,2,1,0:T(8,128)(2,1)S(1)}, u32[]{:S(2)}, u32[]{:S(2)}) collective-permute-start(bf16[4,2,96,128]{3,2,1,0:T(8,128)(2,1)} %get-tuple-element.126), channel_id=1, source_target_pairs={{0,6},{2,4},{4,2},{6,0},{1,7},{3,5},{5,3},{7,1},{8,14},{10,12},{12... | collective-permute-start | bytes 589832 | tf_op jit(solution)/shard_map/ppermute | solution.py:752
  123.4 0.9 copy-done.14
  124.4 2.8 %turn.5 = (bf16[4,2,96,128]{3,2,1,0:T(8,128)(2,1)}, bf16[4,2,96,128]{3,2,1,0:T(8,128)(2,1)}, bf16[4,2,96,128]{3,2,1,0:T(8,128)(2,1)}, bf16[4,2,96,128]{3,2,1,0:T(8,128)(2,1)}) custom-call(s32[4]{0:T(128)S(1)} %pad_add_fusion.1.place_ref, bf16[4,2,96,128]{3,2,1,0:T(8,128)(2,1)S(1)} %copy-done.12, bf16[4,2,96,128]{3,2,1,0:T(8,128)(2,1)} %collective-permute-done.8.refs_1_.__4_, ...), custom_call_target="tpu_custom_call" | custom-call | flops 1100000000 | tf_op jit(solution)/shard_map/turn/pallas_call | solution.py:623
  127.3 3.3 %collective-permute-start.12 = (bf16[4,2,96,128]{3,2,1,0:T(8,128)(2,1)}, bf16[4,2,96,128]{3,2,1,0:T(8,128)(2,1)S(1)}, u32[]{:S(2)}, u32[]{:S(2)}) collective-permute-start(bf16[4,2,96,128]{3,2,1,0:T(8,128)(2,1)} %get-tuple-element.98), channel_id=1, source_target_pairs={{0,16},{8,24},{16,0},{24,8},{1,17},{9,25},{17,1},{25,9},{2,18},{10... | collective-permute-start | bytes 589832 | tf_op jit(solution)/shard_map/ppermute | solution.py:752
  130.6 1.3 collective-permute-start.13
  132.0 0.8 join.1.__0_
  132.8 4.0 %collective-permute-done.23.refs_2_.__2_ = bf16[4,2,96,128]{3,2,1,0:T(8,128)(2,1)S(1)} collective-permute-done((bf16[4,2,96,128]{3,2,1,0:T(8,128)(2,1)}, bf16[4,2,96,128]{3,2,1,0:T(8,128)(2,1)S(1)}, u32[]{:S(2)}, u32[]{:S(2)}) %collective-permute-start.23) | collective-permute-done | bytes 196640 | tf_op jit(solution)/shard_map/ppermute | solution.py:752
  136.9 1.8 collective-permute-done.13.refs_3_.part_3.__6_
  139.4 5.1 %all-to-all-start.1 = ((bf16[32,2,96,128]{3,2,1,0:T(8,128)(2,1)}), bf16[32,2,96,128]{3,2,1,0:T(8,128)(2,1)S(1)}, u32[]{:S(2)}, u32[]{:S(2)}) async-start(bf16[32,2,96,128]{3,2,1,0:T(8,128)(2,1)} %after.7), calls=%async_computation.1 | async-start | bytes 3145728 | tf_op jit(solution)/shard_map/all_to_all | solution.py:832
  144.6 2.7 %turn.7 = (bf16[4,2,96,128]{3,2,1,0:T(8,128)(2,1)}, bf16[4,2,96,128]{3,2,1,0:T(8,128)(2,1)}, bf16[4,2,96,128]{3,2,1,0:T(8,128)(2,1)}, bf16[4,2,96,128]{3,2,1,0:T(8,128)(2,1)}) custom-call(s32[4]{0:T(128)S(1)} %pad_add_fusion.1.place_ref, bf16[4,2,96,128]{3,2,1,0:T(8,128)(2,1)S(1)} %copy-done.15, bf16[4,2,96,128]{3,2,1,0:T(8,128)(2,1)S(1)} %copy-done.7, ...), custom_call_target="tpu_custom_call" | custom-call | flops 1100000000 | tf_op jit(solution)/shard_map/turn/pallas_call | solution.py:623
  147.2 1.9 %collective-permute-start.25 = (bf16[4,2,96,128]{3,2,1,0:T(8,128)(2,1)}, bf16[4,2,96,128]{3,2,1,0:T(8,128)(2,1)S(1)}, u32[]{:S(2)}, u32[]{:S(2)}) collective-permute-start(bf16[4,2,96,128]{3,2,1,0:T(8,128)(2,1)} %get-tuple-element.128), channel_id=1, source_target_pairs={{0,8},{8,0},{16,24},{24,16},{1,9},{9,1},{17,25},{25,17},{2,10},{10... | collective-permute-start | bytes 589832 | tf_op jit(solution)/shard_map/ppermute | solution.py:752
  149.1 2.7 %collective-permute-start.26 = (bf16[4,2,96,128]{3,2,1,0:T(8,128)(2,1)}, bf16[4,2,96,128]{3,2,1,0:T(8,128)(2,1)S(1)}, u32[]{:S(2)}, u32[]{:S(2)}) collective-permute-start(bf16[4,2,96,128]{3,2,1,0:T(8,128)(2,1)} %get-tuple-element.129), channel_id=1, source_target_pairs={{0,16},{8,24},{16,0},{24,8},{1,17},{9,25},{17,1},{25,9},{2,18},{10... | collective-permute-start | bytes 589832 | tf_op jit(solution)/shard_map/ppermute | solution.py:752
  152.1 1.5 other_core.2
  153.6 10.0 %collective-permute-done.25.refs_1_.part_1 = bf16[4,2,96,128]{3,2,1,0:T(8,128)(2,1)S(1)} collective-permute-done((bf16[4,2,96,128]{3,2,1,0:T(8,128)(2,1)}, bf16[4,2,96,128]{3,2,1,0:T(8,128)(2,1)S(1)}, u32[]{:S(2)}, u32[]{:S(2)}) %collective-permute-start.25) | collective-permute-done | bytes 196640 | tf_op jit(solution)/shard_map/ppermute | solution.py:752
  163.6 7.9 %collective-permute-done.26.refs_2_.part_2 = bf16[4,2,96,128]{3,2,1,0:T(8,128)(2,1)S(1)} collective-permute-done((bf16[4,2,96,128]{3,2,1,0:T(8,128)(2,1)}, bf16[4,2,96,128]{3,2,1,0:T(8,128)(2,1)S(1)}, u32[]{:S(2)}, u32[]{:S(2)}) %collective-permute-start.26) | collective-permute-done | bytes 196640 | tf_op jit(solution)/shard_map/ppermute | solution.py:752
  171.5 1.5 other_core.3
  173.1 1.6 rows_of.2
  175.0 1.6 rows_of.3
  176.6 7.2 %all-to-all-done.1.in_ref = bf16[32,2,96,128]{3,2,1,0:T(8,128)(2,1)S(1)} async-done(((bf16[32,2,96,128]{3,2,1,0:T(8,128)(2,1)}), bf16[32,2,96,128]{3,2,1,0:T(8,128)(2,1)S(1)}, u32[]{:S(2)}, u32[]{:S(2)}) %all-to-all-start.1) | async-done | bytes 1572896 | tf_op jit(solution)/shard_map/all_to_all | solution.py:832
  183.7 1.9 %unpack.1 = (bf16[128,3072]{1,0:T(8,128)(2,1)}, bf16[128,3072]{1,0:T(8,128)(2,1)}) custom-call(s32[1]{0:T(128)} %bitcast.mirror_ref, bf16[32,2,96,128]{3,2,1,0:T(8,128)(2,1)S(1)} %all-to-all-done.1.in_ref), custom_call_target="tpu_custom_call" | custom-call | tf_op jit(solution)/shard_map/unpack/pallas_call | solution.py:117
  (111 shorter events, 9.5 us)
Async XLA Ops:
  3.3 48.4 %all-to-all-start = ((bf16[32,2,96,128]{3,2,1,0:T(8,128)(2,1)}), bf16[32,2,96,128]{3,2,1,0:T(8,128)(2,1)S(1)}, u32[]{:S(2)}, u32[]{:S(2)}) async-start(bf16[32,2,96,128]{3,2,1,0:T(8,128)(2,1)} %pack.1), calls=%async_computation | async-start | bytes 3145728 | tf_op jit(solution)/shard_map/all_to_all | solution.py:832
  17.4 3.5 %copy-start.19 = (bf16[4,4,96,128]{3,2,1,0:T(8,128)(2,1)S(1)}, bf16[4,4,96,128]{3,2,1,0:T(8,128)(2,1)}, u32[]{:S(2)}) copy-start(bf16[4,4,96,128]{3,2,1,0:T(8,128)(2,1)} %get-tuple-element.74.own_ref) | copy-start | bytes 1179652
  17.4 3.5 %collective-permute-start.1 = (bf16[4,4,96,128]{3,2,1,0:T(8,128)(2,1)}, bf16[4,4,96,128]{3,2,1,0:T(8,128)(2,1)S(1)}, u32[]{:S(2)}, u32[]{:S(2)}) collective-permute-start(bf16[4,4,96,128]{3,2,1,0:T(8,128)(2,1)} %get-tuple-element.75), channel_id=1, source_target_pairs={{0,1},{1,0},{2,3},{3,2},{4,5},{5,4},{6,7},{7,6},{8,9},{9,8},{10,11... | collective-permute-start | bytes 1179656 | tf_op jit(solution)/shard_map/ppermute | solution.py:718
  20.6 6.9 %collective-permute-start.15 = (bf16[4,4,96,128]{3,2,1,0:T(8,128)(2,1)}, bf16[4,4,96,128]{3,2,1,0:T(8,128)(2,1)S(1)}, u32[]{:S(2)}, u32[]{:S(2)}) collective-permute-start(bf16[4,4,96,128]{3,2,1,0:T(8,128)(2,1)} %get-tuple-element.103), channel_id=1, source_target_pairs={{0,1},{1,0},{2,3},{3,2},{4,5},{5,4},{6,7},{7,6},{8,9},{9,8},{10,11... | collective-permute-start | bytes 1179656 | tf_op jit(solution)/shard_map/ppermute | solution.py:718
  20.9 6.6 %copy-start.18 = (bf16[4,4,96,128]{3,2,1,0:T(8,128)(2,1)S(1)}, bf16[4,4,96,128]{3,2,1,0:T(8,128)(2,1)}, u32[]{:S(2)}) copy-start(bf16[4,4,96,128]{3,2,1,0:T(8,128)(2,1)} %get-tuple-element.102.own_ref) | copy-start | bytes 1179652
  22.7 11.2 %collective-permute-start.2 = (bf16[4,2,96,128]{3,2,1,0:T(8,128)(2,1)}, bf16[4,2,96,128]{3,2,1,0:T(8,128)(2,1)S(1)}, u32[]{:S(2)}, u32[]{:S(2)}) collective-permute-start(bf16[4,2,96,128]{3,2,1,0:T(8,128)(2,1)} %get-tuple-element.77), channel_id=1, source_target_pairs={{0,8},{8,0},{16,24},{24,16},{1,9},{9,1},{17,25},{25,17},{2,10},{10... | collective-permute-start | bytes 589832 | tf_op jit(solution)/shard_map/ppermute | solution.py:752
  24.6 16.4 %collective-permute-start.3 = (bf16[4,2,96,128]{3,2,1,0:T(8,128)(2,1)}, bf16[4,2,96,128]{3,2,1,0:T(8,128)(2,1)S(1)}, u32[]{:S(2)}, u32[]{:S(2)}) collective-permute-start(bf16[4,2,96,128]{3,2,1,0:T(8,128)(2,1)} %get-tuple-element.78), channel_id=1, source_target_pairs={{0,16},{8,24},{16,0},{24,8},{1,17},{9,25},{17,1},{25,9},{2,18},{10... | collective-permute-start | bytes 589832 | tf_op jit(solution)/shard_map/ppermute | solution.py:752
  27.3 17.4 %collective-permute-start.4 = (bf16[4,2,96,128]{3,2,1,0:T(8,128)(2,1)}, bf16[4,2,96,128]{3,2,1,0:T(8,128)(2,1)S(1)}, u32[]{:S(2)}, u32[]{:S(2)}) collective-permute-start(bf16[4,2,96,128]{3,2,1,0:T(8,128)(2,1)} %get-tuple-element.79), channel_id=1, source_target_pairs={{0,24},{8,16},{16,8},{24,0},{1,25},{9,17},{17,9},{25,1},{2,26},{10... | collective-permute-start | bytes 589832 | tf_op jit(solution)/shard_map/ppermute | solution.py:752
  27.5 17.2 %copy-start.21 = (bf16[4,2,96,128]{3,2,1,0:T(8,128)(2,1)S(1)}, bf16[4,2,96,128]{3,2,1,0:T(8,128)(2,1)}, u32[]{:S(2)}) copy-start(bf16[4,2,96,128]{3,2,1,0:T(8,128)(2,1)} %get-tuple-element.76.refs_0_) | copy-start | bytes 589828
  29.4 23.1 %collective-permute-start.16 = (bf16[4,2,96,128]{3,2,1,0:T(8,128)(2,1)}, bf16[4,2,96,128]{3,2,1,0:T(8,128)(2,1)S(1)}, u32[]{:S(2)}, u32[]{:S(2)}) collective-permute-start(bf16[4,2,96,128]{3,2,1,0:T(8,128)(2,1)} %get-tuple-element.105), channel_id=1, source_target_pairs={{0,8},{8,0},{16,24},{24,16},{1,9},{9,1},{17,25},{25,17},{2,10},{10... | collective-permute-start | bytes 589832 | tf_op jit(solution)/shard_map/ppermute | solution.py:752
  30.0 26.8 %collective-permute-start.17 = (bf16[4,2,96,128]{3,2,1,0:T(8,128)(2,1)}, bf16[4,2,96,128]{3,2,1,0:T(8,128)(2,1)S(1)}, u32[]{:S(2)}, u32[]{:S(2)}) collective-permute-start(bf16[4,2,96,128]{3,2,1,0:T(8,128)(2,1)} %get-tuple-element.106), channel_id=1, source_target_pairs={{0,16},{8,24},{16,0},{24,8},{1,17},{9,25},{17,1},{25,9},{2,18},{10... | collective-permute-start | bytes 589832 | tf_op jit(solution)/shard_map/ppermute | solution.py:752
  34.0 22.9 %collective-permute-start.18 = (bf16[4,2,96,128]{3,2,1,0:T(8,128)(2,1)}, bf16[4,2,96,128]{3,2,1,0:T(8,128)(2,1)S(1)}, u32[]{:S(2)}, u32[]{:S(2)}) collective-permute-start(bf16[4,2,96,128]{3,2,1,0:T(8,128)(2,1)} %get-tuple-element.107), channel_id=1, source_target_pairs={{0,24},{8,16},{16,8},{24,0},{1,25},{9,17},{17,9},{25,1},{2,26},{10... | collective-permute-start | bytes 589832 | tf_op jit(solution)/shard_map/ppermute | solution.py:752
  47.4 9.5 %copy-start.20 = (bf16[4,2,96,128]{3,2,1,0:T(8,128)(2,1)S(1)}, bf16[4,2,96,128]{3,2,1,0:T(8,128)(2,1)}, u32[]{:S(2)}) copy-start(bf16[4,2,96,128]{3,2,1,0:T(8,128)(2,1)} %get-tuple-element.104.refs_0_) | copy-start | bytes 589828
  52.5 11.1 %collective-permute-start.6 = (bf16[4,2,96,128]{3,2,1,0:T(8,128)(2,1)}, bf16[4,2,96,128]{3,2,1,0:T(8,128)(2,1)S(1)}, u32[]{:S(2)}, u32[]{:S(2)}) collective-permute-start(bf16[4,2,96,128]{3,2,1,0:T(8,128)(2,1)} %get-tuple-element.86), channel_id=1, source_target_pairs={{0,4},{2,6},{4,0},{6,2},{1,5},{3,7},{5,1},{7,3},{8,12},{10,14},{12... | collective-permute-start | bytes 589832 | tf_op jit(solution)/shard_map/ppermute | solution.py:752
  52.5 15.8 %collective-permute-start.5 = (bf16[4,2,96,128]{3,2,1,0:T(8,128)(2,1)}, bf16[4,2,96,128]{3,2,1,0:T(8,128)(2,1)S(1)}, u32[]{:S(2)}, u32[]{:S(2)}) collective-permute-start(bf16[4,2,96,128]{3,2,1,0:T(8,128)(2,1)} %get-tuple-element.85), channel_id=1, source_target_pairs={{0,2},{2,0},{4,6},{6,4},{1,3},{3,1},{5,7},{7,5},{8,10},{10,8},{12,... | collective-permute-start | bytes 589832 | tf_op jit(solution)/shard_map/ppermute | solution.py:752
  52.5 16.2 %collective-permute-start.7 = (bf16[4,2,96,128]{3,2,1,0:T(8,128)(2,1)}, bf16[4,2,96,128]{3,2,1,0:T(8,128)(2,1)}, u32[]{:S(2)}, u32[]{:S(2)}) collective-permute-start(bf16[4,2,96,128]{3,2,1,0:T(8,128)(2,1)} %get-tuple-element.87), channel_id=1, source_target_pairs={{0,6},{2,4},{4,2},{6,0},{1,7},{3,5},{5,3},{7,1},{8,14},{10,12},{12... | collective-permute-start | bytes 589832 | tf_op jit(solution)/shard_map/ppermute | solution.py:752
  56.9 2.7 %copy-start.22 = (bf16[8,2,96,128]{3,2,1,0:T(8,128)(2,1)S(1)}, bf16[8,2,96,128]{3,2,1,0:T(8,128)(2,1)}, u32[]{:S(2)}) copy-start(bf16[8,2,96,128]{3,2,1,0:T(8,128)(2,1)} %slice.14.__4_) | copy-start | bytes 1179652
  59.6 20.3 %collective-permute-start = (bf16[8,2,96,128]{3,2,1,0:T(8,128)(2,1)S(1)}, bf16[8,2,96,128]{3,2,1,0:T(8,128)(2,1)S(1)}, u32[]{:S(2)}, u32[]{:S(2)}) collective-permute-start(bf16[8,2,96,128]{3,2,1,0:T(8,128)(2,1)S(1)} %copy-done.22), channel_id=1, source_target_pairs={{0,38},{1,39},{2,36},{3,37},{4,34},{5,35},{6,32},{7,33},{8,46},{9,... | collective-permute-start | bytes 1179656 | tf_op jit(solution)/shard_map/ppermute | solution.py:863
  64.3 27.3 %collective-permute-start.19 = (bf16[4,2,96,128]{3,2,1,0:T(8,128)(2,1)}, bf16[4,2,96,128]{3,2,1,0:T(8,128)(2,1)S(1)}, u32[]{:S(2)}, u32[]{:S(2)}) collective-permute-start(bf16[4,2,96,128]{3,2,1,0:T(8,128)(2,1)} %get-tuple-element.113), channel_id=1, source_target_pairs={{0,2},{2,0},{4,6},{6,4},{1,3},{3,1},{5,7},{7,5},{8,10},{10,8},{12,... | collective-permute-start | bytes 589832 | tf_op jit(solution)/shard_map/ppermute | solution.py:752
  65.3 26.2 %collective-permute-start.20 = (bf16[4,2,96,128]{3,2,1,0:T(8,128)(2,1)}, bf16[4,2,96,128]{3,2,1,0:T(8,128)(2,1)S(1)}, u32[]{:S(2)}, u32[]{:S(2)}) collective-permute-start(bf16[4,2,96,128]{3,2,1,0:T(8,128)(2,1)} %get-tuple-element.114), channel_id=1, source_target_pairs={{0,4},{2,6},{4,0},{6,2},{1,5},{3,7},{5,1},{7,3},{8,12},{10,14},{12... | collective-permute-start | bytes 589832 | tf_op jit(solution)/shard_map/ppermute | solution.py:752
  68.3 23.3 %collective-permute-start.21 = (bf16[4,2,96,128]{3,2,1,0:T(8,128)(2,1)}, bf16[4,2,96,128]{3,2,1,0:T(8,128)(2,1)S(1)}, u32[]{:S(2)}, u32[]{:S(2)}) collective-permute-start(bf16[4,2,96,128]{3,2,1,0:T(8,128)(2,1)} %get-tuple-element.115), channel_id=1, source_target_pairs={{0,6},{2,4},{4,2},{6,0},{1,7},{3,5},{5,3},{7,1},{8,14},{10,12},{12... | collective-permute-start | bytes 589832 | tf_op jit(solution)/shard_map/ppermute | solution.py:752
  85.3 31.8 %collective-permute-start.10 = (bf16[4,2,96,128]{3,2,1,0:T(8,128)(2,1)}, bf16[4,2,96,128]{3,2,1,0:T(8,128)(2,1)S(1)}, u32[]{:S(2)}, u32[]{:S(2)}) collective-permute-start(bf16[4,2,96,128]{3,2,1,0:T(8,128)(2,1)} %get-tuple-element.95.out_3), channel_id=1, source_target_pairs={{0,6},{2,4},{4,2},{6,0},{1,7},{3,5},{5,3},{7,1},{8,14},{10,12},{12... | collective-permute-start | bytes 589832 | tf_op jit(solution)/shard_map/ppermute | solution.py:752
  88.6 28.5 %collective-permute-start.8 = (bf16[4,2,96,128]{3,2,1,0:T(8,128)(2,1)}, bf16[4,2,96,128]{3,2,1,0:T(8,128)(2,1)}, u32[]{:S(2)}, u32[]{:S(2)}) collective-permute-start(bf16[4,2,96,128]{3,2,1,0:T(8,128)(2,1)} %get-tuple-element.93.out_1), channel_id=1, source_target_pairs={{0,2},{2,0},{4,6},{6,4},{1,3},{3,1},{5,7},{7,5},{8,10},{10,8},{12,... | collective-permute-start | bytes 589832 | tf_op jit(solution)/shard_map/ppermute | solution.py:752
  91.6 25.6 %collective-permute-start.9 = (bf16[4,2,96,128]{3,2,1,0:T(8,128)(2,1)}, bf16[4,2,96,128]{3,2,1,0:T(8,128)(2,1)}, u32[]{:S(2)}, u32[]{:S(2)}) collective-permute-start(bf16[4,2,96,128]{3,2,1,0:T(8,128)(2,1)} %get-tuple-element.94.out_2), channel_id=1, source_target_pairs={{0,4},{2,6},{4,0},{6,2},{1,5},{3,7},{5,1},{7,3},{8,12},{10,14},{12... | collective-permute-start | bytes 589832 | tf_op jit(solution)/shard_map/ppermute | solution.py:752
  98.7 28.6 %collective-permute-start.29 = (bf16[8,2,96,128]{3,2,1,0:T(8,128)(2,1)}, bf16[8,2,96,128]{3,2,1,0:T(8,128)(2,1)S(1)}, u32[]{:S(2)}, u32[]{:S(2)}) collective-permute-start(bf16[8,2,96,128]{3,2,1,0:T(8,128)(2,1)} %get-tuple-element.131), channel_id=1, source_target_pairs={{38,0},{39,1},{36,2},{37,3},{34,4},{35,5},{32,6},{33,7},{46,8},{47... | collective-permute-start | bytes 1179656 | tf_op jit(solution)/shard_map/ppermute | solution.py:877
  104.0 19.5 %copy-start.12 = (bf16[4,2,96,128]{3,2,1,0:T(8,128)(2,1)S(1)}, bf16[4,2,96,128]{3,2,1,0:T(8,128)(2,1)}, u32[]{:S(2)}) copy-start(bf16[4,2,96,128]{3,2,1,0:T(8,128)(2,1)} %get-tuple-element.92.refs_0_.out_0) | copy-start | bytes 589828
  117.8 12.9 %collective-permute-start.22 = (bf16[4,2,96,128]{3,2,1,0:T(8,128)(2,1)}, bf16[4,2,96,128]{3,2,1,0:T(8,128)(2,1)S(1)}, u32[]{:S(2)}, u32[]{:S(2)}) collective-permute-start(bf16[4,2,96,128]{3,2,1,0:T(8,128)(2,1)} %get-tuple-element.124), channel_id=1, source_target_pairs={{0,2},{2,0},{4,6},{6,4},{1,3},{3,1},{5,7},{7,5},{8,10},{10,8},{12,... | collective-permute-start | bytes 589832 | tf_op jit(solution)/shard_map/ppermute | solution.py:752
  121.1 15.7 %collective-permute-start.23 = (bf16[4,2,96,128]{3,2,1,0:T(8,128)(2,1)}, bf16[4,2,96,128]{3,2,1,0:T(8,128)(2,1)S(1)}, u32[]{:S(2)}, u32[]{:S(2)}) collective-permute-start(bf16[4,2,96,128]{3,2,1,0:T(8,128)(2,1)} %get-tuple-element.125), channel_id=1, source_target_pairs={{0,4},{2,6},{4,0},{6,2},{1,5},{3,7},{5,1},{7,3},{8,12},{10,14},{12... | collective-permute-start | bytes 589832 | tf_op jit(solution)/shard_map/ppermute | solution.py:752
  121.1 15.7 %collective-permute-start.24 = (bf16[4,2,96,128]{3,2,1,0:T(8,128)(2,1)}, bf16[4,2,96,128]{3,2,1,0:T(8,128)(2,1)S(1)}, u32[]{:S(2)}, u32[]{:S(2)}) collective-permute-start(bf16[4,2,96,128]{3,2,1,0:T(8,128)(2,1)} %get-tuple-element.126), channel_id=1, source_target_pairs={{0,6},{2,4},{4,2},{6,0},{1,7},{3,5},{5,3},{7,1},{8,14},{10,12},{12... | collective-permute-start | bytes 589832 | tf_op jit(solution)/shard_map/ppermute | solution.py:752
  127.2 9.6 %collective-permute-start.11 = (bf16[4,2,96,128]{3,2,1,0:T(8,128)(2,1)}, bf16[4,2,96,128]{3,2,1,0:T(8,128)(2,1)S(1)}, u32[]{:S(2)}, u32[]{:S(2)}) collective-permute-start(bf16[4,2,96,128]{3,2,1,0:T(8,128)(2,1)} %get-tuple-element.97), channel_id=1, source_target_pairs={{0,8},{8,0},{16,24},{24,16},{1,9},{9,1},{17,25},{25,17},{2,10},{10... | collective-permute-start | bytes 589832 | tf_op jit(solution)/shard_map/ppermute | solution.py:752
  127.3 9.5 %collective-permute-start.12 = (bf16[4,2,96,128]{3,2,1,0:T(8,128)(2,1)}, bf16[4,2,96,128]{3,2,1,0:T(8,128)(2,1)S(1)}, u32[]{:S(2)}, u32[]{:S(2)}) collective-permute-start(bf16[4,2,96,128]{3,2,1,0:T(8,128)(2,1)} %get-tuple-element.98), channel_id=1, source_target_pairs={{0,16},{8,24},{16,0},{24,8},{1,17},{9,25},{17,1},{25,9},{2,18},{10... | collective-permute-start | bytes 589832 | tf_op jit(solution)/shard_map/ppermute | solution.py:752
  130.6 2.2 %copy-start.6 = (bf16[4,2,96,128]{3,2,1,0:T(8,128)(2,1)}, bf16[4,2,96,128]{3,2,1,0:T(8,128)(2,1)S(1)}, u32[]{:S(2)}) copy-start(bf16[4,2,96,128]{3,2,1,0:T(8,128)(2,1)S(1)} %collective-permute-done.22.refs_1_.__1_) | copy-start | bytes 589828
  130.6 8.1 %collective-permute-start.13 = (bf16[4,2,96,128]{3,2,1,0:T(8,128)(2,1)}, bf16[4,2,96,128]{3,2,1,0:T(8,128)(2,1)S(1)}, u32[]{:S(2)}, u32[]{:S(2)}) collective-permute-start(bf16[4,2,96,128]{3,2,1,0:T(8,128)(2,1)} %get-tuple-element.99), channel_id=1, source_target_pairs={{0,24},{8,16},{16,8},{24,0},{1,25},{9,17},{17,9},{25,1},{2,26},{10... | collective-permute-start | bytes 589832 | tf_op jit(solution)/shard_map/ppermute | solution.py:752
  139.4 5.1 %copy-start.7 = (bf16[4,2,96,128]{3,2,1,0:T(8,128)(2,1)S(1)}, bf16[4,2,96,128]{3,2,1,0:T(8,128)(2,1)}, u32[]{:S(2)}) copy-start(bf16[4,2,96,128]{3,2,1,0:T(8,128)(2,1)} %copy-done.6) | copy-start | bytes 589828
  139.4 5.1 %copy-start.9 = (bf16[4,2,96,128]{3,2,1,0:T(8,128)(2,1)S(1)}, bf16[4,2,96,128]{3,2,1,0:T(8,128)(2,1)}, u32[]{:S(2)}) copy-start(bf16[4,2,96,128]{3,2,1,0:T(8,128)(2,1)} %copy-done.8) | copy-start | bytes 589828
  139.4 5.1 %copy-start.11 = (bf16[4,2,96,128]{3,2,1,0:T(8,128)(2,1)S(1)}, bf16[4,2,96,128]{3,2,1,0:T(8,128)(2,1)}, u32[]{:S(2)}) copy-start(bf16[4,2,96,128]{3,2,1,0:T(8,128)(2,1)} %copy-done.10) | copy-start | bytes 589828
  139.4 5.1 %copy-start.15 = (bf16[4,2,96,128]{3,2,1,0:T(8,128)(2,1)S(1)}, bf16[4,2,96,128]{3,2,1,0:T(8,128)(2,1)}, u32[]{:S(2)}) copy-start(bf16[4,2,96,128]{3,2,1,0:T(8,128)(2,1)} %get-tuple-element.123.refs_0_) | copy-start | bytes 589828
  139.4 44.3 %all-to-all-start.1 = ((bf16[32,2,96,128]{3,2,1,0:T(8,128)(2,1)}), bf16[32,2,96,128]{3,2,1,0:T(8,128)(2,1)S(1)}, u32[]{:S(2)}, u32[]{:S(2)}) async-start(bf16[32,2,96,128]{3,2,1,0:T(8,128)(2,1)} %after.7), calls=%async_computation.1 | async-start | bytes 3145728 | tf_op jit(solution)/shard_map/all_to_all | solution.py:832
  144.5 7.5 %copy-start.1 = (bf16[4,2,96,128]{3,2,1,0:T(8,128)(2,1)S(1)}, bf16[4,2,96,128]{3,2,1,0:T(8,128)(2,1)}, u32[]{:S(2)}) copy-start(bf16[4,2,96,128]{3,2,1,0:T(8,128)(2,1)} %copy-done) | copy-start | bytes 589828
  144.5 7.5 %copy-start.3 = (bf16[4,2,96,128]{3,2,1,0:T(8,128)(2,1)S(1)}, bf16[4,2,96,128]{3,2,1,0:T(8,128)(2,1)}, u32[]{:S(2)}) copy-start(bf16[4,2,96,128]{3,2,1,0:T(8,128)(2,1)} %copy-done.2) | copy-start | bytes 589828
  144.5 7.5 %copy-start.5 = (bf16[4,2,96,128]{3,2,1,0:T(8,128)(2,1)S(1)}, bf16[4,2,96,128]{3,2,1,0:T(8,128)(2,1)}, u32[]{:S(2)}) copy-start(bf16[4,2,96,128]{3,2,1,0:T(8,128)(2,1)} %copy-done.4) | copy-start | bytes 589828
  144.6 7.5 %copy-start.16 = (bf16[4,2,96,128]{3,2,1,0:T(8,128)(2,1)S(1)}, bf16[4,2,96,128]{3,2,1,0:T(8,128)(2,1)}, u32[]{:S(2)}) copy-start(bf16[4,2,96,128]{3,2,1,0:T(8,128)(2,1)} %get-tuple-element.96.refs_0_.part_0) | copy-start | bytes 589828
  147.2 16.4 %collective-permute-start.25 = (bf16[4,2,96,128]{3,2,1,0:T(8,128)(2,1)}, bf16[4,2,96,128]{3,2,1,0:T(8,128)(2,1)S(1)}, u32[]{:S(2)}, u32[]{:S(2)}) collective-permute-start(bf16[4,2,96,128]{3,2,1,0:T(8,128)(2,1)} %get-tuple-element.128), channel_id=1, source_target_pairs={{0,8},{8,0},{16,24},{24,16},{1,9},{9,1},{17,25},{25,17},{2,10},{10... | collective-permute-start | bytes 589832 | tf_op jit(solution)/shard_map/ppermute | solution.py:752
  149.1 22.4 %collective-permute-start.26 = (bf16[4,2,96,128]{3,2,1,0:T(8,128)(2,1)}, bf16[4,2,96,128]{3,2,1,0:T(8,128)(2,1)S(1)}, u32[]{:S(2)}, u32[]{:S(2)}) collective-permute-start(bf16[4,2,96,128]{3,2,1,0:T(8,128)(2,1)} %get-tuple-element.129), channel_id=1, source_target_pairs={{0,16},{8,24},{16,0},{24,8},{1,17},{9,25},{17,1},{25,9},{2,18},{10... | collective-permute-start | bytes 589832 | tf_op jit(solution)/shard_map/ppermute | solution.py:752
  151.8 19.7 %collective-permute-start.27 = (bf16[4,2,96,128]{3,2,1,0:T(8,128)(2,1)}, bf16[4,2,96,128]{3,2,1,0:T(8,128)(2,1)S(1)}, u32[]{:S(2)}, u32[]{:S(2)}) collective-permute-start(bf16[4,2,96,128]{3,2,1,0:T(8,128)(2,1)} %get-tuple-element.130), channel_id=1, source_target_pairs={{0,24},{8,16},{16,8},{24,0},{1,25},{9,17},{17,9},{25,1},{2,26},{10... | collective-permute-start | bytes 589832 | tf_op jit(solution)/shard_map/ppermute | solution.py:752
  152.0 19.5 %copy-start.17 = (bf16[4,2,96,128]{3,2,1,0:T(8,128)(2,1)S(1)}, bf16[4,2,96,128]{3,2,1,0:T(8,128)(2,1)}, u32[]{:S(2)}) copy-start(bf16[4,2,96,128]{3,2,1,0:T(8,128)(2,1)} %get-tuple-element.127.refs_0_.part_0) | copy-start | bytes 589828
  153.5 19.6 %collective-permute-start.14 = (bf16[4,4,96,128]{3,2,1,0:T(8,128)(2,1)}, bf16[4,4,96,128]{3,2,1,0:T(8,128)(2,1)S(1)}, u32[]{:S(2)}, u32[]{:S(2)}) collective-permute-start(bf16[4,4,96,128]{3,2,1,0:T(8,128)(2,1)} %other_core.2), channel_id=1, source_target_pairs={{0,1},{1,0},{2,3},{3,2},{4,5},{5,4},{6,7},{7,6},{8,9},{9,8},{10,11... | collective-permute-start | bytes 1179656 | tf_op jit(solution)/shard_map/ppermute | solution.py:793
  173.0 2.0 %collective-permute-start.28 = (bf16[4,4,96,128]{3,2,1,0:T(8,128)(2,1)}, bf16[4,4,96,128]{3,2,1,0:T(8,128)(2,1)S(1)}, u32[]{:S(2)}, u32[]{:S(2)}) collective-permute-start(bf16[4,4,96,128]{3,2,1,0:T(8,128)(2,1)} %other_core.3), channel_id=1, source_target_pairs={{0,1},{1,0},{2,3},{3,2},{4,5},{5,4},{6,7},{7,6},{8,9},{9,8},{10,11... | collective-permute-start | bytes 1179656 | tf_op jit(solution)/shard_map/ppermute | solution.py:793
  (12 other events, 13.4 us)

commit v8 on v7

--- a/solution.py
+++ b/solution.py
@@ -861,7 +861,7 @@
     pairs = group_pairs()
     last = kv[CHUNKS - HALO :]
     halo = lax.ppermute(last, AXES, pairs)
-    q = by_distance(after(to_parts(place, queries), [last]), "zl")
+    q = by_distance(after(to_parts(place, queries), [kv]), "zl")
     g = by_distance(after(to_parts(place, cotangent), q[2:3]), "zl")
     *out, stat = late_forward(place, tile_start, codes, kv, q)
     *out, early_stat = early_forward(place, tile_start, codes, kv, halo, q, out)

time: 186 us -> 186 us (level)
  Pallas kernels: 67.2 us -> 64.3 us
  waiting for transfers between devices: 46.9 us -> 49.3 us
    ppermute x24, waiting for transfers between devices: 35.1 us -> 37.4 us  [by_distance(): lax.ppermute(parts[d], axis, [(i, i ^ d) for i in range(4)])]
    unnamed x56 -> x60, local copies, waits for them, and re-layouts: 4.11 us -> 5.67 us
  transfers between devices with their start and end apart: 32 -> 32, of which waited for: 11 -> 13; matrix products, arithmetic and copies ran while one was open for 2% -> 1% of each run, Pallas kernels for 34% -> 32%
where the time goes in v8:
time: 186 us; the launch traced here: 185 us
  Pallas kernels  64.3 us (35%)
  starting transfers between devices  61.9 us (33%)
  waiting for transfers between devices  49.3 us (27%)
  local copies, waits for them, and re-layouts  6.55 us (4%)
    ppermute x24, starting transfers between devices, by_distance(): lax.ppermute(parts[d], axis, [(i, i ^ d) for i in range(4)])  40.5 us
    ppermute x24, waiting for transfers between devices, by_distance(): lax.ppermute(parts[d], axis, [(i, i ^ d) for i in range(4)])  37.4 us
    all_to_all x2, starting transfers between devices, to_heads(): lax.all_to_all(array, GROUP_AXES, split_axis=0, concat_axis=0, tiled=True)  13 us
    pallas_call x1, Pallas kernels, late_backward(): pl.pallas_call(late_backward_kernel, in_specs=[smem(), smem(), vmem(), vm...  12.3 us
    all_to_all x2, waiting for transfers between devices, to_heads(): lax.all_to_all(array, GROUP_AXES, split_axis=0, concat_axis=0, tiled=True)  11.5 us
    pallas_call x4, Pallas kernels, turn(): pl.pallas_call(functools.partial(turn_kernel, back), in_specs=[smem()] +...  10.8 us
    pallas_call x1, Pallas kernels, late_forward(): pl.pallas_call(late_forward_kernel, in_specs=[smem(), smem(), vmem(), vme...  10.1 us
    pallas_call x1, Pallas kernels, early_backward(): pl.pallas_call(early_backward_kernel, grid=(1,), in_specs=[smem(), smem()...  5.71 us
  transfers between devices with their start and end apart: 32, of which 13 were waited for; matrix products, arithmetic and copies ran while one was open for 1% of the time, Pallas kernels for 32%

profile of v8, /device:TPU:4, one launch (start us, length us, event | category | flops | bytes accessed | tf_op | source)
XLA Modules:
  0.0 184.6 jit_solution(16411686324426845411)
XLA Ops:
  0.6 2.6 %pack.1 = bf16[32,2,96,128]{3,2,1,0:T(8,128)(2,1)} custom-call(s32[1]{0:T(128)} %bitcast.mirror_ref, bf16[128,3072]{1,0:T(8,128)(2,1)} %refs_0_.1, bf16[128,3072]{1,0:T(8,128)(2,1)} %refs_1_.1), custom_call_target="tpu_custom_call" | custom-call | tf_op jit(solution)/shard_map/pack/pallas_call | solution.py:89
  3.3 8.9 %all-to-all-start = ((bf16[32,2,96,128]{3,2,1,0:T(8,128)(2,1)}), bf16[32,2,96,128]{3,2,1,0:T(8,128)(2,1)S(1)}, u32[]{:S(2)}, u32[]{:S(2)}) async-start(bf16[32,2,96,128]{3,2,1,0:T(8,128)(2,1)} %pack.1), calls=%async_computation | async-start | bytes 3145728 | tf_op jit(solution)/shard_map/all_to_all | solution.py:832
  13.0 0.8 dynamic-slice_select_fusion
  14.6 2.8 %pack_cores.2 = (bf16[4,4,96,128]{3,2,1,0:T(8,128)(2,1)}, bf16[4,4,96,128]{3,2,1,0:T(8,128)(2,1)}) custom-call(s32[4]{0:T(128)S(1)} %pad_add_fusion.1.place_ref, bf16[128,3072]{1,0:T(8,128)(2,1)} %source), custom_call_target="tpu_custom_call" | custom-call | flops 1100000000 | tf_op jit(solution)/shard_map/pack_cores/pallas_call | solution.py:669
  17.8 2.8 %pack_cores.3 = (bf16[4,4,96,128]{3,2,1,0:T(8,128)(2,1)}, bf16[4,4,96,128]{3,2,1,0:T(8,128)(2,1)}) custom-call(s32[4]{0:T(128)S(1)} %pad_add_fusion.1.place_ref, bf16[128,3072]{1,0:T(8,128)(2,1)} %source.1), custom_call_target="tpu_custom_call" | custom-call | flops 1100000000 | tf_op jit(solution)/shard_map/pack_cores/pallas_call | solution.py:669
  21.0 1.8 both_cores.2
  22.7 1.9 %collective-permute-start.2 = (bf16[4,2,96,128]{3,2,1,0:T(8,128)(2,1)}, bf16[4,2,96,128]{3,2,1,0:T(8,128)(2,1)S(1)}, u32[]{:S(2)}, u32[]{:S(2)}) collective-permute-start(bf16[4,2,96,128]{3,2,1,0:T(8,128)(2,1)} %get-tuple-element.77), channel_id=1, source_target_pairs={{0,8},{8,0},{16,24},{24,16},{1,9},{9,1},{17,25},{25,17},{2,10},{10... | collective-permute-start | bytes 589832 | tf_op jit(solution)/shard_map/ppermute | solution.py:752
  24.6 2.7 %collective-permute-start.3 = (bf16[4,2,96,128]{3,2,1,0:T(8,128)(2,1)}, bf16[4,2,96,128]{3,2,1,0:T(8,128)(2,1)S(1)}, u32[]{:S(2)}, u32[]{:S(2)}) collective-permute-start(bf16[4,2,96,128]{3,2,1,0:T(8,128)(2,1)} %get-tuple-element.78), channel_id=1, source_target_pairs={{0,16},{8,24},{16,0},{24,8},{1,17},{9,25},{17,1},{25,9},{2,18},{10... | collective-permute-start | bytes 589832 | tf_op jit(solution)/shard_map/ppermute | solution.py:752
  27.5 1.8 both_cores.3
  30.0 3.9 %collective-permute-start.17 = (bf16[4,2,96,128]{3,2,1,0:T(8,128)(2,1)}, bf16[4,2,96,128]{3,2,1,0:T(8,128)(2,1)S(1)}, u32[]{:S(2)}, u32[]{:S(2)}) collective-permute-start(bf16[4,2,96,128]{3,2,1,0:T(8,128)(2,1)} %get-tuple-element.106), channel_id=1, source_target_pairs={{0,16},{8,24},{16,0},{24,8},{1,17},{9,25},{17,1},{25,9},{2,18},{10... | collective-permute-start | bytes 589832 | tf_op jit(solution)/shard_map/ppermute | solution.py:752
  34.7 6.3 %collective-permute-done.3.refs_2_ = bf16[4,2,96,128]{3,2,1,0:T(8,128)(2,1)S(1)} collective-permute-done((bf16[4,2,96,128]{3,2,1,0:T(8,128)(2,1)}, bf16[4,2,96,128]{3,2,1,0:T(8,128)(2,1)S(1)}, u32[]{:S(2)}, u32[]{:S(2)}) %collective-permute-start.3) | collective-permute-done | bytes 196640 | tf_op jit(solution)/shard_map/ppermute | solution.py:752
  41.0 3.7 %collective-permute-done.4.refs_3_ = bf16[4,2,96,128]{3,2,1,0:T(8,128)(2,1)S(1)} collective-permute-done((bf16[4,2,96,128]{3,2,1,0:T(8,128)(2,1)}, bf16[4,2,96,128]{3,2,1,0:T(8,128)(2,1)S(1)}, u32[]{:S(2)}, u32[]{:S(2)}) %collective-permute-start.4) | collective-permute-done | bytes 196640 | tf_op jit(solution)/shard_map/ppermute | solution.py:752
  44.7 2.6 %turn.4 = (bf16[4,2,96,128]{3,2,1,0:T(8,128)(2,1)}, bf16[4,2,96,128]{3,2,1,0:T(8,128)(2,1)}, bf16[4,2,96,128]{3,2,1,0:T(8,128)(2,1)}, bf16[4,2,96,128]{3,2,1,0:T(8,128)(2,1)}) custom-call(s32[4]{0:T(128)S(1)} %pad_add_fusion.1.place_ref, bf16[4,2,96,128]{3,2,1,0:T(8,128)(2,1)S(1)} %copy-done.23, bf16[4,2,96,128]{3,2,1,0:T(8,128)(2,1)S(1)} %collective-permute-done.2.refs_1_, ...), custom_call_target="tpu_custom_call" | custom-call | flops 1100000000 | tf_op jit(solution)/shard_map/turn/pallas_call | solution.py:623
  47.4 4.3 %all-to-all-done.__4_.kv_ref = bf16[32,2,96,128]{3,2,1,0:T(8,128)(2,1)S(1)} async-done(((bf16[32,2,96,128]{3,2,1,0:T(8,128)(2,1)}), bf16[32,2,96,128]{3,2,1,0:T(8,128)(2,1)S(1)}, u32[]{:S(2)}, u32[]{:S(2)}) %all-to-all-start) | async-done | bytes 1572896 | tf_op jit(solution)/shard_map/all_to_all | solution.py:832
  51.7 1.2 copy-done
  52.9 4.4 %collective-permute-start.7 = (bf16[4,2,96,128]{3,2,1,0:T(8,128)(2,1)}, bf16[4,2,96,128]{3,2,1,0:T(8,128)(2,1)S(1)}, u32[]{:S(2)}, u32[]{:S(2)}) collective-permute-start(bf16[4,2,96,128]{3,2,1,0:T(8,128)(2,1)} %get-tuple-element.87), channel_id=1, source_target_pairs={{0,6},{2,4},{4,2},{6,0},{1,7},{3,5},{5,3},{7,1},{8,14},{10,12},{12... | collective-permute-start | bytes 589832 | tf_op jit(solution)/shard_map/ppermute | solution.py:752
  57.3 2.7 %turn.6 = (bf16[4,2,96,128]{3,2,1,0:T(8,128)(2,1)}, bf16[4,2,96,128]{3,2,1,0:T(8,128)(2,1)}, bf16[4,2,96,128]{3,2,1,0:T(8,128)(2,1)}, bf16[4,2,96,128]{3,2,1,0:T(8,128)(2,1)}) custom-call(s32[4]{0:T(128)S(1)} %pad_add_fusion.1.place_ref, bf16[4,2,96,128]{3,2,1,0:T(8,128)(2,1)S(1)} %copy-done.22, bf16[4,2,96,128]{3,2,1,0:T(8,128)(2,1)S(1)} %collective-permute-done.16.refs_1_, ...), custom_call_target="tpu_custom_call" | custom-call | flops 1100000000 | tf_op jit(solution)/shard_map/turn/pallas_call | solution.py:623
  60.0 3.2 %collective-permute-start = (bf16[8,2,96,128]{3,2,1,0:T(8,128)(2,1)S(1)}, bf16[8,2,96,128]{3,2,1,0:T(8,128)(2,1)S(1)}, u32[]{:S(2)}, u32[]{:S(2)}) collective-permute-start(bf16[8,2,96,128]{3,2,1,0:T(8,128)(2,1)S(1)} %slice.14), channel_id=1, source_target_pairs={{0,38},{1,39},{2,36},{3,37},{4,34},{5,35},{6,32},{7,33},{8,46},{9,... | collective-permute-start | bytes 1179656 | tf_op jit(solution)/shard_map/ppermute | solution.py:863
  63.2 0.8 collective-permute-done.6.q_2.__4_
  65.3 2.9 %collective-permute-start.20 = (bf16[4,2,96,128]{3,2,1,0:T(8,128)(2,1)}, bf16[4,2,96,128]{3,2,1,0:T(8,128)(2,1)S(1)}, u32[]{:S(2)}, u32[]{:S(2)}) collective-permute-start(bf16[4,2,96,128]{3,2,1,0:T(8,128)(2,1)} %get-tuple-element.114), channel_id=1, source_target_pairs={{0,4},{2,6},{4,0},{6,2},{1,5},{3,7},{5,1},{7,3},{8,12},{10,14},{12... | collective-permute-start | bytes 589832 | tf_op jit(solution)/shard_map/ppermute | solution.py:752
  69.7 10.1 %late_forward.1 = (bf16[4,2,96,128]{3,2,1,0:T(8,128)(2,1)}, bf16[4,2,96,128]{3,2,1,0:T(8,128)(2,1)}, bf16[4,2,96,128]{3,2,1,0:T(8,128)(2,1)}, bf16[4,2,96,128]{3,2,1,0:T(8,128)(2,1)}, f32[16,1,256]{2,1,0:T(1,128)S(1)}) custom-call(s32[4]{0:T(128)S(1)} %pad_add_fusion.1.place_ref, s32[16]{0:T(128)S(1)} %and_select_fusion.2.tile_start_ref, ...), custom_call_target="tpu_custom_call" | custom-call | flops 32999999488 | tf_op jit(solution)/shard_map/late_forward/pallas_call | solution.py:301
  79.8 4.8 %early_forward.1 = (bf16[4,2,96,128]{3,2,1,0:T(8,128)(2,1)}, bf16[4,2,96,128]{3,2,1,0:T(8,128)(2,1)}, bf16[4,2,96,128]{3,2,1,0:T(8,128)(2,1)}, bf16[4,2,96,128]{3,2,1,0:T(8,128)(2,1)}, f32[4,1,256]{2,1,0:T(1,128)S(1)}) custom-call(s32[4]{0:T(128)S(1)} %pad_add_fusion.1.place_ref, ...), custom_call_target="tpu_custom_call", output_to_operand_aliasing={{0}: (10, {}), {1}: (11, {}), {2}: (12, {}), {3}: (13, {})} | custom-call | flops 1100000000 | tf_op jit(solution)/shard_map/early_forward/pallas_call | solution.py:497
  84.7 3.5 %collective-permute-start.10 = (bf16[4,2,96,128]{3,2,1,0:T(8,128)(2,1)}, bf16[4,2,96,128]{3,2,1,0:T(8,128)(2,1)S(1)}, u32[]{:S(2)}, u32[]{:S(2)}) collective-permute-start(bf16[4,2,96,128]{3,2,1,0:T(8,128)(2,1)} %get-tuple-element.95.out_3), channel_id=1, source_target_pairs={{0,6},{2,4},{4,2},{6,0},{1,7},{3,5},{5,3},{7,1},{8,14},{10,12},{12... | collective-permute-start | bytes 589832 | tf_op jit(solution)/shard_map/ppermute | solution.py:752
  88.2 3.2 %collective-permute-start.8 = (bf16[4,2,96,128]{3,2,1,0:T(8,128)(2,1)}, bf16[4,2,96,128]{3,2,1,0:T(8,128)(2,1)}, u32[]{:S(2)}, u32[]{:S(2)}) collective-permute-start(bf16[4,2,96,128]{3,2,1,0:T(8,128)(2,1)} %get-tuple-element.93.out_1), channel_id=1, source_target_pairs={{0,2},{2,0},{4,6},{6,4},{1,3},{3,1},{5,7},{7,5},{8,10},{10,8},{12,... | collective-permute-start | bytes 589832 | tf_op jit(solution)/shard_map/ppermute | solution.py:752
  91.4 1.4 collective-permute-done.19.g_1
  93.7 5.7 %early_backward.1 = (bf16[8,2,96,128]{3,2,1,0:T(8,128)(2,1)}, f32[2,96,1024]{2,1,0:T(8,128)}, bf16[8,96,128]{2,1,0:T(8,128)(2,1)}) custom-call(s32[4]{0:T(128)S(1)} %pad_add_fusion.1.place_ref, s32[16]{0:T(128)S(1)} %and_select_fusion.2.tile_start_ref, bf16[16,5120]{1,0:T(8,128)(2,1)S(1)} %select_convert_fusion.key_code_ref, ...), custom_call_target="tpu_custom_call" | custom-call | flops 1100000000 | tf_op jit(solution)/shard_map/early_backward/pallas_call | solution.py:512
  99.4 4.3 %collective-permute-start.29 = (bf16[8,2,96,128]{3,2,1,0:T(8,128)(2,1)}, bf16[8,2,96,128]{3,2,1,0:T(8,128)(2,1)S(1)}, u32[]{:S(2)}, u32[]{:S(2)}) collective-permute-start(bf16[8,2,96,128]{3,2,1,0:T(8,128)(2,1)} %get-tuple-element.131), channel_id=1, source_target_pairs={{38,0},{39,1},{36,2},{37,3},{34,4},{35,5},{32,6},{33,7},{46,8},{47... | collective-permute-start | bytes 1179656 | tf_op jit(solution)/shard_map/ppermute | solution.py:877
  103.7 12.3 %late_backward.1 = (bf16[32,2,96,128]{3,2,1,0:T(8,128)(2,1)}, f32[2,96,1024]{2,1,0:T(8,128)S(1)}, bf16[4,2,96,128]{3,2,1,0:T(8,128)(2,1)}, bf16[4,2,96,128]{3,2,...) custom-call(s32[4]{0:T(128)S(1)} %pad_add_fusion.1.place_ref, ...), custom_call_target="tpu_custom_call" | custom-call | flops 11000000512 | tf_op jit(solution)/shard_map/late_backward/pallas_call | solution.py:541
  116.7 3.3 %collective-permute-start.22 = (bf16[4,2,96,128]{3,2,1,0:T(8,128)(2,1)}, bf16[4,2,96,128]{3,2,1,0:T(8,128)(2,1)S(1)}, u32[]{:S(2)}, u32[]{:S(2)}) collective-permute-start(bf16[4,2,96,128]{3,2,1,0:T(8,128)(2,1)} %get-tuple-element.124), channel_id=1, source_target_pairs={{0,2},{2,0},{4,6},{6,4},{1,3},{3,1},{5,7},{7,5},{8,10},{10,8},{12,... | collective-permute-start | bytes 589832 | tf_op jit(solution)/shard_map/ppermute | solution.py:752
  120.0 2.4 %collective-permute-start.24 = (bf16[4,2,96,128]{3,2,1,0:T(8,128)(2,1)}, bf16[4,2,96,128]{3,2,1,0:T(8,128)(2,1)S(1)}, u32[]{:S(2)}, u32[]{:S(2)}) collective-permute-start(bf16[4,2,96,128]{3,2,1,0:T(8,128)(2,1)} %get-tuple-element.126), channel_id=1, source_target_pairs={{0,6},{2,4},{4,2},{6,0},{1,7},{3,5},{5,3},{7,1},{8,14},{10,12},{12... | collective-permute-start | bytes 589832 | tf_op jit(solution)/shard_map/ppermute | solution.py:752
  122.4 0.9 copy-done.16
  123.3 2.8 %turn.5 = (bf16[4,2,96,128]{3,2,1,0:T(8,128)(2,1)}, bf16[4,2,96,128]{3,2,1,0:T(8,128)(2,1)}, bf16[4,2,96,128]{3,2,1,0:T(8,128)(2,1)}, bf16[4,2,96,128]{3,2,1,0:T(8,128)(2,1)}) custom-call(s32[4]{0:T(128)S(1)} %pad_add_fusion.1.place_ref, bf16[4,2,96,128]{3,2,1,0:T(8,128)(2,1)S(1)} %copy-done.14, bf16[4,2,96,128]{3,2,1,0:T(8,128)(2,1)} %collective-permute-done.8.refs_1_.__4_, ...), custom_call_target="tpu_custom_call" | custom-call | flops 1100000000 | tf_op jit(solution)/shard_map/turn/pallas_call | solution.py:623
  126.3 4.3 %collective-permute-start.12 = (bf16[4,2,96,128]{3,2,1,0:T(8,128)(2,1)}, bf16[4,2,96,128]{3,2,1,0:T(8,128)(2,1)S(1)}, u32[]{:S(2)}, u32[]{:S(2)}) collective-permute-start(bf16[4,2,96,128]{3,2,1,0:T(8,128)(2,1)} %get-tuple-element.98), channel_id=1, source_target_pairs={{0,16},{8,24},{16,0},{24,8},{1,17},{9,25},{17,1},{25,9},{2,18},{10... | collective-permute-start | bytes 589832 | tf_op jit(solution)/shard_map/ppermute | solution.py:752
  131.0 0.8 join.1.__0_
  131.8 4.2 %collective-permute-done.23.refs_2_.__2_ = bf16[4,2,96,128]{3,2,1,0:T(8,128)(2,1)S(1)} collective-permute-done((bf16[4,2,96,128]{3,2,1,0:T(8,128)(2,1)}, bf16[4,2,96,128]{3,2,1,0:T(8,128)(2,1)S(1)}, u32[]{:S(2)}, u32[]{:S(2)}) %collective-permute-start.23) | collective-permute-done | bytes 196640 | tf_op jit(solution)/shard_map/ppermute | solution.py:752
  136.7 2.0 %collective-permute-done.13.refs_3_.part_3.__6_ = bf16[4,2,96,128]{3,2,1,0:T(8,128)(2,1)S(1)} collective-permute-done((bf16[4,2,96,128]{3,2,1,0:T(8,128)(2,1)}, bf16[4,2,96,128]{3,2,1,0:T(8,128)(2,1)S(1)}, u32[]{:S(2)}, u32[]{:S(2)}) %collective-permute-start.13) | collective-permute-done | bytes 196640 | tf_op jit(solution)/shard_map/ppermute | solution.py:752
  139.4 4.1 %all-to-all-start.1 = ((bf16[32,2,96,128]{3,2,1,0:T(8,128)(2,1)}), bf16[32,2,96,128]{3,2,1,0:T(8,128)(2,1)S(1)}, u32[]{:S(2)}, u32[]{:S(2)}) async-start(bf16[32,2,96,128]{3,2,1,0:T(8,128)(2,1)} %after.7), calls=%async_computation.1 | async-start | bytes 3145728 | tf_op jit(solution)/shard_map/all_to_all | solution.py:832
  143.6 2.7 %turn.7 = (bf16[4,2,96,128]{3,2,1,0:T(8,128)(2,1)}, bf16[4,2,96,128]{3,2,1,0:T(8,128)(2,1)}, bf16[4,2,96,128]{3,2,1,0:T(8,128)(2,1)}, bf16[4,2,96,128]{3,2,1,0:T(8,128)(2,1)}) custom-call(s32[4]{0:T(128)S(1)} %pad_add_fusion.1.place_ref, bf16[4,2,96,128]{3,2,1,0:T(8,128)(2,1)S(1)} %copy-done.17, bf16[4,2,96,128]{3,2,1,0:T(8,128)(2,1)S(1)} %copy-done.9, ...), custom_call_target="tpu_custom_call" | custom-call | flops 1100000000 | tf_op jit(solution)/shard_map/turn/pallas_call | solution.py:623
  146.3 1.8 collective-permute-start.25
  148.1 2.8 %collective-permute-start.26 = (bf16[4,2,96,128]{3,2,1,0:T(8,128)(2,1)}, bf16[4,2,96,128]{3,2,1,0:T(8,128)(2,1)S(1)}, u32[]{:S(2)}, u32[]{:S(2)}) collective-permute-start(bf16[4,2,96,128]{3,2,1,0:T(8,128)(2,1)} %get-tuple-element.129), channel_id=1, source_target_pairs={{0,16},{8,24},{16,0},{24,8},{1,17},{9,25},{17,1},{25,9},{2,18},{10... | collective-permute-start | bytes 589832 | tf_op jit(solution)/shard_map/ppermute | solution.py:752
  151.1 1.5 other_core.2
  152.7 9.9 %collective-permute-done.25.refs_1_.part_1 = bf16[4,2,96,128]{3,2,1,0:T(8,128)(2,1)S(1)} collective-permute-done((bf16[4,2,96,128]{3,2,1,0:T(8,128)(2,1)}, bf16[4,2,96,128]{3,2,1,0:T(8,128)(2,1)S(1)}, u32[]{:S(2)}, u32[]{:S(2)}) %collective-permute-start.25) | collective-permute-done | bytes 196640 | tf_op jit(solution)/shard_map/ppermute | solution.py:752
  162.6 7.9 %collective-permute-done.26.refs_2_.part_2 = bf16[4,2,96,128]{3,2,1,0:T(8,128)(2,1)S(1)} collective-permute-done((bf16[4,2,96,128]{3,2,1,0:T(8,128)(2,1)}, bf16[4,2,96,128]{3,2,1,0:T(8,128)(2,1)S(1)}, u32[]{:S(2)}, u32[]{:S(2)}) %collective-permute-start.26) | collective-permute-done | bytes 196640 | tf_op jit(solution)/shard_map/ppermute | solution.py:752
  170.5 1.5 other_core.3
  172.1 1.6 rows_of.2
  174.0 1.6 rows_of.3
  175.6 7.2 %all-to-all-done.1.in_ref = bf16[32,2,96,128]{3,2,1,0:T(8,128)(2,1)S(1)} async-done(((bf16[32,2,96,128]{3,2,1,0:T(8,128)(2,1)}), bf16[32,2,96,128]{3,2,1,0:T(8,128)(2,1)S(1)}, u32[]{:S(2)}, u32[]{:S(2)}) %all-to-all-start.1) | async-done | bytes 1572896 | tf_op jit(solution)/shard_map/all_to_all | solution.py:832
  182.8 1.9 %unpack.1 = (bf16[128,3072]{1,0:T(8,128)(2,1)}, bf16[128,3072]{1,0:T(8,128)(2,1)}) custom-call(s32[1]{0:T(128)} %bitcast.mirror_ref, bf16[32,2,96,128]{3,2,1,0:T(8,128)(2,1)S(1)} %all-to-all-done.1.in_ref), custom_call_target="tpu_custom_call" | custom-call | tf_op jit(solution)/shard_map/unpack/pallas_call | solution.py:117
  (115 shorter events, 10.8 us)
Async XLA Ops:
  3.3 48.4 %all-to-all-start = ((bf16[32,2,96,128]{3,2,1,0:T(8,128)(2,1)}), bf16[32,2,96,128]{3,2,1,0:T(8,128)(2,1)S(1)}, u32[]{:S(2)}, u32[]{:S(2)}) async-start(bf16[32,2,96,128]{3,2,1,0:T(8,128)(2,1)} %pack.1), calls=%async_computation | async-start | bytes 3145728 | tf_op jit(solution)/shard_map/all_to_all | solution.py:832
  17.4 3.5 %copy-start.21 = (bf16[4,4,96,128]{3,2,1,0:T(8,128)(2,1)S(1)}, bf16[4,4,96,128]{3,2,1,0:T(8,128)(2,1)}, u32[]{:S(2)}) copy-start(bf16[4,4,96,128]{3,2,1,0:T(8,128)(2,1)} %get-tuple-element.74.own_ref) | copy-start | bytes 1179652
  17.4 3.5 %collective-permute-start.1 = (bf16[4,4,96,128]{3,2,1,0:T(8,128)(2,1)}, bf16[4,4,96,128]{3,2,1,0:T(8,128)(2,1)S(1)}, u32[]{:S(2)}, u32[]{:S(2)}) collective-permute-start(bf16[4,4,96,128]{3,2,1,0:T(8,128)(2,1)} %get-tuple-element.75), channel_id=1, source_target_pairs={{0,1},{1,0},{2,3},{3,2},{4,5},{5,4},{6,7},{7,6},{8,9},{9,8},{10,11... | collective-permute-start | bytes 1179656 | tf_op jit(solution)/shard_map/ppermute | solution.py:718
  20.6 6.9 %collective-permute-start.15 = (bf16[4,4,96,128]{3,2,1,0:T(8,128)(2,1)}, bf16[4,4,96,128]{3,2,1,0:T(8,128)(2,1)S(1)}, u32[]{:S(2)}, u32[]{:S(2)}) collective-permute-start(bf16[4,4,96,128]{3,2,1,0:T(8,128)(2,1)} %get-tuple-element.103), channel_id=1, source_target_pairs={{0,1},{1,0},{2,3},{3,2},{4,5},{5,4},{6,7},{7,6},{8,9},{9,8},{10,11... | collective-permute-start | bytes 1179656 | tf_op jit(solution)/shard_map/ppermute | solution.py:718
  20.9 6.6 %copy-start.20 = (bf16[4,4,96,128]{3,2,1,0:T(8,128)(2,1)S(1)}, bf16[4,4,96,128]{3,2,1,0:T(8,128)(2,1)}, u32[]{:S(2)}) copy-start(bf16[4,4,96,128]{3,2,1,0:T(8,128)(2,1)} %get-tuple-element.102.own_ref) | copy-start | bytes 1179652
  22.7 11.2 %collective-permute-start.2 = (bf16[4,2,96,128]{3,2,1,0:T(8,128)(2,1)}, bf16[4,2,96,128]{3,2,1,0:T(8,128)(2,1)S(1)}, u32[]{:S(2)}, u32[]{:S(2)}) collective-permute-start(bf16[4,2,96,128]{3,2,1,0:T(8,128)(2,1)} %get-tuple-element.77), channel_id=1, source_target_pairs={{0,8},{8,0},{16,24},{24,16},{1,9},{9,1},{17,25},{25,17},{2,10},{10... | collective-permute-start | bytes 589832 | tf_op jit(solution)/shard_map/ppermute | solution.py:752
  24.6 16.4 %collective-permute-start.3 = (bf16[4,2,96,128]{3,2,1,0:T(8,128)(2,1)}, bf16[4,2,96,128]{3,2,1,0:T(8,128)(2,1)S(1)}, u32[]{:S(2)}, u32[]{:S(2)}) collective-permute-start(bf16[4,2,96,128]{3,2,1,0:T(8,128)(2,1)} %get-tuple-element.78), channel_id=1, source_target_pairs={{0,16},{8,24},{16,0},{24,8},{1,17},{9,25},{17,1},{25,9},{2,18},{10... | collective-permute-start | bytes 589832 | tf_op jit(solution)/shard_map/ppermute | solution.py:752
  27.3 17.4 %collective-permute-start.4 = (bf16[4,2,96,128]{3,2,1,0:T(8,128)(2,1)}, bf16[4,2,96,128]{3,2,1,0:T(8,128)(2,1)S(1)}, u32[]{:S(2)}, u32[]{:S(2)}) collective-permute-start(bf16[4,2,96,128]{3,2,1,0:T(8,128)(2,1)} %get-tuple-element.79), channel_id=1, source_target_pairs={{0,24},{8,16},{16,8},{24,0},{1,25},{9,17},{17,9},{25,1},{2,26},{10... | collective-permute-start | bytes 589832 | tf_op jit(solution)/shard_map/ppermute | solution.py:752
  27.5 17.2 %copy-start.23 = (bf16[4,2,96,128]{3,2,1,0:T(8,128)(2,1)S(1)}, bf16[4,2,96,128]{3,2,1,0:T(8,128)(2,1)}, u32[]{:S(2)}) copy-start(bf16[4,2,96,128]{3,2,1,0:T(8,128)(2,1)} %get-tuple-element.76.refs_0_) | copy-start | bytes 589828
  29.3 23.5 %collective-permute-start.16 = (bf16[4,2,96,128]{3,2,1,0:T(8,128)(2,1)}, bf16[4,2,96,128]{3,2,1,0:T(8,128)(2,1)S(1)}, u32[]{:S(2)}, u32[]{:S(2)}) collective-permute-start(bf16[4,2,96,128]{3,2,1,0:T(8,128)(2,1)} %get-tuple-element.105), channel_id=1, source_target_pairs={{0,8},{8,0},{16,24},{24,16},{1,9},{9,1},{17,25},{25,17},{2,10},{10... | collective-permute-start | bytes 589832 | tf_op jit(solution)/shard_map/ppermute | solution.py:752
  30.0 27.2 %collective-permute-start.17 = (bf16[4,2,96,128]{3,2,1,0:T(8,128)(2,1)}, bf16[4,2,96,128]{3,2,1,0:T(8,128)(2,1)S(1)}, u32[]{:S(2)}, u32[]{:S(2)}) collective-permute-start(bf16[4,2,96,128]{3,2,1,0:T(8,128)(2,1)} %get-tuple-element.106), channel_id=1, source_target_pairs={{0,16},{8,24},{16,0},{24,8},{1,17},{9,25},{17,1},{25,9},{2,18},{10... | collective-permute-start | bytes 589832 | tf_op jit(solution)/shard_map/ppermute | solution.py:752
  33.9 23.3 %collective-permute-start.18 = (bf16[4,2,96,128]{3,2,1,0:T(8,128)(2,1)}, bf16[4,2,96,128]{3,2,1,0:T(8,128)(2,1)S(1)}, u32[]{:S(2)}, u32[]{:S(2)}) collective-permute-start(bf16[4,2,96,128]{3,2,1,0:T(8,128)(2,1)} %get-tuple-element.107), channel_id=1, source_target_pairs={{0,24},{8,16},{16,8},{24,0},{1,25},{9,17},{17,9},{25,1},{2,26},{10... | collective-permute-start | bytes 589832 | tf_op jit(solution)/shard_map/ppermute | solution.py:752
  47.4 9.9 %copy-start.22 = (bf16[4,2,96,128]{3,2,1,0:T(8,128)(2,1)S(1)}, bf16[4,2,96,128]{3,2,1,0:T(8,128)(2,1)}, u32[]{:S(2)}) copy-start(bf16[4,2,96,128]{3,2,1,0:T(8,128)(2,1)} %get-tuple-element.104.refs_0_) | copy-start | bytes 589828
  52.9 11.1 %collective-permute-start.6 = (bf16[4,2,96,128]{3,2,1,0:T(8,128)(2,1)}, bf16[4,2,96,128]{3,2,1,0:T(8,128)(2,1)S(1)}, u32[]{:S(2)}, u32[]{:S(2)}) collective-permute-start(bf16[4,2,96,128]{3,2,1,0:T(8,128)(2,1)} %get-tuple-element.86), channel_id=1, source_target_pairs={{0,4},{2,6},{4,0},{6,2},{1,5},{3,7},{5,1},{7,3},{8,12},{10,14},{12... | collective-permute-start | bytes 589832 | tf_op jit(solution)/shard_map/ppermute | solution.py:752
  52.9 15.8 %collective-permute-start.5 = (bf16[4,2,96,128]{3,2,1,0:T(8,128)(2,1)}, bf16[4,2,96,128]{3,2,1,0:T(8,128)(2,1)S(1)}, u32[]{:S(2)}, u32[]{:S(2)}) collective-permute-start(bf16[4,2,96,128]{3,2,1,0:T(8,128)(2,1)} %get-tuple-element.85), channel_id=1, source_target_pairs={{0,2},{2,0},{4,6},{6,4},{1,3},{3,1},{5,7},{7,5},{8,10},{10,8},{12,... | collective-permute-start | bytes 589832 | tf_op jit(solution)/shard_map/ppermute | solution.py:752
  52.9 16.2 %collective-permute-start.7 = (bf16[4,2,96,128]{3,2,1,0:T(8,128)(2,1)}, bf16[4,2,96,128]{3,2,1,0:T(8,128)(2,1)S(1)}, u32[]{:S(2)}, u32[]{:S(2)}) collective-permute-start(bf16[4,2,96,128]{3,2,1,0:T(8,128)(2,1)} %get-tuple-element.87), channel_id=1, source_target_pairs={{0,6},{2,4},{4,2},{6,0},{1,7},{3,5},{5,3},{7,1},{8,14},{10,12},{12... | collective-permute-start | bytes 589832 | tf_op jit(solution)/shard_map/ppermute | solution.py:752
  57.3 2.7 %copy-start.1 = (bf16[32,2,96,128]{3,2,1,0:T(8,128)(2,1)S(1)}, bf16[32,2,96,128]{3,2,1,0:T(8,128)(2,1)}, u32[]{:S(2)}) copy-start(bf16[32,2,96,128]{3,2,1,0:T(8,128)(2,1)} %copy-done) | copy-start | bytes 4718596
  60.0 19.8 %collective-permute-start = (bf16[8,2,96,128]{3,2,1,0:T(8,128)(2,1)S(1)}, bf16[8,2,96,128]{3,2,1,0:T(8,128)(2,1)S(1)}, u32[]{:S(2)}, u32[]{:S(2)}) collective-permute-start(bf16[8,2,96,128]{3,2,1,0:T(8,128)(2,1)S(1)} %slice.14), channel_id=1, source_target_pairs={{0,38},{1,39},{2,36},{3,37},{4,34},{5,35},{6,32},{7,33},{8,46},{9,... | collective-permute-start | bytes 1179656 | tf_op jit(solution)/shard_map/ppermute | solution.py:863
  64.7 28.2 %collective-permute-start.19 = (bf16[4,2,96,128]{3,2,1,0:T(8,128)(2,1)}, bf16[4,2,96,128]{3,2,1,0:T(8,128)(2,1)S(1)}, u32[]{:S(2)}, u32[]{:S(2)}) collective-permute-start(bf16[4,2,96,128]{3,2,1,0:T(8,128)(2,1)} %get-tuple-element.113), channel_id=1, source_target_pairs={{0,2},{2,0},{4,6},{6,4},{1,3},{3,1},{5,7},{7,5},{8,10},{10,8},{12,... | collective-permute-start | bytes 589832 | tf_op jit(solution)/shard_map/ppermute | solution.py:752
  65.3 27.5 %collective-permute-start.20 = (bf16[4,2,96,128]{3,2,1,0:T(8,128)(2,1)}, bf16[4,2,96,128]{3,2,1,0:T(8,128)(2,1)S(1)}, u32[]{:S(2)}, u32[]{:S(2)}) collective-permute-start(bf16[4,2,96,128]{3,2,1,0:T(8,128)(2,1)} %get-tuple-element.114), channel_id=1, source_target_pairs={{0,4},{2,6},{4,0},{6,2},{1,5},{3,7},{5,1},{7,3},{8,12},{10,14},{12... | collective-permute-start | bytes 589832 | tf_op jit(solution)/shard_map/ppermute | solution.py:752
  68.7 24.2 %collective-permute-start.21 = (bf16[4,2,96,128]{3,2,1,0:T(8,128)(2,1)}, bf16[4,2,96,128]{3,2,1,0:T(8,128)(2,1)S(1)}, u32[]{:S(2)}, u32[]{:S(2)}) collective-permute-start(bf16[4,2,96,128]{3,2,1,0:T(8,128)(2,1)} %get-tuple-element.115), channel_id=1, source_target_pairs={{0,6},{2,4},{4,2},{6,0},{1,7},{3,5},{5,3},{7,1},{8,14},{10,12},{12... | collective-permute-start | bytes 589832 | tf_op jit(solution)/shard_map/ppermute | solution.py:752
  84.7 31.3 %collective-permute-start.10 = (bf16[4,2,96,128]{3,2,1,0:T(8,128)(2,1)}, bf16[4,2,96,128]{3,2,1,0:T(8,128)(2,1)S(1)}, u32[]{:S(2)}, u32[]{:S(2)}) collective-permute-start(bf16[4,2,96,128]{3,2,1,0:T(8,128)(2,1)} %get-tuple-element.95.out_3), channel_id=1, source_target_pairs={{0,6},{2,4},{4,2},{6,0},{1,7},{3,5},{5,3},{7,1},{8,14},{10,12},{12... | collective-permute-start | bytes 589832 | tf_op jit(solution)/shard_map/ppermute | solution.py:752
  88.2 27.8 %collective-permute-start.8 = (bf16[4,2,96,128]{3,2,1,0:T(8,128)(2,1)}, bf16[4,2,96,128]{3,2,1,0:T(8,128)(2,1)}, u32[]{:S(2)}, u32[]{:S(2)}) collective-permute-start(bf16[4,2,96,128]{3,2,1,0:T(8,128)(2,1)} %get-tuple-element.93.out_1), channel_id=1, source_target_pairs={{0,2},{2,0},{4,6},{6,4},{1,3},{3,1},{5,7},{7,5},{8,10},{10,8},{12,... | collective-permute-start | bytes 589832 | tf_op jit(solution)/shard_map/ppermute | solution.py:752
  92.8 23.2 %collective-permute-start.9 = (bf16[4,2,96,128]{3,2,1,0:T(8,128)(2,1)}, bf16[4,2,96,128]{3,2,1,0:T(8,128)(2,1)}, u32[]{:S(2)}, u32[]{:S(2)}) collective-permute-start(bf16[4,2,96,128]{3,2,1,0:T(8,128)(2,1)} %get-tuple-element.94.out_2), channel_id=1, source_target_pairs={{0,4},{2,6},{4,0},{6,2},{1,5},{3,7},{5,1},{7,3},{8,12},{10,14},{12... | collective-permute-start | bytes 589832 | tf_op jit(solution)/shard_map/ppermute | solution.py:752
  99.4 26.9 %collective-permute-start.29 = (bf16[8,2,96,128]{3,2,1,0:T(8,128)(2,1)}, bf16[8,2,96,128]{3,2,1,0:T(8,128)(2,1)S(1)}, u32[]{:S(2)}, u32[]{:S(2)}) collective-permute-start(bf16[8,2,96,128]{3,2,1,0:T(8,128)(2,1)} %get-tuple-element.131), channel_id=1, source_target_pairs={{38,0},{39,1},{36,2},{37,3},{34,4},{35,5},{32,6},{33,7},{46,8},{47... | collective-permute-start | bytes 1179656 | tf_op jit(solution)/shard_map/ppermute | solution.py:877
  103.7 18.7 %copy-start.14 = (bf16[4,2,96,128]{3,2,1,0:T(8,128)(2,1)S(1)}, bf16[4,2,96,128]{3,2,1,0:T(8,128)(2,1)}, u32[]{:S(2)}) copy-start(bf16[4,2,96,128]{3,2,1,0:T(8,128)(2,1)} %get-tuple-element.92.refs_0_.out_0) | copy-start | bytes 589828
  116.7 13.9 %collective-permute-start.22 = (bf16[4,2,96,128]{3,2,1,0:T(8,128)(2,1)}, bf16[4,2,96,128]{3,2,1,0:T(8,128)(2,1)S(1)}, u32[]{:S(2)}, u32[]{:S(2)}) collective-permute-start(bf16[4,2,96,128]{3,2,1,0:T(8,128)(2,1)} %get-tuple-element.124), channel_id=1, source_target_pairs={{0,2},{2,0},{4,6},{6,4},{1,3},{3,1},{5,7},{7,5},{8,10},{10,8},{12,... | collective-permute-start | bytes 589832 | tf_op jit(solution)/shard_map/ppermute | solution.py:752
  120.0 16.0 %collective-permute-start.23 = (bf16[4,2,96,128]{3,2,1,0:T(8,128)(2,1)}, bf16[4,2,96,128]{3,2,1,0:T(8,128)(2,1)S(1)}, u32[]{:S(2)}, u32[]{:S(2)}) collective-permute-start(bf16[4,2,96,128]{3,2,1,0:T(8,128)(2,1)} %get-tuple-element.125), channel_id=1, source_target_pairs={{0,4},{2,6},{4,0},{6,2},{1,5},{3,7},{5,1},{7,3},{8,12},{10,14},{12... | collective-permute-start | bytes 589832 | tf_op jit(solution)/shard_map/ppermute | solution.py:752
  120.0 16.0 %collective-permute-start.24 = (bf16[4,2,96,128]{3,2,1,0:T(8,128)(2,1)}, bf16[4,2,96,128]{3,2,1,0:T(8,128)(2,1)S(1)}, u32[]{:S(2)}, u32[]{:S(2)}) collective-permute-start(bf16[4,2,96,128]{3,2,1,0:T(8,128)(2,1)} %get-tuple-element.126), channel_id=1, source_target_pairs={{0,6},{2,4},{4,2},{6,0},{1,7},{3,5},{5,3},{7,1},{8,14},{10,12},{12... | collective-permute-start | bytes 589832 | tf_op jit(solution)/shard_map/ppermute | solution.py:752
  126.2 9.9 %collective-permute-start.11 = (bf16[4,2,96,128]{3,2,1,0:T(8,128)(2,1)}, bf16[4,2,96,128]{3,2,1,0:T(8,128)(2,1)S(1)}, u32[]{:S(2)}, u32[]{:S(2)}) collective-permute-start(bf16[4,2,96,128]{3,2,1,0:T(8,128)(2,1)} %get-tuple-element.97), channel_id=1, source_target_pairs={{0,8},{8,0},{16,24},{24,16},{1,9},{9,1},{17,25},{25,17},{2,10},{10... | collective-permute-start | bytes 589832 | tf_op jit(solution)/shard_map/ppermute | solution.py:752
  126.3 10.4 %collective-permute-start.12 = (bf16[4,2,96,128]{3,2,1,0:T(8,128)(2,1)}, bf16[4,2,96,128]{3,2,1,0:T(8,128)(2,1)S(1)}, u32[]{:S(2)}, u32[]{:S(2)}) collective-permute-start(bf16[4,2,96,128]{3,2,1,0:T(8,128)(2,1)} %get-tuple-element.98), channel_id=1, source_target_pairs={{0,16},{8,24},{16,0},{24,8},{1,17},{9,25},{17,1},{25,9},{2,18},{10... | collective-permute-start | bytes 589832 | tf_op jit(solution)/shard_map/ppermute | solution.py:752
  130.6 8.1 %collective-permute-start.13 = (bf16[4,2,96,128]{3,2,1,0:T(8,128)(2,1)}, bf16[4,2,96,128]{3,2,1,0:T(8,128)(2,1)S(1)}, u32[]{:S(2)}, u32[]{:S(2)}) collective-permute-start(bf16[4,2,96,128]{3,2,1,0:T(8,128)(2,1)} %get-tuple-element.99), channel_id=1, source_target_pairs={{0,24},{8,16},{16,8},{24,0},{1,25},{9,17},{17,9},{25,1},{2,26},{10... | collective-permute-start | bytes 589832 | tf_op jit(solution)/shard_map/ppermute | solution.py:752
  136.0 2.6 %copy-start.10 = (bf16[4,2,96,128]{3,2,1,0:T(8,128)(2,1)}, bf16[4,2,96,128]{3,2,1,0:T(8,128)(2,1)S(1)}, u32[]{:S(2)}) copy-start(bf16[4,2,96,128]{3,2,1,0:T(8,128)(2,1)S(1)} %collective-permute-done.23.refs_2_.__2_) | copy-start | bytes 589828
  139.4 4.1 %copy-start.9 = (bf16[4,2,96,128]{3,2,1,0:T(8,128)(2,1)S(1)}, bf16[4,2,96,128]{3,2,1,0:T(8,128)(2,1)}, u32[]{:S(2)}) copy-start(bf16[4,2,96,128]{3,2,1,0:T(8,128)(2,1)} %copy-done.8) | copy-start | bytes 589828
  139.4 4.1 %copy-start.11 = (bf16[4,2,96,128]{3,2,1,0:T(8,128)(2,1)S(1)}, bf16[4,2,96,128]{3,2,1,0:T(8,128)(2,1)}, u32[]{:S(2)}) copy-start(bf16[4,2,96,128]{3,2,1,0:T(8,128)(2,1)} %copy-done.10) | copy-start | bytes 589828
  139.4 4.2 %copy-start.13 = (bf16[4,2,96,128]{3,2,1,0:T(8,128)(2,1)S(1)}, bf16[4,2,96,128]{3,2,1,0:T(8,128)(2,1)}, u32[]{:S(2)}) copy-start(bf16[4,2,96,128]{3,2,1,0:T(8,128)(2,1)} %copy-done.12) | copy-start | bytes 589828
  139.4 4.2 %copy-start.17 = (bf16[4,2,96,128]{3,2,1,0:T(8,128)(2,1)S(1)}, bf16[4,2,96,128]{3,2,1,0:T(8,128)(2,1)}, u32[]{:S(2)}) copy-start(bf16[4,2,96,128]{3,2,1,0:T(8,128)(2,1)} %get-tuple-element.123.refs_0_) | copy-start | bytes 589828
  139.4 43.4 %all-to-all-start.1 = ((bf16[32,2,96,128]{3,2,1,0:T(8,128)(2,1)}), bf16[32,2,96,128]{3,2,1,0:T(8,128)(2,1)S(1)}, u32[]{:S(2)}, u32[]{:S(2)}) async-start(bf16[32,2,96,128]{3,2,1,0:T(8,128)(2,1)} %after.7), calls=%async_computation.1 | async-start | bytes 3145728 | tf_op jit(solution)/shard_map/all_to_all | solution.py:832
  143.5 7.5 %copy-start.3 = (bf16[4,2,96,128]{3,2,1,0:T(8,128)(2,1)S(1)}, bf16[4,2,96,128]{3,2,1,0:T(8,128)(2,1)}, u32[]{:S(2)}) copy-start(bf16[4,2,96,128]{3,2,1,0:T(8,128)(2,1)} %copy-done.2) | copy-start | bytes 589828
  143.6 7.5 %copy-start.5 = (bf16[4,2,96,128]{3,2,1,0:T(8,128)(2,1)S(1)}, bf16[4,2,96,128]{3,2,1,0:T(8,128)(2,1)}, u32[]{:S(2)}) copy-start(bf16[4,2,96,128]{3,2,1,0:T(8,128)(2,1)} %copy-done.4) | copy-start | bytes 589828
  143.6 7.5 %copy-start.7 = (bf16[4,2,96,128]{3,2,1,0:T(8,128)(2,1)S(1)}, bf16[4,2,96,128]{3,2,1,0:T(8,128)(2,1)}, u32[]{:S(2)}) copy-start(bf16[4,2,96,128]{3,2,1,0:T(8,128)(2,1)} %copy-done.6) | copy-start | bytes 589828
  143.6 7.5 %copy-start.18 = (bf16[4,2,96,128]{3,2,1,0:T(8,128)(2,1)S(1)}, bf16[4,2,96,128]{3,2,1,0:T(8,128)(2,1)}, u32[]{:S(2)}) copy-start(bf16[4,2,96,128]{3,2,1,0:T(8,128)(2,1)} %get-tuple-element.96.refs_0_.part_0) | copy-start | bytes 589828
  146.3 16.3 %collective-permute-start.25 = (bf16[4,2,96,128]{3,2,1,0:T(8,128)(2,1)}, bf16[4,2,96,128]{3,2,1,0:T(8,128)(2,1)S(1)}, u32[]{:S(2)}, u32[]{:S(2)}) collective-permute-start(bf16[4,2,96,128]{3,2,1,0:T(8,128)(2,1)} %get-tuple-element.128), channel_id=1, source_target_pairs={{0,8},{8,0},{16,24},{24,16},{1,9},{9,1},{17,25},{25,17},{2,10},{10... | collective-permute-start | bytes 589832 | tf_op jit(solution)/shard_map/ppermute | solution.py:752
  148.1 22.4 %collective-permute-start.26 = (bf16[4,2,96,128]{3,2,1,0:T(8,128)(2,1)}, bf16[4,2,96,128]{3,2,1,0:T(8,128)(2,1)S(1)}, u32[]{:S(2)}, u32[]{:S(2)}) collective-permute-start(bf16[4,2,96,128]{3,2,1,0:T(8,128)(2,1)} %get-tuple-element.129), channel_id=1, source_target_pairs={{0,16},{8,24},{16,0},{24,8},{1,17},{9,25},{17,1},{25,9},{2,18},{10... | collective-permute-start | bytes 589832 | tf_op jit(solution)/shard_map/ppermute | solution.py:752
  150.9 19.7 %collective-permute-start.27 = (bf16[4,2,96,128]{3,2,1,0:T(8,128)(2,1)}, bf16[4,2,96,128]{3,2,1,0:T(8,128)(2,1)S(1)}, u32[]{:S(2)}, u32[]{:S(2)}) collective-permute-start(bf16[4,2,96,128]{3,2,1,0:T(8,128)(2,1)} %get-tuple-element.130), channel_id=1, source_target_pairs={{0,24},{8,16},{16,8},{24,0},{1,25},{9,17},{17,9},{25,1},{2,26},{10... | collective-permute-start | bytes 589832 | tf_op jit(solution)/shard_map/ppermute | solution.py:752
  151.1 19.5 %copy-start.19 = (bf16[4,2,96,128]{3,2,1,0:T(8,128)(2,1)S(1)}, bf16[4,2,96,128]{3,2,1,0:T(8,128)(2,1)}, u32[]{:S(2)}) copy-start(bf16[4,2,96,128]{3,2,1,0:T(8,128)(2,1)} %get-tuple-element.127.refs_0_.part_0) | copy-start | bytes 589828
  152.6 19.5 %collective-permute-start.14 = (bf16[4,4,96,128]{3,2,1,0:T(8,128)(2,1)}, bf16[4,4,96,128]{3,2,1,0:T(8,128)(2,1)S(1)}, u32[]{:S(2)}, u32[]{:S(2)}) collective-permute-start(bf16[4,4,96,128]{3,2,1,0:T(8,128)(2,1)} %other_core.2), channel_id=1, source_target_pairs={{0,1},{1,0},{2,3},{3,2},{4,5},{5,4},{6,7},{7,6},{8,9},{9,8},{10,11... | collective-permute-start | bytes 1179656 | tf_op jit(solution)/shard_map/ppermute | solution.py:793
  172.0 2.0 %collective-permute-start.28 = (bf16[4,4,96,128]{3,2,1,0:T(8,128)(2,1)}, bf16[4,4,96,128]{3,2,1,0:T(8,128)(2,1)S(1)}, u32[]{:S(2)}, u32[]{:S(2)}) collective-permute-start(bf16[4,4,96,128]{3,2,1,0:T(8,128)(2,1)} %other_core.3), channel_id=1, source_target_pairs={{0,1},{1,0},{2,3},{3,2},{4,5},{5,4},{6,7},{7,6},{8,9},{9,8},{10,11... | collective-permute-start | bytes 1179656 | tf_op jit(solution)/shard_map/ppermute | solution.py:793
  (14 other events, 16.2 us)
